TPU v7x, 32 devices: a whole 2x2x4 slice. The times are simulated.
32 devices in a mesh: dp: 8 (over z, x), mp: 4 (over y, core).
Axes of the slice: x: 2, y: 2, z: 4, core: 2. Of those that a mesh axis runs over, the one named last changes fastest.
Arguments:
- history: bfloat16 [128, 32, 1024], P('dp', None, 'mp'), may hold values from -6 to 6
- lengths: int32 [128], replicated, may hold values from 1 to 32, 2048 in all
- source: int32 [128], replicated, may hold values from 0 to 127, as said below
- owners: int32 [4096, 8], P(('dp', 'mp')), may hold values from 0 to 31, all different within a row; in each aligned block of 128 rows (0 to 127, 128 to 255, ...) at most 48 rows name the same one
- item_rows: int32 [4096, 8], P(('dp', 'mp')), may hold values from 0 to 511
- catalogue: bfloat16 [16384, 1024], P(('dp', 'mp')), may hold values from -6 to 6
- w_in: bfloat16 [4, 1024, 1024], P(None, None, 'mp'), may hold values from -0.1875 to 0.1875
- w_out: bfloat16 [1024, 1024], P('mp'), may hold values from -0.1875 to 0.1875
Outputs:
- w_in_grad: float32 [4, 1024, 1024], P(None, 'dp', 'mp')
- w_out_grad: float32 [1024, 1024], P('mp', 'dp')
- cat_grad: float32 [16384, 1024], P(('dp', 'mp'))
Inputs may be any that keep to these rules, and one draw needn't show every extreme that they name: `source`: a permutation; balanced slot k lies on index k // 16 of dp, and the 16 histories that start on one index of dp go to one index of dp at most (16 + 8 - 1) // 8 at a time, that many for some index. Each event names 8 different owners, column 0 the positive item's; the events of one device (aligned blocks of 128) name one owner at most 48 times.
All inputs are finite; a program needn't handle non-finite values.
Results may differ from a plain program's by a relative error of at most 0.017.
Values may be sent and summed in bfloat16 or wider, within the bound.
No kernel may reach another device: no remote copies, remote signals or barrier semaphores. Data moves between devices by JAX's collectives and lax.ppermute only.
A program may use at most 128 MiB of HBM per device.

v0:
```python
import jax
import jax.numpy as jnp
from jax import lax
from jax.sharding import PartitionSpec as P

DH = 128


cosine_divisor = 0.05
epsilon_norm = 1e-05
epsilon_unit = 1e-06


def normalize(rows_in):
    centered = rows_in - jnp.mean(rows_in, axis=-1, keepdims=True)
    spread = jnp.mean(centered * centered, axis=-1, keepdims=True)
    return centered / jnp.sqrt(spread + epsilon_norm)


def attend(projected, length_here):
    gating = projected[0]
    values = projected[1]
    queries = projected[2]
    key_rows = projected[3]
    steps_n = projected.shape[1]
    scores = jnp.einsum(
        "thd,shd->hts", queries, key_rows, preferred_element_type=jnp.float32
    ) / jnp.sqrt(jnp.float32(projected.shape[3]))
    places = jnp.arange(steps_n, dtype=jnp.int32)
    allowed = (places[None, :] <= places[:, None]) & (places[None, :] < length_here)
    weights = jnp.where(
        allowed[None], jax.nn.silu(scores) / length_here.astype(jnp.float32), 0.0
    ).astype(jnp.bfloat16)
    mixed_out = jnp.einsum("hts,shd->thd", weights, values, preferred_element_type=jnp.float32)
    return (normalize(mixed_out) * gating.astype(jnp.float32)).astype(jnp.bfloat16)


def loss_block(out_rows, valid_rows, fetched):
    out_norm = jnp.sqrt(jnp.sum(out_rows * out_rows, axis=-1, keepdims=True) + epsilon_unit)
    request_unit_vector = out_rows / out_norm
    item_f = fetched.astype(jnp.float32)
    item_norm = jnp.sqrt(jnp.sum(item_f * item_f, axis=-1, keepdims=True) + epsilon_unit)
    catalog_unit_vector = item_f / item_norm
    cosine_match_raw = (
        jnp.einsum("qn,qgn->qg", request_unit_vector, catalog_unit_vector) / cosine_divisor
    )
    expo = jnp.exp(cosine_match_raw)
    probs = expo / jnp.sum(expo, axis=-1, keepdims=True)
    column = jnp.arange(cosine_match_raw.shape[1], dtype=jnp.int32)
    exponent_shares = (probs - (column[None, :] == 0).astype(jnp.float32)) * valid_rows[
        :, None
    ].astype(jnp.float32)
    request_unit_vector_slope = (
        jnp.einsum("as,asy->ay", exponent_shares, catalog_unit_vector) / cosine_divisor
    )
    out_grad = (
        request_unit_vector_slope
        - request_unit_vector
        * jnp.sum(request_unit_vector * request_unit_vector_slope, axis=-1, keepdims=True)
    ) / out_norm
    catalog_unit_vector_slope = (
        exponent_shares[:, :, None] * request_unit_vector[:, None, :] / cosine_divisor
    )
    item_grad = (
        catalog_unit_vector_slope
        - catalog_unit_vector
        * jnp.sum(catalog_unit_vector * catalog_unit_vector_slope, axis=-1, keepdims=True)
    ) / item_norm
    return (out_grad, item_grad)


def silu_slope(preact):
    sigma = jax.nn.sigmoid(preact)
    return sigma * (1.0 + preact * (1.0 - sigma))


def earlier_same(labels):
    order_ids = jnp.arange(labels.shape[0], dtype=jnp.int32)
    same = (labels[None, :] == labels[:, None]) & (order_ids[None, :] < order_ids[:, None])
    return jnp.sum(same.astype(jnp.int32), axis=1)


def per_device(history, lengths, source, owners, item_rows, catalogue, w_in, w_out):
    dp_count = lax.axis_size("dp")
    mp_count = lax.axis_size("mp")
    dev_count = dp_count * mp_count
    here_dp = lax.axis_index("dp")
    here_mp = lax.axis_index("mp")
    seq_dev, steps_n, cols_here = history.shape
    seq_total = source.shape[0]
    per_peer = (seq_dev + dp_count - 1) // dp_count
    target = (
        jnp.zeros((seq_total,), jnp.int32).at[source].set(jnp.arange(seq_total, dtype=jnp.int32))
    )
    slot_ids = jnp.arange(seq_dev, dtype=jnp.int32)
    my_seqs = here_dp * seq_dev + slot_ids
    dest_dev = target[my_seqs] // seq_dev
    send_rank = earlier_same(dest_dev)
    outgoing = (
        jnp.zeros((dp_count, per_peer, steps_n, cols_here), jnp.bfloat16)
        .at[dest_dev, send_rank]
        .set(history)
    )
    arrived = lax.all_to_all(outgoing, "dp", split_axis=0, concat_axis=0, tiled=True)
    taken = source[my_seqs]
    anchor = taken // seq_dev
    anchor_block = anchor[:, None] * seq_dev + slot_ids[None, :]
    goes_here = target[anchor_block] // seq_dev == here_dp
    earlier = slot_ids[None, :] < (taken % seq_dev)[:, None]
    recv_rank = jnp.sum((goes_here & earlier).astype(jnp.int32), axis=1)
    counts = lengths[taken]
    local_rows = jnp.take(
        arrived.reshape(dp_count * per_peer, steps_n, cols_here),
        anchor * per_peer + recv_rank,
        axis=0,
    )
    features = lax.all_gather(local_rows, "mp", axis=2, tiled=True)
    rows_all = seq_dev * steps_n
    width = features.shape[2]
    flat_rows = features.reshape(rows_all, width)
    normed = normalize(flat_rows.astype(jnp.float32)).astype(jnp.bfloat16)
    preact = jnp.einsum("rd,cdh->crh", normed, w_in, preferred_element_type=jnp.float32)
    projected = jax.nn.silu(preact).astype(jnp.bfloat16)
    cols_heads = w_in.shape[2]
    heads_here = cols_heads // DH
    grouped = projected.reshape(4, seq_dev, steps_n, heads_here, DH)

    def run_all(inputs):
        return jax.vmap(attend, in_axes=(1, 0))(inputs, counts)

    gated, back = jax.vjp(run_all, grouped)
    gated_flat = gated.reshape(rows_all, cols_heads)
    partial_out = jnp.dot(gated_flat, w_out, preferred_element_type=jnp.float32)
    quarter = rows_all // mp_count
    out_rows = lax.psum_scatter(partial_out, "mp", scatter_dimension=0, tiled=True)
    out_rows = out_rows + lax.dynamic_slice_in_dim(flat_rows, here_mp * quarter, quarter, 0).astype(
        jnp.float32
    )
    position = here_mp * quarter + jnp.arange(quarter, dtype=jnp.int32)
    valid_rows = position % steps_n < counts[position // steps_n]
    top_n = owners.shape[1]
    asks = quarter * top_n
    capacity = max(2, (3 * asks + 2 * dev_count - 1) // (2 * dev_count))
    owner_flat = owners.reshape(-1)
    row_flat = item_rows.reshape(-1)
    rank_in = earlier_same(owner_flat)
    address = owner_flat * capacity + rank_in
    slot_table = (
        jnp.full((dev_count * capacity,), asks, jnp.int32)
        .at[address]
        .set(jnp.arange(asks, dtype=jnp.int32))
    )
    is_used = slot_table < asks
    safe_index = jnp.minimum(slot_table, asks - 1)
    wanted = jnp.where(is_used, row_flat[safe_index], 0).reshape(dp_count, mp_count, capacity)
    incoming = lax.all_to_all(
        lax.all_to_all(wanted, "dp", split_axis=0, concat_axis=0, tiled=True),
        "mp",
        split_axis=1,
        concat_axis=1,
        tiled=True,
    )
    incoming_flat = incoming.reshape(-1)
    looked = jnp.take(catalogue, incoming_flat, axis=0).reshape(dp_count, mp_count, capacity, width)
    returned = lax.all_to_all(
        lax.all_to_all(looked, "dp", split_axis=0, concat_axis=0, tiled=True),
        "mp",
        split_axis=1,
        concat_axis=1,
        tiled=True,
    )
    fetched = jnp.take(returned.reshape(dev_count * capacity, width), address, axis=0).reshape(
        quarter, top_n, width
    )
    out_grad, item_grad = loss_block(out_rows, valid_rows, fetched)
    item_flat = item_grad.reshape(asks, width)
    sending = jnp.where(is_used[:, None], jnp.take(item_flat, safe_index, axis=0), 0.0)
    landed = lax.all_to_all(
        lax.all_to_all(
            sending.reshape(dp_count, mp_count, capacity, width).astype(jnp.bfloat16),
            "dp",
            split_axis=0,
            concat_axis=0,
            tiled=True,
        ),
        "mp",
        split_axis=1,
        concat_axis=1,
        tiled=True,
    ).astype(jnp.float32)
    cat_grad = (
        jnp.zeros((catalogue.shape[0], width), jnp.float32)
        .at[incoming_flat]
        .add(landed.reshape(-1, width))
    )
    out_cotangent = lax.all_gather(out_grad.astype(jnp.bfloat16), "mp", axis=0, tiled=True)
    w_out_part = jnp.einsum(
        "rh,rd->hd", gated_flat, out_cotangent, preferred_element_type=jnp.float32
    )
    gated_cotangent = jnp.einsum(
        "rd,hd->rh", out_cotangent, w_out, preferred_element_type=jnp.float32
    ).astype(jnp.bfloat16)
    (grouped_cotangent,) = back(gated_cotangent.reshape(seq_dev, steps_n, heads_here, DH))
    projected_cotangent = grouped_cotangent.reshape(4, rows_all, cols_heads)
    preact_cotangent = (projected_cotangent.astype(jnp.float32) * silu_slope(preact)).astype(
        jnp.bfloat16
    )
    w_in_part = jnp.einsum(
        "rd,crh->cdh", normed, preact_cotangent, preferred_element_type=jnp.float32
    )
    w_in_grad, w_out_grad = (
        lax.psum_scatter(w_in_part, "dp", scatter_dimension=1, tiled=True),
        lax.psum_scatter(w_out_part, "dp", scatter_dimension=1, tiled=True),
    )
    return (w_in_grad, w_out_grad, cat_grad)


def solution(mesh):
    placed = (
        P("dp", None, "mp"),
        P(),
        P(),
        P(("dp", "mp"), None),
        P(("dp", "mp"), None),
        P(("dp", "mp"), None),
        P(None, None, "mp"),
        P("mp", None),
    )
    return jax.shard_map(
        per_device,
        mesh=mesh,
        in_specs=placed,
        out_specs=(P(None, "dp", "mp"), P("mp", "dp"), P(("dp", "mp"), None)),
        check_vma=False,
    )
```

profile of v0, /device:TPU:13, one launch (start us, length us, event | category | flops | bytes accessed | tf_op | source)
XLA Modules:
  0.0 445.8 jit_solution(11529903387103644689)
XLA Ops:
  10.6 2.9 scatter_fusion
  13.5 5.7 %all-to-all-start = ((bf16[8,2,32,256]{3,2,1,0:T(8,128)(2,1)}), bf16[8,2,32,256]{3,2,1,0:T(8,128)(2,1)S(1)}, u32[]{:S(2)}, u32[]{:S(2)}) async-start(bf16[8,2,32,256]{3,2,1,0:T(8,128)(2,1)} %scatter_fusion), calls=%async_computation | async-start | bytes 524288 | tf_op jit(solution)/shard_map/all_to_all | solution.py:104
  20.3 1.9 gather_fusion.2
  22.9 4.3 scatter_custom_fusion.2
  27.7 5.9 %gather_fusion.5 = s32[1536]{0:T(1024)S(1)} fusion(s32[1024]{0:T(1024)S(1)} %reshape.657, s32[2048]{0:T(1024)S(1)} %pad_clamp_fusion.1), kind=kCustom, calls=%fused_computation.5 | custom fusion | bytes 18432 | tf_op jit(solution)/shard_map/gather | solution.py:155
  34.3 1.5 gather_fusion.4
  38.0 5.4 %all-to-all-start.1 = ((s32[8,1,192]{2,1,0:T(1,128)}), s32[8,1,192]{2,1,0:T(1,128)S(1)}, u32[]{:S(2)}, u32[]{:S(2)}) async-start(s32[8,1,192]{2,1,0:T(1,128)} %reshape.854), calls=%async_computation.2 | async-start | bytes 16384 | tf_op jit(solution)/shard_map/all_to_all | solution.py:157
  44.2 3.4 all-to-all-done.1
  49.5 6.0 %all-to-all-start.2 = ((s32[4,1,384]{2,1,0:T(1,128)}), s32[4,1,384]{2,1,0:T(1,128)S(1)}, u32[]{:S(2)}, u32[]{:S(2)}) async-start(s32[4,1,384]{2,1,0:T(1,128)} %reshape.856), calls=%async_computation.3 | async-start | bytes 12288 | tf_op jit(solution)/shard_map/all_to_all | solution.py:156
  58.0 5.9 %gather_fusion.6 = bf16[1536,1024]{1,0:T(8,128)(2,1)} fusion(bf16[512,1024]{1,0:T(8,128)(2,1)S(1)} %copy-done.2, s32[2048]{0:T(1024)S(1)} %pad_clamp_fusion), kind=kCustom, calls=%fused_computation.6 | custom fusion | bytes 6297600 | tf_op jit(solution)/shard_map/jit(_take)/gather | solution.py:164
  63.9 3.3 broadcast_select_fusion
  67.2 5.6 %all-to-all-start.3 = ((bf16[8,4,48,1024]{3,2,1,0:T(8,128)(2,1)}), bf16[8,4,48,1024]{3,2,1,0:T(8,128)(2,1)}, u32[]{:S(2)}, u32[]{:S(2)}) async-start(bf16[8,4,48,1024]{3,2,1,0:T(8,128)(2,1)} %broadcast_select_fusion), calls=%async_computation.4 | async-start | bytes 6291456 | tf_op jit(solution)/shard_map/all_to_all | solution.py:166
  72.8 1.5 convert_reduce_fusion.1
  74.4 1.7 fusion.12
  76.1 2.8 fusion.16
  83.0 1.7 fusion.53
  84.8 57.0 %all-to-all-done.3 = bf16[8,4,48,1024]{3,2,1,0:T(8,128)(2,1)} async-done(((bf16[8,4,48,1024]{3,2,1,0:T(8,128)(2,1)}), bf16[8,4,48,1024]{3,2,1,0:T(8,128)(2,1)}, u32[]{:S(2)}, u32[]{:S(2)}) %all-to-all-start.3) | async-done | bytes 3145760 | tf_op jit(solution)/shard_map/all_to_all | solution.py:166
  141.8 4.0 copy.130
  145.8 6.8 %all-to-all-start.4 = ((bf16[8,4,48,1024]{3,2,0,1:T(8,128)(2,1)}), bf16[8,4,48,1024]{3,2,0,1:T(8,128)(2,1)}, u32[]{:S(2)}, u32[]{:S(2)}) async-start(bf16[8,4,48,1024]{3,2,0,1:T(8,128)(2,1)} %copy.130), calls=%async_computation.5 | async-start | bytes 6291456 | tf_op jit(solution)/shard_map/all_to_all | solution.py:165
  154.0 10.3 %compare_convert_fusion = f32[128]{0:T(128)} fusion(s32[]{:T(128)} %bitcast.39, s32[]{:T(128)} %bitcast.40, s32[]{:T(128)} %bitcast.41, s32[]{:T(128)} %bitcast.42, s32[]{:T(128)} %bitcast.43, s32[]{:T(128)} %bitcast.45, s32[]{:T(128)} %bitcast.44, s32[]{:T(128)} %bitcast.22, s32[]{:T(128)} %bitcast.24, s32[]{:T(128)} %bitcast.26, s32[]{:T(128)} %bitcast.28, ...), kind=kLoop, calls=%fused_computation.193 | loop fusion | flops 8064 | bytes 580 | tf_op jit(solution)/shard_map/convert_element_type | solution.py:52
  164.4 1.2 multiply_reduce_fusion.2
  165.6 2.0 fusion.49
  167.6 20.1 %all-to-all-done.4 = bf16[8,4,48,1024]{3,2,0,1:T(8,128)(2,1)} async-done(((bf16[8,4,48,1024]{3,2,0,1:T(8,128)(2,1)}), bf16[8,4,48,1024]{3,2,0,1:T(8,128)(2,1)}, u32[]{:S(2)}, u32[]{:S(2)}) %all-to-all-start.4) | async-done | bytes 3145760 | tf_op jit(solution)/shard_map/all_to_all | solution.py:165
  187.7 2.3 copy.131
  190.0 5.3 %gather_fusion.7 = bf16[1024,1024]{1,0:T(8,128)(2,1)} fusion(bf16[1536,1024]{1,0:T(8,128)(2,1)S(1)} %bitcast.237, s32[1024]{0:T(1024)S(1)} %broadcast_clamp_fusion), kind=kCustom, calls=%fused_computation.7 | custom fusion | bytes 4198400 | tf_op jit(solution)/shard_map/jit(_take)/gather | solution.py:172
  195.4 2.5 fusion.2
  198.0 2.7 fusion.10
  203.2 17.5 %all-gather.5.cloned.1.call-done = bf16[512,1024]{1,0:T(8,128)(2,1)} async-done(((bf16[128,1024]{1,0:T(8,128)(2,1)}), bf16[512,1024]{1,0:T(8,128)(2,1)}) %all-gather.5.cloned.1.call-update) | async-done | bytes 1048592 | tf_op jit(solution)/shard_map/all_gather | solution.py:196
  220.7 2.6 fusion.26
  223.3 2.1 reshape.664
  225.4 1.8 multiply_reduce_fusion
  227.3 1.9 fusion.87
  231.3 3.3 copy.140
  234.6 3.9 reshape.665
  238.5 6.4 %convolution_bitcast_fusion = f32[4,1024,256]{1,2,0:T(8,128)} fusion(f32[4,512,256]{2,1,0:T(8,128)} %reshape.665, f32[512,4,256]{2,0,1:T(8,128)} %get-tuple-element.54, bf16[512,1024]{1,0:T(8,128)(2,1)} %bitcast.242, f32[512]{0:T(512)S(1)} %copy-done.41, f32[512]{0:T(512)S(1)} %copy-done.39), kind=kOutput, calls=%fused_computation.34 | convolution fusion | flops 1080557568 | bytes 9441280 | tf_op jit(solution)/shard_map/rd,crh->cdh/dot_general | solution.py:208
  245.9 1.7 fusion.7
  247.6 1.7 fusion.6
  249.3 5.8 %gather_fusion.8 = bf16[1536,1024]{1,0:T(8,128)(2,1)} fusion(bf16[1024,1024]{1,0:T(8,128)(2,1)S(1)} %fusion.6, s32[2048]{0:T(1024)S(1)} %pad_clamp_fusion.1), kind=kCustom, calls=%fused_computation.8 | custom fusion | bytes 6297600 | tf_op jit(solution)/shard_map/jit(_take)/gather | solution.py:177
  255.0 2.4 select_convert_fusion
  257.4 104.5 %all_to_all.35 = bf16[8,4,48,1024]{3,2,1,0:T(8,128)(2,1)S(1)} all-to-all(bf16[8,4,48,1024]{3,2,1,0:T(8,128)(2,1)S(1)} %select_convert_fusion), channel_id=1, replica_groups=mesh['dp'=8,'mp'=4] {'dp'}, dimensions={0} | all-to-all | bytes 6291456 | tf_op jit(solution)/shard_map/all_to_all | solution.py:179
  361.9 2.2 copy.142
  364.1 4.8 %all-to-all-start.6 = ((bf16[8,4,48,1024]{3,2,0,1:T(8,128)(2,1)}), bf16[8,4,48,1024]{3,2,0,1:T(8,128)(2,1)S(1)}, u32[]{:S(2)}, u32[]{:S(2)}) async-start(bf16[8,4,48,1024]{3,2,0,1:T(8,128)(2,1)} %copy.142), calls=%async_computation.9 | async-start | bytes 6291456 | tf_op jit(solution)/shard_map/all_to_all | solution.py:178
  368.9 2.7 fusion.51
  371.6 32.4 %all-to-all-done.6 = bf16[8,4,48,1024]{3,2,0,1:T(8,128)(2,1)S(1)} async-done(((bf16[8,4,48,1024]{3,2,0,1:T(8,128)(2,1)}), bf16[8,4,48,1024]{3,2,0,1:T(8,128)(2,1)S(1)}, u32[]{:S(2)}, u32[]{:S(2)}) %all-to-all-start.6) | async-done | bytes 3145760 | tf_op jit(solution)/shard_map/all_to_all | solution.py:178
  404.0 2.1 copy.143
  406.1 15.4 %scatter_custom_fusion.3 = f32[512,1024]{1,0:T(8,128)} fusion(s32[1536]{0:T(1024)S(1)} %fusion.72, bf16[1536,1024]{1,0:T(8,128)(2,1)} %bitcast.239, f32[]{:T(128)} %constant.182.clone.1), kind=kCustom, calls=%fused_computation.13 | custom fusion | flops 3145728 | bytes 5242884 | tf_op jit(solution)/shard_map/scatter-add | solution.py:194
  421.5 2.0 copy.144
  423.5 15.7 %reduce-scatter.8.cloned.1.call-done = f32[256,128]{1,0:T(8,128)} async-done(((f32[256,1024]{1,0:T(8,128)}), f32[256,128]{1,0:T(8,128)}) %reduce-scatter.8.cloned.1.call-update) | async-done | bytes 131088 | tf_op jit(solution)/shard_map/reduce_scatter | solution.py:213
  (203 shorter events, 24.7 us)
Async XLA Ops:
  7.2 69.0 %copy-start = (bf16[4,1024,256]{2,1,0:T(8,128)(2,1)S(1)}, bf16[4,1024,256]{2,1,0:T(8,128)(2,1)}, u32[]{:S(2)}) copy-start(bf16[4,1024,256]{2,1,0:T(8,128)(2,1)} %param.14) | copy-start | bytes 6291460
  7.2 12.0 %copy-start.3 = (s32[128]{0:T(128)S(1)}, s32[128]{0:T(128)}, u32[]{:S(2)}) copy-start(s32[128]{0:T(128)} %param.10) | copy-start | bytes 1540
  7.2 12.7 %copy-start.33 = (s32[128,8]{0,1:T(8,128)S(1)}, s32[128,8]{0,1:T(8,128)}, u32[]{:S(2)}) copy-start(s32[128,8]{0,1:T(8,128)} %param.11) | copy-start | bytes 12292
  13.5 20.1 %all-to-all-start = ((bf16[8,2,32,256]{3,2,1,0:T(8,128)(2,1)}), bf16[8,2,32,256]{3,2,1,0:T(8,128)(2,1)S(1)}, u32[]{:S(2)}, u32[]{:S(2)}) async-start(bf16[8,2,32,256]{3,2,1,0:T(8,128)(2,1)} %scatter_fusion), calls=%async_computation | async-start | bytes 524288 | tf_op jit(solution)/shard_map/all_to_all | solution.py:104
  19.2 53.5 %all-gather.3.cloned.1.call-start = ((), (), s32[]{:S(2)}) async-start(), calls=%async_computation.10 | async-start | bytes 1310720 | tf_op jit(solution)/shard_map/all_gather | solution.py:117
  20.1 2.2 copy-start.26
  20.3 7.0 %copy-start.34 = (s32[128,8]{0,1:T(8,128)S(1)}, s32[128,8]{0,1:T(8,128)}, u32[]{:S(2)}) copy-start(s32[128,8]{0,1:T(8,128)} %param.12) | copy-start | bytes 12292
  22.9 4.3 copy-start.28
  27.7 15.8 %copy-start.4 = (s32[128]{0:T(128)S(1)}, s32[128]{0:T(128)}, u32[]{:S(2)}) copy-start(s32[128]{0:T(128)} %param.9) | copy-start | bytes 1540
  33.5 24.5 %copy-start.2 = (bf16[512,1024]{1,0:T(8,128)(2,1)S(1)}, bf16[512,1024]{1,0:T(8,128)(2,1)}, u32[]{:S(2)}) copy-start(bf16[512,1024]{1,0:T(8,128)(2,1)} %param.13) | copy-start | bytes 3145732
  38.0 9.6 %all-to-all-start.1 = ((s32[8,1,192]{2,1,0:T(1,128)}), s32[8,1,192]{2,1,0:T(1,128)S(1)}, u32[]{:S(2)}, u32[]{:S(2)}) async-start(s32[8,1,192]{2,1,0:T(1,128)} %reshape.854), calls=%async_computation.2 | async-start | bytes 16384 | tf_op jit(solution)/shard_map/all_to_all | solution.py:157
  49.5 7.6 %all-to-all-start.2 = ((s32[4,1,384]{2,1,0:T(1,128)}), s32[4,1,384]{2,1,0:T(1,128)S(1)}, u32[]{:S(2)}, u32[]{:S(2)}) async-start(s32[4,1,384]{2,1,0:T(1,128)} %reshape.856), calls=%async_computation.3 | async-start | bytes 12288 | tf_op jit(solution)/shard_map/all_to_all | solution.py:156
  56.2 23.3 %copy-start.43 = (f32[16]{0:T(128)}, f32[16]{0:T(128)S(1)}, u32[]{:S(2)}) copy-start(f32[16]{0:T(128)S(1)} %convert_element_type.130) | copy-start | bytes 196
  67.2 74.6 %all-to-all-start.3 = ((bf16[8,4,48,1024]{3,2,1,0:T(8,128)(2,1)}), bf16[8,4,48,1024]{3,2,1,0:T(8,128)(2,1)}, u32[]{:S(2)}, u32[]{:S(2)}) async-start(bf16[8,4,48,1024]{3,2,1,0:T(8,128)(2,1)} %broadcast_select_fusion), calls=%async_computation.4 | async-start | bytes 6291456 | tf_op jit(solution)/shard_map/all_to_all | solution.py:166
  72.8 91.6 %reduce-scatter.4.cloned.1.call-start = ((), (), s32[]{:S(2)}) async-start(), calls=%async_computation.11 | async-start | bytes 2621440 | tf_op jit(solution)/shard_map/reduce_scatter | solution.py:135
  72.8 3.4 copy-start.11
  74.4 4.6 %copy-start.38 = (f32[512]{0:T(512)}, f32[512]{0:T(512)S(1)}, u32[]{:S(2)}) copy-start(f32[512]{0:T(512)S(1)} %div.230) | copy-start | bytes 6148
  76.1 2.8 copy-start.40
  79.1 1.8 copy-start.18
  79.2 1.7 copy-start.13
  79.3 1.6 copy-start.15
  79.8 2.6 copy-start.10
  80.9 3.8 copy-start.20
  80.9 2.1 copy-start.12
  145.8 18.6 %copy-start.29 = (s32[1024,1]{0,1:T(1,128)S(1)}, s32[1024,1]{0,1:T(1,128)}, u32[]{:S(2)}) copy-start(s32[1024,1]{0,1:T(1,128)} %copy-done.28) | copy-start | bytes 12292
  145.8 41.9 %all-to-all-start.4 = ((bf16[8,4,48,1024]{3,2,0,1:T(8,128)(2,1)}), bf16[8,4,48,1024]{3,2,0,1:T(8,128)(2,1)}, u32[]{:S(2)}, u32[]{:S(2)}) async-start(bf16[8,4,48,1024]{3,2,0,1:T(8,128)(2,1)} %copy.130), calls=%async_computation.5 | async-start | bytes 6291456 | tf_op jit(solution)/shard_map/all_to_all | solution.py:165
  152.6 68.1 %all-gather.5.cloned.1.call-start = ((), (), s32[]{:S(2)}) async-start(), calls=%async_computation.12 | async-start | bytes 1310720 | tf_op jit(solution)/shard_map/all_gather | solution.py:196
  152.7 14.9 %copy-start.22 = (pred[128,8]{1,0:T(8,128)(4,1)}, pred[128,8]{1,0:T(8,128)(4,1)S(1)}, u32[]{:S(2)}) copy-start(pred[128,8]{1,0:T(8,128)(4,1)S(1)} %compare_and_fusion) | copy-start | bytes 3076
  152.8 42.5 %copy-start.30 = (pred[1024]{0:T(1024)(128)(4,1)}, pred[1024]{0:T(1024)(128)(4,1)S(1)}, u32[]{:S(2)}) copy-start(pred[1024]{0:T(1024)(128)(4,1)S(1)} %broadcast_in_dim.164) | copy-start | bytes 3076
  165.6 24.4 %copy-start.35 = (f32[128]{0:T(128)}, f32[128]{0:T(128)S(1)}, u32[]{:S(2)}) copy-start(f32[128]{0:T(128)S(1)} %add_sqrt_fusion.2) | copy-start | bytes 1540
  195.4 2.6 copy-start.5
  195.4 2.6 copy-start.23
  198.0 2.8 copy-start.37
  198.0 2.8 copy-start.42
  201.0 1.3 copy-start.36
  202.2 23.2 %copy-start.8 = (f32[16,32,2,128]{3,1,2,0:T(8,128)S(1)}, f32[16,32,2,128]{3,1,2,0:T(8,128)}, u32[]{:S(2)}) copy-start(f32[16,32,2,128]{3,1,2,0:T(8,128)} %copy-done.7) | copy-start | bytes 1572868
  203.1 218.4 %reduce-scatter.6.cloned.1.call-start = ((), (), s32[]{:S(2)}) async-start(), calls=%async_computation.13 | async-start | bytes 4718592 | tf_op jit(solution)/shard_map/reduce_scatter | solution.py:212
  225.4 3.8 copy-start.21
  227.2 2.5 copy-start.19
  227.2 2.5 copy-start.25
  227.2 2.5 copy-start.44
  227.2 2.5 copy-start.45
  234.6 3.9 copy-start.39
  234.6 3.9 copy-start.41
  245.8 1.7 copy-start.6
  364.1 39.9 %all-to-all-start.6 = ((bf16[8,4,48,1024]{3,2,0,1:T(8,128)(2,1)}), bf16[8,4,48,1024]{3,2,0,1:T(8,128)(2,1)S(1)}, u32[]{:S(2)}, u32[]{:S(2)}) async-start(bf16[8,4,48,1024]{3,2,0,1:T(8,128)(2,1)} %copy.142), calls=%async_computation.9 | async-start | bytes 6291456 | tf_op jit(solution)/shard_map/all_to_all | solution.py:178
  368.9 70.3 %reduce-scatter.8.cloned.1.call-start = ((), (), s32[]{:S(2)}) async-start(), calls=%async_computation.14 | async-start | bytes 1179648 | tf_op jit(solution)/shard_map/reduce_scatter | solution.py:213
  406.1 33.1 %copy-start.1 = (bf16[4,1024,256]{2,1,0:T(8,128)(2,1)S(1)}, bf16[4,1024,256]{2,1,0:T(8,128)(2,1)}, u32[]{:S(2)}) copy-start(bf16[4,1024,256]{2,1,0:T(8,128)(2,1)} %param.14) | copy-start | bytes 6291460
  (9 other events, 8.1 us)
Sparse Core Ops, SparseCore 0:
  36.8 17.7 all-gather.2
  84.9 32.1 reduce-scatter.3
  203.3 17.3 all-gather.4
  245.1 128.2 reduce-scatter.5
  377.3 61.9 reduce-scatter.7
where the time goes:
time: 451 us; the launch traced here: 446 us
  waiting for transfers between devices  147 us (33%)
  blocking collectives  105 us (23%)
  local copies, waits for them, and re-layouts  66.1 us (15%)
  other arithmetic  56.2 us (12%)
  starting transfers between devices  34.3 us (8%)
  matrix products  22.9 us (5%)
  between operations  14.7 us (3%)
    all_to_all x1, blocking collectives, per_device(): lax.all_to_all(sending.reshape(dp_count, mp_count, capacity, width).astyp...  105 us
    all_to_all x1, waiting for transfers between devices, per_device(): lax.all_to_all(looked, 'dp', split_axis=0, concat_axis=0, tiled=True)  57 us
    all_to_all x1, waiting for transfers between devices, per_device(): lax.all_to_all(lax.all_to_all(sending.reshape(dp_count, mp_count, capacit...  32.4 us
    all_to_all x1, waiting for transfers between devices, per_device(): lax.all_to_all(lax.all_to_all(looked, 'dp', split_axis=0, concat_axis=0,...  20.1 us
    all_gather x1, waiting for transfers between devices, per_device(): lax.all_gather(out_grad.astype(jnp.bfloat16), 'mp', axis=0, tiled=True)  17.5 us
    reduce_scatter x1, waiting for transfers between devices, per_device(): lax.psum_scatter(w_out_part, 'dp', scatter_dimension=1, tiled=True)  15.7 us
    scatter-add x1, other arithmetic, per_device(): cat_grad = jnp.zeros((catalogue.shape[0], width), jnp.float32).at[incomin...  15.4 us
    convert_element_type x1, other arithmetic, loss_block(): exponent_shares = (probs - (column[None, :] == 0).astype(jnp.float32)) *...  10.3 us
  transfers between devices with their start and end apart: 11, of which 7 were waited for; matrix products, arithmetic and copies ran while one was open for 21% of the time, Pallas kernels for 0%

commit v1 on v0

v1 whole, which is shorter than its diff:
```python
import functools
import math

import jax
import jax.numpy as jnp
from jax import lax
from jax.experimental import pallas as pl
from jax.experimental.pallas import tpu as pltpu
from jax.sharding import PartitionSpec as P

DH = 128
COSINE_DIVISOR = 0.05
EPS_NORM = 1e-05
EPS_UNIT = 1e-06
BF = jnp.bfloat16
F32 = jnp.float32
I32 = jnp.int32
BLOCK = 128

VM = pl.BlockSpec(memory_space=pltpu.VMEM)
SM = pl.BlockSpec(memory_space=pltpu.SMEM)


def call(body, out_shape, in_specs, flops, nbytes, scratch=(), trans=0):
    many = isinstance(out_shape, (list, tuple))
    return pl.pallas_call(
        body,
        out_shape=out_shape,
        in_specs=in_specs,
        out_specs=[VM] * len(out_shape) if many else VM,
        scratch_shapes=list(scratch),
        compiler_params=pltpu.CompilerParams(vmem_limit_bytes=48 * 1024 * 1024),
        cost_estimate=pl.CostEstimate(
            flops=int(flops), bytes_accessed=int(nbytes), transcendentals=int(trans)
        ),
    )


def dot_nt(a, b):
    return lax.dot_general(a, b, (((1,), (1,)), ((), ())), preferred_element_type=F32)


def dot_tn(a, b):
    return lax.dot_general(a, b, (((0,), (0,)), ((), ())), preferred_element_type=F32)


def dot_nn(a, b):
    return jnp.dot(a, b, preferred_element_type=F32)


def iota(shape, dim):
    return lax.broadcasted_iota(I32, shape, dim)


def pack_kernel(source, place, hist, out, *, dp, seq_dev, per_peer):
    here = place[0]

    def per_dest(d, carry):
        def per_slot(i, count):
            src = source[d * seq_dev + i]
            hit = lax.div(src, seq_dev) == here

            @pl.when(hit)
            def _():
                out[d * per_peer + count] = hist[src - here * seq_dev]

            return count + hit.astype(I32)

        lax.fori_loop(0, seq_dev, per_slot, jnp.int32(0))
        return carry

    lax.fori_loop(0, dp, per_dest, jnp.int32(0))


def forward_kernel(
    source, lengths, place, *refs, mp, seq_dev, per_peer, steps, width, cols, quarter
):
    blocks = refs[:mp]
    w_in = refs[mp]
    normed_t, projected, slope, weights_o, dscale, norm_o, inv_o, gated, gated_t, own = refs[
        mp + 1 : mp + 11
    ]
    feat = refs[mp + 11]
    here_dp = place[0]
    here_mp = place[1]
    part = width // mp
    sources = [source[here_dp * seq_dev + k] for k in range(seq_dev)]
    anchors = [lax.div(s, seq_dev) for s in sources]
    counts = [lengths[s] for s in sources]
    for k in range(seq_dev):
        rank = jnp.int32(0)
        for earlier in range(k):
            rank = rank + (anchors[earlier] == anchors[k]).astype(I32)
        slot = anchors[k] * per_peer + rank
        for j in range(mp):
            start = pl.multiple_of(jnp.bitwise_xor(here_mp, j) * part, part)
            feat[k * steps : (k + 1) * steps, pl.ds(start, part)] = blocks[j][slot]
    rows_all = seq_dev * steps
    own[...] = feat[pl.ds(pl.multiple_of(here_mp * quarter, quarter), quarter), :]
    normed = []
    for g in range(rows_all // BLOCK):
        rows = slice(g * BLOCK, (g + 1) * BLOCK)
        x = feat[rows, :].astype(F32)
        centered = x - jnp.mean(x, axis=-1, keepdims=True)
        spread = jnp.mean(centered * centered, axis=-1, keepdims=True)
        y = (centered * lax.rsqrt(spread + EPS_NORM)).astype(BF)
        feat[rows, :] = y
        normed_t[:, rows] = y.T
    for c in range(4):
        pre = dot_nn(feat[...], w_in[c])
        sigma = jax.nn.sigmoid(pre)
        projected[c] = (pre * sigma).astype(BF)
        slope[c] = sigma * (1.0 + pre * (1.0 - sigma))
    root = 1.0 / math.sqrt(DH)
    t_id = iota((BLOCK, BLOCK), 0)
    s_id = iota((BLOCK, BLOCK), 1)
    per_block = BLOCK // steps
    causal = (t_id // steps == s_id // steps) & (s_id <= t_id)
    for g in range(rows_all // BLOCK):
        rows = slice(g * BLOCK, (g + 1) * BLOCK)
        count = jnp.zeros((BLOCK, BLOCK), I32)
        for i in range(per_block):
            count = jnp.where(t_id // steps == i, counts[g * per_block + i], count)
        allowed = causal & (s_id % steps < count)
        scale = jnp.where(allowed, 1.0 / count.astype(F32), 0.0)
        for h in range(cols // DH):
            lanes = slice(h * DH, (h + 1) * DH)
            scores = dot_nt(projected[2, rows, lanes], projected[3, rows, lanes]) * root
            sigma = jax.nn.sigmoid(scores)
            weights = (scores * sigma * scale).astype(BF)
            weights_o[h, rows, :] = weights
            dscale[h, rows, :] = sigma * (1.0 + scores * (1.0 - sigma)) * (scale * root)
            mixed = dot_nn(weights, projected[1, rows, lanes])
            centered = mixed - jnp.mean(mixed, axis=-1, keepdims=True)
            spread = jnp.mean(centered * centered, axis=-1, keepdims=True)
            inv = lax.rsqrt(spread + EPS_NORM)
            norm = centered * inv
            norm_o[rows, lanes] = norm
            inv_o[rows, lanes] = jnp.broadcast_to(inv, norm.shape)
            done = (norm * projected[0, rows, lanes].astype(F32)).astype(BF)
            gated[rows, lanes] = done
            gated_t[lanes, rows] = done.T


def out_kernel(place, gathered, own, *refs, mp):
    weights = refs[:mp]
    unit, unit_bf, inv_o = refs[mp:]
    here_mp = place[1]
    total = own[...].astype(F32)
    for j in range(mp):
        total = total + dot_nn(gathered[jnp.bitwise_xor(here_mp, j)], weights[j][...])
    inv = lax.rsqrt(jnp.sum(total * total, axis=-1, keepdims=True) + EPS_UNIT)
    u = total * inv
    unit[...] = u
    unit_bf[...] = u.astype(BF)
    inv_o[...] = jnp.broadcast_to(inv, inv_o.shape)


def ask_kernel(owners, rows, wanted, code, *, devices, capacity):
    events, top = owners.shape
    eye = (iota((events, events), 0) == iota((events, events), 1)).astype(F32)

    def turned(x):
        return lax.dot_general(
            x.astype(F32),
            eye,
            (((0,), (0,)), ((), ())),
            precision=lax.Precision.HIGHEST,
            preferred_element_type=F32,
        )

    owners_t = turned(owners[...])
    rows_t = turned(rows[...])
    o_id = iota((devices, events), 0).astype(F32)
    named = jnp.zeros((devices, events), F32)
    row = jnp.zeros((devices, events), F32)
    positive = jnp.zeros((devices, events), F32)
    for j in range(top):
        same = jnp.where(owners_t[j : j + 1, :] == o_id, 1.0, 0.0)
        named = named + same
        row = row + same * rows_t[j : j + 1, :]
        if j == 0:
            positive = same
    before = (iota((events, events), 0) < iota((events, events), 1)).astype(BF)
    rank = dot_nn(named.astype(BF), before)
    code[...] = jnp.where(named > 0.0, 2.0 * rank + 1.0 + positive, 0.0)
    rank = jnp.where(named > 0.0, rank, -1.0)
    lane = iota((devices, capacity), 1)
    result = jnp.zeros((devices, capacity), F32)
    for c in range(capacity):
        one = jnp.sum(jnp.where(rank == float(c), row, 0.0), axis=1, keepdims=True)
        result = jnp.where(lane == c, one, result)
    wanted[...] = result.astype(I32)


def look_kernel(incoming, catalogue, looked, *, chunk):
    stock, _ = catalogue.shape
    slots = incoming.shape[1]
    for s in range(0, slots, chunk):
        hot = jnp.where(iota((stock, chunk), 0) == incoming[:, s : s + chunk], 1.0, 0.0).astype(BF)
        looked[s : s + chunk, :] = dot_tn(hot, catalogue[...]).astype(BF)


def loss_kernel(
    source, lengths, place, items, code, unit, unit_bf, inv_out, out_cot, sending, hot, share,
    *, seq_dev, steps, devices, capacity, chunk,
):
    events, width = unit.shape
    slots = devices * capacity
    position = place[1] * events + iota((1, events), 1)
    valid = jnp.zeros((1, events), F32)
    for k in range(seq_dev):
        count = lengths[source[place[0] * seq_dev + k]]
        step = position - k * steps
        valid = jnp.where((step >= 0) & (step < count), 1.0, valid)
    total = jnp.zeros((1, events), F32)
    scaled = []
    for s in range(0, slots, chunk):
        rows = slice(s, s + chunk)
        x = items[rows, :]
        xf = x.astype(F32)
        inv = lax.rsqrt(jnp.sum(xf * xf, axis=-1, keepdims=True) + EPS_UNIT)
        logits = dot_nt(x, unit_bf[...]) * (inv * (1.0 / COSINE_DIVISOR))
        slot = s + iota((chunk, 1), 0).astype(F32)
        owner = jnp.floor((slot + 0.5) * (1.0 / capacity))
        local = slot - owner * capacity
        spread = (owner == iota((chunk, devices), 1).astype(F32)).astype(BF)
        codes = dot_nn(spread, code[...].astype(BF))
        first = codes == 2.0 * local + 2.0
        mine = first | (codes == 2.0 * local + 1.0)
        hot[rows, :] = mine.astype(BF)
        expo = jnp.where(mine, jnp.exp(logits), 0.0)
        total = total + jnp.sum(expo, axis=0, keepdims=True)
        share[rows, :] = expo
        scaled.append((first, inv))
    factor = valid / total
    slope = jnp.zeros((events, width), F32)
    for n, s in enumerate(range(0, slots, chunk)):
        rows = slice(s, s + chunk)
        first, inv = scaled[n]
        part = share[rows, :] * factor - jnp.where(first, valid, 0.0)
        part = part * (1.0 / COSINE_DIVISOR)
        slope = slope + dot_tn((part * inv).astype(BF), items[rows, :])
        weight = jnp.sum(part, axis=1, keepdims=True)
        sending[rows, :] = (dot_nn(hot[rows, :], unit_bf[...]) * weight).astype(BF)
    u = unit[...]
    along = jnp.sum(u * slope, axis=-1, keepdims=True)
    out_cot[...] = ((slope - u * along) * inv_out[:, 0:1]).astype(BF)


def spread_kernel(incoming, landed, catalogue, out, *, chunk):
    stock, _ = catalogue.shape
    slots = incoming.shape[1]
    for r in range(0, stock, chunk):
        hot = jnp.where(r + iota((chunk, slots), 0) == incoming[...], 1.0, 0.0).astype(BF)
        v = dot_nn(hot, landed[...])
        c = catalogue[r : r + chunk, :].astype(F32)
        inv = lax.rsqrt(jnp.sum(c * c, axis=-1, keepdims=True) + EPS_UNIT)
        c = c * inv
        out[r : r + chunk, :] = (v - c * jnp.sum(c * v, axis=-1, keepdims=True)) * inv


def w_out_kernel(place, *refs, mp, dp):
    blocks = refs[:mp]
    gated_t, out, whole = refs[mp:]
    quarter, width = blocks[0].shape
    for j in range(mp):
        start = pl.multiple_of(jnp.bitwise_xor(place[1], j) * quarter, quarter)
        whole[pl.ds(start, quarter), :] = blocks[j][...]
    part = dot_nn(gated_t[...], whole[...]).astype(BF)
    lanes = width // dp
    for d in range(dp):
        out[d] = part[:, d * lanes : (d + 1) * lanes]


def backward_kernel(place, *refs, mp, dp):
    blocks = refs[:mp]
    w_out, projected, slope, weights, dscale, norm, inv, normed_t, out, whole, cot = refs[mp:]
    quarter, width = blocks[0].shape
    for j in range(mp):
        start = pl.multiple_of(jnp.bitwise_xor(place[1], j) * quarter, quarter)
        whole[pl.ds(start, quarter), :] = blocks[j][...]
    rows_all = whole.shape[0]
    cols = w_out.shape[0]
    gated_cot = dot_nt(whole[...], w_out[...]).astype(BF).astype(F32)
    for g in range(rows_all // BLOCK):
        rows = slice(g * BLOCK, (g + 1) * BLOCK)
        for h in range(cols // DH):
            lanes = slice(h * DH, (h + 1) * DH)
            d_gated = gated_cot[rows, lanes]
            n = norm[rows, lanes]
            d_norm = d_gated * projected[0, rows, lanes].astype(F32)
            d_mixed = inv[rows, lanes] * (
                d_norm
                - jnp.mean(d_norm, axis=-1, keepdims=True)
                - n * jnp.mean(d_norm * n, axis=-1, keepdims=True)
            )
            d_mixed = d_mixed.astype(BF)
            d_weights = dot_nt(d_mixed, projected[1, rows, lanes]).astype(BF).astype(F32)
            d_values = dot_tn(weights[h, rows, :], d_mixed)
            d_scores = (d_weights * dscale[h, rows, :]).astype(BF)
            d_queries = dot_nn(d_scores, projected[3, rows, lanes])
            d_keys = dot_tn(d_scores, projected[2, rows, lanes])
            for c, d in enumerate((d_gated * n, d_values, d_queries, d_keys)):
                cot[c, rows, lanes] = (d.astype(BF).astype(F32) * slope[c, rows, lanes]).astype(BF)
    share = width // dp
    for c in range(4):
        part = dot_nn(normed_t[...], cot[c]).astype(BF)
        for d in range(dp):
            out[d, c] = part[d * share : (d + 1) * share, :]


def swapped(x, axis, bit):
    size = lax.axis_size(axis)
    return lax.ppermute(x, axis, [(a, a ^ bit) for a in range(size)])


def gather_blocks(x, axis):
    size = lax.axis_size(axis)
    blocks = {0: x}
    bit = size // 2
    while bit:
        for j in list(blocks):
            blocks[j ^ bit] = swapped(blocks[j], axis, bit)
        bit //= 2
    return [blocks[j] for j in range(size)]


def per_device(history, lengths, source, owners, item_rows, catalogue, w_in, w_out):
    dp = lax.axis_size("dp")
    mp = lax.axis_size("mp")
    devices = dp * mp
    seq_dev, steps, part = history.shape
    width = part * mp
    cols = w_in.shape[2]
    rows_all = seq_dev * steps
    quarter = rows_all // mp
    events, top = owners.shape
    asks = events * top
    capacity = max(2, (3 * asks + 2 * devices - 1) // (2 * devices))
    slots = devices * capacity
    stock = catalogue.shape[0]
    per_peer = (seq_dev + dp - 1) // dp
    chunk = math.gcd(slots, 512)
    S = jax.ShapeDtypeStruct
    place = jnp.stack([lax.axis_index("dp"), lax.axis_index("mp")]).astype(I32)

    wanted, code = call(
        functools.partial(ask_kernel, devices=devices, capacity=capacity),
        [S((devices, capacity), I32), S((devices, events), F32)],
        [VM, VM],
        1e6,
        1e5,
    )(owners, item_rows)
    incoming = lax.all_to_all(
        wanted, ("dp", "mp"), split_axis=0, concat_axis=0, tiled=True
    ).reshape(1, slots)
    looked = call(
        functools.partial(look_kernel, chunk=chunk),
        S((slots, width), BF),
        [VM, VM],
        2 * slots * stock * width,
        2 * (slots + stock) * width,
    )(incoming, catalogue)
    returned = lax.all_to_all(
        looked.reshape(devices, capacity, width),
        ("dp", "mp"),
        split_axis=0,
        concat_axis=0,
        tiled=True,
    ).reshape(slots, width)

    outgoing = call(
        functools.partial(pack_kernel, dp=dp, seq_dev=seq_dev, per_peer=per_peer),
        S((dp * per_peer, steps, part), BF),
        [SM, SM, VM],
        1e5,
        4 * history.size,
    )(source, place, history)
    arrived = lax.all_to_all(outgoing, "dp", split_axis=0, concat_axis=0, tiled=True)
    features = gather_blocks(arrived, "mp")
    heads = cols // DH
    (normed_t, projected, slope, weights, dscale, norm, inv, gated, gated_t, own) = call(
        functools.partial(
            forward_kernel,
            mp=mp,
            seq_dev=seq_dev,
            per_peer=per_peer,
            steps=steps,
            width=width,
            cols=cols,
            quarter=quarter,
        ),
        [
            S((width, rows_all), BF),
            S((4, rows_all, cols), BF),
            S((4, rows_all, cols), F32),
            S((heads, rows_all, BLOCK), BF),
            S((heads, rows_all, BLOCK), F32),
            S((rows_all, cols), F32),
            S((rows_all, cols), F32),
            S((rows_all, cols), BF),
            S((cols, rows_all), BF),
            S((quarter, width), BF),
        ],
        [SM, SM, SM] + [VM] * (mp + 1),
        8 * rows_all * width * cols,
        12 * 2**20,
        scratch=[pltpu.VMEM((rows_all, width), BF)],
        trans=6 * rows_all * cols,
    )(source, lengths, place, *features, w_in)
    w_out_blocks = gather_blocks(w_out, "mp")
    gathered = lax.all_to_all(
        gated.reshape(mp, quarter, cols), "mp", split_axis=0, concat_axis=0, tiled=True
    )
    unit, unit_bf, inv_out = call(
        functools.partial(out_kernel, mp=mp),
        [S((quarter, width), F32), S((quarter, width), BF), S((quarter, BLOCK), F32)],
        [SM] + [VM] * (mp + 2),
        2 * quarter * width * width,
        4 * 2**20,
    )(place, gathered, own, *w_out_blocks)

    out_cot, sending = call(
        functools.partial(
            loss_kernel,
            seq_dev=seq_dev,
            steps=steps,
            devices=devices,
            capacity=capacity,
            chunk=chunk,
        ),
        [S((quarter, width), BF), S((slots, width), BF)],
        [SM, SM, SM] + [VM] * 5,
        6 * slots * width * events,
        4 * slots * width,
        scratch=[pltpu.VMEM((slots, events), BF), pltpu.VMEM((slots, events), F32)],
    )(source, lengths, place, returned, code, unit, unit_bf, inv_out)
    landed = lax.all_to_all(
        sending.reshape(devices, capacity, width),
        ("dp", "mp"),
        split_axis=0,
        concat_axis=0,
        tiled=True,
    ).reshape(slots, width)

    cots = gather_blocks(out_cot, "mp")
    w_out_part = call(
        functools.partial(w_out_kernel, mp=mp, dp=dp),
        S((dp, cols, width // dp), BF),
        [SM] + [VM] * (mp + 1),
        2 * rows_all * width * cols,
        3 * 2**20,
        scratch=[pltpu.VMEM((rows_all, width), BF)],
    )(place, *cots, gated_t)
    w_in_part = call(
        functools.partial(backward_kernel, mp=mp, dp=dp),
        S((dp, 4, width // dp, cols), BF),
        [SM] + [VM] * (mp + 8),
        10 * rows_all * width * cols,
        12 * 2**20,
        scratch=[pltpu.VMEM((rows_all, width), BF), pltpu.VMEM((4, rows_all, cols), BF)],
    )(place, *cots, w_out, projected, slope, weights, dscale, norm, inv, normed_t)

    def summed(x):
        got = lax.all_to_all(x, "dp", split_axis=0, concat_axis=0, tiled=True)
        return jnp.sum(got.astype(F32), axis=0)

    w_out_grad = summed(w_out_part)
    w_in_grad = summed(w_in_part)
    cat_grad = call(
        functools.partial(spread_kernel, chunk=math.gcd(stock, 128)),
        S((stock, width), F32),
        [VM] * 3,
        2 * slots * stock * width,
        2 * slots * width + 6 * stock * width,
    )(incoming, landed, catalogue)
    return (w_in_grad, w_out_grad, cat_grad)


def solution(mesh):
    placed = (
        P("dp", None, "mp"),
        P(),
        P(),
        P(("dp", "mp"), None),
        P(("dp", "mp"), None),
        P(("dp", "mp"), None),
        P(None, None, "mp"),
        P("mp", None),
    )
    return jax.shard_map(
        per_device,
        mesh=mesh,
        in_specs=placed,
        out_specs=(P(None, "dp", "mp"), P("mp", "dp"), P(("dp", "mp"), None)),
        check_vma=False,
    )
```

time: 451 us -> 313 us (0.69)
  other arithmetic: 56.2 us -> 5.26 us
  blocking collectives: 105 us -> 65.1 us
  local copies, waits for them, and re-layouts: 66.1 us -> 26.7 us
  Pallas kernels: 0 us -> 31.9 us
  matrix products: 22.9 us -> 0 us
  between operations: 14.7 us -> 0.82 us
  waiting for transfers between devices: 147 us -> 139 us
  starting transfers between devices: 34.3 us -> 38.9 us
    ppermute x0 -> x9, waiting for transfers between devices: none -> 44.2 us  [swapped(): return lax.ppermute(x, axis, [(a, a ^ bit) for a in range(size)])]
    all_to_all x1 -> x2, blocking collectives: 105 us -> 65.1 us  [the longest x1 53.4 us: summed(): got = lax.all_to_all(x, 'dp', split_axis=0, concat_axis=0, tiled=True)]
    pallas_call x0 -> x9, Pallas kernels: none -> 31.9 us  [the longest x1 6.44 us: per_device(): call(functools.partial(backward_kernel, mp=mp, dp=dp), S((dp, 4, width //...]
    gather x11 -> x0, local copies, waits for them, and re-layouts: 29 us -> none  [the longest x1 5.86 us: per_device(): jnp.take(catalogue, incoming_flat, axis=0)]
    dot_general x13 -> x0, matrix products: 22.9 us -> none  [the longest x1 6.44 us: per_device(): jnp.einsum('rd,crh->cdh', normed, preact_cotangent, preferred_element_typ...]
    unnamed x99 -> x72, local copies, waits for them, and re-layouts: 5.88 us -> 26.1 us
    all_to_all x6 -> x5, waiting for transfers between devices: 114 us -> 95.1 us  [the longest x1 64.5 us: per_device(): lax.all_to_all(sending.reshape(devices, capacity, width), ('dp', 'mp'), s...]
    all_gather x2 -> x0, waiting for transfers between devices: 17.5 us -> none  [the longest x1 17.5 us: per_device(): lax.all_gather(out_grad.astype(jnp.bfloat16), 'mp', axis=0, tiled=True)]
  transfers between devices with their start and end apart: 11 -> 14, of which waited for: 7 -> 7; matrix products, arithmetic and copies ran while one was open for 21% -> 2% of each run, Pallas kernels for 0% -> 6%
where the time goes in v1:
time: 313 us; the launch traced here: 308 us
  waiting for transfers between devices  139 us (44%)
  blocking collectives  65.1 us (21%)
  starting transfers between devices  38.9 us (12%)
  Pallas kernels  31.9 us (10%)
  local copies, waits for them, and re-layouts  26.7 us (9%)
  other arithmetic  5.26 us (2%)
    all_to_all x1, waiting for transfers between devices, per_device(): lax.all_to_all(sending.reshape(devices, capacity, width), ('dp', 'mp'), s...  64.5 us
    all_to_all x1, blocking collectives, summed(): got = lax.all_to_all(x, 'dp', split_axis=0, concat_axis=0, tiled=True)  53.4 us
    ppermute x9, waiting for transfers between devices, swapped(): return lax.ppermute(x, axis, [(a, a ^ bit) for a in range(size)])  44.2 us
    all_to_all x1, waiting for transfers between devices, per_device(): lax.all_to_all(looked.reshape(devices, capacity, width), ('dp', 'mp'), sp...  30.6 us
    unnamed x72, local copies, waits for them, and re-layouts  26.1 us
    all_to_all x1, blocking collectives, per_device(): lax.all_to_all(outgoing, 'dp', split_axis=0, concat_axis=0, tiled=True)  11.8 us
    ppermute x9, starting transfers between devices, swapped(): return lax.ppermute(x, axis, [(a, a ^ bit) for a in range(size)])  10.8 us
    all_to_all x1, starting transfers between devices, summed(): got = lax.all_to_all(x, 'dp', split_axis=0, concat_axis=0, tiled=True)  6.88 us
  transfers between devices with their start and end apart: 14, of which 7 were waited for; matrix products, arithmetic and copies ran while one was open for 2% of the time, Pallas kernels for 6%

profile of v1, /device:TPU:13, one launch (start us, length us, event | category | flops | bytes accessed | tf_op | source)
XLA Modules:
  0.0 308.0 jit_solution(17081486742121961934)
XLA Ops:
  0.7 0.9 copy-done.14
  2.3 2.9 shard_map.105
  5.2 11.8 %all_to_all.39.refs_0_ = bf16[16,32,256]{2,1,0:T(8,128)(2,1)S(1)} all-to-all(bf16[16,32,256]{2,1,0:T(8,128)(2,1)S(1)} %shard_map.105), channel_id=1, replica_groups=mesh['dp'=8,'mp'=4] {'dp'}, dimensions={0} | all-to-all | bytes 524288 | tf_op jit(solution)/shard_map/all_to_all | solution.py:380
  17.2 3.2 %collective-permute-start = (bf16[16,32,256]{2,1,0:T(8,128)(2,1)S(1)}, bf16[16,32,256]{2,1,0:T(8,128)(2,1)S(1)}, u32[]{:S(2)}, u32[]{:S(2)}) collective-permute-start(bf16[16,32,256]{2,1,0:T(8,128)(2,1)S(1)} %all_to_all.39.refs_0_), channel_id=1, source_target_pairs={{0,1},{1,0},{2,3},{3,2},{4,5},{5,4},{6,7},{7,6},{8,9},{9,8},{10,11... | collective-permute-start | bytes 786440 | tf_op jit(solution)/shard_map/ppermute | solution.py:315
  20.4 1.8 collective-permute-done.1.refs_2_
  22.2 4.1 %collective-permute-start.2 = (bf16[16,32,256]{2,1,0:T(8,128)(2,1)S(1)}, bf16[16,32,256]{2,1,0:T(8,128)(2,1)S(1)}, u32[]{:S(2)}, u32[]{:S(2)}) collective-permute-start(bf16[16,32,256]{2,1,0:T(8,128)(2,1)S(1)} %collective-permute-done.1.refs_2_), channel_id=1, source_target_pairs={{0,1},{1,0},{2,3},{3,2},{4,5},{5,4},{6,7},{7,6},{8,9},{9,8},{10,11... | collective-permute-start | bytes 786440 | tf_op jit(solution)/shard_map/ppermute | solution.py:315
  26.3 0.8 copy.13.owners
  27.1 0.8 copy.14.rows
  27.9 1.3 shard_map.103
  29.1 5.4 %all-to-all-start = ((s32[32,1,48]{2,1,0:T(1,128)}), s32[32,1,48]{2,1,0:T(1,128)S(1)}, u32[]{:S(2)}, u32[]{:S(2)}) async-start(s32[32,1,48]{2,1,0:T(1,128)} %bitcast.3), calls=%async_computation | async-start | bytes 32768 | tf_op jit(solution)/shard_map/all_to_all | solution.py:355
  36.6 0.9 copy-done.26
  37.6 0.9 copy-done.28
  38.5 0.9 copy-done.30
  40.1 6.0 %shard_map.106 = (bf16[1024,512]{1,0:T(8,128)(2,1)S(1)}, bf16[4,512,256]{2,1,0:T(8,128)(2,1)S(1)}, f32[4,512,256]{2,1,0:T(8,128)}, bf16[2,512,128]{2,1,0:T(8,128...) custom-call(s32[128]{0:T(128)S(1)} %copy-done.21, ...), custom_call_target="tpu_custom_call" | custom-call | flops 1073741824 | bytes 12582912 | tf_op jit(solution)/shard_map/pallas_call | solution.py:383
  46.2 0.8 copy-done.6
  46.9 0.8 copy-done.8
  47.7 0.8 copy-done.10
  51.4 3.9 %all-to-all-start.3 = ((bf16[4,128,256]{2,1,0:T(8,128)(2,1)}), bf16[4,128,256]{2,1,0:T(8,128)(2,1)S(1)}, u32[]{:S(2)}, u32[]{:S(2)}) async-start(bf16[4,128,256]{2,1,0:T(8,128)(2,1)} %bitcast.12), calls=%async_computation.3 | async-start | bytes 524288 | tf_op jit(solution)/shard_map/all_to_all | solution.py:413
  56.7 3.5 %shard_map.104 = bf16[1536,1024]{1,0:T(8,128)(2,1)} custom-call(s32[1,1536]{1,0:T(1,128)S(1)} %reshape.27.incoming, bf16[512,1024]{1,0:T(8,128)(2,1)S(1)} %copy-done.2), custom_call_target="tpu_custom_call" | custom-call | flops 1610612736 | bytes 4194304 | tf_op jit(solution)/shard_map/pallas_call | solution.py:358
  60.2 5.9 %all-to-all-start.1 = ((bf16[32,48,1024]{2,1,0:T(8,128)(2,1)}), bf16[32,48,1024]{2,1,0:T(8,128)(2,1)}, u32[]{:S(2)}, u32[]{:S(2)}) async-start(bf16[32,48,1024]{2,1,0:T(8,128)(2,1)} %bitcast.4), calls=%async_computation.1 | async-start | bytes 6291456 | tf_op jit(solution)/shard_map/all_to_all | solution.py:365
  67.1 32.3 %collective-permute-done.4.refs_2_ = bf16[256,1024]{1,0:T(8,128)(2,1)S(1)} collective-permute-done((bf16[256,1024]{1,0:T(8,128)(2,1)S(1)}, bf16[256,1024]{1,0:T(8,128)(2,1)S(1)}, u32[]{:S(2)}, u32[]{:S(2)}) %collective-permute-start.4) | collective-permute-done | bytes 524320 | tf_op jit(solution)/shard_map/ppermute | solution.py:315
  99.4 0.9 collective-permute-start.5
  100.3 1.5 collective-permute-done.5.refs_3_
  101.8 1.1 shard_map.107
  103.0 0.8 copy-done.23
  104.5 30.6 %all-to-all-done.1 = bf16[32,48,1024]{2,1,0:T(8,128)(2,1)} async-done(((bf16[32,48,1024]{2,1,0:T(8,128)(2,1)}), bf16[32,48,1024]{2,1,0:T(8,128)(2,1)}, u32[]{:S(2)}, u32[]{:S(2)}) %all-to-all-start.1) | async-done | bytes 3145760 | tf_op jit(solution)/shard_map/all_to_all | solution.py:365
  135.1 1.0 copy-done.24
  136.1 0.9 copy-done.32
  137.1 5.3 %shard_map.108 = (bf16[128,1024]{1,0:T(8,128)(2,1)S(1)}, bf16[1536,1024]{1,0:T(8,128)(2,1)S(1)}) custom-call(s32[128]{0:T(128)S(1)} %copy-done.22, s32[128]{0:T(128)S(1)} %copy-done.34, s32[2]{0:T(128)S(1)} %pad_add_fusion.place, bf16[1536,1024]{1,0:T(8,128)(2,1)} %bitcast.5.items, f32[32,128]{1,0:T(8,128)S(1)} %get-tuple-element.21.code, ...), custom_call_target="tpu_custom_call" | custom-call | flops 1207959552 | bytes 6291456 | tf_op jit(solution)/shard_map/pallas_call | solution.py:424
  142.3 1.6 copy-done
  144.5 7.3 %collective-permute-done.7.refs_2_ = bf16[128,1024]{1,0:T(8,128)(2,1)S(1)} collective-permute-done((bf16[128,1024]{1,0:T(8,128)(2,1)S(1)}, bf16[128,1024]{1,0:T(8,128)(2,1)S(1)}, u32[]{:S(2)}, u32[]{:S(2)}) %collective-permute-start.7) | collective-permute-done | bytes 262176 | tf_op jit(solution)/shard_map/ppermute | solution.py:315
  151.9 0.8 collective-permute-start.8
  152.7 1.2 collective-permute-done.8.refs_3_
  153.9 1.8 shard_map.110
  156.4 6.9 %all-to-all-start.5 = ((bf16[8,256,128]{2,1,0:T(8,128)(2,1)}), bf16[8,256,128]{2,1,0:T(8,128)(2,1)}, u32[]{:S(2)}, u32[]{:S(2)}) async-start(bf16[8,256,128]{2,1,0:T(8,128)(2,1)} %shard_map.110), calls=%async_computation.5 | async-start | bytes 1048576 | tf_op jit(solution)/shard_map/all_to_all | solution.py:466
  163.3 0.9 copy-done.5
  164.2 1.0 copy-done.7
  165.3 1.0 copy-done.9
  166.3 1.0 copy-done.11
  167.4 0.9 copy-done.13
  168.3 6.4 %shard_map.109 = bf16[8,4,128,256]{3,2,1,0:T(8,128)(2,1)} custom-call(s32[2]{0:T(128)S(1)} %pad_add_fusion.place, bf16[128,1024]{1,0:T(8,128)(2,1)S(1)} %get-tuple-element.27.refs_0_, bf16[128,1024]{1,0:T(8,128)(2,1)S(1)} %collective-permute-done.6.refs_1_, bf16[128,1024]{1,0:T(8,128)(2,1)S(1)} %collective-permute-done.7.refs_2_, ...), custom_call_target="tpu_custom_call" | custom-call | flops 1342177280 | bytes 12582912 | tf_op jit(solution)/shard_map/pallas_call | solution.py:456
  174.8 53.4 %all_to_all.40 = bf16[8,4,128,256]{3,2,1,0:T(8,128)(2,1)} all-to-all(bf16[8,4,128,256]{3,2,1,0:T(8,128)(2,1)} %shard_map.109), channel_id=1, replica_groups=mesh['dp'=8,'mp'=4] {'dp'}, dimensions={0} | all-to-all | bytes 4194304 | tf_op jit(solution)/shard_map/all_to_all | solution.py:466
  228.1 6.1 %all-to-all-start.6 = ((bf16[32,48,1024]{2,1,0:T(8,128)(2,1)}), bf16[32,48,1024]{2,1,0:T(8,128)(2,1)S(1)}, u32[]{:S(2)}, u32[]{:S(2)}) async-start(bf16[32,48,1024]{2,1,0:T(8,128)(2,1)} %bitcast.11), calls=%async_computation.6 | async-start | bytes 6291456 | tf_op jit(solution)/shard_map/all_to_all | solution.py:439
  234.2 1.8 convert_reduce_fusion.1
  236.0 2.7 convert_reduce_fusion
  238.7 64.5 %all-to-all-done.6 = bf16[32,48,1024]{2,1,0:T(8,128)(2,1)S(1)} async-done(((bf16[32,48,1024]{2,1,0:T(8,128)(2,1)}), bf16[32,48,1024]{2,1,0:T(8,128)(2,1)S(1)}, u32[]{:S(2)}, u32[]{:S(2)}) %all-to-all-start.6) | async-done | bytes 3145760 | tf_op jit(solution)/shard_map/all_to_all | solution.py:439
  303.2 1.2 copy-done.3
  304.5 3.6 %shard_map.111 = f32[512,1024]{1,0:T(8,128)} custom-call(s32[1,1536]{1,0:T(1,128)S(1)} %reshape.27.incoming, bf16[1536,1024]{1,0:T(8,128)(2,1)S(1)} %bitcast.10, bf16[512,1024]{1,0:T(8,128)(2,1)S(1)} %copy-done.3), custom_call_target="tpu_custom_call" | custom-call | flops 1610612736 | bytes 6291456 | tf_op jit(solution)/shard_map/pallas_call | solution.py:471
  (69 shorter events, 10.8 us)
Async XLA Ops:
  0.7 1.0 copy-start.14
  1.7 0.7 copy-start.20
  17.0 5.2 %collective-permute-start.1 = (bf16[16,32,256]{2,1,0:T(8,128)(2,1)S(1)}, bf16[16,32,256]{2,1,0:T(8,128)(2,1)S(1)}, u32[]{:S(2)}, u32[]{:S(2)}) collective-permute-start(bf16[16,32,256]{2,1,0:T(8,128)(2,1)S(1)} %all_to_all.39.refs_0_), channel_id=1, source_target_pairs={{0,2},{1,3},{2,0},{3,1},{4,6},{5,7},{6,4},{7,5},{8,10},{9,11},{10,... | collective-permute-start | bytes 786440 | tf_op jit(solution)/shard_map/ppermute | solution.py:315
  17.2 17.3 %collective-permute-start = (bf16[16,32,256]{2,1,0:T(8,128)(2,1)S(1)}, bf16[16,32,256]{2,1,0:T(8,128)(2,1)S(1)}, u32[]{:S(2)}, u32[]{:S(2)}) collective-permute-start(bf16[16,32,256]{2,1,0:T(8,128)(2,1)S(1)} %all_to_all.39.refs_0_), channel_id=1, source_target_pairs={{0,1},{1,0},{2,3},{3,2},{4,5},{5,4},{6,7},{7,6},{8,9},{9,8},{10,11... | collective-permute-start | bytes 786440 | tf_op jit(solution)/shard_map/ppermute | solution.py:315
  22.2 12.3 %copy-start.25 = (bf16[16,32,256]{2,1,0:T(8,128)(2,1)}, bf16[16,32,256]{2,1,0:T(8,128)(2,1)S(1)}, u32[]{:S(2)}) copy-start(bf16[16,32,256]{2,1,0:T(8,128)(2,1)S(1)} %collective-permute-done.1.refs_2_) | copy-start | bytes 786436
  22.2 13.0 %collective-permute-start.2 = (bf16[16,32,256]{2,1,0:T(8,128)(2,1)S(1)}, bf16[16,32,256]{2,1,0:T(8,128)(2,1)S(1)}, u32[]{:S(2)}, u32[]{:S(2)}) collective-permute-start(bf16[16,32,256]{2,1,0:T(8,128)(2,1)S(1)} %collective-permute-done.1.refs_2_), channel_id=1, source_target_pairs={{0,1},{1,0},{2,3},{3,2},{4,5},{5,4},{6,7},{7,6},{8,9},{9,8},{10,11... | collective-permute-start | bytes 786440 | tf_op jit(solution)/shard_map/ppermute | solution.py:315
  29.1 22.3 %all-to-all-start = ((s32[32,1,48]{2,1,0:T(1,128)}), s32[32,1,48]{2,1,0:T(1,128)S(1)}, u32[]{:S(2)}, u32[]{:S(2)}) async-start(s32[32,1,48]{2,1,0:T(1,128)} %bitcast.3), calls=%async_computation | async-start | bytes 32768 | tf_op jit(solution)/shard_map/all_to_all | solution.py:355
  34.5 22.1 %copy-start.2 = (bf16[512,1024]{1,0:T(8,128)(2,1)S(1)}, bf16[512,1024]{1,0:T(8,128)(2,1)}, u32[]{:S(2)}) copy-start(bf16[512,1024]{1,0:T(8,128)(2,1)} %catalogue.3) | copy-start | bytes 3145732
  34.5 0.7 copy-start.27
  35.2 0.7 copy-start.29
  36.0 0.7 copy-start.21
  36.6 0.9 copy-start.26
  37.6 0.9 copy-start.28
  38.5 0.9 copy-start.30
  46.2 0.8 copy-start.6
  46.9 0.8 copy-start.8
  47.7 0.8 copy-start.10
  48.6 0.7 copy-start.12
  49.3 0.7 copy-start.15
  50.0 0.7 copy-start.16
  50.7 0.7 copy-start.18
  51.4 8.8 %all-to-all-start.3 = ((bf16[4,128,256]{2,1,0:T(8,128)(2,1)}), bf16[4,128,256]{2,1,0:T(8,128)(2,1)S(1)}, u32[]{:S(2)}, u32[]{:S(2)}) async-start(bf16[4,128,256]{2,1,0:T(8,128)(2,1)} %bitcast.12), calls=%async_computation.3 | async-start | bytes 524288 | tf_op jit(solution)/shard_map/all_to_all | solution.py:413
  60.2 5.9 %copy-start.1 = (bf16[256,1024]{1,0:T(8,128)(2,1)S(1)}, bf16[256,1024]{1,0:T(8,128)(2,1)}, u32[]{:S(2)}) copy-start(bf16[256,1024]{1,0:T(8,128)(2,1)} %refs_4_.3) | copy-start | bytes 1572868
  60.2 41.7 %copy-start.19 = (bf16[128,1024]{1,0:T(8,128)(2,1)S(1)}, bf16[128,1024]{1,0:T(8,128)(2,1)}, u32[]{:S(2)}) copy-start(bf16[128,1024]{1,0:T(8,128)(2,1)} %copy-done.18) | copy-start | bytes 786436
  60.2 74.9 %all-to-all-start.1 = ((bf16[32,48,1024]{2,1,0:T(8,128)(2,1)}), bf16[32,48,1024]{2,1,0:T(8,128)(2,1)}, u32[]{:S(2)}, u32[]{:S(2)}) async-start(bf16[32,48,1024]{2,1,0:T(8,128)(2,1)} %bitcast.4), calls=%async_computation.1 | async-start | bytes 6291456 | tf_op jit(solution)/shard_map/all_to_all | solution.py:365
  66.0 69.0 %copy-start.22 = (s32[128]{0:T(128)S(1)}, s32[128]{0:T(128)}, u32[]{:S(2)}) copy-start(s32[128]{0:T(128)} %source.5) | copy-start | bytes 1540
  66.1 69.0 %copy-start.34 = (s32[128]{0:T(128)S(1)}, s32[128]{0:T(128)}, u32[]{:S(2)}) copy-start(s32[128]{0:T(128)} %lengths.3) | copy-start | bytes 1540
  66.1 33.3 %collective-permute-start.4 = (bf16[256,1024]{1,0:T(8,128)(2,1)S(1)}, bf16[256,1024]{1,0:T(8,128)(2,1)S(1)}, u32[]{:S(2)}, u32[]{:S(2)}) collective-permute-start(bf16[256,1024]{1,0:T(8,128)(2,1)S(1)} %copy-done.1), channel_id=1, source_target_pairs={{0,2},{1,3},{2,0},{3,1},{4,6},{5,7},{6,4},{7,5},{8,10},{9,11},{10,... | collective-permute-start | bytes 1572872 | tf_op jit(solution)/shard_map/ppermute | solution.py:315
  66.4 33.9 %collective-permute-start.3 = (bf16[256,1024]{1,0:T(8,128)(2,1)S(1)}, bf16[256,1024]{1,0:T(8,128)(2,1)S(1)}, u32[]{:S(2)}, u32[]{:S(2)}) collective-permute-start(bf16[256,1024]{1,0:T(8,128)(2,1)S(1)} %copy-done.1), channel_id=1, source_target_pairs={{0,1},{1,0},{2,3},{3,2},{4,5},{5,4},{6,7},{7,6},{8,9},{9,8},{10,11... | collective-permute-start | bytes 1572872 | tf_op jit(solution)/shard_map/ppermute | solution.py:315
  99.4 2.5 collective-permute-start.5
  103.0 0.8 copy-start.23
  103.8 0.7 copy-start.31
  135.1 1.0 copy-start.24
  136.1 0.9 copy-start.32
  137.1 16.8 %copy-start.17 = (bf16[256,512]{1,0:T(8,128)(2,1)S(1)}, bf16[256,512]{1,0:T(8,128)(2,1)}, u32[]{:S(2)}) copy-start(bf16[256,512]{1,0:T(8,128)(2,1)} %copy-done.16) | copy-start | bytes 786436
  142.3 1.6 copy-start
  144.0 7.9 %collective-permute-start.7 = (bf16[128,1024]{1,0:T(8,128)(2,1)S(1)}, bf16[128,1024]{1,0:T(8,128)(2,1)S(1)}, u32[]{:S(2)}, u32[]{:S(2)}) collective-permute-start(bf16[128,1024]{1,0:T(8,128)(2,1)S(1)} %get-tuple-element.27.refs_0_), channel_id=1, source_target_pairs={{0,2},{1,3},{2,0},{3,1},{4,6},{5,7},{6,4},{7,5},{8,10},{9,11},{10,... | collective-permute-start | bytes 786440 | tf_op jit(solution)/shard_map/ppermute | solution.py:315
  144.5 8.2 %collective-permute-start.6 = (bf16[128,1024]{1,0:T(8,128)(2,1)S(1)}, bf16[128,1024]{1,0:T(8,128)(2,1)S(1)}, u32[]{:S(2)}, u32[]{:S(2)}) collective-permute-start(bf16[128,1024]{1,0:T(8,128)(2,1)S(1)} %get-tuple-element.27.refs_0_), channel_id=1, source_target_pairs={{0,1},{1,0},{2,3},{3,2},{4,5},{5,4},{6,7},{7,6},{8,9},{9,8},{10,11... | collective-permute-start | bytes 786440 | tf_op jit(solution)/shard_map/ppermute | solution.py:315
  151.9 2.0 collective-permute-start.8
  155.7 0.7 copy-start.4
  156.4 18.4 %all-to-all-start.5 = ((bf16[8,256,128]{2,1,0:T(8,128)(2,1)}), bf16[8,256,128]{2,1,0:T(8,128)(2,1)}, u32[]{:S(2)}, u32[]{:S(2)}) async-start(bf16[8,256,128]{2,1,0:T(8,128)(2,1)} %shard_map.110), calls=%async_computation.5 | async-start | bytes 1048576 | tf_op jit(solution)/shard_map/all_to_all | solution.py:466
  163.3 0.9 copy-start.5
  164.2 1.0 copy-start.7
  165.3 1.0 copy-start.9
  166.3 1.0 copy-start.11
  167.4 0.9 copy-start.13
  228.1 75.1 %all-to-all-start.6 = ((bf16[32,48,1024]{2,1,0:T(8,128)(2,1)}), bf16[32,48,1024]{2,1,0:T(8,128)(2,1)S(1)}, u32[]{:S(2)}, u32[]{:S(2)}) async-start(bf16[32,48,1024]{2,1,0:T(8,128)(2,1)} %bitcast.11), calls=%async_computation.6 | async-start | bytes 6291456 | tf_op jit(solution)/shard_map/all_to_all | solution.py:439
  303.2 1.2 copy-start.3
  (1 other events, 0.7 us)

commit v2 on v1

--- a/solution.py
+++ b/solution.py
@@ -21,7 +21,7 @@
 SM = pl.BlockSpec(memory_space=pltpu.SMEM)
 
 
-def call(body, out_shape, in_specs, flops, nbytes, scratch=(), trans=0):
+def call(body, out_shape, in_specs, flops, nbytes, scratch=(), trans=0, limit=24):
     many = isinstance(out_shape, (list, tuple))
     return pl.pallas_call(
         body,
@@ -29,7 +29,7 @@
         in_specs=in_specs,
         out_specs=[VM] * len(out_shape) if many else VM,
         scratch_shapes=list(scratch),
-        compiler_params=pltpu.CompilerParams(vmem_limit_bytes=48 * 1024 * 1024),
+        compiler_params=pltpu.CompilerParams(vmem_limit_bytes=limit * 2**20),
         cost_estimate=pl.CostEstimate(
             flops=int(flops), bytes_accessed=int(nbytes), transcendentals=int(trans)
         ),
@@ -52,52 +52,75 @@
     return lax.broadcasted_iota(I32, shape, dim)
 
 
-def pack_kernel(source, place, hist, out, *, dp, seq_dev, per_peer):
+def pack_kernel(source, place, hist, *outs, dp, seq_dev, per_peer):
     here = place[0]
 
-    def per_dest(d, carry):
+    def per_dest(d, put):
         def per_slot(i, count):
             src = source[d * seq_dev + i]
             hit = lax.div(src, seq_dev) == here
 
             @pl.when(hit)
             def _():
-                out[d * per_peer + count] = hist[src - here * seq_dev]
+                put(count, hist[src - here * seq_dev])
 
             return count + hit.astype(I32)
 
         lax.fori_loop(0, seq_dev, per_slot, jnp.int32(0))
-        return carry
-
-    lax.fori_loop(0, dp, per_dest, jnp.int32(0))
-
-
-def forward_kernel(
-    source, lengths, place, *refs, mp, seq_dev, per_peer, steps, width, cols, quarter
-):
-    blocks = refs[:mp]
-    w_in = refs[mp]
-    normed_t, projected, slope, weights_o, dscale, norm_o, inv_o, gated, gated_t, own = refs[
-        mp + 1 : mp + 11
-    ]
-    feat = refs[mp + 11]
-    here_dp = place[0]
-    here_mp = place[1]
-    part = width // mp
-    sources = [source[here_dp * seq_dev + k] for k in range(seq_dev)]
-    anchors = [lax.div(s, seq_dev) for s in sources]
-    counts = [lengths[s] for s in sources]
+
+    if len(outs) == dp:
+        for j in range(dp):
+
+            def put(count, value, j=j):
+                outs[j][count] = value
+
+            per_dest(jnp.bitwise_xor(here, j), put)
+    else:
+
+        def body(d, carry):
+            def put(count, value):
+                outs[0][d, count] = value
+
+            per_dest(d, put)
+            return carry
+
+        lax.fori_loop(0, dp, body, jnp.int32(0))
+
+
+def take_kernel(source, place, *refs, dp, seq_dev, per_peer, steps):
+    arrived, out, held = refs[:-2], refs[-2], refs[-1]
+    here = place[0]
+    if len(arrived) == dp:
+        for j in range(dp):
+            held[j] = arrived[j][...]
+    else:
+        held[...] = arrived[0][...]
+    anchors = [lax.div(source[here * seq_dev + k], seq_dev) for k in range(seq_dev)]
     for k in range(seq_dev):
         rank = jnp.int32(0)
         for earlier in range(k):
             rank = rank + (anchors[earlier] == anchors[k]).astype(I32)
-        slot = anchors[k] * per_peer + rank
-        for j in range(mp):
-            start = pl.multiple_of(jnp.bitwise_xor(here_mp, j) * part, part)
-            feat[k * steps : (k + 1) * steps, pl.ds(start, part)] = blocks[j][slot]
+        piece = jnp.bitwise_xor(here, anchors[k]) if len(arrived) == dp else anchors[k]
+        out[k * steps : (k + 1) * steps, :] = held[piece, rank]
+
+
+def forward_kernel(source, lengths, place, *refs, mp, seq_dev, steps, width, cols, quarter):
+    blocks = refs[:mp]
+    w_in = refs[mp]
+    normed_t, projected, slope, weights_o, dscale, norm_o, inv_o, gated_t, own = refs[
+        mp + 1 : mp + 10
+    ]
+    gated_out = refs[mp + 10 : 2 * mp + 10]
+    feat, gated = refs[2 * mp + 10 :]
+    here_dp = place[0]
+    here_mp = place[1]
+    part = width // mp
+    counts = [lengths[source[here_dp * seq_dev + k]] for k in range(seq_dev)]
+    for j in range(mp):
+        start = pl.multiple_of(jnp.bitwise_xor(here_mp, j) * part, part)
+        feat[:, pl.ds(start, part)] = blocks[j][...]
     rows_all = seq_dev * steps
     own[...] = feat[pl.ds(pl.multiple_of(here_mp * quarter, quarter), quarter), :]
-    normed = []
     for g in range(rows_all // BLOCK):
         rows = slice(g * BLOCK, (g + 1) * BLOCK)
         x = feat[rows, :].astype(F32)
@@ -140,15 +163,17 @@
             done = (norm * projected[0, rows, lanes].astype(F32)).astype(BF)
             gated[rows, lanes] = done
             gated_t[lanes, rows] = done.T
-
-
-def out_kernel(place, gathered, own, *refs, mp):
-    weights = refs[:mp]
-    unit, unit_bf, inv_o = refs[mp:]
-    here_mp = place[1]
+    for j in range(mp):
+        start = pl.multiple_of(jnp.bitwise_xor(here_mp, j) * quarter, quarter)
+        gated_out[j][...] = gated[pl.ds(start, quarter), :]
+
+
+def out_kernel(own, *refs, mp):
+    gathered, weights = refs[:mp], refs[mp : 2 * mp]
+    unit, unit_bf, inv_o = refs[2 * mp :]
     total = own[...].astype(F32)
     for j in range(mp):
-        total = total + dot_nn(gathered[jnp.bitwise_xor(here_mp, j)], weights[j][...])
+        total = total + dot_nn(gathered[j][...], weights[j][...])
     inv = lax.rsqrt(jnp.sum(total * total, axis=-1, keepdims=True) + EPS_UNIT)
     u = total * inv
     unit[...] = u
@@ -201,51 +226,92 @@
         looked[s : s + chunk, :] = dot_tn(hot, catalogue[...]).astype(BF)
 
 
-def loss_kernel(
-    source, lengths, place, items, code, unit, unit_bf, inv_out, out_cot, sending, hot, share,
-    *, seq_dev, steps, devices, capacity, chunk,
+def score_kernel(
+    place, items, code, code_far, unit, unit_far, expo, inv_o, total_o,
+    *, dp, devices, capacity, chunk,
 ):
-    events, width = unit.shape
-    slots = devices * capacity
-    position = place[1] * events + iota((1, events), 1)
-    valid = jnp.zeros((1, events), F32)
-    for k in range(seq_dev):
-        count = lengths[source[place[0] * seq_dev + k]]
-        step = position - k * steps
-        valid = jnp.where((step >= 0) & (step < count), 1.0, valid)
-    total = jnp.zeros((1, events), F32)
-    scaled = []
+    events = unit.shape[0]
+    near = devices // 2
+    slots = items.shape[0]
+    half = pl.multiple_of(lax.div(place[0], dp // 2) * near, near)
+    codes_in = [c[pl.ds(half, near), :].astype(BF) for c in (code, code_far)]
     for s in range(0, slots, chunk):
         rows = slice(s, s + chunk)
         x = items[rows, :]
         xf = x.astype(F32)
         inv = lax.rsqrt(jnp.sum(xf * xf, axis=-1, keepdims=True) + EPS_UNIT)
-        logits = dot_nt(x, unit_bf[...]) * (inv * (1.0 / COSINE_DIVISOR))
+        inv_o[rows, :] = jnp.broadcast_to(inv, (chunk, BLOCK))
         slot = s + iota((chunk, 1), 0).astype(F32)
-        owner = jnp.floor((slot + 0.5) * (1.0 / capacity))
-        local = slot - owner * capacity
-        spread = (owner == iota((chunk, devices), 1).astype(F32)).astype(BF)
-        codes = dot_nn(spread, code[...].astype(BF))
-        first = codes == 2.0 * local + 2.0
-        mine = first | (codes == 2.0 * local + 1.0)
-        hot[rows, :] = mine.astype(BF)
-        expo = jnp.where(mine, jnp.exp(logits), 0.0)
-        total = total + jnp.sum(expo, axis=0, keepdims=True)
-        share[rows, :] = expo
-        scaled.append((first, inv))
-    factor = valid / total
-    slope = jnp.zeros((events, width), F32)
-    for n, s in enumerate(range(0, slots, chunk)):
+        owner = jnp.floor((slot + 0.5) * (1.0 / (2 * capacity)))
+        local = slot - owner * (2 * capacity)
+        far = local >= capacity
+        local = jnp.where(far, local - capacity, local)
+        named = owner == iota((chunk, near), 1).astype(F32)
+        for side in range(2):
+            lanes = slice(side * events, (side + 1) * events)
+            u = (unit, unit_far)[side][...]
+            logits = dot_nt(x, u) * (inv * (1.0 / COSINE_DIVISOR))
+            spread = jnp.where(named & (far == (side == 1)), 1.0, 0.0).astype(BF)
+            codes = dot_nn(spread, codes_in[side])
+            first = codes == 2.0 * local + 2.0
+            other = codes == 2.0 * local + 1.0
+            e = jnp.exp(logits)
+            total_o[:, lanes] = (
+                jnp.sum(jnp.where(first | other, e, 0.0), axis=0, keepdims=True)
+                + (total_o[:, lanes] if s else 0.0)
+            )
+            expo[rows, lanes] = jnp.where(first, -e, jnp.where(other, e, 0.0))
+
+
+def shares(source, lengths, place, expo, total, total_far, dp, seq_dev, steps):
+    events = total.shape[1] // 2
+    position = place[1] * events + iota((1, events), 1)
+    valid = []
+    for base in (place[0], jnp.bitwise_xor(place[0], dp // 2)):
+        v = jnp.zeros((1, events), F32)
+        for k in range(seq_dev):
+            step = position - k * steps
+            v = jnp.where((step >= 0) & (step < lengths[source[base * seq_dev + k]]), 1.0, v)
+        valid.append(v)
+    valid = jnp.concatenate(valid, axis=1) * (1.0 / COSINE_DIVISOR)
+    full = total[...] + jnp.concatenate([total_far[:, events:], total_far[:, :events]], axis=1)
+    factor = valid / full
+    return lambda rows: jnp.abs(expo[rows, :]) * factor - jnp.where(expo[rows, :] < 0.0, valid, 0.0)
+
+
+def slope_kernel(
+    source, lengths, place, items, expo, inv, total, total_far, slope, slope_far,
+    *, dp, seq_dev, steps, chunk,
+):
+    share = shares(source, lengths, place, expo, total, total_far, dp, seq_dev, steps)
+    events, width = slope.shape
+    both = jnp.zeros((2 * events, width), F32)
+    for s in range(0, items.shape[0], chunk):
         rows = slice(s, s + chunk)
-        first, inv = scaled[n]
-        part = share[rows, :] * factor - jnp.where(first, valid, 0.0)
-        part = part * (1.0 / COSINE_DIVISOR)
-        slope = slope + dot_tn((part * inv).astype(BF), items[rows, :])
-        weight = jnp.sum(part, axis=1, keepdims=True)
-        sending[rows, :] = (dot_nn(hot[rows, :], unit_bf[...]) * weight).astype(BF)
+        both = both + dot_tn((share(rows) * inv[rows, 0:1]).astype(BF), items[rows, :])
+    slope[...] = both[:events]
+    slope_far[...] = both[events:].astype(BF)
+
+
+def send_kernel(
+    source, lengths, place, expo, total, total_far, unit, unit_far, sending,
+    *, dp, seq_dev, steps, chunk,
+):
+    share = shares(source, lengths, place, expo, total, total_far, dp, seq_dev, steps)
+    events = unit.shape[0]
+    for s in range(0, expo.shape[0], chunk):
+        rows = slice(s, s + chunk)
+        hot = jnp.where(expo[rows, :] == 0.0, 0.0, 1.0).astype(BF)
+        unit_rows = dot_nn(hot[:, :events], unit[...]) + dot_nn(hot[:, events:], unit_far[...])
+        weight = jnp.sum(share(rows), axis=1, keepdims=True)
+        sending[rows, :] = (unit_rows * weight).astype(BF)
+
+
+def out_cot_kernel(unit, inv_out, slope, slope_far, out_cot):
     u = unit[...]
-    along = jnp.sum(u * slope, axis=-1, keepdims=True)
-    out_cot[...] = ((slope - u * along) * inv_out[:, 0:1]).astype(BF)
+    s = slope[...] + slope_far[...].astype(F32)
+    along = jnp.sum(u * s, axis=-1, keepdims=True)
+    out_cot[...] = ((s - u * along) * inv_out[:, 0:1]).astype(BF)
 
 
 def spread_kernel(incoming, landed, catalogue, out, *, chunk):
@@ -260,22 +326,42 @@
         out[r : r + chunk, :] = (v - c * jnp.sum(c * v, axis=-1, keepdims=True)) * inv
 
 
+def put_pieces(outs, index, here, dp, whole, share):
+    if len(outs) == dp:
+        for j in range(dp):
+            start = pl.multiple_of(jnp.bitwise_xor(here, j) * share, share)
+            outs[j][index] = whole[pl.ds(start, share), :]
+    else:
+        for d in range(dp):
+            outs[0][(d,) + index] = whole[d * share : (d + 1) * share, :]
+
+
 def w_out_kernel(place, *refs, mp, dp):
-    blocks = refs[:mp]
-    gated_t, out, whole = refs[mp:]
+    blocks, gated_t, outs, whole = refs[:mp], refs[mp], refs[mp + 1 : -1], refs[-1]
     quarter, width = blocks[0].shape
     for j in range(mp):
         start = pl.multiple_of(jnp.bitwise_xor(place[1], j) * quarter, quarter)
         whole[pl.ds(start, quarter), :] = blocks[j][...]
     part = dot_nn(gated_t[...], whole[...]).astype(BF)
     lanes = width // dp
-    for d in range(dp):
-        out[d] = part[:, d * lanes : (d + 1) * lanes]
+    if len(outs) == dp:
+        spare = jnp.stack([part[:, d * lanes : (d + 1) * lanes] for d in range(dp)])
+        for d in range(dp):
+            for j in range(dp):
+
+                @pl.when(jnp.bitwise_xor(place[0], j) == d)
+                def _(d=d, j=j):
+                    outs[j][...] = spare[d]
+    else:
+        for d in range(dp):
+            outs[0][d] = part[:, d * lanes : (d + 1) * lanes]
 
 
 def backward_kernel(place, *refs, mp, dp):
     blocks = refs[:mp]
-    w_out, projected, slope, weights, dscale, norm, inv, normed_t, out, whole, cot = refs[mp:]
+    w_out, projected, slope, weights, dscale, norm, inv, normed_t = refs[mp : mp + 8]
+    outs = refs[mp + 8 : -3]
+    whole, cot, parts = refs[-3:]
     quarter, width = blocks[0].shape
     for j in range(mp):
         start = pl.multiple_of(jnp.bitwise_xor(place[1], j) * quarter, quarter)
@@ -305,9 +391,8 @@
                 cot[c, rows, lanes] = (d.astype(BF).astype(F32) * slope[c, rows, lanes]).astype(BF)
     share = width // dp
     for c in range(4):
-        part = dot_nn(normed_t[...], cot[c]).astype(BF)
-        for d in range(dp):
-            out[d, c] = part[d * share : (d + 1) * share, :]
+        parts[...] = dot_nn(normed_t[...], cot[c]).astype(BF)
+        put_pieces(outs, (c,), place[0], dp, parts, share)
 
 
 def swapped(x, axis, bit):
@@ -326,10 +411,31 @@
     return [blocks[j] for j in range(size)]
 
 
+def pieces(n, shape, dtype):
+    S = jax.ShapeDtypeStruct
+    return [S(shape, dtype)] * n if n <= 8 else [S((n,) + shape, dtype)]
+
+
+def exchange(parts, axis):
+    if len(parts) > 1:
+        return [p if j == 0 else swapped(p, axis, j) for j, p in enumerate(parts)]
+    return [lax.all_to_all(parts[0], axis, split_axis=0, concat_axis=0, tiled=True)]
+
+
+def summed(parts):
+    if len(parts) == 1:
+        return jnp.sum(parts[0].astype(F32), axis=0)
+    total = parts[0].astype(F32)
+    for p in parts[1:]:
+        total = total + p.astype(F32)
+    return total
+
+
 def per_device(history, lengths, source, owners, item_rows, catalogue, w_in, w_out):
     dp = lax.axis_size("dp")
     mp = lax.axis_size("mp")
     devices = dp * mp
+    near = devices // 2
     seq_dev, steps, part = history.shape
     width = part * mp
     cols = w_in.shape[2]
@@ -342,8 +448,24 @@
     stock = catalogue.shape[0]
     per_peer = (seq_dev + dp - 1) // dp
     chunk = math.gcd(slots, 512)
+    heads = cols // DH
     S = jax.ShapeDtypeStruct
-    place = jnp.stack([lax.axis_index("dp"), lax.axis_index("mp")]).astype(I32)
+    here_dp = lax.axis_index("dp")
+    place = jnp.stack([here_dp, lax.axis_index("mp")]).astype(I32)
+    halves = [list(range(near)), list(range(near, devices))]
+
+    def partner(x):
+        return swapped(x, "dp", dp // 2)
+
+    def in_half(x):
+        return lax.all_to_all(
+            x.reshape(near, 2 * capacity, width),
+            ("dp", "mp"),
+            split_axis=0,
+            concat_axis=0,
+            tiled=True,
+            axis_index_groups=halves,
+        ).reshape(slots, width)
 
     wanted, code = call(
         functools.partial(ask_kernel, devices=devices, capacity=capacity),
@@ -352,9 +474,10 @@
         1e6,
         1e5,
     )(owners, item_rows)
-    incoming = lax.all_to_all(
-        wanted, ("dp", "mp"), split_axis=0, concat_axis=0, tiled=True
-    ).reshape(1, slots)
+    asked = lax.all_to_all(wanted, ("dp", "mp"), split_axis=0, concat_axis=0, tiled=True)
+    asked = asked.reshape(2, near, capacity)
+    incoming = jnp.where(here_dp < dp // 2, asked, asked[::-1])
+    incoming = incoming.transpose(1, 0, 2).reshape(1, slots)
     looked = call(
         functools.partial(look_kernel, chunk=chunk),
         S((slots, width), BF),
@@ -362,30 +485,33 @@
         2 * slots * stock * width,
         2 * (slots + stock) * width,
     )(incoming, catalogue)
-    returned = lax.all_to_all(
-        looked.reshape(devices, capacity, width),
-        ("dp", "mp"),
-        split_axis=0,
-        concat_axis=0,
-        tiled=True,
-    ).reshape(slots, width)
-
-    outgoing = call(
+    items = in_half(looked)
+
+    packed = call(
         functools.partial(pack_kernel, dp=dp, seq_dev=seq_dev, per_peer=per_peer),
-        S((dp * per_peer, steps, part), BF),
+        pieces(dp, (per_peer, steps, part), BF),
         [SM, SM, VM],
         1e5,
         4 * history.size,
     )(source, place, history)
-    arrived = lax.all_to_all(outgoing, "dp", split_axis=0, concat_axis=0, tiled=True)
-    features = gather_blocks(arrived, "mp")
-    heads = cols // DH
-    (normed_t, projected, slope, weights, dscale, norm, inv, gated, gated_t, own) = call(
+    arrived = exchange(packed, "dp")
+    looked, arrived = lax.optimization_barrier((looked, arrived))
+    rows = call(
+        functools.partial(take_kernel, dp=dp, seq_dev=seq_dev, per_peer=per_peer, steps=steps),
+        S((rows_all, part), BF),
+        [SM, SM] + [VM] * len(arrived),
+        1e5,
+        4 * history.size,
+        scratch=[pltpu.VMEM((dp, per_peer, steps, part), BF)],
+    )(source, place, *arrived)
+    features = gather_blocks(rows, "mp")
+    w_out_blocks = gather_blocks(w_out, "mp")
+    features, w_out_blocks = lax.optimization_barrier((features, w_out_blocks))
+    (normed_t, projected, slope, weights, dscale, norm, inv, gated_t, own, *gated) = call(
         functools.partial(
             forward_kernel,
             mp=mp,
             seq_dev=seq_dev,
-            per_peer=per_peer,
             steps=steps,
             width=width,
             cols=cols,
@@ -399,55 +525,62 @@
             S((heads, rows_all, BLOCK), F32),
             S((rows_all, cols), F32),
             S((rows_all, cols), F32),
-            S((rows_all, cols), BF),
             S((cols, rows_all), BF),
             S((quarter, width), BF),
-        ],
+        ]
+        + [S((quarter, cols), BF)] * mp,
         [SM, SM, SM] + [VM] * (mp + 1),
         8 * rows_all * width * cols,
         12 * 2**20,
-        scratch=[pltpu.VMEM((rows_all, width), BF)],
+        scratch=[pltpu.VMEM((rows_all, width), BF), pltpu.VMEM((rows_all, cols), BF)],
         trans=6 * rows_all * cols,
     )(source, lengths, place, *features, w_in)
-    w_out_blocks = gather_blocks(w_out, "mp")
-    gathered = lax.all_to_all(
-        gated.reshape(mp, quarter, cols), "mp", split_axis=0, concat_axis=0, tiled=True
-    )
+    gathered = exchange(gated, "mp")
     unit, unit_bf, inv_out = call(
         functools.partial(out_kernel, mp=mp),
         [S((quarter, width), F32), S((quarter, width), BF), S((quarter, BLOCK), F32)],
-        [SM] + [VM] * (mp + 2),
+        [VM] * (2 * mp + 1),
         2 * quarter * width * width,
         4 * 2**20,
-    )(place, gathered, own, *w_out_blocks)
-
-    out_cot, sending = call(
+    )(own, *gathered, *w_out_blocks)
+
+    code_far = partner(code)
+    unit_far = partner(unit_bf)
+    expo, inv_item, total = call(
         functools.partial(
-            loss_kernel,
-            seq_dev=seq_dev,
-            steps=steps,
-            devices=devices,
-            capacity=capacity,
-            chunk=chunk,
+            score_kernel, dp=dp, devices=devices, capacity=capacity, chunk=chunk
         ),
-        [S((quarter, width), BF), S((slots, width), BF)],
+        [S((slots, 2 * events), F32), S((slots, BLOCK), F32), S((1, 2 * events), F32)],
+        [SM] + [VM] * 5,
+        4 * slots * width * events,
+        2 * slots * width,
+    )(place, items, code, code_far, unit_bf, unit_far)
+    total_far = partner(total)
+    sizes = dict(dp=dp, seq_dev=seq_dev, steps=steps, chunk=chunk)
+    item_slope, slope_far = call(
+        functools.partial(slope_kernel, **sizes),
+        [S((events, width), F32), S((events, width), BF)],
         [SM, SM, SM] + [VM] * 5,
-        6 * slots * width * events,
-        4 * slots * width,
-        scratch=[pltpu.VMEM((slots, events), BF), pltpu.VMEM((slots, events), F32)],
-    )(source, lengths, place, returned, code, unit, unit_bf, inv_out)
-    landed = lax.all_to_all(
-        sending.reshape(devices, capacity, width),
-        ("dp", "mp"),
-        split_axis=0,
-        concat_axis=0,
-        tiled=True,
-    ).reshape(slots, width)
+        4 * slots * width * events,
+        2 * slots * width,
+    )(source, lengths, place, items, expo, inv_item, total, total_far)
+    slope_back = partner(slope_far)
+    sending = call(
+        functools.partial(send_kernel, **sizes),
+        S((slots, width), BF),
+        [SM, SM, SM] + [VM] * 5,
+        4 * slots * width * events,
+        2 * slots * width,
+    )(source, lengths, place, expo, total, total_far, unit_bf, unit_far)
+    landed = in_half(sending)
+    out_cot = call(
+        out_cot_kernel, S((events, width), BF), [VM] * 4, 1e6, 2 * 2**20
+    )(unit, inv_out, item_slope, slope_back)
 
     cots = gather_blocks(out_cot, "mp")
     w_out_part = call(
         functools.partial(w_out_kernel, mp=mp, dp=dp),
-        S((dp, cols, width // dp), BF),
+        pieces(dp, (cols, width // dp), BF),
         [SM] + [VM] * (mp + 1),
         2 * rows_all * width * cols,
         3 * 2**20,
@@ -455,19 +588,18 @@
     )(place, *cots, gated_t)
     w_in_part = call(
         functools.partial(backward_kernel, mp=mp, dp=dp),
-        S((dp, 4, width // dp, cols), BF),
+        pieces(dp, (4, width // dp, cols), BF),
         [SM] + [VM] * (mp + 8),
         10 * rows_all * width * cols,
         12 * 2**20,
-        scratch=[pltpu.VMEM((rows_all, width), BF), pltpu.VMEM((4, rows_all, cols), BF)],
+        scratch=[
+            pltpu.VMEM((rows_all, width), BF),
+            pltpu.VMEM((4, rows_all, cols), BF),
+            pltpu.VMEM((width, cols), BF),
+        ],
     )(place, *cots, w_out, projected, slope, weights, dscale, norm, inv, normed_t)
-
-    def summed(x):
-        got = lax.all_to_all(x, "dp", split_axis=0, concat_axis=0, tiled=True)
-        return jnp.sum(got.astype(F32), axis=0)
-
-    w_out_grad = summed(w_out_part)
-    w_in_grad = summed(w_in_part)
+    w_out_grad = summed(exchange(w_out_part, "dp"))
+    w_in_grad = summed(exchange(w_in_part, "dp"))
     cat_grad = call(
         functools.partial(spread_kernel, chunk=math.gcd(stock, 128)),
         S((stock, width), F32),

time: 313 us -> 281 us (0.90)
  blocking collectives: 65.1 us -> 0 us
  starting transfers between devices: 38.9 us -> 68.6 us
  waiting for transfers between devices: 139 us -> 155 us
  local copies, waits for them, and re-layouts: 26.7 us -> 18.1 us
  other arithmetic: 5.26 us -> 1.87 us
    ppermute x9 -> x37, waiting for transfers between devices: 44.2 us -> 151 us  [swapped(): return lax.ppermute(x, axis, [(a, a ^ bit) for a in range(size)])]
    all_to_all x4 -> x2, waiting for transfers between devices: 95.1 us -> 0.01 us  [in_half(): lax.all_to_all(x.reshape(near, 2 * capacity, width), ('dp', 'mp'), split_...]
    all_to_all x2 -> x0, blocking collectives: 65.1 us -> none  [the longest x1 53.4 us: summed(): got = lax.all_to_all(x, 'dp', split_axis=0, concat_axis=0, tiled=True)]
    ppermute x9 -> x37, starting transfers between devices: 10.8 us -> 48.6 us  [swapped(): return lax.ppermute(x, axis, [(a, a ^ bit) for a in range(size)])]
    all_to_all x4 -> x2, starting transfers between devices: 22.8 us -> 13.7 us  [in_half(): lax.all_to_all(x.reshape(near, 2 * capacity, width), ('dp', 'mp'), split_...]
    unnamed x72, local copies, waits for them, and re-layouts: 26.1 us -> 17.9 us
    all_to_all x1, waiting for transfers between devices: 0.01 us -> 4.66 us  [per_device(): lax.all_to_all(wanted, ('dp', 'mp'), split_axis=0, concat_axis=0, tiled=T...]
    reduce_sum x2 -> x0, other arithmetic: 4.5 us -> none  [summed(): return jnp.sum(got.astype(F32), axis=0)]
  transfers between devices with their start and end apart: 14 -> 40, of which waited for: 7 -> 22; matrix products, arithmetic and copies ran while one was open for 2% -> 1% of each run, Pallas kernels for 6% -> 6%
where the time goes in v2:
time: 281 us; the launch traced here: 276 us
  waiting for transfers between devices  155 us (55%)
  starting transfers between devices  68.6 us (24%)
  Pallas kernels  31.2 us (11%)
  local copies, waits for them, and re-layouts  18.1 us (6%)
    ppermute x37, waiting for transfers between devices, swapped(): return lax.ppermute(x, axis, [(a, a ^ bit) for a in range(size)])  151 us
    ppermute x37, starting transfers between devices, swapped(): return lax.ppermute(x, axis, [(a, a ^ bit) for a in range(size)])  48.6 us
    unnamed x72, local copies, waits for them, and re-layouts  17.9 us
    all_to_all x2, starting transfers between devices, in_half(): lax.all_to_all(x.reshape(near, 2 * capacity, width), ('dp', 'mp'), split_...  13.7 us
    all_to_all x1, starting transfers between devices, per_device(): lax.all_to_all(wanted, ('dp', 'mp'), split_axis=0, concat_axis=0, tiled=T...  6.3 us
  transfers between devices with their start and end apart: 40, of which 22 were waited for; matrix products, arithmetic and copies ran while one was open for 1% of the time, Pallas kernels for 6%

profile of v2, /device:TPU:13, one launch (start us, length us, event | category | flops | bytes accessed | tf_op | source)
XLA Modules:
  0.0 276.1 jit_solution(1952118670098955314)
XLA Ops:
  3.5 6.3 %all-to-all-start = ((s32[32,1,48]{2,1,0:T(1,128)}), s32[32,1,48]{2,1,0:T(1,128)S(1)}, u32[]{:S(2)}, u32[]{:S(2)}) async-start(s32[32,1,48]{2,1,0:T(1,128)} %bitcast.3), calls=%async_computation | async-start | bytes 32768 | tf_op jit(solution)/shard_map/all_to_all | solution.py:477
  9.8 4.7 %all-to-all-done = s32[32,1,48]{2,1,0:T(1,128)S(1)} async-done(((s32[32,1,48]{2,1,0:T(1,128)}), s32[32,1,48]{2,1,0:T(1,128)S(1)}, u32[]{:S(2)}, u32[]{:S(2)}) %all-to-all-start) | async-done | bytes 6176 | tf_op jit(solution)/shard_map/all_to_all | solution.py:477
  15.9 1.8 shard_map.104
  17.7 1.6 copy-done.3
  19.3 6.4 %all-to-all-start.1 = ((bf16[16,96,1024]{2,1,0:T(8,128)(2,1)}), bf16[16,96,1024]{2,1,0:T(8,128)(2,1)S(1)}, u32[]{:S(2)}, u32[]{:S(2)}) async-start(bf16[16,96,1024]{2,1,0:T(8,128)(2,1)} %bitcast.15), calls=%async_computation.1 | async-start | bytes 6291456 | tf_op jit(solution)/shard_map/all_to_all | solution.py:461
  26.1 2.9 %shard_map.105 = (bf16[2,32,256]{2,1,0:T(8,128)(2,1)S(1)}, bf16[2,32,256]{2,1,0:T(8,128)(2,1)S(1)}, bf16[2,32,256]{2,1,0:T(8,128)(2,1)S(1)}, bf16[2,32,256]{2,1,...) custom-call(s32[128]{0:T(128)S(1)} %copy-done.32, ...), custom_call_target="tpu_custom_call" | custom-call | flops 100000 | bytes 524288 | tf_op jit(solution)/shard_map/pallas_call | solution.py:490
  32.0 35.9 %collective-permute-done.refs_1_ = bf16[2,32,256]{2,1,0:T(8,128)(2,1)S(1)} collective-permute-done((bf16[2,32,256]{2,1,0:T(8,128)(2,1)S(1)}, bf16[2,32,256]{2,1,0:T(8,128)(2,1)S(1)}, u32[]{:S(2)}, u32[]{:S(2)}) %collective-permute-start) | collective-permute-done | bytes 32800 | tf_op jit(solution)/shard_map/ppermute | solution.py:400
  68.0 2.3 collective-permute-start.4
  71.5 1.3 collective-permute-start.10
  76.4 3.7 %collective-permute-start.12 = (bf16[256,1024]{1,0:T(8,128)(2,1)}, bf16[256,1024]{1,0:T(8,128)(2,1)S(1)}, u32[]{:S(2)}, u32[]{:S(2)}) collective-permute-start(bf16[256,1024]{1,0:T(8,128)(2,1)} %collective-permute-done.11.refs_6_), channel_id=1, source_target_pairs={{0,1},{1,0},{2,3},{3,2},{4,5},{5,4},{6,7},{7,6},{8,9},{9,8},{10,11... | collective-permute-start | bytes 1572872 | tf_op jit(solution)/shard_map/ppermute | solution.py:400
  80.6 3.8 %collective-permute-start.9 = (bf16[512,256]{1,0:T(8,128)(2,1)S(1)}, bf16[512,256]{1,0:T(8,128)(2,1)S(1)}, u32[]{:S(2)}, u32[]{:S(2)}) collective-permute-start(bf16[512,256]{1,0:T(8,128)(2,1)S(1)} %collective-permute-done.8.refs_2_), channel_id=1, source_target_pairs={{0,1},{1,0},{2,3},{3,2},{4,5},{5,4},{6,7},{7,6},{8,9},{9,8},{10,11... | collective-permute-start | bytes 786440 | tf_op jit(solution)/shard_map/ppermute | solution.py:400
  85.6 1.6 copy-done.34
  87.2 4.2 %shard_map.107 = (bf16[1024,512]{1,0:T(8,128)(2,1)S(1)}, bf16[4,512,256]{2,1,0:T(8,128)(2,1)S(1)}, f32[4,512,256]{2,1,0:T(8,128)S(1)}, bf16[2,512,128]{2,1,0:T(8...) custom-call(s32[128]{0:T(128)S(1)} %copy-done.32, ...), custom_call_target="tpu_custom_call" | custom-call | flops 1073741824 | bytes 12582912 | tf_op jit(solution)/shard_map/pallas_call | solution.py:510
  91.4 1.3 copy-done.4
  96.1 1.7 collective-permute-start.14
  97.9 2.2 collective-permute-done.14.refs_2_
  100.2 1.9 collective-permute-done.15.refs_3_
  102.1 1.6 shard_map.108
  104.5 3.5 %collective-permute-start.17 = (bf16[128,1024]{1,0:T(8,128)(2,1)S(1)}, bf16[128,1024]{1,0:T(8,128)(2,1)S(1)}, u32[]{:S(2)}, u32[]{:S(2)}) collective-permute-start(bf16[128,1024]{1,0:T(8,128)(2,1)S(1)} %get-tuple-element.99.unit), channel_id=1, source_target_pairs={{0,16},{4,20},{8,24},{12,28},{16,0},{20,4},{24,8},{28,12},{1,17},{... | collective-permute-start | bytes 786440 | tf_op jit(solution)/shard_map/ppermute | solution.py:400
  108.0 12.1 %collective-permute-done.16.code_far = f32[32,128]{1,0:T(8,128)S(1)} collective-permute-done((f32[32,128]{1,0:T(8,128)S(1)}, f32[32,128]{1,0:T(8,128)S(1)}, u32[]{:S(2)}, u32[]{:S(2)}) %collective-permute-start.16) | collective-permute-done | bytes 16416 | tf_op jit(solution)/shard_map/ppermute | solution.py:400
  121.8 3.0 %shard_map.109 = (f32[1536,256]{1,0:T(8,128)S(1)}, f32[1536,128]{1,0:T(8,128)S(1)}, f32[1,256]{1,0:T(1,128)S(1)}) custom-call(s32[2]{0:T(128)S(1)} %pad_add_fusion.place, bf16[1536,1024]{1,0:T(8,128)(2,1)S(1)} %bitcast.12, f32[32,128]{1,0:T(8,128)S(1)} %get-tuple-element.98.code, f32[32,128]{1,0:T(8,128)S(1)} %collective-permute-done.16.code_far, ...), custom_call_target="tpu_custom_call" | custom-call | flops 805306368 | bytes 3145728 | tf_op jit(solution)/shard_map/pallas_call | solution.py:549
  125.7 3.1 %collective-permute-start.18 = (f32[1,256]{1,0:T(1,128)S(1)}, f32[1,256]{1,0:T(1,128)S(1)}, u32[]{:S(2)}, u32[]{:S(2)}) collective-permute-start(f32[1,256]{1,0:T(1,128)S(1)} %get-tuple-element.102.total), channel_id=1, source_target_pairs={{0,16},{4,20},{8,24},{12,28},{16,0},{20,4},{24,8},{28,12},{1,17},{... | collective-permute-start | bytes 3080 | tf_op jit(solution)/shard_map/ppermute | solution.py:400
  129.8 2.3 shard_map.114
  132.2 1.7 copy-done
  133.8 7.3 %all-to-all-start.2 = ((bf16[16,96,1024]{2,1,0:T(8,128)(2,1)}), bf16[16,96,1024]{2,1,0:T(8,128)(2,1)}, u32[]{:S(2)}, u32[]{:S(2)}) async-start(bf16[16,96,1024]{2,1,0:T(8,128)(2,1)} %bitcast.14), calls=%async_computation.2 | async-start | bytes 6291456 | tf_op jit(solution)/shard_map/all_to_all | solution.py:461
  141.2 1.4 copy-done.2
  143.8 1.7 shard_map.110
  146.0 41.0 %collective-permute-done.19.slope_far = bf16[128,1024]{1,0:T(8,128)(2,1)S(1)} collective-permute-done((bf16[128,1024]{1,0:T(8,128)(2,1)S(1)}, bf16[128,1024]{1,0:T(8,128)(2,1)S(1)}, u32[]{:S(2)}, u32[]{:S(2)}) %collective-permute-start.19) | collective-permute-done | bytes 262176 | tf_op jit(solution)/shard_map/ppermute | solution.py:400
  188.6 5.4 %collective-permute-done.21.refs_2_ = bf16[128,1024]{1,0:T(8,128)(2,1)S(1)} collective-permute-done((bf16[128,1024]{1,0:T(8,128)(2,1)S(1)}, bf16[128,1024]{1,0:T(8,128)(2,1)S(1)}, u32[]{:S(2)}, u32[]{:S(2)}) %collective-permute-start.21) | collective-permute-done | bytes 262176 | tf_op jit(solution)/shard_map/ppermute | solution.py:400
  194.0 2.1 collective-permute-start.22
  197.3 4.3 %shard_map.112 = (bf16[4,128,256]{2,1,0:T(8,128)(2,1)S(1)}, bf16[4,128,256]{2,1,0:T(8,128)(2,1)S(1)}, bf16[4,128,256]{2,1,0:T(8,128)(2,1)S(1)}, bf16[4,128,256]{...) custom-call(s32[2]{0:T(128)S(1)} %pad_add_fusion.place, ...), custom_call_target="tpu_custom_call" | custom-call | flops 1342177280 | bytes 12582912 | tf_op jit(solution)/shard_map/pallas_call | solution.py:589
  201.6 1.5 collective-permute-start.23
  203.1 2.0 collective-permute-start.24
  205.1 1.6 shard_map.113
  206.9 2.5 collective-permute-start.32
  210.7 1.7 collective-permute-start.33
  212.5 2.1 collective-permute-start.34
  214.7 2.4 collective-permute-start.35
  217.1 1.9 collective-permute-start.36
  219.0 2.5 collective-permute-done.34
  221.5 2.4 collective-permute-start.25
  224.6 2.4 collective-permute-done.36
  227.8 1.6 collective-permute-start.29
  230.0 3.7 %collective-permute-done.26 = bf16[4,128,256]{2,1,0:T(8,128)(2,1)S(1)} collective-permute-done((bf16[4,128,256]{2,1,0:T(8,128)(2,1)S(1)}, bf16[4,128,256]{2,1,0:T(8,128)(2,1)S(1)}, u32[]{:S(2)}, u32[]{:S(2)}) %collective-permute-start.26) | collective-permute-done | bytes 262176 | tf_op jit(solution)/shard_map/ppermute | solution.py:400
  233.8 23.0 %collective-permute-done.27 = bf16[4,128,256]{2,1,0:T(8,128)(2,1)S(1)} collective-permute-done((bf16[4,128,256]{2,1,0:T(8,128)(2,1)S(1)}, bf16[4,128,256]{2,1,0:T(8,128)(2,1)S(1)}, u32[]{:S(2)}, u32[]{:S(2)}) %collective-permute-start.27) | collective-permute-done | bytes 262176 | tf_op jit(solution)/shard_map/ppermute | solution.py:400
  256.7 9.2 %collective-permute-done.28 = bf16[4,128,256]{2,1,0:T(8,128)(2,1)S(1)} collective-permute-done((bf16[4,128,256]{2,1,0:T(8,128)(2,1)S(1)}, bf16[4,128,256]{2,1,0:T(8,128)(2,1)S(1)}, u32[]{:S(2)}, u32[]{:S(2)}) %collective-permute-start.28) | collective-permute-done | bytes 262176 | tf_op jit(solution)/shard_map/ppermute | solution.py:400
  265.9 3.7 %collective-permute-done.29 = bf16[4,128,256]{2,1,0:T(8,128)(2,1)S(1)} collective-permute-done((bf16[4,128,256]{2,1,0:T(8,128)(2,1)S(1)}, bf16[4,128,256]{2,1,0:T(8,128)(2,1)S(1)}, u32[]{:S(2)}, u32[]{:S(2)}) %collective-permute-start.29) | collective-permute-done | bytes 262176 | tf_op jit(solution)/shard_map/ppermute | solution.py:400
  270.7 5.5 %shard_map.115 = f32[512,1024]{1,0:T(8,128)} custom-call(s32[1,1536]{1,0:T(1,128)S(1)} %reshape.28.incoming, bf16[1536,1024]{1,0:T(8,128)(2,1)} %bitcast.9.landed, bf16[512,1024]{1,0:T(8,128)(2,1)S(1)} %copy-done.9), custom_call_target="tpu_custom_call" | custom-call | flops 1610612736 | bytes 6291456 | tf_op jit(solution)/shard_map/pallas_call | solution.py:603
  (124 shorter events, 31.2 us)
Async XLA Ops:
  3.5 11.0 %all-to-all-start = ((s32[32,1,48]{2,1,0:T(1,128)}), s32[32,1,48]{2,1,0:T(1,128)S(1)}, u32[]{:S(2)}, u32[]{:S(2)}) async-start(s32[32,1,48]{2,1,0:T(1,128)} %bitcast.3), calls=%async_computation | async-start | bytes 32768 | tf_op jit(solution)/shard_map/all_to_all | solution.py:477
  19.3 66.3 %copy-start.33 = (s32[128]{0:T(128)S(1)}, s32[128]{0:T(128)}, u32[]{:S(2)}) copy-start(s32[128]{0:T(128)} %lengths.5) | copy-start | bytes 1540
  19.3 101.6 %all-to-all-start.1 = ((bf16[16,96,1024]{2,1,0:T(8,128)(2,1)}), bf16[16,96,1024]{2,1,0:T(8,128)(2,1)S(1)}, u32[]{:S(2)}, u32[]{:S(2)}) async-start(bf16[16,96,1024]{2,1,0:T(8,128)(2,1)} %bitcast.15), calls=%async_computation.1 | async-start | bytes 6291456 | tf_op jit(solution)/shard_map/all_to_all | solution.py:461
  25.7 50.7 %collective-permute-start.11 = (bf16[256,1024]{1,0:T(8,128)(2,1)}, bf16[256,1024]{1,0:T(8,128)(2,1)}, u32[]{:S(2)}, u32[]{:S(2)}) collective-permute-start(bf16[256,1024]{1,0:T(8,128)(2,1)} %refs_4_.4), channel_id=1, source_target_pairs={{0,2},{1,3},{2,0},{3,1},{4,6},{5,7},{6,4},{7,5},{8,10},{9,11},{10,... | collective-permute-start | bytes 1572872 | tf_op jit(solution)/shard_map/ppermute | solution.py:400
  26.1 76.0 %copy-start.6 = (bf16[256,1024]{1,0:T(8,128)(2,1)S(1)}, bf16[256,1024]{1,0:T(8,128)(2,1)}, u32[]{:S(2)}) copy-start(bf16[256,1024]{1,0:T(8,128)(2,1)} %refs_4_.4) | copy-start | bytes 1572868
  29.0 39.0 %collective-permute-start = (bf16[2,32,256]{2,1,0:T(8,128)(2,1)S(1)}, bf16[2,32,256]{2,1,0:T(8,128)(2,1)S(1)}, u32[]{:S(2)}, u32[]{:S(2)}) collective-permute-start(bf16[2,32,256]{2,1,0:T(8,128)(2,1)S(1)} %get-tuple-element.68), channel_id=1, source_target_pairs={{0,4},{4,0},{8,12},{12,8},{16,20},{20,16},{24,28},{28,24},{1,5},{5... | collective-permute-start | bytes 98312 | tf_op jit(solution)/shard_map/ppermute | solution.py:400
  30.3 40.0 %collective-permute-start.1 = (bf16[2,32,256]{2,1,0:T(8,128)(2,1)S(1)}, bf16[2,32,256]{2,1,0:T(8,128)(2,1)S(1)}, u32[]{:S(2)}, u32[]{:S(2)}) collective-permute-start(bf16[2,32,256]{2,1,0:T(8,128)(2,1)S(1)} %get-tuple-element.69), channel_id=1, source_target_pairs={{0,8},{4,12},{8,0},{12,4},{16,24},{20,28},{24,16},{28,20},{1,9},{5... | collective-permute-start | bytes 98312 | tf_op jit(solution)/shard_map/ppermute | solution.py:400
  30.5 39.7 %collective-permute-start.2 = (bf16[2,32,256]{2,1,0:T(8,128)(2,1)S(1)}, bf16[2,32,256]{2,1,0:T(8,128)(2,1)S(1)}, u32[]{:S(2)}, u32[]{:S(2)}) collective-permute-start(bf16[2,32,256]{2,1,0:T(8,128)(2,1)S(1)} %get-tuple-element.70), channel_id=1, source_target_pairs={{0,12},{4,8},{8,4},{12,0},{16,28},{20,24},{24,20},{28,16},{1,13},{... | collective-permute-start | bytes 98312 | tf_op jit(solution)/shard_map/ppermute | solution.py:400
  31.7 39.7 %collective-permute-start.3 = (bf16[2,32,256]{2,1,0:T(8,128)(2,1)S(1)}, bf16[2,32,256]{2,1,0:T(8,128)(2,1)S(1)}, u32[]{:S(2)}, u32[]{:S(2)}) collective-permute-start(bf16[2,32,256]{2,1,0:T(8,128)(2,1)S(1)} %get-tuple-element.71), channel_id=1, source_target_pairs={{0,16},{4,20},{8,24},{12,28},{16,0},{20,4},{24,8},{28,12},{1,17},{... | collective-permute-start | bytes 98312 | tf_op jit(solution)/shard_map/ppermute | solution.py:400
  68.0 4.8 %collective-permute-start.4 = (bf16[2,32,256]{2,1,0:T(8,128)(2,1)S(1)}, bf16[2,32,256]{2,1,0:T(8,128)(2,1)S(1)}, u32[]{:S(2)}, u32[]{:S(2)}) collective-permute-start(bf16[2,32,256]{2,1,0:T(8,128)(2,1)S(1)} %get-tuple-element.72), channel_id=1, source_target_pairs={{0,20},{4,16},{8,28},{12,24},{16,4},{20,0},{24,12},{28,8},{1,21},{... | collective-permute-start | bytes 98312 | tf_op jit(solution)/shard_map/ppermute | solution.py:400
  70.3 3.1 %collective-permute-start.5 = (bf16[2,32,256]{2,1,0:T(8,128)(2,1)S(1)}, bf16[2,32,256]{2,1,0:T(8,128)(2,1)S(1)}, u32[]{:S(2)}, u32[]{:S(2)}) collective-permute-start(bf16[2,32,256]{2,1,0:T(8,128)(2,1)S(1)} %get-tuple-element.73), channel_id=1, source_target_pairs={{0,24},{4,28},{8,16},{12,20},{16,8},{20,12},{24,0},{28,4},{1,25},{... | collective-permute-start | bytes 98312 | tf_op jit(solution)/shard_map/ppermute | solution.py:400
  70.3 4.3 %collective-permute-start.6 = (bf16[2,32,256]{2,1,0:T(8,128)(2,1)S(1)}, bf16[2,32,256]{2,1,0:T(8,128)(2,1)S(1)}, u32[]{:S(2)}, u32[]{:S(2)}) collective-permute-start(bf16[2,32,256]{2,1,0:T(8,128)(2,1)S(1)} %get-tuple-element.74), channel_id=1, source_target_pairs={{0,28},{4,24},{8,20},{12,16},{16,12},{20,8},{24,4},{28,0},{1,29},{... | collective-permute-start | bytes 98312 | tf_op jit(solution)/shard_map/ppermute | solution.py:400
  71.5 13.0 %collective-permute-start.10 = (bf16[256,1024]{1,0:T(8,128)(2,1)}, bf16[256,1024]{1,0:T(8,128)(2,1)S(1)}, u32[]{:S(2)}, u32[]{:S(2)}) collective-permute-start(bf16[256,1024]{1,0:T(8,128)(2,1)} %refs_4_.4), channel_id=1, source_target_pairs={{0,1},{1,0},{2,3},{3,2},{4,5},{5,4},{6,7},{7,6},{8,9},{9,8},{10,11... | collective-permute-start | bytes 1572872 | tf_op jit(solution)/shard_map/ppermute | solution.py:400
  75.3 5.3 %collective-permute-start.8 = (bf16[512,256]{1,0:T(8,128)(2,1)S(1)}, bf16[512,256]{1,0:T(8,128)(2,1)S(1)}, u32[]{:S(2)}, u32[]{:S(2)}) collective-permute-start(bf16[512,256]{1,0:T(8,128)(2,1)S(1)} %shard_map.106.refs_0_), channel_id=1, source_target_pairs={{0,2},{1,3},{2,0},{3,1},{4,6},{5,7},{6,4},{7,5},{8,10},{9,11},{10,... | collective-permute-start | bytes 786440 | tf_op jit(solution)/shard_map/ppermute | solution.py:400
  76.4 9.2 %collective-permute-start.12 = (bf16[256,1024]{1,0:T(8,128)(2,1)}, bf16[256,1024]{1,0:T(8,128)(2,1)S(1)}, u32[]{:S(2)}, u32[]{:S(2)}) collective-permute-start(bf16[256,1024]{1,0:T(8,128)(2,1)} %collective-permute-done.11.refs_6_), channel_id=1, source_target_pairs={{0,1},{1,0},{2,3},{3,2},{4,5},{5,4},{6,7},{7,6},{8,9},{9,8},{10,11... | collective-permute-start | bytes 1572872 | tf_op jit(solution)/shard_map/ppermute | solution.py:400
  80.1 4.4 %collective-permute-start.7 = (bf16[512,256]{1,0:T(8,128)(2,1)S(1)}, bf16[512,256]{1,0:T(8,128)(2,1)S(1)}, u32[]{:S(2)}, u32[]{:S(2)}) collective-permute-start(bf16[512,256]{1,0:T(8,128)(2,1)S(1)} %shard_map.106.refs_0_), channel_id=1, source_target_pairs={{0,1},{1,0},{2,3},{3,2},{4,5},{5,4},{6,7},{7,6},{8,9},{9,8},{10,11... | collective-permute-start | bytes 786440 | tf_op jit(solution)/shard_map/ppermute | solution.py:400
  80.6 5.0 %collective-permute-start.9 = (bf16[512,256]{1,0:T(8,128)(2,1)S(1)}, bf16[512,256]{1,0:T(8,128)(2,1)S(1)}, u32[]{:S(2)}, u32[]{:S(2)}) collective-permute-start(bf16[512,256]{1,0:T(8,128)(2,1)S(1)} %collective-permute-done.8.refs_2_), channel_id=1, source_target_pairs={{0,1},{1,0},{2,3},{3,2},{4,5},{5,4},{6,7},{7,6},{8,9},{9,8},{10,11... | collective-permute-start | bytes 786440 | tf_op jit(solution)/shard_map/ppermute | solution.py:400
  95.7 2.2 collective-permute-start.13
  96.1 4.1 %collective-permute-start.14 = (bf16[128,256]{1,0:T(8,128)(2,1)S(1)}, bf16[128,256]{1,0:T(8,128)(2,1)S(1)}, u32[]{:S(2)}, u32[]{:S(2)}) collective-permute-start(bf16[128,256]{1,0:T(8,128)(2,1)S(1)} %get-tuple-element.90), channel_id=1, source_target_pairs={{0,2},{1,3},{2,0},{3,1},{4,6},{5,7},{6,4},{7,5},{8,10},{9,11},{10,... | collective-permute-start | bytes 196616 | tf_op jit(solution)/shard_map/ppermute | solution.py:400
  97.9 4.2 %collective-permute-start.15 = (bf16[128,256]{1,0:T(8,128)(2,1)S(1)}, bf16[128,256]{1,0:T(8,128)(2,1)S(1)}, u32[]{:S(2)}, u32[]{:S(2)}) collective-permute-start(bf16[128,256]{1,0:T(8,128)(2,1)S(1)} %get-tuple-element.91), channel_id=1, source_target_pairs={{0,3},{1,2},{2,1},{3,0},{4,7},{5,6},{6,5},{7,4},{8,11},{9,10},{10,... | collective-permute-start | bytes 196616 | tf_op jit(solution)/shard_map/ppermute | solution.py:400
  104.5 15.7 %collective-permute-start.17 = (bf16[128,1024]{1,0:T(8,128)(2,1)S(1)}, bf16[128,1024]{1,0:T(8,128)(2,1)S(1)}, u32[]{:S(2)}, u32[]{:S(2)}) collective-permute-start(bf16[128,1024]{1,0:T(8,128)(2,1)S(1)} %get-tuple-element.99.unit), channel_id=1, source_target_pairs={{0,16},{4,20},{8,24},{12,28},{16,0},{20,4},{24,8},{28,12},{1,17},{... | collective-permute-start | bytes 786440 | tf_op jit(solution)/shard_map/ppermute | solution.py:400
  108.0 12.2 %collective-permute-start.16 = (f32[32,128]{1,0:T(8,128)S(1)}, f32[32,128]{1,0:T(8,128)S(1)}, u32[]{:S(2)}, u32[]{:S(2)}) collective-permute-start(f32[32,128]{1,0:T(8,128)S(1)} %get-tuple-element.98.code), channel_id=1, source_target_pairs={{0,16},{4,20},{8,24},{12,28},{16,0},{20,4},{24,8},{28,12},{1,17},{... | collective-permute-start | bytes 49160 | tf_op jit(solution)/shard_map/ppermute | solution.py:400
  125.7 4.1 %collective-permute-start.18 = (f32[1,256]{1,0:T(1,128)S(1)}, f32[1,256]{1,0:T(1,128)S(1)}, u32[]{:S(2)}, u32[]{:S(2)}) collective-permute-start(f32[1,256]{1,0:T(1,128)S(1)} %get-tuple-element.102.total), channel_id=1, source_target_pairs={{0,16},{4,20},{8,24},{12,28},{16,0},{20,4},{24,8},{28,12},{1,17},{... | collective-permute-start | bytes 3080 | tf_op jit(solution)/shard_map/ppermute | solution.py:400
  133.8 136.8 %all-to-all-start.2 = ((bf16[16,96,1024]{2,1,0:T(8,128)(2,1)}), bf16[16,96,1024]{2,1,0:T(8,128)(2,1)}, u32[]{:S(2)}, u32[]{:S(2)}) async-start(bf16[16,96,1024]{2,1,0:T(8,128)(2,1)} %bitcast.14), calls=%async_computation.2 | async-start | bytes 6291456 | tf_op jit(solution)/shard_map/all_to_all | solution.py:461
  143.7 53.5 %copy-start.5 = (f32[4,512,256]{2,1,0:T(8,128)S(1)}, f32[4,512,256]{2,1,0:T(8,128)}, u32[]{:S(2)}) copy-start(f32[4,512,256]{2,1,0:T(8,128)} %copy-done.4) | copy-start | bytes 6291460
  143.7 53.5 %copy-start.7 = (bf16[256,1024]{1,0:T(8,128)(2,1)S(1)}, bf16[256,1024]{1,0:T(8,128)(2,1)}, u32[]{:S(2)}) copy-start(bf16[256,1024]{1,0:T(8,128)(2,1)} %refs_4_.4) | copy-start | bytes 1572868
  143.7 53.5 %copy-start.14 = (bf16[1024,512]{1,0:T(8,128)(2,1)S(1)}, bf16[1024,512]{1,0:T(8,128)(2,1)}, u32[]{:S(2)}) copy-start(bf16[1024,512]{1,0:T(8,128)(2,1)} %copy-done.13) | copy-start | bytes 3145732
  143.7 53.5 %copy-start.16 = (bf16[4,512,256]{2,1,0:T(8,128)(2,1)S(1)}, bf16[4,512,256]{2,1,0:T(8,128)(2,1)}, u32[]{:S(2)}) copy-start(bf16[4,512,256]{2,1,0:T(8,128)(2,1)} %copy-done.15) | copy-start | bytes 3145732
  143.7 53.5 %copy-start.22 = (f32[2,512,128]{2,1,0:T(8,128)S(1)}, f32[2,512,128]{2,1,0:T(8,128)}, u32[]{:S(2)}) copy-start(f32[2,512,128]{2,1,0:T(8,128)} %copy-done.21) | copy-start | bytes 1572868
  145.5 41.5 %collective-permute-start.19 = (bf16[128,1024]{1,0:T(8,128)(2,1)S(1)}, bf16[128,1024]{1,0:T(8,128)(2,1)S(1)}, u32[]{:S(2)}, u32[]{:S(2)}) collective-permute-start(bf16[128,1024]{1,0:T(8,128)(2,1)S(1)} %get-tuple-element.104), channel_id=1, source_target_pairs={{0,16},{4,20},{8,24},{12,28},{16,0},{20,4},{24,8},{28,12},{1,17},{... | collective-permute-start | bytes 786440 | tf_op jit(solution)/shard_map/ppermute | solution.py:400
  187.3 6.7 %collective-permute-start.21 = (bf16[128,1024]{1,0:T(8,128)(2,1)S(1)}, bf16[128,1024]{1,0:T(8,128)(2,1)S(1)}, u32[]{:S(2)}, u32[]{:S(2)}) collective-permute-start(bf16[128,1024]{1,0:T(8,128)(2,1)S(1)} %shard_map.111.refs_0_), channel_id=1, source_target_pairs={{0,2},{1,3},{2,0},{3,1},{4,6},{5,7},{6,4},{7,5},{8,10},{9,11},{10,... | collective-permute-start | bytes 786440 | tf_op jit(solution)/shard_map/ppermute | solution.py:400
  187.4 8.7 %collective-permute-start.20 = (bf16[128,1024]{1,0:T(8,128)(2,1)S(1)}, bf16[128,1024]{1,0:T(8,128)(2,1)S(1)}, u32[]{:S(2)}, u32[]{:S(2)}) collective-permute-start(bf16[128,1024]{1,0:T(8,128)(2,1)S(1)} %shard_map.111.refs_0_), channel_id=1, source_target_pairs={{0,1},{1,0},{2,3},{3,2},{4,5},{5,4},{6,7},{7,6},{8,9},{9,8},{10,11... | collective-permute-start | bytes 786440 | tf_op jit(solution)/shard_map/ppermute | solution.py:400
  194.0 3.2 %collective-permute-start.22 = (bf16[128,1024]{1,0:T(8,128)(2,1)S(1)}, bf16[128,1024]{1,0:T(8,128)(2,1)S(1)}, u32[]{:S(2)}, u32[]{:S(2)}) collective-permute-start(bf16[128,1024]{1,0:T(8,128)(2,1)S(1)} %collective-permute-done.21.refs_2_), channel_id=1, source_target_pairs={{0,1},{1,0},{2,3},{3,2},{4,5},{5,4},{6,7},{7,6},{8,9},{9,8},{10,11... | collective-permute-start | bytes 786440 | tf_op jit(solution)/shard_map/ppermute | solution.py:400
  201.6 69.1 %copy-start.9 = (bf16[512,1024]{1,0:T(8,128)(2,1)S(1)}, bf16[512,1024]{1,0:T(8,128)(2,1)}, u32[]{:S(2)}) copy-start(bf16[512,1024]{1,0:T(8,128)(2,1)} %catalogue.3) | copy-start | bytes 3145732
  201.6 26.0 %collective-permute-start.23 = (bf16[4,128,256]{2,1,0:T(8,128)(2,1)S(1)}, bf16[4,128,256]{2,1,0:T(8,128)(2,1)S(1)}, u32[]{:S(2)}, u32[]{:S(2)}) collective-permute-start(bf16[4,128,256]{2,1,0:T(8,128)(2,1)S(1)} %get-tuple-element.113), channel_id=1, source_target_pairs={{0,4},{4,0},{8,12},{12,8},{16,20},{20,16},{24,28},{28,24},{1,5},{5... | collective-permute-start | bytes 786440 | tf_op jit(solution)/shard_map/ppermute | solution.py:400
  203.1 24.7 %collective-permute-start.24 = (bf16[4,128,256]{2,1,0:T(8,128)(2,1)S(1)}, bf16[4,128,256]{2,1,0:T(8,128)(2,1)S(1)}, u32[]{:S(2)}, u32[]{:S(2)}) collective-permute-start(bf16[4,128,256]{2,1,0:T(8,128)(2,1)S(1)} %get-tuple-element.114), channel_id=1, source_target_pairs={{0,8},{4,12},{8,0},{12,4},{16,24},{20,28},{24,16},{28,20},{1,9},{5... | collective-permute-start | bytes 786440 | tf_op jit(solution)/shard_map/ppermute | solution.py:400
  206.7 4.0 %collective-permute-start.30 = (bf16[256,128]{1,0:T(8,128)(2,1)S(1)}, bf16[256,128]{1,0:T(8,128)(2,1)S(1)}, u32[]{:S(2)}, u32[]{:S(2)}) collective-permute-start(bf16[256,128]{1,0:T(8,128)(2,1)S(1)} %get-tuple-element.122), channel_id=1, source_target_pairs={{0,4},{4,0},{8,12},{12,8},{16,20},{20,16},{24,28},{28,24},{1,5},{5... | collective-permute-start | bytes 196616 | tf_op jit(solution)/shard_map/ppermute | solution.py:400
  206.9 5.7 %collective-permute-start.31 = (bf16[256,128]{1,0:T(8,128)(2,1)S(1)}, bf16[256,128]{1,0:T(8,128)(2,1)S(1)}, u32[]{:S(2)}, u32[]{:S(2)}) collective-permute-start(bf16[256,128]{1,0:T(8,128)(2,1)S(1)} %get-tuple-element.123), channel_id=1, source_target_pairs={{0,8},{4,12},{8,0},{12,4},{16,24},{20,28},{24,16},{28,20},{1,9},{5... | collective-permute-start | bytes 196616 | tf_op jit(solution)/shard_map/ppermute | solution.py:400
  206.9 7.8 %collective-permute-start.32 = (bf16[256,128]{1,0:T(8,128)(2,1)S(1)}, bf16[256,128]{1,0:T(8,128)(2,1)S(1)}, u32[]{:S(2)}, u32[]{:S(2)}) collective-permute-start(bf16[256,128]{1,0:T(8,128)(2,1)S(1)} %get-tuple-element.124), channel_id=1, source_target_pairs={{0,12},{4,8},{8,4},{12,0},{16,28},{20,24},{24,20},{28,16},{1,13},{... | collective-permute-start | bytes 196616 | tf_op jit(solution)/shard_map/ppermute | solution.py:400
  210.7 6.4 %collective-permute-start.33 = (bf16[256,128]{1,0:T(8,128)(2,1)S(1)}, bf16[256,128]{1,0:T(8,128)(2,1)S(1)}, u32[]{:S(2)}, u32[]{:S(2)}) collective-permute-start(bf16[256,128]{1,0:T(8,128)(2,1)S(1)} %get-tuple-element.125), channel_id=1, source_target_pairs={{0,16},{4,20},{8,24},{12,28},{16,0},{20,4},{24,8},{28,12},{1,17},{... | collective-permute-start | bytes 196616 | tf_op jit(solution)/shard_map/ppermute | solution.py:400
  212.5 8.9 %collective-permute-start.34 = (bf16[256,128]{1,0:T(8,128)(2,1)S(1)}, bf16[256,128]{1,0:T(8,128)(2,1)S(1)}, u32[]{:S(2)}, u32[]{:S(2)}) collective-permute-start(bf16[256,128]{1,0:T(8,128)(2,1)S(1)} %get-tuple-element.126), channel_id=1, source_target_pairs={{0,20},{4,16},{8,28},{12,24},{16,4},{20,0},{24,12},{28,8},{1,21},{... | collective-permute-start | bytes 196616 | tf_op jit(solution)/shard_map/ppermute | solution.py:400
  214.7 9.9 %collective-permute-start.35 = (bf16[256,128]{1,0:T(8,128)(2,1)S(1)}, bf16[256,128]{1,0:T(8,128)(2,1)S(1)}, u32[]{:S(2)}, u32[]{:S(2)}) collective-permute-start(bf16[256,128]{1,0:T(8,128)(2,1)S(1)} %get-tuple-element.127), channel_id=1, source_target_pairs={{0,24},{4,28},{8,16},{12,20},{16,8},{20,12},{24,0},{28,4},{1,25},{... | collective-permute-start | bytes 196616 | tf_op jit(solution)/shard_map/ppermute | solution.py:400
  217.1 9.9 %collective-permute-start.36 = (bf16[256,128]{1,0:T(8,128)(2,1)S(1)}, bf16[256,128]{1,0:T(8,128)(2,1)S(1)}, u32[]{:S(2)}, u32[]{:S(2)}) collective-permute-start(bf16[256,128]{1,0:T(8,128)(2,1)S(1)} %get-tuple-element.128), channel_id=1, source_target_pairs={{0,28},{4,24},{8,20},{12,16},{16,12},{20,8},{24,4},{28,0},{1,29},{... | collective-permute-start | bytes 196616 | tf_op jit(solution)/shard_map/ppermute | solution.py:400
  221.5 8.6 %collective-permute-start.25 = (bf16[4,128,256]{2,1,0:T(8,128)(2,1)S(1)}, bf16[4,128,256]{2,1,0:T(8,128)(2,1)S(1)}, u32[]{:S(2)}, u32[]{:S(2)}) collective-permute-start(bf16[4,128,256]{2,1,0:T(8,128)(2,1)S(1)} %get-tuple-element.115), channel_id=1, source_target_pairs={{0,12},{4,8},{8,4},{12,0},{16,28},{20,24},{24,20},{28,16},{1,13},{... | collective-permute-start | bytes 786440 | tf_op jit(solution)/shard_map/ppermute | solution.py:400
  224.6 9.2 %collective-permute-start.26 = (bf16[4,128,256]{2,1,0:T(8,128)(2,1)S(1)}, bf16[4,128,256]{2,1,0:T(8,128)(2,1)S(1)}, u32[]{:S(2)}, u32[]{:S(2)}) collective-permute-start(bf16[4,128,256]{2,1,0:T(8,128)(2,1)S(1)} %get-tuple-element.116), channel_id=1, source_target_pairs={{0,16},{4,20},{8,24},{12,28},{16,0},{20,4},{24,8},{28,12},{1,17},{... | collective-permute-start | bytes 786440 | tf_op jit(solution)/shard_map/ppermute | solution.py:400
  227.0 29.8 %collective-permute-start.27 = (bf16[4,128,256]{2,1,0:T(8,128)(2,1)S(1)}, bf16[4,128,256]{2,1,0:T(8,128)(2,1)S(1)}, u32[]{:S(2)}, u32[]{:S(2)}) collective-permute-start(bf16[4,128,256]{2,1,0:T(8,128)(2,1)S(1)} %get-tuple-element.117), channel_id=1, source_target_pairs={{0,20},{4,16},{8,28},{12,24},{16,4},{20,0},{24,12},{28,8},{1,21},{... | collective-permute-start | bytes 786440 | tf_op jit(solution)/shard_map/ppermute | solution.py:400
  227.6 38.3 %collective-permute-start.28 = (bf16[4,128,256]{2,1,0:T(8,128)(2,1)S(1)}, bf16[4,128,256]{2,1,0:T(8,128)(2,1)S(1)}, u32[]{:S(2)}, u32[]{:S(2)}) collective-permute-start(bf16[4,128,256]{2,1,0:T(8,128)(2,1)S(1)} %get-tuple-element.118), channel_id=1, source_target_pairs={{0,24},{4,28},{8,16},{12,20},{16,8},{20,12},{24,0},{28,4},{1,25},{... | collective-permute-start | bytes 786440 | tf_op jit(solution)/shard_map/ppermute | solution.py:400
  227.8 41.8 %collective-permute-start.29 = (bf16[4,128,256]{2,1,0:T(8,128)(2,1)S(1)}, bf16[4,128,256]{2,1,0:T(8,128)(2,1)S(1)}, u32[]{:S(2)}, u32[]{:S(2)}) collective-permute-start(bf16[4,128,256]{2,1,0:T(8,128)(2,1)S(1)} %get-tuple-element.119), channel_id=1, source_target_pairs={{0,28},{4,24},{8,20},{12,16},{16,12},{20,8},{24,4},{28,0},{1,29},{... | collective-permute-start | bytes 786440 | tf_op jit(solution)/shard_map/ppermute | solution.py:400
  (27 other events, 329.3 us)

commit v3 on v2

--- a/solution.py
+++ b/solution.py
@@ -21,7 +21,7 @@
 SM = pl.BlockSpec(memory_space=pltpu.SMEM)
 
 
-def call(body, out_shape, in_specs, flops, nbytes, scratch=(), trans=0, limit=24):
+def call(body, out_shape, in_specs, flops, nbytes, scratch=(), trans=0, limit=12):
     many = isinstance(out_shape, (list, tuple))
     return pl.pallas_call(
         body,
@@ -467,6 +467,18 @@
             axis_index_groups=halves,
         ).reshape(slots, width)
 
+    w_out_blocks = gather_blocks(w_out, "mp")
+    packed = call(
+        functools.partial(pack_kernel, dp=dp, seq_dev=seq_dev, per_peer=per_peer),
+        pieces(dp, (per_peer, steps, part), BF),
+        [SM, SM, VM],
+        1e5,
+        4 * history.size,
+    )(source, place, history)
+    packed, owners = lax.optimization_barrier((packed, owners))
+    arrived = exchange(packed, "dp")
+    arrived, w_out_blocks = lax.optimization_barrier((arrived, w_out_blocks))
+
     wanted, code = call(
         functools.partial(ask_kernel, devices=devices, capacity=capacity),
         [S((devices, capacity), I32), S((devices, events), F32)],
@@ -485,17 +497,7 @@
         2 * slots * stock * width,
         2 * (slots + stock) * width,
     )(incoming, catalogue)
-    items = in_half(looked)
-
-    packed = call(
-        functools.partial(pack_kernel, dp=dp, seq_dev=seq_dev, per_peer=per_peer),
-        pieces(dp, (per_peer, steps, part), BF),
-        [SM, SM, VM],
-        1e5,
-        4 * history.size,
-    )(source, place, history)
-    arrived = exchange(packed, "dp")
-    looked, arrived = lax.optimization_barrier((looked, arrived))
+
     rows = call(
         functools.partial(take_kernel, dp=dp, seq_dev=seq_dev, per_peer=per_peer, steps=steps),
         S((rows_all, part), BF),
@@ -505,8 +507,9 @@
         scratch=[pltpu.VMEM((dp, per_peer, steps, part), BF)],
     )(source, place, *arrived)
     features = gather_blocks(rows, "mp")
-    w_out_blocks = gather_blocks(w_out, "mp")
-    features, w_out_blocks = lax.optimization_barrier((features, w_out_blocks))
+    code_far = partner(code)
+    looked, features, code_far = lax.optimization_barrier((looked, features, code_far))
+    items = in_half(looked)
     (normed_t, projected, slope, weights, dscale, norm, inv, gated_t, own, *gated) = call(
         functools.partial(
             forward_kernel,
@@ -544,7 +547,6 @@
         4 * 2**20,
     )(own, *gathered, *w_out_blocks)
 
-    code_far = partner(code)
     unit_far = partner(unit_bf)
     expo, inv_item, total = call(
         functools.partial(
@@ -572,12 +574,13 @@
         4 * slots * width * events,
         2 * slots * width,
     )(source, lengths, place, expo, total, total_far, unit_bf, unit_far)
-    landed = in_half(sending)
     out_cot = call(
         out_cot_kernel, S((events, width), BF), [VM] * 4, 1e6, 2 * 2**20
     )(unit, inv_out, item_slope, slope_back)
 
     cots = gather_blocks(out_cot, "mp")
+    sending, cots = lax.optimization_barrier((sending, cots))
+    landed = in_half(sending)
     w_out_part = call(
         functools.partial(w_out_kernel, mp=mp, dp=dp),
         pieces(dp, (cols, width // dp), BF),

time: 281 us -> 275 us (0.979)
  waiting for transfers between devices: 155 us -> 132 us
  local copies, waits for them, and re-layouts: 18.1 us -> 36.1 us
  starting transfers between devices: 68.6 us -> 73.1 us
  Pallas kernels: 31.2 us -> 28.2 us
    ppermute x37, waiting for transfers between devices: 151 us -> 130 us  [swapped(): return lax.ppermute(x, axis, [(a, a ^ bit) for a in range(size)])]
    unnamed x72 -> x105, local copies, waits for them, and re-layouts: 17.9 us -> 35.2 us
    all_to_all x1, starting transfers between devices: 6.3 us -> 10.4 us  [per_device(): lax.all_to_all(wanted, ('dp', 'mp'), split_axis=0, concat_axis=0, tiled=T...]
  transfers between devices with their start and end apart: 40 -> 40, of which waited for: 22 -> 18; matrix products, arithmetic and copies ran while one was open for 1% -> 1% of each run, Pallas kernels for 6% -> 7%
where the time goes in v3:
time: 275 us; the launch traced here: 273 us
  waiting for transfers between devices  132 us (48%)
  starting transfers between devices  73.1 us (27%)
  local copies, waits for them, and re-layouts  36.1 us (13%)
  Pallas kernels  28.2 us (10%)
    ppermute x37, waiting for transfers between devices, swapped(): return lax.ppermute(x, axis, [(a, a ^ bit) for a in range(size)])  130 us
    ppermute x37, starting transfers between devices, swapped(): return lax.ppermute(x, axis, [(a, a ^ bit) for a in range(size)])  49.6 us
    unnamed x105, local copies, waits for them, and re-layouts  35.2 us
    all_to_all x2, starting transfers between devices, in_half(): lax.all_to_all(x.reshape(near, 2 * capacity, width), ('dp', 'mp'), split_...  13.2 us
    all_to_all x1, starting transfers between devices, per_device(): lax.all_to_all(wanted, ('dp', 'mp'), split_axis=0, concat_axis=0, tiled=T...  10.4 us
  transfers between devices with their start and end apart: 40, of which 18 were waited for; matrix products, arithmetic and copies ran while one was open for 1% of the time, Pallas kernels for 7%

profile of v3, /device:TPU:13, one launch (start us, length us, event | category | flops | bytes accessed | tf_op | source)
XLA Modules:
  0.0 272.6 jit_solution(17258085938825885506)
XLA Ops:
  1.9 11.8 %collective-permute-done.8.refs_6_ = bf16[256,1024]{1,0:T(8,128)(2,1)S(1)} collective-permute-done((bf16[256,1024]{1,0:T(8,128)(2,1)}, bf16[256,1024]{1,0:T(8,128)(2,1)S(1)}, u32[]{:S(2)}, u32[]{:S(2)}) %collective-permute-start.8) | collective-permute-done | bytes 524320 | tf_op jit(solution)/shard_map/ppermute | solution.py:400
  13.7 1.5 collective-permute-start.9
  16.9 2.9 %shard_map.103 = (bf16[2,32,256]{2,1,0:T(8,128)(2,1)S(1)}, bf16[2,32,256]{2,1,0:T(8,128)(2,1)S(1)}, bf16[2,32,256]{2,1,0:T(8,128)(2,1)S(1)}, bf16[2,32,256]{2,1,...) custom-call(s32[128]{0:T(128)S(1)} %copy-done.42, ...), custom_call_target="tpu_custom_call" | custom-call | flops 100000 | bytes 524288 | tf_op jit(solution)/shard_map/pallas_call | solution.py:471
  19.8 1.3 collective-permute-start
  22.6 2.3 collective-permute-start.3
  27.4 1.4 collective-permute-start.6
  29.5 2.0 collective-permute-done.6.refs_7_
  34.2 1.3 shard_map.104
  35.5 10.4 %all-to-all-start = ((s32[32,1,48]{2,1,0:T(1,128)}), s32[32,1,48]{2,1,0:T(1,128)S(1)}, u32[]{:S(2)}, u32[]{:S(2)}) async-start(s32[32,1,48]{2,1,0:T(1,128)} %bitcast.3), calls=%async_computation | async-start | bytes 32768 | tf_op jit(solution)/shard_map/all_to_all | solution.py:489
  45.8 2.2 collective-permute-start.13
  48.1 2.4 all-to-all-done
  52.7 1.8 shard_map.105
  54.6 1.6 copy-done.1
  57.7 6.2 %all-to-all-start.1 = ((bf16[16,96,1024]{2,1,0:T(8,128)(2,1)}), bf16[16,96,1024]{2,1,0:T(8,128)(2,1)S(1)}, u32[]{:S(2)}, u32[]{:S(2)}) async-start(bf16[16,96,1024]{2,1,0:T(8,128)(2,1)} %bitcast.16), calls=%async_computation.1 | async-start | bytes 6291456 | tf_op jit(solution)/shard_map/all_to_all | solution.py:461
  63.8 1.6 copy-done.45
  68.3 4.2 %shard_map.107 = (bf16[1024,512]{1,0:T(8,128)(2,1)S(1)}, bf16[4,512,256]{2,1,0:T(8,128)(2,1)S(1)}, f32[4,512,256]{2,1,0:T(8,128)S(1)}, bf16[2,512,128]{2,1,0:T(8...) custom-call(s32[128]{0:T(128)S(1)} %copy-done.43, ...), custom_call_target="tpu_custom_call" | custom-call | flops 1073741824 | bytes 12582912 | tf_op jit(solution)/shard_map/pallas_call | solution.py:513
  72.5 1.3 copy-done.2
  77.4 1.5 collective-permute-start.16
  79.0 16.3 %collective-permute-done.15.refs_2_ = bf16[128,256]{1,0:T(8,128)(2,1)S(1)} collective-permute-done((bf16[128,256]{1,0:T(8,128)(2,1)S(1)}, bf16[128,256]{1,0:T(8,128)(2,1)S(1)}, u32[]{:S(2)}, u32[]{:S(2)}) %collective-permute-start.15) | collective-permute-done | bytes 65568 | tf_op jit(solution)/shard_map/ppermute | solution.py:400
  95.3 1.4 collective-permute-done.16.refs_3_
  98.5 11.4 %collective-permute-done.17.unit_far = bf16[128,1024]{1,0:T(8,128)(2,1)S(1)} collective-permute-done((bf16[128,1024]{1,0:T(8,128)(2,1)S(1)}, bf16[128,1024]{1,0:T(8,128)(2,1)S(1)}, u32[]{:S(2)}, u32[]{:S(2)}) %collective-permute-start.17) | collective-permute-done | bytes 262176 | tf_op jit(solution)/shard_map/ppermute | solution.py:400
  111.5 3.0 %shard_map.109 = (f32[1536,256]{1,0:T(8,128)S(1)}, f32[1536,128]{1,0:T(8,128)S(1)}, f32[1,256]{1,0:T(1,128)S(1)}) custom-call(s32[2]{0:T(128)S(1)} %pad_add_fusion.place, bf16[1536,1024]{1,0:T(8,128)(2,1)S(1)} %bitcast.12, f32[32,128]{1,0:T(8,128)S(1)} %get-tuple-element.108.code, f32[32,128]{1,0:T(8,128)S(1)} %collective-permute-done.13.code_far, ...), custom_call_target="tpu_custom_call" | custom-call | flops 805306368 | bytes 3145728 | tf_op jit(solution)/shard_map/pallas_call | solution.py:551
  114.6 2.7 %collective-permute-start.18 = (f32[1,256]{1,0:T(1,128)S(1)}, f32[1,256]{1,0:T(1,128)S(1)}, u32[]{:S(2)}, u32[]{:S(2)}) collective-permute-start(f32[1,256]{1,0:T(1,128)S(1)} %get-tuple-element.126.total), channel_id=1, source_target_pairs={{0,16},{4,20},{8,24},{12,28},{16,0},{20,4},{24,8},{28,12},{1,17},{... | collective-permute-start | bytes 3080 | tf_op jit(solution)/shard_map/ppermute | solution.py:400
  118.3 1.7 shard_map.111
  120.0 2.4 collective-permute-start.19
  122.4 10.6 %collective-permute-done.19.slope_far = bf16[128,1024]{1,0:T(8,128)(2,1)S(1)} collective-permute-done((bf16[128,1024]{1,0:T(8,128)(2,1)S(1)}, bf16[128,1024]{1,0:T(8,128)(2,1)S(1)}, u32[]{:S(2)}, u32[]{:S(2)}) %collective-permute-start.19) | collective-permute-done | bytes 262176 | tf_op jit(solution)/shard_map/ppermute | solution.py:400
  133.3 3.0 %collective-permute-start.21 = (bf16[128,1024]{1,0:T(8,128)(2,1)S(1)}, bf16[128,1024]{1,0:T(8,128)(2,1)S(1)}, u32[]{:S(2)}, u32[]{:S(2)}) collective-permute-start(bf16[128,1024]{1,0:T(8,128)(2,1)S(1)} %shard_map.112.refs_0_), channel_id=1, source_target_pairs={{0,2},{1,3},{2,0},{3,1},{4,6},{5,7},{6,4},{7,5},{8,10},{9,11},{10,... | collective-permute-start | bytes 786440 | tf_op jit(solution)/shard_map/ppermute | solution.py:400
  137.0 5.5 %collective-permute-done.21.refs_2_ = bf16[128,1024]{1,0:T(8,128)(2,1)S(1)} collective-permute-done((bf16[128,1024]{1,0:T(8,128)(2,1)S(1)}, bf16[128,1024]{1,0:T(8,128)(2,1)S(1)}, u32[]{:S(2)}, u32[]{:S(2)}) %collective-permute-start.21) | collective-permute-done | bytes 262176 | tf_op jit(solution)/shard_map/ppermute | solution.py:400
  144.5 2.3 shard_map.110
  146.8 1.6 copy-done
  149.9 7.0 %all-to-all-start.2 = ((bf16[16,96,1024]{2,1,0:T(8,128)(2,1)}), bf16[16,96,1024]{2,1,0:T(8,128)(2,1)S(1)}, u32[]{:S(2)}, u32[]{:S(2)}) async-start(bf16[16,96,1024]{2,1,0:T(8,128)(2,1)} %bitcast.15), calls=%async_computation.2 | async-start | bytes 6291456 | tf_op jit(solution)/shard_map/all_to_all | solution.py:461
  156.9 1.6 copy-done.3
  168.9 4.2 %shard_map.113 = (bf16[4,128,256]{2,1,0:T(8,128)(2,1)S(1)}, bf16[4,128,256]{2,1,0:T(8,128)(2,1)S(1)}, bf16[4,128,256]{2,1,0:T(8,128)(2,1)S(1)}, bf16[4,128,256]{...) custom-call(s32[2]{0:T(128)S(1)} %pad_add_fusion.place, ...), custom_call_target="tpu_custom_call" | custom-call | flops 1342177280 | bytes 12582912 | tf_op jit(solution)/shard_map/pallas_call | solution.py:592
  173.1 1.3 collective-permute-start.23
  174.6 1.6 shard_map.114
  179.0 27.1 %collective-permute-done.30 = bf16[256,128]{1,0:T(8,128)(2,1)S(1)} collective-permute-done((bf16[256,128]{1,0:T(8,128)(2,1)S(1)}, bf16[256,128]{1,0:T(8,128)(2,1)S(1)}, u32[]{:S(2)}, u32[]{:S(2)}) %collective-permute-start.30) | collective-permute-done | bytes 65568 | tf_op jit(solution)/shard_map/ppermute | solution.py:400
  206.5 3.9 %collective-permute-start.34 = (bf16[256,128]{1,0:T(8,128)(2,1)S(1)}, bf16[256,128]{1,0:T(8,128)(2,1)S(1)}, u32[]{:S(2)}, u32[]{:S(2)}) collective-permute-start(bf16[256,128]{1,0:T(8,128)(2,1)S(1)} %get-tuple-element.157), channel_id=1, source_target_pairs={{0,20},{4,16},{8,28},{12,24},{16,4},{20,0},{24,12},{28,8},{1,21},{... | collective-permute-start | bytes 196616 | tf_op jit(solution)/shard_map/ppermute | solution.py:400
  210.7 6.0 %collective-permute-start.36 = (bf16[256,128]{1,0:T(8,128)(2,1)S(1)}, bf16[256,128]{1,0:T(8,128)(2,1)S(1)}, u32[]{:S(2)}, u32[]{:S(2)}) collective-permute-start(bf16[256,128]{1,0:T(8,128)(2,1)S(1)} %get-tuple-element.159), channel_id=1, source_target_pairs={{0,28},{4,24},{8,20},{12,16},{16,12},{20,8},{24,4},{28,0},{1,29},{... | collective-permute-start | bytes 196616 | tf_op jit(solution)/shard_map/ppermute | solution.py:400
  216.8 2.1 collective-permute-start.25
  218.8 2.1 collective-permute-start.26
  221.0 1.8 collective-permute-done.36
  223.5 2.4 collective-permute-start.28
  226.7 4.1 %collective-permute-done.25 = bf16[4,128,256]{2,1,0:T(8,128)(2,1)S(1)} collective-permute-done((bf16[4,128,256]{2,1,0:T(8,128)(2,1)S(1)}, bf16[4,128,256]{2,1,0:T(8,128)(2,1)S(1)}, u32[]{:S(2)}, u32[]{:S(2)}) %collective-permute-start.25) | collective-permute-done | bytes 262176 | tf_op jit(solution)/shard_map/ppermute | solution.py:400
  230.7 2.8 %collective-permute-done.26 = bf16[4,128,256]{2,1,0:T(8,128)(2,1)S(1)} collective-permute-done((bf16[4,128,256]{2,1,0:T(8,128)(2,1)S(1)}, bf16[4,128,256]{2,1,0:T(8,128)(2,1)S(1)}, u32[]{:S(2)}, u32[]{:S(2)}) %collective-permute-start.26) | collective-permute-done | bytes 262176 | tf_op jit(solution)/shard_map/ppermute | solution.py:400
  233.5 20.8 %collective-permute-done.27 = bf16[4,128,256]{2,1,0:T(8,128)(2,1)S(1)} collective-permute-done((bf16[4,128,256]{2,1,0:T(8,128)(2,1)S(1)}, bf16[4,128,256]{2,1,0:T(8,128)(2,1)S(1)}, u32[]{:S(2)}, u32[]{:S(2)}) %collective-permute-start.27) | collective-permute-done | bytes 262176 | tf_op jit(solution)/shard_map/ppermute | solution.py:400
  254.4 7.8 %collective-permute-done.28 = bf16[4,128,256]{2,1,0:T(8,128)(2,1)S(1)} collective-permute-done((bf16[4,128,256]{2,1,0:T(8,128)(2,1)S(1)}, bf16[4,128,256]{2,1,0:T(8,128)(2,1)S(1)}, u32[]{:S(2)}, u32[]{:S(2)}) %collective-permute-start.28) | collective-permute-done | bytes 262176 | tf_op jit(solution)/shard_map/ppermute | solution.py:400
  262.1 4.7 %collective-permute-done.29 = bf16[4,128,256]{2,1,0:T(8,128)(2,1)S(1)} collective-permute-done((bf16[4,128,256]{2,1,0:T(8,128)(2,1)S(1)}, bf16[4,128,256]{2,1,0:T(8,128)(2,1)S(1)}, u32[]{:S(2)}, u32[]{:S(2)}) %collective-permute-start.29) | collective-permute-done | bytes 262176 | tf_op jit(solution)/shard_map/ppermute | solution.py:400
  269.1 3.6 %shard_map.115 = f32[512,1024]{1,0:T(8,128)} custom-call(s32[1,1536]{1,0:T(1,128)S(1)} %reshape.28.incoming, bf16[1536,1024]{1,0:T(8,128)(2,1)S(1)} %bitcast.14, bf16[512,1024]{1,0:T(8,128)(2,1)S(1)} %copy-done.7), custom_call_target="tpu_custom_call" | custom-call | flops 1610612736 | bytes 6291456 | tf_op jit(solution)/shard_map/pallas_call | solution.py:606
  (158 shorter events, 46.9 us)
Async XLA Ops:
  0.6 13.1 %collective-permute-start.8 = (bf16[256,1024]{1,0:T(8,128)(2,1)}, bf16[256,1024]{1,0:T(8,128)(2,1)S(1)}, u32[]{:S(2)}, u32[]{:S(2)}) collective-permute-start(bf16[256,1024]{1,0:T(8,128)(2,1)} %refs_4_.4), channel_id=1, source_target_pairs={{0,2},{1,3},{2,0},{3,1},{4,6},{5,7},{6,4},{7,5},{8,10},{9,11},{10,... | collective-permute-start | bytes 1572872 | tf_op jit(solution)/shard_map/ppermute | solution.py:400
  0.9 30.6 %collective-permute-start.7 = (bf16[256,1024]{1,0:T(8,128)(2,1)}, bf16[256,1024]{1,0:T(8,128)(2,1)S(1)}, u32[]{:S(2)}, u32[]{:S(2)}) collective-permute-start(bf16[256,1024]{1,0:T(8,128)(2,1)} %refs_4_.4), channel_id=1, source_target_pairs={{0,1},{1,0},{2,3},{3,2},{4,5},{5,4},{6,7},{7,6},{8,9},{9,8},{10,11... | collective-permute-start | bytes 1572872 | tf_op jit(solution)/shard_map/ppermute | solution.py:400
  13.7 40.8 %copy-start.23 = (bf16[256,1024]{1,0:T(8,128)(2,1)}, bf16[256,1024]{1,0:T(8,128)(2,1)S(1)}, u32[]{:S(2)}) copy-start(bf16[256,1024]{1,0:T(8,128)(2,1)S(1)} %collective-permute-done.8.refs_6_) | copy-start | bytes 1572868
  13.7 17.9 %collective-permute-start.9 = (bf16[256,1024]{1,0:T(8,128)(2,1)S(1)}, bf16[256,1024]{1,0:T(8,128)(2,1)S(1)}, u32[]{:S(2)}, u32[]{:S(2)}) collective-permute-start(bf16[256,1024]{1,0:T(8,128)(2,1)S(1)} %collective-permute-done.8.refs_6_), channel_id=1, source_target_pairs={{0,1},{1,0},{2,3},{3,2},{4,5},{5,4},{6,7},{7,6},{8,9},{9,8},{10,11... | collective-permute-start | bytes 1572872 | tf_op jit(solution)/shard_map/ppermute | solution.py:400
  19.8 2.8 %collective-permute-start = (bf16[2,32,256]{2,1,0:T(8,128)(2,1)S(1)}, bf16[2,32,256]{2,1,0:T(8,128)(2,1)S(1)}, u32[]{:S(2)}, u32[]{:S(2)}) collective-permute-start(bf16[2,32,256]{2,1,0:T(8,128)(2,1)S(1)} %get-tuple-element.93), channel_id=1, source_target_pairs={{0,4},{4,0},{8,12},{12,8},{16,20},{20,16},{24,28},{28,24},{1,5},{5... | collective-permute-start | bytes 98312 | tf_op jit(solution)/shard_map/ppermute | solution.py:400
  21.1 3.9 %collective-permute-start.1 = (bf16[2,32,256]{2,1,0:T(8,128)(2,1)S(1)}, bf16[2,32,256]{2,1,0:T(8,128)(2,1)S(1)}, u32[]{:S(2)}, u32[]{:S(2)}) collective-permute-start(bf16[2,32,256]{2,1,0:T(8,128)(2,1)S(1)} %get-tuple-element.94), channel_id=1, source_target_pairs={{0,8},{4,12},{8,0},{12,4},{16,24},{20,28},{24,16},{28,20},{1,9},{5... | collective-permute-start | bytes 98312 | tf_op jit(solution)/shard_map/ppermute | solution.py:400
  21.3 4.9 %collective-permute-start.2 = (bf16[2,32,256]{2,1,0:T(8,128)(2,1)S(1)}, bf16[2,32,256]{2,1,0:T(8,128)(2,1)S(1)}, u32[]{:S(2)}, u32[]{:S(2)}) collective-permute-start(bf16[2,32,256]{2,1,0:T(8,128)(2,1)S(1)} %get-tuple-element.95), channel_id=1, source_target_pairs={{0,12},{4,8},{8,4},{12,0},{16,28},{20,24},{24,20},{28,16},{1,13},{... | collective-permute-start | bytes 98312 | tf_op jit(solution)/shard_map/ppermute | solution.py:400
  22.6 4.7 %collective-permute-start.3 = (bf16[2,32,256]{2,1,0:T(8,128)(2,1)S(1)}, bf16[2,32,256]{2,1,0:T(8,128)(2,1)S(1)}, u32[]{:S(2)}, u32[]{:S(2)}) collective-permute-start(bf16[2,32,256]{2,1,0:T(8,128)(2,1)S(1)} %get-tuple-element.96), channel_id=1, source_target_pairs={{0,16},{4,20},{8,24},{12,28},{16,0},{20,4},{24,8},{28,12},{1,17},{... | collective-permute-start | bytes 98312 | tf_op jit(solution)/shard_map/ppermute | solution.py:400
  25.0 4.6 %collective-permute-start.4 = (bf16[2,32,256]{2,1,0:T(8,128)(2,1)S(1)}, bf16[2,32,256]{2,1,0:T(8,128)(2,1)S(1)}, u32[]{:S(2)}, u32[]{:S(2)}) collective-permute-start(bf16[2,32,256]{2,1,0:T(8,128)(2,1)S(1)} %get-tuple-element.97), channel_id=1, source_target_pairs={{0,20},{4,16},{8,28},{12,24},{16,4},{20,0},{24,12},{28,8},{1,21},{... | collective-permute-start | bytes 98312 | tf_op jit(solution)/shard_map/ppermute | solution.py:400
  26.1 3.4 %collective-permute-start.5 = (bf16[2,32,256]{2,1,0:T(8,128)(2,1)S(1)}, bf16[2,32,256]{2,1,0:T(8,128)(2,1)S(1)}, u32[]{:S(2)}, u32[]{:S(2)}) collective-permute-start(bf16[2,32,256]{2,1,0:T(8,128)(2,1)S(1)} %get-tuple-element.98), channel_id=1, source_target_pairs={{0,24},{4,28},{8,16},{12,20},{16,8},{20,12},{24,0},{28,4},{1,25},{... | collective-permute-start | bytes 98312 | tf_op jit(solution)/shard_map/ppermute | solution.py:400
  27.4 4.2 %collective-permute-start.6 = (bf16[2,32,256]{2,1,0:T(8,128)(2,1)S(1)}, bf16[2,32,256]{2,1,0:T(8,128)(2,1)S(1)}, u32[]{:S(2)}, u32[]{:S(2)}) collective-permute-start(bf16[2,32,256]{2,1,0:T(8,128)(2,1)S(1)} %get-tuple-element.99), channel_id=1, source_target_pairs={{0,28},{4,24},{8,20},{12,16},{16,12},{20,8},{24,4},{28,0},{1,29},{... | collective-permute-start | bytes 98312 | tf_op jit(solution)/shard_map/ppermute | solution.py:400
  31.6 23.0 %copy-start.25 = (bf16[256,1024]{1,0:T(8,128)(2,1)}, bf16[256,1024]{1,0:T(8,128)(2,1)S(1)}, u32[]{:S(2)}) copy-start(bf16[256,1024]{1,0:T(8,128)(2,1)S(1)} %collective-permute-done.7.refs_5_) | copy-start | bytes 1572868
  31.6 23.0 %copy-start.27 = (bf16[256,1024]{1,0:T(8,128)(2,1)}, bf16[256,1024]{1,0:T(8,128)(2,1)S(1)}, u32[]{:S(2)}) copy-start(bf16[256,1024]{1,0:T(8,128)(2,1)S(1)} %collective-permute-done.9.refs_7_) | copy-start | bytes 1572868
  32.3 18.9 %collective-permute-start.11 = (bf16[512,256]{1,0:T(8,128)(2,1)S(1)}, bf16[512,256]{1,0:T(8,128)(2,1)S(1)}, u32[]{:S(2)}, u32[]{:S(2)}) collective-permute-start(bf16[512,256]{1,0:T(8,128)(2,1)S(1)} %shard_map.106.refs_0_), channel_id=1, source_target_pairs={{0,2},{1,3},{2,0},{3,1},{4,6},{5,7},{6,4},{7,5},{8,10},{9,11},{10,... | collective-permute-start | bytes 786440 | tf_op jit(solution)/shard_map/ppermute | solution.py:400
  35.5 15.0 %all-to-all-start = ((s32[32,1,48]{2,1,0:T(1,128)}), s32[32,1,48]{2,1,0:T(1,128)S(1)}, u32[]{:S(2)}, u32[]{:S(2)}) async-start(s32[32,1,48]{2,1,0:T(1,128)} %bitcast.3), calls=%async_computation | async-start | bytes 32768 | tf_op jit(solution)/shard_map/all_to_all | solution.py:489
  45.8 10.4 %collective-permute-start.13 = (f32[32,128]{1,0:T(8,128)S(1)}, f32[32,128]{1,0:T(8,128)S(1)}, u32[]{:S(2)}, u32[]{:S(2)}) collective-permute-start(f32[32,128]{1,0:T(8,128)S(1)} %get-tuple-element.108.code), channel_id=1, source_target_pairs={{0,16},{4,20},{8,24},{12,28},{16,0},{20,4},{24,8},{28,12},{1,17},{... | collective-permute-start | bytes 49160 | tf_op jit(solution)/shard_map/ppermute | solution.py:400
  50.6 5.7 %collective-permute-start.10 = (bf16[512,256]{1,0:T(8,128)(2,1)S(1)}, bf16[512,256]{1,0:T(8,128)(2,1)S(1)}, u32[]{:S(2)}, u32[]{:S(2)}) collective-permute-start(bf16[512,256]{1,0:T(8,128)(2,1)S(1)} %shard_map.106.refs_0_), channel_id=1, source_target_pairs={{0,1},{1,0},{2,3},{3,2},{4,5},{5,4},{6,7},{7,6},{8,9},{9,8},{10,11... | collective-permute-start | bytes 786440 | tf_op jit(solution)/shard_map/ppermute | solution.py:400
  51.3 5.7 %collective-permute-start.12 = (bf16[512,256]{1,0:T(8,128)(2,1)S(1)}, bf16[512,256]{1,0:T(8,128)(2,1)S(1)}, u32[]{:S(2)}, u32[]{:S(2)}) collective-permute-start(bf16[512,256]{1,0:T(8,128)(2,1)S(1)} %collective-permute-done.11.refs_2_), channel_id=1, source_target_pairs={{0,1},{1,0},{2,3},{3,2},{4,5},{5,4},{6,7},{7,6},{8,9},{9,8},{10,11... | collective-permute-start | bytes 786440 | tf_op jit(solution)/shard_map/ppermute | solution.py:400
  57.7 52.9 %all-to-all-start.1 = ((bf16[16,96,1024]{2,1,0:T(8,128)(2,1)}), bf16[16,96,1024]{2,1,0:T(8,128)(2,1)S(1)}, u32[]{:S(2)}, u32[]{:S(2)}) async-start(bf16[16,96,1024]{2,1,0:T(8,128)(2,1)} %bitcast.16), calls=%async_computation.1 | async-start | bytes 6291456 | tf_op jit(solution)/shard_map/all_to_all | solution.py:461
  68.3 28.5 %copy-start.4 = (bf16[256,1024]{1,0:T(8,128)(2,1)S(1)}, bf16[256,1024]{1,0:T(8,128)(2,1)}, u32[]{:S(2)}) copy-start(bf16[256,1024]{1,0:T(8,128)(2,1)} %refs_4_.4) | copy-start | bytes 1572868
  68.3 28.5 %copy-start.24 = (bf16[256,1024]{1,0:T(8,128)(2,1)S(1)}, bf16[256,1024]{1,0:T(8,128)(2,1)}, u32[]{:S(2)}) copy-start(bf16[256,1024]{1,0:T(8,128)(2,1)} %copy-done.23) | copy-start | bytes 1572868
  68.3 28.5 %copy-start.26 = (bf16[256,1024]{1,0:T(8,128)(2,1)S(1)}, bf16[256,1024]{1,0:T(8,128)(2,1)}, u32[]{:S(2)}) copy-start(bf16[256,1024]{1,0:T(8,128)(2,1)} %copy-done.25) | copy-start | bytes 1572868
  68.3 28.5 %copy-start.28 = (bf16[256,1024]{1,0:T(8,128)(2,1)S(1)}, bf16[256,1024]{1,0:T(8,128)(2,1)}, u32[]{:S(2)}) copy-start(bf16[256,1024]{1,0:T(8,128)(2,1)} %copy-done.27) | copy-start | bytes 1572868
  76.8 2.2 collective-permute-start.14
  77.2 18.1 %collective-permute-start.15 = (bf16[128,256]{1,0:T(8,128)(2,1)S(1)}, bf16[128,256]{1,0:T(8,128)(2,1)S(1)}, u32[]{:S(2)}, u32[]{:S(2)}) collective-permute-start(bf16[128,256]{1,0:T(8,128)(2,1)S(1)} %get-tuple-element.118), channel_id=1, source_target_pairs={{0,2},{1,3},{2,0},{3,1},{4,6},{5,7},{6,4},{7,5},{8,10},{9,11},{10,... | collective-permute-start | bytes 196616 | tf_op jit(solution)/shard_map/ppermute | solution.py:400
  77.4 19.3 %collective-permute-start.16 = (bf16[128,256]{1,0:T(8,128)(2,1)S(1)}, bf16[128,256]{1,0:T(8,128)(2,1)S(1)}, u32[]{:S(2)}, u32[]{:S(2)}) collective-permute-start(bf16[128,256]{1,0:T(8,128)(2,1)S(1)} %get-tuple-element.119), channel_id=1, source_target_pairs={{0,3},{1,2},{2,1},{3,0},{4,7},{5,6},{6,5},{7,4},{8,11},{9,10},{10,... | collective-permute-start | bytes 196616 | tf_op jit(solution)/shard_map/ppermute | solution.py:400
  98.1 11.7 %collective-permute-start.17 = (bf16[128,1024]{1,0:T(8,128)(2,1)S(1)}, bf16[128,1024]{1,0:T(8,128)(2,1)S(1)}, u32[]{:S(2)}, u32[]{:S(2)}) collective-permute-start(bf16[128,1024]{1,0:T(8,128)(2,1)S(1)} %get-tuple-element.124.unit), channel_id=1, source_target_pairs={{0,16},{4,20},{8,24},{12,28},{16,0},{20,4},{24,8},{28,12},{1,17},{... | collective-permute-start | bytes 786440 | tf_op jit(solution)/shard_map/ppermute | solution.py:400
  114.6 3.7 %collective-permute-start.18 = (f32[1,256]{1,0:T(1,128)S(1)}, f32[1,256]{1,0:T(1,128)S(1)}, u32[]{:S(2)}, u32[]{:S(2)}) collective-permute-start(f32[1,256]{1,0:T(1,128)S(1)} %get-tuple-element.126.total), channel_id=1, source_target_pairs={{0,16},{4,20},{8,24},{12,28},{16,0},{20,4},{24,8},{28,12},{1,17},{... | collective-permute-start | bytes 3080 | tf_op jit(solution)/shard_map/ppermute | solution.py:400
  118.3 25.3 %copy-start.16 = (bf16[128,1024]{1,0:T(8,128)(2,1)S(1)}, bf16[128,1024]{1,0:T(8,128)(2,1)}, u32[]{:S(2)}) copy-start(bf16[128,1024]{1,0:T(8,128)(2,1)} %copy-done.14) | copy-start | bytes 786436
  120.0 13.1 %collective-permute-start.19 = (bf16[128,1024]{1,0:T(8,128)(2,1)S(1)}, bf16[128,1024]{1,0:T(8,128)(2,1)S(1)}, u32[]{:S(2)}, u32[]{:S(2)}) collective-permute-start(bf16[128,1024]{1,0:T(8,128)(2,1)S(1)} %get-tuple-element.131), channel_id=1, source_target_pairs={{0,16},{4,20},{8,24},{12,28},{16,0},{20,4},{24,8},{28,12},{1,17},{... | collective-permute-start | bytes 786440 | tf_op jit(solution)/shard_map/ppermute | solution.py:400
  133.3 9.2 %collective-permute-start.21 = (bf16[128,1024]{1,0:T(8,128)(2,1)S(1)}, bf16[128,1024]{1,0:T(8,128)(2,1)S(1)}, u32[]{:S(2)}, u32[]{:S(2)}) collective-permute-start(bf16[128,1024]{1,0:T(8,128)(2,1)S(1)} %shard_map.112.refs_0_), channel_id=1, source_target_pairs={{0,2},{1,3},{2,0},{3,1},{4,6},{5,7},{6,4},{7,5},{8,10},{9,11},{10,... | collective-permute-start | bytes 786440 | tf_op jit(solution)/shard_map/ppermute | solution.py:400
  136.3 12.2 %collective-permute-start.20 = (bf16[128,1024]{1,0:T(8,128)(2,1)S(1)}, bf16[128,1024]{1,0:T(8,128)(2,1)S(1)}, u32[]{:S(2)}, u32[]{:S(2)}) collective-permute-start(bf16[128,1024]{1,0:T(8,128)(2,1)S(1)} %shard_map.112.refs_0_), channel_id=1, source_target_pairs={{0,1},{1,0},{2,3},{3,2},{4,5},{5,4},{6,7},{7,6},{8,9},{9,8},{10,11... | collective-permute-start | bytes 786440 | tf_op jit(solution)/shard_map/ppermute | solution.py:400
  142.5 6.7 %collective-permute-start.22 = (bf16[128,1024]{1,0:T(8,128)(2,1)S(1)}, bf16[128,1024]{1,0:T(8,128)(2,1)S(1)}, u32[]{:S(2)}, u32[]{:S(2)}) collective-permute-start(bf16[128,1024]{1,0:T(8,128)(2,1)S(1)} %collective-permute-done.21.refs_2_), channel_id=1, source_target_pairs={{0,1},{1,0},{2,3},{3,2},{4,5},{5,4},{6,7},{7,6},{8,9},{9,8},{10,11... | collective-permute-start | bytes 786440 | tf_op jit(solution)/shard_map/ppermute | solution.py:400
  149.9 118.0 %all-to-all-start.2 = ((bf16[16,96,1024]{2,1,0:T(8,128)(2,1)}), bf16[16,96,1024]{2,1,0:T(8,128)(2,1)S(1)}, u32[]{:S(2)}, u32[]{:S(2)}) async-start(bf16[16,96,1024]{2,1,0:T(8,128)(2,1)} %bitcast.15), calls=%async_computation.2 | async-start | bytes 6291456 | tf_op jit(solution)/shard_map/all_to_all | solution.py:461
  173.1 50.4 %collective-permute-start.23 = (bf16[4,128,256]{2,1,0:T(8,128)(2,1)S(1)}, bf16[4,128,256]{2,1,0:T(8,128)(2,1)S(1)}, u32[]{:S(2)}, u32[]{:S(2)}) collective-permute-start(bf16[4,128,256]{2,1,0:T(8,128)(2,1)S(1)} %get-tuple-element.144), channel_id=1, source_target_pairs={{0,4},{4,0},{8,12},{12,8},{16,20},{20,16},{24,28},{28,24},{1,5},{5... | collective-permute-start | bytes 786440 | tf_op jit(solution)/shard_map/ppermute | solution.py:400
  174.4 51.5 %collective-permute-start.24 = (bf16[4,128,256]{2,1,0:T(8,128)(2,1)S(1)}, bf16[4,128,256]{2,1,0:T(8,128)(2,1)S(1)}, u32[]{:S(2)}, u32[]{:S(2)}) collective-permute-start(bf16[4,128,256]{2,1,0:T(8,128)(2,1)S(1)} %get-tuple-element.145), channel_id=1, source_target_pairs={{0,8},{4,12},{8,0},{12,4},{16,24},{20,28},{24,16},{28,20},{1,9},{5... | collective-permute-start | bytes 786440 | tf_op jit(solution)/shard_map/ppermute | solution.py:400
  176.3 29.8 %collective-permute-start.30 = (bf16[256,128]{1,0:T(8,128)(2,1)S(1)}, bf16[256,128]{1,0:T(8,128)(2,1)S(1)}, u32[]{:S(2)}, u32[]{:S(2)}) collective-permute-start(bf16[256,128]{1,0:T(8,128)(2,1)S(1)} %get-tuple-element.153), channel_id=1, source_target_pairs={{0,4},{4,0},{8,12},{12,8},{16,20},{20,16},{24,28},{28,24},{1,5},{5... | collective-permute-start | bytes 196616 | tf_op jit(solution)/shard_map/ppermute | solution.py:400
  176.6 29.9 %collective-permute-start.31 = (bf16[256,128]{1,0:T(8,128)(2,1)S(1)}, bf16[256,128]{1,0:T(8,128)(2,1)S(1)}, u32[]{:S(2)}, u32[]{:S(2)}) collective-permute-start(bf16[256,128]{1,0:T(8,128)(2,1)S(1)} %get-tuple-element.154), channel_id=1, source_target_pairs={{0,8},{4,12},{8,0},{12,4},{16,24},{20,28},{24,16},{28,20},{1,9},{5... | collective-permute-start | bytes 196616 | tf_op jit(solution)/shard_map/ppermute | solution.py:400
  177.8 32.5 %collective-permute-start.32 = (bf16[256,128]{1,0:T(8,128)(2,1)S(1)}, bf16[256,128]{1,0:T(8,128)(2,1)S(1)}, u32[]{:S(2)}, u32[]{:S(2)}) collective-permute-start(bf16[256,128]{1,0:T(8,128)(2,1)S(1)} %get-tuple-element.155), channel_id=1, source_target_pairs={{0,12},{4,8},{8,4},{12,0},{16,28},{20,24},{24,20},{28,16},{1,13},{... | collective-permute-start | bytes 196616 | tf_op jit(solution)/shard_map/ppermute | solution.py:400
  206.1 4.6 %collective-permute-start.33 = (bf16[256,128]{1,0:T(8,128)(2,1)S(1)}, bf16[256,128]{1,0:T(8,128)(2,1)S(1)}, u32[]{:S(2)}, u32[]{:S(2)}) collective-permute-start(bf16[256,128]{1,0:T(8,128)(2,1)S(1)} %get-tuple-element.156), channel_id=1, source_target_pairs={{0,16},{4,20},{8,24},{12,28},{16,0},{20,4},{24,8},{28,12},{1,17},{... | collective-permute-start | bytes 196616 | tf_op jit(solution)/shard_map/ppermute | solution.py:400
  206.5 10.3 %collective-permute-start.34 = (bf16[256,128]{1,0:T(8,128)(2,1)S(1)}, bf16[256,128]{1,0:T(8,128)(2,1)S(1)}, u32[]{:S(2)}, u32[]{:S(2)}) collective-permute-start(bf16[256,128]{1,0:T(8,128)(2,1)S(1)} %get-tuple-element.157), channel_id=1, source_target_pairs={{0,20},{4,16},{8,28},{12,24},{16,4},{20,0},{24,12},{28,8},{1,21},{... | collective-permute-start | bytes 196616 | tf_op jit(solution)/shard_map/ppermute | solution.py:400
  210.4 8.5 %collective-permute-start.35 = (bf16[256,128]{1,0:T(8,128)(2,1)S(1)}, bf16[256,128]{1,0:T(8,128)(2,1)S(1)}, u32[]{:S(2)}, u32[]{:S(2)}) collective-permute-start(bf16[256,128]{1,0:T(8,128)(2,1)S(1)} %get-tuple-element.158), channel_id=1, source_target_pairs={{0,24},{4,28},{8,16},{12,20},{16,8},{20,12},{24,0},{28,4},{1,25},{... | collective-permute-start | bytes 196616 | tf_op jit(solution)/shard_map/ppermute | solution.py:400
  210.7 12.1 %collective-permute-start.36 = (bf16[256,128]{1,0:T(8,128)(2,1)S(1)}, bf16[256,128]{1,0:T(8,128)(2,1)S(1)}, u32[]{:S(2)}, u32[]{:S(2)}) collective-permute-start(bf16[256,128]{1,0:T(8,128)(2,1)S(1)} %get-tuple-element.159), channel_id=1, source_target_pairs={{0,28},{4,24},{8,20},{12,16},{16,12},{20,8},{24,4},{28,0},{1,29},{... | collective-permute-start | bytes 196616 | tf_op jit(solution)/shard_map/ppermute | solution.py:400
  216.8 14.0 %collective-permute-start.25 = (bf16[4,128,256]{2,1,0:T(8,128)(2,1)S(1)}, bf16[4,128,256]{2,1,0:T(8,128)(2,1)S(1)}, u32[]{:S(2)}, u32[]{:S(2)}) collective-permute-start(bf16[4,128,256]{2,1,0:T(8,128)(2,1)S(1)} %get-tuple-element.146), channel_id=1, source_target_pairs={{0,12},{4,8},{8,4},{12,0},{16,28},{20,24},{24,20},{28,16},{1,13},{... | collective-permute-start | bytes 786440 | tf_op jit(solution)/shard_map/ppermute | solution.py:400
  218.8 14.7 %collective-permute-start.26 = (bf16[4,128,256]{2,1,0:T(8,128)(2,1)S(1)}, bf16[4,128,256]{2,1,0:T(8,128)(2,1)S(1)}, u32[]{:S(2)}, u32[]{:S(2)}) collective-permute-start(bf16[4,128,256]{2,1,0:T(8,128)(2,1)S(1)} %get-tuple-element.147), channel_id=1, source_target_pairs={{0,16},{4,20},{8,24},{12,28},{16,0},{20,4},{24,8},{28,12},{1,17},{... | collective-permute-start | bytes 786440 | tf_op jit(solution)/shard_map/ppermute | solution.py:400
  222.8 31.5 %collective-permute-start.27 = (bf16[4,128,256]{2,1,0:T(8,128)(2,1)S(1)}, bf16[4,128,256]{2,1,0:T(8,128)(2,1)S(1)}, u32[]{:S(2)}, u32[]{:S(2)}) collective-permute-start(bf16[4,128,256]{2,1,0:T(8,128)(2,1)S(1)} %get-tuple-element.148), channel_id=1, source_target_pairs={{0,20},{4,16},{8,28},{12,24},{16,4},{20,0},{24,12},{28,8},{1,21},{... | collective-permute-start | bytes 786440 | tf_op jit(solution)/shard_map/ppermute | solution.py:400
  223.5 38.6 %collective-permute-start.28 = (bf16[4,128,256]{2,1,0:T(8,128)(2,1)S(1)}, bf16[4,128,256]{2,1,0:T(8,128)(2,1)S(1)}, u32[]{:S(2)}, u32[]{:S(2)}) collective-permute-start(bf16[4,128,256]{2,1,0:T(8,128)(2,1)S(1)} %get-tuple-element.149), channel_id=1, source_target_pairs={{0,24},{4,28},{8,16},{12,20},{16,8},{20,12},{24,0},{28,4},{1,25},{... | collective-permute-start | bytes 786440 | tf_op jit(solution)/shard_map/ppermute | solution.py:400
  225.9 40.9 %collective-permute-start.29 = (bf16[4,128,256]{2,1,0:T(8,128)(2,1)S(1)}, bf16[4,128,256]{2,1,0:T(8,128)(2,1)S(1)}, u32[]{:S(2)}, u32[]{:S(2)}) collective-permute-start(bf16[4,128,256]{2,1,0:T(8,128)(2,1)S(1)} %get-tuple-element.150), channel_id=1, source_target_pairs={{0,28},{4,24},{8,20},{12,16},{16,12},{20,8},{24,4},{28,0},{1,29},{... | collective-permute-start | bytes 786440 | tf_op jit(solution)/shard_map/ppermute | solution.py:400
  (44 other events, 170.1 us)

commit v4 on v3

--- a/solution.py
+++ b/solution.py
@@ -19,21 +19,63 @@
 
 VM = pl.BlockSpec(memory_space=pltpu.VMEM)
 SM = pl.BlockSpec(memory_space=pltpu.SMEM)
-
-
-def call(body, out_shape, in_specs, flops, nbytes, scratch=(), trans=0, limit=12):
+HB = pl.BlockSpec(memory_space=pl.ANY)
+
+
+def call(body, out_shape, in_specs, us, scratch=(), limit=16, out_specs=None):
     many = isinstance(out_shape, (list, tuple))
-    return pl.pallas_call(
-        body,
-        out_shape=out_shape,
-        in_specs=in_specs,
-        out_specs=[VM] * len(out_shape) if many else VM,
-        scratch_shapes=list(scratch),
-        compiler_params=pltpu.CompilerParams(vmem_limit_bytes=limit * 2**20),
-        cost_estimate=pl.CostEstimate(
-            flops=int(flops), bytes_accessed=int(nbytes), transcendentals=int(trans)
-        ),
-    )
+    outs = list(out_shape) if many else [out_shape]
+    out_specs = list(out_specs or [VM] * len(outs))
+
+    def run(*args):
+        args = list(args)
+        far_in = [n for n, spec in enumerate(in_specs) if spec is HB]
+        far_out = [n for n, spec in enumerate(out_specs) if spec is HB]
+        n_in, n_out, n_own = len(in_specs), len(outs), len(scratch)
+        extra = [pltpu.VMEM(args[n].shape, args[n].dtype) for n in far_in]
+        extra += [pltpu.VMEM(outs[n].shape, outs[n].dtype) for n in far_out]
+        moved = len(far_in) + len(far_out)
+
+        def kernel(*refs):
+            ins, res = list(refs[:n_in]), list(refs[n_in : n_in + n_out])
+            own = refs[n_in + n_out : n_in + n_out + n_own]
+            held = refs[n_in + n_out + n_own :]
+            sems = held[-1] if moved else None
+            copies = []
+            for m, n in enumerate(far_in):
+                copies.append(pltpu.make_async_copy(ins[n], held[m], sems.at[m]))
+                ins[n] = held[m]
+            for c in copies:
+                c.start()
+            for c in copies:
+                c.wait()
+            copies = []
+            for m, n in enumerate(far_out):
+                m += len(far_in)
+                copies.append(pltpu.make_async_copy(held[m], res[n], sems.at[m]))
+                res[n] = held[m]
+            body(*ins, *res, *own)
+            for c in copies:
+                c.start()
+            for c in copies:
+                c.wait()
+
+        result = pl.pallas_call(
+            kernel,
+            out_shape=outs,
+            in_specs=list(in_specs),
+            out_specs=out_specs,
+            scratch_shapes=list(scratch)
+            + extra
+            + ([pltpu.SemaphoreType.DMA((moved,))] if moved else []),
+            compiler_params=pltpu.CompilerParams(vmem_limit_bytes=limit * 2**20),
+            cost_estimate=pl.CostEstimate(
+                flops=0, bytes_accessed=int(us * 3.3e6), transcendentals=0
+            ),
+        )(*args)
+        return result if many else result[0]
+
+    return run
 
 
 def dot_nt(a, b):
@@ -52,12 +94,16 @@
     return lax.broadcasted_iota(I32, shape, dim)
 
 
-def pack_kernel(source, place, hist, *outs, dp, seq_dev, per_peer):
-    here = place[0]
+def length_of(meta, slot, seqs):
+    return meta[2 + seqs + meta[2 + slot]]
+
+
+def pack_kernel(meta, hist, *outs, dp, seq_dev, per_peer):
+    here = meta[0]
 
     def per_dest(d, put):
         def per_slot(i, count):
-            src = source[d * seq_dev + i]
+            src = meta[2 + d * seq_dev + i]
             hit = lax.div(src, seq_dev) == here
 
             @pl.when(hit)
@@ -87,15 +133,15 @@
         lax.fori_loop(0, dp, body, jnp.int32(0))
 
 
-def take_kernel(source, place, *refs, dp, seq_dev, per_peer, steps):
+def take_kernel(meta, *refs, dp, seq_dev, per_peer, steps):
     arrived, out, held = refs[:-2], refs[-2], refs[-1]
-    here = place[0]
+    here = meta[0]
     if len(arrived) == dp:
         for j in range(dp):
             held[j] = arrived[j][...]
     else:
         held[...] = arrived[0][...]
-    anchors = [lax.div(source[here * seq_dev + k], seq_dev) for k in range(seq_dev)]
+    anchors = [lax.div(meta[2 + here * seq_dev + k], seq_dev) for k in range(seq_dev)]
     for k in range(seq_dev):
         rank = jnp.int32(0)
         for earlier in range(k):
@@ -104,7 +150,7 @@
         out[k * steps : (k + 1) * steps, :] = held[piece, rank]
 
 
-def forward_kernel(source, lengths, place, *refs, mp, seq_dev, steps, width, cols, quarter):
+def forward_kernel(meta, *refs, mp, seqs, seq_dev, steps, width, cols, quarter):
     blocks = refs[:mp]
     w_in = refs[mp]
     normed_t, projected, slope, weights_o, dscale, norm_o, inv_o, gated_t, own = refs[
@@ -112,10 +158,10 @@
     ]
     gated_out = refs[mp + 10 : 2 * mp + 10]
     feat, gated = refs[2 * mp + 10 :]
-    here_dp = place[0]
-    here_mp = place[1]
+    here_dp = meta[0]
+    here_mp = meta[1]
     part = width // mp
-    counts = [lengths[source[here_dp * seq_dev + k]] for k in range(seq_dev)]
+    counts = [length_of(meta, here_dp * seq_dev + k, seqs) for k in range(seq_dev)]
     for j in range(mp):
         start = pl.multiple_of(jnp.bitwise_xor(here_mp, j) * part, part)
         feat[:, pl.ds(start, part)] = blocks[j][...]
@@ -227,13 +273,13 @@
 
 
 def score_kernel(
-    place, items, code, code_far, unit, unit_far, expo, inv_o, total_o,
+    meta, items, code, code_far, unit, unit_far, expo, inv_o, total_o,
     *, dp, devices, capacity, chunk,
 ):
     events = unit.shape[0]
     near = devices // 2
     slots = items.shape[0]
-    half = pl.multiple_of(lax.div(place[0], dp // 2) * near, near)
+    half = pl.multiple_of(lax.div(meta[0], dp // 2) * near, near)
     codes_in = [c[pl.ds(half, near), :].astype(BF) for c in (code, code_far)]
     for s in range(0, slots, chunk):
         rows = slice(s, s + chunk)
@@ -263,15 +309,15 @@
             expo[rows, lanes] = jnp.where(first, -e, jnp.where(other, e, 0.0))
 
 
-def shares(source, lengths, place, expo, total, total_far, dp, seq_dev, steps):
+def shares(meta, expo, total, total_far, dp, seqs, seq_dev, steps):
     events = total.shape[1] // 2
-    position = place[1] * events + iota((1, events), 1)
+    position = meta[1] * events + iota((1, events), 1)
     valid = []
-    for base in (place[0], jnp.bitwise_xor(place[0], dp // 2)):
+    for base in (meta[0], jnp.bitwise_xor(meta[0], dp // 2)):
         v = jnp.zeros((1, events), F32)
         for k in range(seq_dev):
             step = position - k * steps
-            v = jnp.where((step >= 0) & (step < lengths[source[base * seq_dev + k]]), 1.0, v)
+            v = jnp.where((step >= 0) & (step < length_of(meta, base * seq_dev + k, seqs)), 1.0, v)
         valid.append(v)
     valid = jnp.concatenate(valid, axis=1) * (1.0 / COSINE_DIVISOR)
     full = total[...] + jnp.concatenate([total_far[:, events:], total_far[:, :events]], axis=1)
@@ -280,10 +326,10 @@
 
 
 def slope_kernel(
-    source, lengths, place, items, expo, inv, total, total_far, slope, slope_far,
-    *, dp, seq_dev, steps, chunk,
+    meta, items, expo, inv, total, total_far, slope, slope_far,
+    *, dp, seqs, seq_dev, steps, chunk,
 ):
-    share = shares(source, lengths, place, expo, total, total_far, dp, seq_dev, steps)
+    share = shares(meta, expo, total, total_far, dp, seqs, seq_dev, steps)
     events, width = slope.shape
     both = jnp.zeros((2 * events, width), F32)
     for s in range(0, items.shape[0], chunk):
@@ -294,10 +340,10 @@
 
 
 def send_kernel(
-    source, lengths, place, expo, total, total_far, unit, unit_far, sending,
-    *, dp, seq_dev, steps, chunk,
+    meta, expo, total, total_far, unit, unit_far, sending,
+    *, dp, seqs, seq_dev, steps, chunk,
 ):
-    share = shares(source, lengths, place, expo, total, total_far, dp, seq_dev, steps)
+    share = shares(meta, expo, total, total_far, dp, seqs, seq_dev, steps)
     events = unit.shape[0]
     for s in range(0, expo.shape[0], chunk):
         rows = slice(s, s + chunk)
@@ -336,11 +382,11 @@
             outs[0][(d,) + index] = whole[d * share : (d + 1) * share, :]
 
 
-def w_out_kernel(place, *refs, mp, dp):
+def w_out_kernel(meta, *refs, mp, dp):
     blocks, gated_t, outs, whole = refs[:mp], refs[mp], refs[mp + 1 : -1], refs[-1]
     quarter, width = blocks[0].shape
     for j in range(mp):
-        start = pl.multiple_of(jnp.bitwise_xor(place[1], j) * quarter, quarter)
+        start = pl.multiple_of(jnp.bitwise_xor(meta[1], j) * quarter, quarter)
         whole[pl.ds(start, quarter), :] = blocks[j][...]
     part = dot_nn(gated_t[...], whole[...]).astype(BF)
     lanes = width // dp
@@ -349,7 +395,7 @@
         for d in range(dp):
             for j in range(dp):
 
-                @pl.when(jnp.bitwise_xor(place[0], j) == d)
+                @pl.when(jnp.bitwise_xor(meta[0], j) == d)
                 def _(d=d, j=j):
                     outs[j][...] = spare[d]
     else:
@@ -357,14 +403,14 @@
             outs[0][d] = part[:, d * lanes : (d + 1) * lanes]
 
 
-def backward_kernel(place, *refs, mp, dp):
+def backward_kernel(meta, *refs, mp, dp):
     blocks = refs[:mp]
     w_out, projected, slope, weights, dscale, norm, inv, normed_t = refs[mp : mp + 8]
     outs = refs[mp + 8 : -3]
     whole, cot, parts = refs[-3:]
     quarter, width = blocks[0].shape
     for j in range(mp):
-        start = pl.multiple_of(jnp.bitwise_xor(place[1], j) * quarter, quarter)
+        start = pl.multiple_of(jnp.bitwise_xor(meta[1], j) * quarter, quarter)
         whole[pl.ds(start, quarter), :] = blocks[j][...]
     rows_all = whole.shape[0]
     cols = w_out.shape[0]
@@ -392,7 +438,7 @@
     share = width // dp
     for c in range(4):
         parts[...] = dot_nn(normed_t[...], cot[c]).astype(BF)
-        put_pieces(outs, (c,), place[0], dp, parts, share)
+        put_pieces(outs, (c,), meta[0], dp, parts, share)
 
 
 def swapped(x, axis, bit):
@@ -452,6 +498,8 @@
     S = jax.ShapeDtypeStruct
     here_dp = lax.axis_index("dp")
     place = jnp.stack([here_dp, lax.axis_index("mp")]).astype(I32)
+    meta = jnp.concatenate([place, source, lengths])
+    seqs = source.shape[0]
     halves = [list(range(near)), list(range(near, devices))]
 
     def partner(x):
@@ -467,24 +515,29 @@
             axis_index_groups=halves,
         ).reshape(slots, width)
 
-    w_out_blocks = gather_blocks(w_out, "mp")
     packed = call(
         functools.partial(pack_kernel, dp=dp, seq_dev=seq_dev, per_peer=per_peer),
-        pieces(dp, (per_peer, steps, part), BF),
-        [SM, SM, VM],
-        1e5,
-        4 * history.size,
-    )(source, place, history)
-    packed, owners = lax.optimization_barrier((packed, owners))
+        [S((dp, per_peer, steps, part), BF)],
+        [SM, VM],
+        3,
+    )(meta, history)
+    w_out_blocks = gather_blocks(w_out, "mp")
     arrived = exchange(packed, "dp")
-    arrived, w_out_blocks = lax.optimization_barrier((arrived, w_out_blocks))
+    arrived, w_out_blocks, owners = lax.optimization_barrier((arrived, w_out_blocks, owners))
+    rows = call(
+        functools.partial(take_kernel, dp=dp, seq_dev=seq_dev, per_peer=per_peer, steps=steps),
+        S((rows_all, part), BF),
+        [SM] + [VM] * len(arrived),
+        1,
+        scratch=[pltpu.VMEM((dp, per_peer, steps, part), BF)],
+    )(meta, *arrived)
+    features = gather_blocks(rows, "mp")
 
     wanted, code = call(
         functools.partial(ask_kernel, devices=devices, capacity=capacity),
         [S((devices, capacity), I32), S((devices, events), F32)],
         [VM, VM],
-        1e6,
-        1e5,
+        2,
     )(owners, item_rows)
     asked = lax.all_to_all(wanted, ("dp", "mp"), split_axis=0, concat_axis=0, tiled=True)
     asked = asked.reshape(2, near, capacity)
@@ -493,27 +546,19 @@
     looked = call(
         functools.partial(look_kernel, chunk=chunk),
         S((slots, width), BF),
-        [VM, VM],
-        2 * slots * stock * width,
-        2 * (slots + stock) * width,
+        [VM, HB],
+        3,
+        out_specs=[HB],
     )(incoming, catalogue)
-
-    rows = call(
-        functools.partial(take_kernel, dp=dp, seq_dev=seq_dev, per_peer=per_peer, steps=steps),
-        S((rows_all, part), BF),
-        [SM, SM] + [VM] * len(arrived),
-        1e5,
-        4 * history.size,
-        scratch=[pltpu.VMEM((dp, per_peer, steps, part), BF)],
-    )(source, place, *arrived)
-    features = gather_blocks(rows, "mp")
     code_far = partner(code)
     looked, features, code_far = lax.optimization_barrier((looked, features, code_far))
     items = in_half(looked)
+
     (normed_t, projected, slope, weights, dscale, norm, inv, gated_t, own, *gated) = call(
         functools.partial(
             forward_kernel,
             mp=mp,
+            seqs=seqs,
             seq_dev=seq_dev,
             steps=steps,
             width=width,
@@ -532,19 +577,18 @@
             S((quarter, width), BF),
         ]
         + [S((quarter, cols), BF)] * mp,
-        [SM, SM, SM] + [VM] * (mp + 1),
-        8 * rows_all * width * cols,
-        12 * 2**20,
+        [SM] + [HB] * (mp + 1),
+        6,
         scratch=[pltpu.VMEM((rows_all, width), BF), pltpu.VMEM((rows_all, cols), BF)],
-        trans=6 * rows_all * cols,
-    )(source, lengths, place, *features, w_in)
+        out_specs=[HB] * 9 + [VM] * mp,
+        limit=24,
+    )(meta, *features, w_in)
     gathered = exchange(gated, "mp")
     unit, unit_bf, inv_out = call(
         functools.partial(out_kernel, mp=mp),
         [S((quarter, width), F32), S((quarter, width), BF), S((quarter, BLOCK), F32)],
-        [VM] * (2 * mp + 1),
-        2 * quarter * width * width,
-        4 * 2**20,
+        [HB] + [VM] * mp + [HB] * mp,
+        2,
     )(own, *gathered, *w_out_blocks)
 
     unit_far = partner(unit_bf)
@@ -553,30 +597,28 @@
             score_kernel, dp=dp, devices=devices, capacity=capacity, chunk=chunk
         ),
         [S((slots, 2 * events), F32), S((slots, BLOCK), F32), S((1, 2 * events), F32)],
-        [SM] + [VM] * 5,
-        4 * slots * width * events,
-        2 * slots * width,
-    )(place, items, code, code_far, unit_bf, unit_far)
+        [SM, HB] + [VM] * 4,
+        4,
+    )(meta, items, code, code_far, unit_bf, unit_far)
     total_far = partner(total)
-    sizes = dict(dp=dp, seq_dev=seq_dev, steps=steps, chunk=chunk)
+    sizes = dict(dp=dp, seqs=seqs, seq_dev=seq_dev, steps=steps, chunk=chunk)
     item_slope, slope_far = call(
         functools.partial(slope_kernel, **sizes),
         [S((events, width), F32), S((events, width), BF)],
-        [SM, SM, SM] + [VM] * 5,
-        4 * slots * width * events,
-        2 * slots * width,
-    )(source, lengths, place, items, expo, inv_item, total, total_far)
+        [SM, HB] + [VM] * 4,
+        2,
+    )(meta, items, expo, inv_item, total, total_far)
     slope_back = partner(slope_far)
     sending = call(
         functools.partial(send_kernel, **sizes),
         S((slots, width), BF),
-        [SM, SM, SM] + [VM] * 5,
-        4 * slots * width * events,
-        2 * slots * width,
-    )(source, lengths, place, expo, total, total_far, unit_bf, unit_far)
-    out_cot = call(
-        out_cot_kernel, S((events, width), BF), [VM] * 4, 1e6, 2 * 2**20
-    )(unit, inv_out, item_slope, slope_back)
+        [SM] + [VM] * 5,
+        3,
+        out_specs=[HB],
+    )(meta, expo, total, total_far, unit_bf, unit_far)
+    out_cot = call(out_cot_kernel, S((events, width), BF), [VM] * 4, 1)(
+        unit, inv_out, item_slope, slope_back
+    )
 
     cots = gather_blocks(out_cot, "mp")
     sending, cots = lax.optimization_barrier((sending, cots))
@@ -584,31 +626,31 @@
     w_out_part = call(
         functools.partial(w_out_kernel, mp=mp, dp=dp),
         pieces(dp, (cols, width // dp), BF),
-        [SM] + [VM] * (mp + 1),
-        2 * rows_all * width * cols,
-        3 * 2**20,
+        [SM] + [HB] * (mp + 1),
+        2,
         scratch=[pltpu.VMEM((rows_all, width), BF)],
-    )(place, *cots, gated_t)
+    )(meta, *cots, gated_t)
     w_in_part = call(
         functools.partial(backward_kernel, mp=mp, dp=dp),
         pieces(dp, (4, width // dp, cols), BF),
-        [SM] + [VM] * (mp + 8),
-        10 * rows_all * width * cols,
-        12 * 2**20,
+        [SM] + [HB] * (mp + 8),
+        6,
         scratch=[
             pltpu.VMEM((rows_all, width), BF),
             pltpu.VMEM((4, rows_all, cols), BF),
             pltpu.VMEM((width, cols), BF),
         ],
-    )(place, *cots, w_out, projected, slope, weights, dscale, norm, inv, normed_t)
+        limit=24,
+    )(meta, *cots, w_out, projected, slope, weights, dscale, norm, inv, normed_t)
     w_out_grad = summed(exchange(w_out_part, "dp"))
     w_in_grad = summed(exchange(w_in_part, "dp"))
     cat_grad = call(
         functools.partial(spread_kernel, chunk=math.gcd(stock, 128)),
         S((stock, width), F32),
-        [VM] * 3,
-        2 * slots * stock * width,
-        2 * slots * width + 6 * stock * width,
+        [VM, HB, HB],
+        4,
+        out_specs=[HB],
+        limit=24,
     )(incoming, landed, catalogue)
     return (w_in_grad, w_out_grad, cat_grad)
 

time: 275 us -> 282 us (1.025)
  blocking collectives: 0 us -> 12.2 us
  starting transfers between devices: 73.1 us -> 65.9 us
  Pallas kernels: 28.2 us -> 32.9 us
  waiting for transfers between devices: 132 us -> 129 us
    all_to_all x0 -> x1, blocking collectives: none -> 12.2 us  [exchange(): lax.all_to_all(parts[0], axis, split_axis=0, concat_axis=0, tiled=True)]
    pallas_call x13, Pallas kernels: 28.2 us -> 32.9 us  [run(): pl.pallas_call(kernel, out_shape=outs, in_specs=list(in_specs), out_specs...]
    all_to_all x1, starting transfers between devices: 10.4 us -> 5.9 us  [per_device(): lax.all_to_all(wanted, ('dp', 'mp'), split_axis=0, concat_axis=0, tiled=T...]
    ppermute x37 -> x30, waiting for transfers between devices: 130 us -> 127 us  [swapped(): return lax.ppermute(x, axis, [(a, a ^ bit) for a in range(size)])]
    ppermute x37 -> x30, starting transfers between devices: 49.6 us -> 46.7 us  [swapped(): return lax.ppermute(x, axis, [(a, a ^ bit) for a in range(size)])]
    unnamed x105 -> x97, local copies, waits for them, and re-layouts: 35.2 us -> 34.4 us
  transfers between devices with their start and end apart: 40 -> 33, of which waited for: 18 -> 16; matrix products, arithmetic and copies ran while one was open for 1% -> 2% of each run, Pallas kernels for 7% -> 8%
where the time goes in v4:
time: 282 us; the launch traced here: 279 us
  waiting for transfers between devices  129 us (46%)
  starting transfers between devices  65.9 us (23%)
  local copies, waits for them, and re-layouts  35.3 us (13%)
  Pallas kernels  32.9 us (12%)
  blocking collectives  12.2 us (4%)
    ppermute x30, waiting for transfers between devices, swapped(): return lax.ppermute(x, axis, [(a, a ^ bit) for a in range(size)])  127 us
    ppermute x30, starting transfers between devices, swapped(): return lax.ppermute(x, axis, [(a, a ^ bit) for a in range(size)])  46.7 us
    unnamed x97, local copies, waits for them, and re-layouts  34.4 us
    pallas_call x13, Pallas kernels, run(): pl.pallas_call(kernel, out_shape=outs, in_specs=list(in_specs), out_specs...  32.9 us
    all_to_all x2, starting transfers between devices, in_half(): lax.all_to_all(x.reshape(near, 2 * capacity, width), ('dp', 'mp'), split_...  13.3 us
    all_to_all x1, blocking collectives, exchange(): lax.all_to_all(parts[0], axis, split_axis=0, concat_axis=0, tiled=True)  12.2 us
    all_to_all x1, starting transfers between devices, per_device(): lax.all_to_all(wanted, ('dp', 'mp'), split_axis=0, concat_axis=0, tiled=T...  5.9 us
  transfers between devices with their start and end apart: 33, of which 16 were waited for; matrix products, arithmetic and copies ran while one was open for 2% of the time, Pallas kernels for 8%

profile of v4, /device:TPU:13, one launch (start us, length us, event | category | flops | bytes accessed | tf_op | source)
XLA Modules:
  0.0 279.0 jit_solution(7257887627412276614)
XLA Ops:
  1.9 11.8 %collective-permute-done.1.refs_7_ = bf16[256,1024]{1,0:T(8,128)(2,1)S(1)} collective-permute-done((bf16[256,1024]{1,0:T(8,128)(2,1)}, bf16[256,1024]{1,0:T(8,128)(2,1)S(1)}, u32[]{:S(2)}, u32[]{:S(2)}) %collective-permute-start.1) | collective-permute-done | bytes 524320 | tf_op jit(solution)/shard_map/ppermute | solution.py:446
  13.7 1.5 collective-permute-start.2
  16.9 3.0 %shard_map.103 = bf16[8,2,32,256]{3,2,1,0:T(8,128)(2,1)S(1)} custom-call(s32[258]{0:T(512)S(1)} %pad_add_fusion.refs_0_, bf16[16,32,256]{2,1,0:T(8,128)(2,1)S(1)} %copy-done.41), custom_call_target="tpu_custom_call" | custom-call | bytes 9900000 | tf_op jit(solution)/shard_map/pallas_call | solution.py:63
  20.0 12.2 %all_to_all.24.refs_1_ = bf16[8,2,32,256]{3,2,1,0:T(8,128)(2,1)S(1)} all-to-all(bf16[8,2,32,256]{3,2,1,0:T(8,128)(2,1)S(1)} %shard_map.103), channel_id=1, replica_groups=mesh['dp'=8,'mp'=4] {'dp'}, dimensions={0} | all-to-all | bytes 524288 | tf_op jit(solution)/shard_map/all_to_all | solution.py:468
  34.1 2.8 collective-permute-start.3
  36.9 2.2 collective-permute-done.4.refs_3_
  39.1 3.6 %collective-permute-start.5 = (bf16[512,256]{1,0:T(8,128)(2,1)S(1)}, bf16[512,256]{1,0:T(8,128)(2,1)S(1)}, u32[]{:S(2)}, u32[]{:S(2)}) collective-permute-start(bf16[512,256]{1,0:T(8,128)(2,1)S(1)} %collective-permute-done.4.refs_3_), channel_id=1, source_target_pairs={{0,1},{1,0},{2,3},{3,2},{4,5},{5,4},{6,7},{7,6},{8,9},{9,8},{10,11... | collective-permute-start | bytes 786440 | tf_op jit(solution)/shard_map/ppermute | solution.py:446
  44.3 1.3 shard_map.104
  45.6 5.9 %all-to-all-start.1 = ((s32[32,1,48]{2,1,0:T(1,128)}), s32[32,1,48]{2,1,0:T(1,128)S(1)}, u32[]{:S(2)}, u32[]{:S(2)}) async-start(s32[32,1,48]{2,1,0:T(1,128)} %bitcast.3), calls=%async_computation.1 | async-start | bytes 32768 | tf_op jit(solution)/shard_map/all_to_all | solution.py:542
  51.5 2.2 collective-permute-start.6
  53.7 2.4 all-to-all-done.1
  57.5 2.2 shard_map.105
  59.7 1.6 copy-done
  62.8 6.3 %all-to-all-start.2 = ((bf16[16,96,1024]{2,1,0:T(8,128)(2,1)}), bf16[16,96,1024]{2,1,0:T(8,128)(2,1)S(1)}, u32[]{:S(2)}, u32[]{:S(2)}) async-start(bf16[16,96,1024]{2,1,0:T(8,128)(2,1)} %bitcast.15), calls=%async_computation.2 | async-start | bytes 6291456 | tf_op jit(solution)/shard_map/all_to_all | solution.py:509
  69.1 1.6 copy-done.5
  73.5 5.0 %shard_map.107 = (bf16[1024,512]{1,0:T(8,128)(2,1)S(1)}, bf16[4,512,256]{2,1,0:T(8,128)(2,1)S(1)}, f32[4,512,256]{2,1,0:T(8,128)S(1)}, bf16[2,512,128]{2,1,0:T(8...) custom-call(s32[258]{0:T(512)S(1)} %pad_add_fusion.refs_0_, ...), custom_call_target="tpu_custom_call" | custom-call | bytes 19800000 | tf_op jit(solution)/shard_map/pallas_call | solution.py:63
  84.2 1.5 collective-permute-start.9
  85.7 14.9 %collective-permute-done.8.refs_3_ = bf16[128,256]{1,0:T(8,128)(2,1)S(1)} collective-permute-done((bf16[128,256]{1,0:T(8,128)(2,1)S(1)}, bf16[128,256]{1,0:T(8,128)(2,1)S(1)}, u32[]{:S(2)}, u32[]{:S(2)}) %collective-permute-start.8) | collective-permute-done | bytes 65568 | tf_op jit(solution)/shard_map/ppermute | solution.py:446
  100.5 1.4 collective-permute-done.9.refs_4_
  103.9 11.2 %collective-permute-done.10.refs_5_ = bf16[128,1024]{1,0:T(8,128)(2,1)S(1)} collective-permute-done((bf16[128,1024]{1,0:T(8,128)(2,1)S(1)}, bf16[128,1024]{1,0:T(8,128)(2,1)S(1)}, u32[]{:S(2)}, u32[]{:S(2)}) %collective-permute-start.10) | collective-permute-done | bytes 262176 | tf_op jit(solution)/shard_map/ppermute | solution.py:446
  116.8 3.3 %shard_map.109 = (f32[1536,256]{1,0:T(8,128)S(1)}, f32[1536,128]{1,0:T(8,128)S(1)}, f32[1,256]{1,0:T(1,128)S(1)}) custom-call(s32[258]{0:T(512)S(1)} %pad_add_fusion.refs_0_, bf16[1536,1024]{1,0:T(8,128)(2,1)S(1)} %bitcast.12, f32[32,128]{1,0:T(8,128)S(1)} %get-tuple-element.62.refs_2_, f32[32,128]{1,0:T(8,128)S(1)} %collective-permute-done.6.refs_3_, ...), custom_call_target="tpu_custom_call" | custom-call | bytes 13200000 | tf_op jit(solution)/shard_map/pallas_call | solution.py:63
  120.0 2.8 %collective-permute-start.11 = (f32[1,256]{1,0:T(1,128)S(1)}, f32[1,256]{1,0:T(1,128)S(1)}, u32[]{:S(2)}, u32[]{:S(2)}) collective-permute-start(f32[1,256]{1,0:T(1,128)S(1)} %get-tuple-element.80.refs_2_.refs_4_), channel_id=1, source_target_pairs={{0,16},{4,20},{8,24},{12,28},{16,0},{20,4},{24,8},{28,12},{1,17},{... | collective-permute-start | bytes 3080 | tf_op jit(solution)/shard_map/ppermute | solution.py:446
  123.8 1.9 shard_map.111
  125.8 2.4 collective-permute-start.12
  128.2 10.4 %collective-permute-done.12.refs_3_ = bf16[128,1024]{1,0:T(8,128)(2,1)S(1)} collective-permute-done((bf16[128,1024]{1,0:T(8,128)(2,1)S(1)}, bf16[128,1024]{1,0:T(8,128)(2,1)S(1)}, u32[]{:S(2)}, u32[]{:S(2)}) %collective-permute-start.12) | collective-permute-done | bytes 262176 | tf_op jit(solution)/shard_map/ppermute | solution.py:446
  138.9 3.2 %collective-permute-start.14 = (bf16[128,1024]{1,0:T(8,128)(2,1)S(1)}, bf16[128,1024]{1,0:T(8,128)(2,1)S(1)}, u32[]{:S(2)}, u32[]{:S(2)}) collective-permute-start(bf16[128,1024]{1,0:T(8,128)(2,1)S(1)} %shard_map.112.refs_1_), channel_id=1, source_target_pairs={{0,2},{1,3},{2,0},{3,1},{4,6},{5,7},{6,4},{7,5},{8,10},{9,11},{10,... | collective-permute-start | bytes 786440 | tf_op jit(solution)/shard_map/ppermute | solution.py:446
  142.9 5.5 %collective-permute-done.14.refs_3_ = bf16[128,1024]{1,0:T(8,128)(2,1)S(1)} collective-permute-done((bf16[128,1024]{1,0:T(8,128)(2,1)S(1)}, bf16[128,1024]{1,0:T(8,128)(2,1)S(1)}, u32[]{:S(2)}, u32[]{:S(2)}) %collective-permute-start.14) | collective-permute-done | bytes 262176 | tf_op jit(solution)/shard_map/ppermute | solution.py:446
  150.3 4.0 %shard_map.110 = bf16[1536,1024]{1,0:T(8,128)(2,1)} custom-call(s32[258]{0:T(512)S(1)} %pad_add_fusion.refs_0_, f32[1536,256]{1,0:T(8,128)S(1)} %get-tuple-element.79.refs_1_.refs_2_, f32[1,256]{1,0:T(1,128)S(1)} %get-tuple-element.80.refs_2_.refs_4_, f32[1,256]{1,0:T(1,128)S(1)} %collective-permute-done.11.refs_3_.refs_5_, bf16[128,1024]{1,0:T(8,128)(2,1)S(1)} %copy-done.9, ...), custom_call_target="tpu_custom_call" | custom-call | bytes 9900000 | tf_op jit(solution)/shard_map/pallas_call | solution.py:63
  155.8 7.0 %all-to-all-start.3 = ((bf16[16,96,1024]{2,1,0:T(8,128)(2,1)}), bf16[16,96,1024]{2,1,0:T(8,128)(2,1)S(1)}, u32[]{:S(2)}, u32[]{:S(2)}) async-start(bf16[16,96,1024]{2,1,0:T(8,128)(2,1)} %bitcast.8), calls=%async_computation.3 | async-start | bytes 6291456 | tf_op jit(solution)/shard_map/all_to_all | solution.py:509
  163.9 1.6 copy-done.7
  174.9 4.9 %shard_map.113 = (bf16[4,128,256]{2,1,0:T(8,128)(2,1)S(1)}, bf16[4,128,256]{2,1,0:T(8,128)(2,1)S(1)}, bf16[4,128,256]{2,1,0:T(8,128)(2,1)S(1)}, bf16[4,128,256]{...) custom-call(s32[258]{0:T(512)S(1)} %pad_add_fusion.refs_0_, ...), custom_call_target="tpu_custom_call" | custom-call | bytes 19800000 | tf_op jit(solution)/shard_map/pallas_call | solution.py:63
  179.7 1.3 collective-permute-start.16
  181.2 1.8 shard_map.114
  183.4 1.2 collective-permute-start.24
  185.8 26.3 %collective-permute-done.23 = bf16[256,128]{1,0:T(8,128)(2,1)S(1)} collective-permute-done((bf16[256,128]{1,0:T(8,128)(2,1)S(1)}, bf16[256,128]{1,0:T(8,128)(2,1)S(1)}, u32[]{:S(2)}, u32[]{:S(2)}) %collective-permute-start.23) | collective-permute-done | bytes 65568 | tf_op jit(solution)/shard_map/ppermute | solution.py:446
  212.4 3.9 %collective-permute-start.27 = (bf16[256,128]{1,0:T(8,128)(2,1)S(1)}, bf16[256,128]{1,0:T(8,128)(2,1)S(1)}, u32[]{:S(2)}, u32[]{:S(2)}) collective-permute-start(bf16[256,128]{1,0:T(8,128)(2,1)S(1)} %get-tuple-element.111), channel_id=1, source_target_pairs={{0,20},{4,16},{8,28},{12,24},{16,4},{20,0},{24,12},{28,8},{1,21},{... | collective-permute-start | bytes 196616 | tf_op jit(solution)/shard_map/ppermute | solution.py:446
  216.6 6.1 %collective-permute-start.29 = (bf16[256,128]{1,0:T(8,128)(2,1)S(1)}, bf16[256,128]{1,0:T(8,128)(2,1)S(1)}, u32[]{:S(2)}, u32[]{:S(2)}) collective-permute-start(bf16[256,128]{1,0:T(8,128)(2,1)S(1)} %get-tuple-element.113), channel_id=1, source_target_pairs={{0,28},{4,24},{8,20},{12,16},{16,12},{20,8},{24,4},{28,0},{1,29},{... | collective-permute-start | bytes 196616 | tf_op jit(solution)/shard_map/ppermute | solution.py:446
  222.7 2.1 collective-permute-start.18
  224.8 2.1 collective-permute-start.19
  226.9 1.8 collective-permute-done.29
  229.5 2.4 collective-permute-start.21
  232.6 4.1 %collective-permute-done.18 = bf16[4,128,256]{2,1,0:T(8,128)(2,1)S(1)} collective-permute-done((bf16[4,128,256]{2,1,0:T(8,128)(2,1)S(1)}, bf16[4,128,256]{2,1,0:T(8,128)(2,1)S(1)}, u32[]{:S(2)}, u32[]{:S(2)}) %collective-permute-start.18) | collective-permute-done | bytes 262176 | tf_op jit(solution)/shard_map/ppermute | solution.py:446
  236.7 2.8 %collective-permute-done.19 = bf16[4,128,256]{2,1,0:T(8,128)(2,1)S(1)} collective-permute-done((bf16[4,128,256]{2,1,0:T(8,128)(2,1)S(1)}, bf16[4,128,256]{2,1,0:T(8,128)(2,1)S(1)}, u32[]{:S(2)}, u32[]{:S(2)}) %collective-permute-start.19) | collective-permute-done | bytes 262176 | tf_op jit(solution)/shard_map/ppermute | solution.py:446
  239.5 20.8 %collective-permute-done.20 = bf16[4,128,256]{2,1,0:T(8,128)(2,1)S(1)} collective-permute-done((bf16[4,128,256]{2,1,0:T(8,128)(2,1)S(1)}, bf16[4,128,256]{2,1,0:T(8,128)(2,1)S(1)}, u32[]{:S(2)}, u32[]{:S(2)}) %collective-permute-start.20) | collective-permute-done | bytes 262176 | tf_op jit(solution)/shard_map/ppermute | solution.py:446
  260.3 7.8 %collective-permute-done.21 = bf16[4,128,256]{2,1,0:T(8,128)(2,1)S(1)} collective-permute-done((bf16[4,128,256]{2,1,0:T(8,128)(2,1)S(1)}, bf16[4,128,256]{2,1,0:T(8,128)(2,1)S(1)}, u32[]{:S(2)}, u32[]{:S(2)}) %collective-permute-start.21) | collective-permute-done | bytes 262176 | tf_op jit(solution)/shard_map/ppermute | solution.py:446
  268.1 4.7 %collective-permute-done.22 = bf16[4,128,256]{2,1,0:T(8,128)(2,1)S(1)} collective-permute-done((bf16[4,128,256]{2,1,0:T(8,128)(2,1)S(1)}, bf16[4,128,256]{2,1,0:T(8,128)(2,1)S(1)}, u32[]{:S(2)}, u32[]{:S(2)}) %collective-permute-start.22) | collective-permute-done | bytes 262176 | tf_op jit(solution)/shard_map/ppermute | solution.py:446
  273.8 1.2 copy-done.2
  275.0 3.8 %shard_map.115 = f32[512,1024]{1,0:T(8,128)} custom-call(s32[1,1536]{1,0:T(1,128)S(1)} %reshape.28.refs_0_, bf16[1536,1024]{1,0:T(8,128)(2,1)S(1)} %bitcast.14, bf16[512,1024]{1,0:T(8,128)(2,1)S(1)} %copy-done.2), custom_call_target="tpu_custom_call" | custom-call | bytes 13200000 | tf_op jit(solution)/shard_map/pallas_call | solution.py:63
  (137 shorter events, 41.9 us)
Async XLA Ops:
  0.6 13.1 %collective-permute-start.1 = (bf16[256,1024]{1,0:T(8,128)(2,1)}, bf16[256,1024]{1,0:T(8,128)(2,1)S(1)}, u32[]{:S(2)}, u32[]{:S(2)}) collective-permute-start(bf16[256,1024]{1,0:T(8,128)(2,1)} %refs_5_.4), channel_id=1, source_target_pairs={{0,2},{1,3},{2,0},{3,1},{4,6},{5,7},{6,4},{7,5},{8,10},{9,11},{10,... | collective-permute-start | bytes 1572872 | tf_op jit(solution)/shard_map/ppermute | solution.py:446
  0.9 31.2 %collective-permute-start = (bf16[256,1024]{1,0:T(8,128)(2,1)}, bf16[256,1024]{1,0:T(8,128)(2,1)S(1)}, u32[]{:S(2)}, u32[]{:S(2)}) collective-permute-start(bf16[256,1024]{1,0:T(8,128)(2,1)} %refs_5_.4), channel_id=1, source_target_pairs={{0,1},{1,0},{2,3},{3,2},{4,5},{5,4},{6,7},{7,6},{8,9},{9,8},{10,11... | collective-permute-start | bytes 1572872 | tf_op jit(solution)/shard_map/ppermute | solution.py:446
  13.7 49.1 %copy-start.23 = (bf16[256,1024]{1,0:T(8,128)(2,1)}, bf16[256,1024]{1,0:T(8,128)(2,1)S(1)}, u32[]{:S(2)}) copy-start(bf16[256,1024]{1,0:T(8,128)(2,1)S(1)} %collective-permute-done.1.refs_7_) | copy-start | bytes 1572868
  13.7 18.4 %collective-permute-start.2 = (bf16[256,1024]{1,0:T(8,128)(2,1)S(1)}, bf16[256,1024]{1,0:T(8,128)(2,1)S(1)}, u32[]{:S(2)}, u32[]{:S(2)}) collective-permute-start(bf16[256,1024]{1,0:T(8,128)(2,1)S(1)} %collective-permute-done.1.refs_7_), channel_id=1, source_target_pairs={{0,1},{1,0},{2,3},{3,2},{4,5},{5,4},{6,7},{7,6},{8,9},{9,8},{10,11... | collective-permute-start | bytes 1572872 | tf_op jit(solution)/shard_map/ppermute | solution.py:446
  32.1 30.6 %copy-start.25 = (bf16[256,1024]{1,0:T(8,128)(2,1)}, bf16[256,1024]{1,0:T(8,128)(2,1)S(1)}, u32[]{:S(2)}) copy-start(bf16[256,1024]{1,0:T(8,128)(2,1)S(1)} %collective-permute-done.refs_6_) | copy-start | bytes 1572868
  33.8 5.3 %collective-permute-start.4 = (bf16[512,256]{1,0:T(8,128)(2,1)S(1)}, bf16[512,256]{1,0:T(8,128)(2,1)S(1)}, u32[]{:S(2)}, u32[]{:S(2)}) collective-permute-start(bf16[512,256]{1,0:T(8,128)(2,1)S(1)} %shard_map.106.refs_1_), channel_id=1, source_target_pairs={{0,2},{1,3},{2,0},{3,1},{4,6},{5,7},{6,4},{7,5},{8,10},{9,11},{10,... | collective-permute-start | bytes 786440 | tf_op jit(solution)/shard_map/ppermute | solution.py:446
  34.1 27.3 %collective-permute-start.3 = (bf16[512,256]{1,0:T(8,128)(2,1)S(1)}, bf16[512,256]{1,0:T(8,128)(2,1)S(1)}, u32[]{:S(2)}, u32[]{:S(2)}) collective-permute-start(bf16[512,256]{1,0:T(8,128)(2,1)S(1)} %shard_map.106.refs_1_), channel_id=1, source_target_pairs={{0,1},{1,0},{2,3},{3,2},{4,5},{5,4},{6,7},{7,6},{8,9},{9,8},{10,11... | collective-permute-start | bytes 786440 | tf_op jit(solution)/shard_map/ppermute | solution.py:446
  39.1 23.7 %copy-start.42 = (bf16[512,256]{1,0:T(8,128)(2,1)}, bf16[512,256]{1,0:T(8,128)(2,1)S(1)}, u32[]{:S(2)}) copy-start(bf16[512,256]{1,0:T(8,128)(2,1)S(1)} %collective-permute-done.4.refs_3_) | copy-start | bytes 786436
  39.1 23.0 %collective-permute-start.5 = (bf16[512,256]{1,0:T(8,128)(2,1)S(1)}, bf16[512,256]{1,0:T(8,128)(2,1)S(1)}, u32[]{:S(2)}, u32[]{:S(2)}) collective-permute-start(bf16[512,256]{1,0:T(8,128)(2,1)S(1)} %collective-permute-done.4.refs_3_), channel_id=1, source_target_pairs={{0,1},{1,0},{2,3},{3,2},{4,5},{5,4},{6,7},{7,6},{8,9},{9,8},{10,11... | collective-permute-start | bytes 786440 | tf_op jit(solution)/shard_map/ppermute | solution.py:446
  45.6 10.6 %all-to-all-start.1 = ((s32[32,1,48]{2,1,0:T(1,128)}), s32[32,1,48]{2,1,0:T(1,128)S(1)}, u32[]{:S(2)}, u32[]{:S(2)}) async-start(s32[32,1,48]{2,1,0:T(1,128)} %bitcast.3), calls=%async_computation.1 | async-start | bytes 32768 | tf_op jit(solution)/shard_map/all_to_all | solution.py:542
  51.5 9.9 %collective-permute-start.6 = (f32[32,128]{1,0:T(8,128)S(1)}, f32[32,128]{1,0:T(8,128)S(1)}, u32[]{:S(2)}, u32[]{:S(2)}) collective-permute-start(f32[32,128]{1,0:T(8,128)S(1)} %get-tuple-element.62.refs_2_), channel_id=1, source_target_pairs={{0,16},{4,20},{8,24},{12,28},{16,0},{20,4},{24,8},{28,12},{1,17},{... | collective-permute-start | bytes 49160 | tf_op jit(solution)/shard_map/ppermute | solution.py:446
  59.7 1.6 copy-start
  62.8 53.0 %all-to-all-start.2 = ((bf16[16,96,1024]{2,1,0:T(8,128)(2,1)}), bf16[16,96,1024]{2,1,0:T(8,128)(2,1)S(1)}, u32[]{:S(2)}, u32[]{:S(2)}) async-start(bf16[16,96,1024]{2,1,0:T(8,128)(2,1)} %bitcast.15), calls=%async_computation.2 | async-start | bytes 6291456 | tf_op jit(solution)/shard_map/all_to_all | solution.py:509
  73.5 28.5 %copy-start.3 = (bf16[256,1024]{1,0:T(8,128)(2,1)S(1)}, bf16[256,1024]{1,0:T(8,128)(2,1)}, u32[]{:S(2)}) copy-start(bf16[256,1024]{1,0:T(8,128)(2,1)} %refs_5_.4) | copy-start | bytes 1572868
  73.5 28.5 %copy-start.24 = (bf16[256,1024]{1,0:T(8,128)(2,1)S(1)}, bf16[256,1024]{1,0:T(8,128)(2,1)}, u32[]{:S(2)}) copy-start(bf16[256,1024]{1,0:T(8,128)(2,1)} %copy-done.23) | copy-start | bytes 1572868
  73.5 28.5 %copy-start.26 = (bf16[256,1024]{1,0:T(8,128)(2,1)S(1)}, bf16[256,1024]{1,0:T(8,128)(2,1)}, u32[]{:S(2)}) copy-start(bf16[256,1024]{1,0:T(8,128)(2,1)} %copy-done.25) | copy-start | bytes 1572868
  73.5 28.5 %copy-start.34 = (bf16[256,1024]{1,0:T(8,128)(2,1)S(1)}, bf16[256,1024]{1,0:T(8,128)(2,1)}, u32[]{:S(2)}) copy-start(bf16[256,1024]{1,0:T(8,128)(2,1)} %copy-done.33) | copy-start | bytes 1572868
  83.5 20.4 %copy-start.6 = (f32[4,512,256]{2,1,0:T(8,128)}, f32[4,512,256]{2,1,0:T(8,128)S(1)}, u32[]{:S(2)}) copy-start(f32[4,512,256]{2,1,0:T(8,128)S(1)} %get-tuple-element.91.refs_7_) | copy-start | bytes 6291460
  83.5 20.4 %copy-start.27 = (f32[2,512,128]{2,1,0:T(8,128)}, f32[2,512,128]{2,1,0:T(8,128)S(1)}, u32[]{:S(2)}) copy-start(f32[2,512,128]{2,1,0:T(8,128)S(1)} %get-tuple-element.93.refs_9_) | copy-start | bytes 1572868
  83.5 2.2 collective-permute-start.7
  83.9 16.7 %collective-permute-start.8 = (bf16[128,256]{1,0:T(8,128)(2,1)S(1)}, bf16[128,256]{1,0:T(8,128)(2,1)S(1)}, u32[]{:S(2)}, u32[]{:S(2)}) collective-permute-start(bf16[128,256]{1,0:T(8,128)(2,1)S(1)} %get-tuple-element.72), channel_id=1, source_target_pairs={{0,2},{1,3},{2,0},{3,1},{4,6},{5,7},{6,4},{7,5},{8,10},{9,11},{10,... | collective-permute-start | bytes 196616 | tf_op jit(solution)/shard_map/ppermute | solution.py:446
  84.2 17.8 %collective-permute-start.9 = (bf16[128,256]{1,0:T(8,128)(2,1)S(1)}, bf16[128,256]{1,0:T(8,128)(2,1)S(1)}, u32[]{:S(2)}, u32[]{:S(2)}) collective-permute-start(bf16[128,256]{1,0:T(8,128)(2,1)S(1)} %get-tuple-element.73), channel_id=1, source_target_pairs={{0,3},{1,2},{2,1},{3,0},{4,7},{5,6},{6,5},{7,4},{8,11},{9,10},{10,... | collective-permute-start | bytes 196616 | tf_op jit(solution)/shard_map/ppermute | solution.py:446
  103.6 22.2 %copy-start.8 = (bf16[128,1024]{1,0:T(8,128)(2,1)}, bf16[128,1024]{1,0:T(8,128)(2,1)S(1)}, u32[]{:S(2)}) copy-start(bf16[128,1024]{1,0:T(8,128)(2,1)S(1)} %get-tuple-element.78.refs_4_) | copy-start | bytes 786436
  103.6 11.5 %collective-permute-start.10 = (bf16[128,1024]{1,0:T(8,128)(2,1)S(1)}, bf16[128,1024]{1,0:T(8,128)(2,1)S(1)}, u32[]{:S(2)}, u32[]{:S(2)}) collective-permute-start(bf16[128,1024]{1,0:T(8,128)(2,1)S(1)} %get-tuple-element.78.refs_4_), channel_id=1, source_target_pairs={{0,16},{4,20},{8,24},{12,28},{16,0},{20,4},{24,8},{28,12},{1,17},{... | collective-permute-start | bytes 786440 | tf_op jit(solution)/shard_map/ppermute | solution.py:446
  120.0 18.6 %copy-start.36 = (f32[128,1024]{1,0:T(8,128)S(1)}, f32[128,1024]{1,0:T(8,128)}, u32[]{:S(2)}) copy-start(f32[128,1024]{1,0:T(8,128)} %copy-done.35) | copy-start | bytes 1572868
  120.0 3.8 %collective-permute-start.11 = (f32[1,256]{1,0:T(1,128)S(1)}, f32[1,256]{1,0:T(1,128)S(1)}, u32[]{:S(2)}, u32[]{:S(2)}) collective-permute-start(f32[1,256]{1,0:T(1,128)S(1)} %get-tuple-element.80.refs_2_.refs_4_), channel_id=1, source_target_pairs={{0,16},{4,20},{8,24},{12,28},{16,0},{20,4},{24,8},{28,12},{1,17},{... | collective-permute-start | bytes 3080 | tf_op jit(solution)/shard_map/ppermute | solution.py:446
  123.8 25.6 %copy-start.16 = (bf16[128,1024]{1,0:T(8,128)(2,1)S(1)}, bf16[128,1024]{1,0:T(8,128)(2,1)}, u32[]{:S(2)}) copy-start(bf16[128,1024]{1,0:T(8,128)(2,1)} %copy-done.14) | copy-start | bytes 786436
  125.8 12.8 %collective-permute-start.12 = (bf16[128,1024]{1,0:T(8,128)(2,1)S(1)}, bf16[128,1024]{1,0:T(8,128)(2,1)S(1)}, u32[]{:S(2)}, u32[]{:S(2)}) collective-permute-start(bf16[128,1024]{1,0:T(8,128)(2,1)S(1)} %get-tuple-element.85), channel_id=1, source_target_pairs={{0,16},{4,20},{8,24},{12,28},{16,0},{20,4},{24,8},{28,12},{1,17},{... | collective-permute-start | bytes 786440 | tf_op jit(solution)/shard_map/ppermute | solution.py:446
  138.9 9.5 %collective-permute-start.14 = (bf16[128,1024]{1,0:T(8,128)(2,1)S(1)}, bf16[128,1024]{1,0:T(8,128)(2,1)S(1)}, u32[]{:S(2)}, u32[]{:S(2)}) collective-permute-start(bf16[128,1024]{1,0:T(8,128)(2,1)S(1)} %shard_map.112.refs_1_), channel_id=1, source_target_pairs={{0,2},{1,3},{2,0},{3,1},{4,6},{5,7},{6,4},{7,5},{8,10},{9,11},{10,... | collective-permute-start | bytes 786440 | tf_op jit(solution)/shard_map/ppermute | solution.py:446
  142.1 12.2 %collective-permute-start.13 = (bf16[128,1024]{1,0:T(8,128)(2,1)S(1)}, bf16[128,1024]{1,0:T(8,128)(2,1)S(1)}, u32[]{:S(2)}, u32[]{:S(2)}) collective-permute-start(bf16[128,1024]{1,0:T(8,128)(2,1)S(1)} %shard_map.112.refs_1_), channel_id=1, source_target_pairs={{0,1},{1,0},{2,3},{3,2},{4,5},{5,4},{6,7},{7,6},{8,9},{9,8},{10,11... | collective-permute-start | bytes 786440 | tf_op jit(solution)/shard_map/ppermute | solution.py:446
  148.4 6.0 %copy-start.10 = (bf16[128,1024]{1,0:T(8,128)(2,1)}, bf16[128,1024]{1,0:T(8,128)(2,1)S(1)}, u32[]{:S(2)}) copy-start(bf16[128,1024]{1,0:T(8,128)(2,1)S(1)} %collective-permute-done.14.refs_3_) | copy-start | bytes 786436
  148.4 6.7 %collective-permute-start.15 = (bf16[128,1024]{1,0:T(8,128)(2,1)S(1)}, bf16[128,1024]{1,0:T(8,128)(2,1)S(1)}, u32[]{:S(2)}, u32[]{:S(2)}) collective-permute-start(bf16[128,1024]{1,0:T(8,128)(2,1)S(1)} %collective-permute-done.14.refs_3_), channel_id=1, source_target_pairs={{0,1},{1,0},{2,3},{3,2},{4,5},{5,4},{6,7},{7,6},{8,9},{9,8},{10,11... | collective-permute-start | bytes 786440 | tf_op jit(solution)/shard_map/ppermute | solution.py:446
  155.8 118.0 %all-to-all-start.3 = ((bf16[16,96,1024]{2,1,0:T(8,128)(2,1)}), bf16[16,96,1024]{2,1,0:T(8,128)(2,1)S(1)}, u32[]{:S(2)}, u32[]{:S(2)}) async-start(bf16[16,96,1024]{2,1,0:T(8,128)(2,1)} %bitcast.8), calls=%async_computation.3 | async-start | bytes 6291456 | tf_op jit(solution)/shard_map/all_to_all | solution.py:509
  174.9 6.4 %copy-start.38 = (bf16[256,512]{1,0:T(8,128)(2,1)S(1)}, bf16[256,512]{1,0:T(8,128)(2,1)}, u32[]{:S(2)}) copy-start(bf16[256,512]{1,0:T(8,128)(2,1)} %copy-done.37) | copy-start | bytes 786436
  179.7 49.7 %collective-permute-start.16 = (bf16[4,128,256]{2,1,0:T(8,128)(2,1)S(1)}, bf16[4,128,256]{2,1,0:T(8,128)(2,1)S(1)}, u32[]{:S(2)}, u32[]{:S(2)}) collective-permute-start(bf16[4,128,256]{2,1,0:T(8,128)(2,1)S(1)} %get-tuple-element.98), channel_id=1, source_target_pairs={{0,4},{4,0},{8,12},{12,8},{16,20},{20,16},{24,28},{28,24},{1,5},{5... | collective-permute-start | bytes 786440 | tf_op jit(solution)/shard_map/ppermute | solution.py:446
  181.0 50.9 %collective-permute-start.17 = (bf16[4,128,256]{2,1,0:T(8,128)(2,1)S(1)}, bf16[4,128,256]{2,1,0:T(8,128)(2,1)S(1)}, u32[]{:S(2)}, u32[]{:S(2)}) collective-permute-start(bf16[4,128,256]{2,1,0:T(8,128)(2,1)S(1)} %get-tuple-element.99), channel_id=1, source_target_pairs={{0,8},{4,12},{8,0},{12,4},{16,24},{20,28},{24,16},{28,20},{1,9},{5... | collective-permute-start | bytes 786440 | tf_op jit(solution)/shard_map/ppermute | solution.py:446
  183.0 29.0 %collective-permute-start.23 = (bf16[256,128]{1,0:T(8,128)(2,1)S(1)}, bf16[256,128]{1,0:T(8,128)(2,1)S(1)}, u32[]{:S(2)}, u32[]{:S(2)}) collective-permute-start(bf16[256,128]{1,0:T(8,128)(2,1)S(1)} %get-tuple-element.107), channel_id=1, source_target_pairs={{0,4},{4,0},{8,12},{12,8},{16,20},{20,16},{24,28},{28,24},{1,5},{5... | collective-permute-start | bytes 196616 | tf_op jit(solution)/shard_map/ppermute | solution.py:446
  183.4 29.0 %collective-permute-start.24 = (bf16[256,128]{1,0:T(8,128)(2,1)S(1)}, bf16[256,128]{1,0:T(8,128)(2,1)S(1)}, u32[]{:S(2)}, u32[]{:S(2)}) collective-permute-start(bf16[256,128]{1,0:T(8,128)(2,1)S(1)} %get-tuple-element.108), channel_id=1, source_target_pairs={{0,8},{4,12},{8,0},{12,4},{16,24},{20,28},{24,16},{28,20},{1,9},{5... | collective-permute-start | bytes 196616 | tf_op jit(solution)/shard_map/ppermute | solution.py:446
  184.6 31.7 %collective-permute-start.25 = (bf16[256,128]{1,0:T(8,128)(2,1)S(1)}, bf16[256,128]{1,0:T(8,128)(2,1)S(1)}, u32[]{:S(2)}, u32[]{:S(2)}) collective-permute-start(bf16[256,128]{1,0:T(8,128)(2,1)S(1)} %get-tuple-element.109), channel_id=1, source_target_pairs={{0,12},{4,8},{8,4},{12,0},{16,28},{20,24},{24,20},{28,16},{1,13},{... | collective-permute-start | bytes 196616 | tf_op jit(solution)/shard_map/ppermute | solution.py:446
  212.0 4.6 %collective-permute-start.26 = (bf16[256,128]{1,0:T(8,128)(2,1)S(1)}, bf16[256,128]{1,0:T(8,128)(2,1)S(1)}, u32[]{:S(2)}, u32[]{:S(2)}) collective-permute-start(bf16[256,128]{1,0:T(8,128)(2,1)S(1)} %get-tuple-element.110), channel_id=1, source_target_pairs={{0,16},{4,20},{8,24},{12,28},{16,0},{20,4},{24,8},{28,12},{1,17},{... | collective-permute-start | bytes 196616 | tf_op jit(solution)/shard_map/ppermute | solution.py:446
  212.4 10.3 %collective-permute-start.27 = (bf16[256,128]{1,0:T(8,128)(2,1)S(1)}, bf16[256,128]{1,0:T(8,128)(2,1)S(1)}, u32[]{:S(2)}, u32[]{:S(2)}) collective-permute-start(bf16[256,128]{1,0:T(8,128)(2,1)S(1)} %get-tuple-element.111), channel_id=1, source_target_pairs={{0,20},{4,16},{8,28},{12,24},{16,4},{20,0},{24,12},{28,8},{1,21},{... | collective-permute-start | bytes 196616 | tf_op jit(solution)/shard_map/ppermute | solution.py:446
  216.3 8.5 %collective-permute-start.28 = (bf16[256,128]{1,0:T(8,128)(2,1)S(1)}, bf16[256,128]{1,0:T(8,128)(2,1)S(1)}, u32[]{:S(2)}, u32[]{:S(2)}) collective-permute-start(bf16[256,128]{1,0:T(8,128)(2,1)S(1)} %get-tuple-element.112), channel_id=1, source_target_pairs={{0,24},{4,28},{8,16},{12,20},{16,8},{20,12},{24,0},{28,4},{1,25},{... | collective-permute-start | bytes 196616 | tf_op jit(solution)/shard_map/ppermute | solution.py:446
  216.6 12.2 %collective-permute-start.29 = (bf16[256,128]{1,0:T(8,128)(2,1)S(1)}, bf16[256,128]{1,0:T(8,128)(2,1)S(1)}, u32[]{:S(2)}, u32[]{:S(2)}) collective-permute-start(bf16[256,128]{1,0:T(8,128)(2,1)S(1)} %get-tuple-element.113), channel_id=1, source_target_pairs={{0,28},{4,24},{8,20},{12,16},{16,12},{20,8},{24,4},{28,0},{1,29},{... | collective-permute-start | bytes 196616 | tf_op jit(solution)/shard_map/ppermute | solution.py:446
  222.7 14.0 %collective-permute-start.18 = (bf16[4,128,256]{2,1,0:T(8,128)(2,1)S(1)}, bf16[4,128,256]{2,1,0:T(8,128)(2,1)S(1)}, u32[]{:S(2)}, u32[]{:S(2)}) collective-permute-start(bf16[4,128,256]{2,1,0:T(8,128)(2,1)S(1)} %get-tuple-element.100), channel_id=1, source_target_pairs={{0,12},{4,8},{8,4},{12,0},{16,28},{20,24},{24,20},{28,16},{1,13},{... | collective-permute-start | bytes 786440 | tf_op jit(solution)/shard_map/ppermute | solution.py:446
  224.8 14.7 %collective-permute-start.19 = (bf16[4,128,256]{2,1,0:T(8,128)(2,1)S(1)}, bf16[4,128,256]{2,1,0:T(8,128)(2,1)S(1)}, u32[]{:S(2)}, u32[]{:S(2)}) collective-permute-start(bf16[4,128,256]{2,1,0:T(8,128)(2,1)S(1)} %get-tuple-element.101), channel_id=1, source_target_pairs={{0,16},{4,20},{8,24},{12,28},{16,0},{20,4},{24,8},{28,12},{1,17},{... | collective-permute-start | bytes 786440 | tf_op jit(solution)/shard_map/ppermute | solution.py:446
  228.8 31.5 %collective-permute-start.20 = (bf16[4,128,256]{2,1,0:T(8,128)(2,1)S(1)}, bf16[4,128,256]{2,1,0:T(8,128)(2,1)S(1)}, u32[]{:S(2)}, u32[]{:S(2)}) collective-permute-start(bf16[4,128,256]{2,1,0:T(8,128)(2,1)S(1)} %get-tuple-element.102), channel_id=1, source_target_pairs={{0,20},{4,16},{8,28},{12,24},{16,4},{20,0},{24,12},{28,8},{1,21},{... | collective-permute-start | bytes 786440 | tf_op jit(solution)/shard_map/ppermute | solution.py:446
  229.5 38.6 %collective-permute-start.21 = (bf16[4,128,256]{2,1,0:T(8,128)(2,1)S(1)}, bf16[4,128,256]{2,1,0:T(8,128)(2,1)S(1)}, u32[]{:S(2)}, u32[]{:S(2)}) collective-permute-start(bf16[4,128,256]{2,1,0:T(8,128)(2,1)S(1)} %get-tuple-element.103), channel_id=1, source_target_pairs={{0,24},{4,28},{8,16},{12,20},{16,8},{20,12},{24,0},{28,4},{1,25},{... | collective-permute-start | bytes 786440 | tf_op jit(solution)/shard_map/ppermute | solution.py:446
  231.9 40.9 %collective-permute-start.22 = (bf16[4,128,256]{2,1,0:T(8,128)(2,1)S(1)}, bf16[4,128,256]{2,1,0:T(8,128)(2,1)S(1)}, u32[]{:S(2)}, u32[]{:S(2)}) collective-permute-start(bf16[4,128,256]{2,1,0:T(8,128)(2,1)S(1)} %get-tuple-element.104), channel_id=1, source_target_pairs={{0,28},{4,24},{8,20},{12,16},{16,12},{20,8},{24,4},{28,0},{1,29},{... | collective-permute-start | bytes 786440 | tf_op jit(solution)/shard_map/ppermute | solution.py:446
  (33 other events, 32.0 us)

commit v5 on v4

--- a/solution.py
+++ b/solution.py
@@ -98,66 +98,81 @@
     return meta[2 + seqs + meta[2 + slot]]
 
 
-def pack_kernel(meta, hist, *outs, dp, seq_dev, per_peer):
+def pack_kernel(meta, hist, owners_t, rows_t, out, code, *, dp, seq_dev, per_peer, mp, capacity):
     here = meta[0]
-
-    def per_dest(d, put):
+    steps, part = hist.shape[1], hist.shape[2]
+
+    def per_dest(d, carry):
         def per_slot(i, count):
             src = meta[2 + d * seq_dev + i]
             hit = lax.div(src, seq_dev) == here
 
             @pl.when(hit)
             def _():
-                put(count, hist[src - here * seq_dev])
+                start = pl.multiple_of(count * steps, steps)
+                out[d, pl.ds(start, steps), :] = hist[src - here * seq_dev]
 
             return count + hit.astype(I32)
 
         lax.fori_loop(0, seq_dev, per_slot, jnp.int32(0))
-
-    if len(outs) == dp:
-        for j in range(dp):
-
-            def put(count, value, j=j):
-                outs[j][count] = value
-
-            per_dest(jnp.bitwise_xor(here, j), put)
-    else:
-
-        def body(d, carry):
-            def put(count, value):
-                outs[0][d, count] = value
-
-            per_dest(d, put)
-            return carry
-
-        lax.fori_loop(0, dp, body, jnp.int32(0))
-
-
-def take_kernel(meta, *refs, dp, seq_dev, per_peer, steps):
-    arrived, out, held = refs[:-2], refs[-2], refs[-1]
+        return carry
+
+    lax.fori_loop(0, dp, per_dest, jnp.int32(0))
+    top, events = owners_t.shape
+    devices = dp * mp
+    o_id = iota((devices, events), 0)
+    named = jnp.zeros((devices, events), F32)
+    row = jnp.zeros((devices, events), F32)
+    positive = jnp.zeros((devices, events), F32)
+    for j in range(top):
+        same = jnp.where(owners_t[j : j + 1, :] == o_id, 1.0, 0.0)
+        named = named + same
+        row = row + same * rows_t[j : j + 1, :].astype(F32)
+        if j == 0:
+            positive = same
+    before = (iota((events, events), 0) < iota((events, events), 1)).astype(BF)
+    rank = dot_nn(named.astype(BF), before)
+    code[...] = jnp.where(named > 0.0, 2.0 * rank + 1.0 + positive, 0.0)
+    rank = jnp.where(named > 0.0, rank, -1.0)
+    lane = iota((devices, part), 1)
+    wanted = jnp.zeros((devices, part), F32)
+    for c in range(capacity):
+        one = jnp.sum(jnp.where(rank == float(c), row, 0.0), axis=1, keepdims=True)
+        wanted = jnp.where(lane == c, one, wanted)
+    high = jnp.floor(wanted * (1.0 / 256.0))
+    low = wanted - 256.0 * high
+    none = jnp.zeros((8 - mp, part), F32)
+    for d in range(dp):
+        mine = slice(d * mp, (d + 1) * mp)
+        digits = [high[mine], none, low[mine], none] if mp < 8 else [high[mine], low[mine]]
+        out[d, per_peer * steps :, :] = jnp.concatenate(digits, axis=0).astype(BF)
+
+
+def take_kernel(meta, arrived, out, *refs, dp, mp, seq_dev, per_peer, steps):
+    asked, digits = refs[:mp], refs[mp]
     here = meta[0]
-    if len(arrived) == dp:
-        for j in range(dp):
-            held[j] = arrived[j][...]
-    else:
-        held[...] = arrived[0][...]
     anchors = [lax.div(meta[2 + here * seq_dev + k], seq_dev) for k in range(seq_dev)]
     for k in range(seq_dev):
         rank = jnp.int32(0)
         for earlier in range(k):
             rank = rank + (anchors[earlier] == anchors[k]).astype(I32)
-        piece = jnp.bitwise_xor(here, anchors[k]) if len(arrived) == dp else anchors[k]
-        out[k * steps : (k + 1) * steps, :] = held[piece, rank]
+        start = pl.multiple_of(rank * steps, steps)
+        out[k * steps : (k + 1) * steps, :] = arrived[anchors[k], pl.ds(start, steps), :]
+    digits[...] = arrived[:, per_peer * steps :, :].astype(F32)
+    capacity = asked[0].shape[1]
+    for j in range(mp):
+        owner = jnp.bitwise_xor(meta[1], j)
+        for d in range(dp):
+            number = 256.0 * digits[d, pl.ds(owner, 1), :] + digits[d, pl.ds(8 + owner, 1), :]
+            asked[j][d : d + 1, :] = number[:, :capacity].astype(I32)
 
 
 def forward_kernel(meta, *refs, mp, seqs, seq_dev, steps, width, cols, quarter):
     blocks = refs[:mp]
     w_in = refs[mp]
-    normed_t, projected, slope, weights_o, dscale, norm_o, inv_o, gated_t, own = refs[
-        mp + 1 : mp + 10
-    ]
-    gated_out = refs[mp + 10 : 2 * mp + 10]
-    feat, gated = refs[2 * mp + 10 :]
+    wide, projected, turned, own = refs[mp + 1 : mp + 5]
+    gated_out = refs[mp + 5 : 2 * mp + 5]
+    feat, gated = refs[2 * mp + 5 :]
     here_dp = meta[0]
     here_mp = meta[1]
     part = width // mp
@@ -174,12 +189,12 @@
         spread = jnp.mean(centered * centered, axis=-1, keepdims=True)
         y = (centered * lax.rsqrt(spread + EPS_NORM)).astype(BF)
         feat[rows, :] = y
-        normed_t[:, rows] = y.T
+        turned[:width, rows] = y.T
     for c in range(4):
         pre = dot_nn(feat[...], w_in[c])
         sigma = jax.nn.sigmoid(pre)
         projected[c] = (pre * sigma).astype(BF)
-        slope[c] = sigma * (1.0 + pre * (1.0 - sigma))
+        wide[c] = sigma * (1.0 + pre * (1.0 - sigma))
     root = 1.0 / math.sqrt(DH)
     t_id = iota((BLOCK, BLOCK), 0)
     s_id = iota((BLOCK, BLOCK), 1)
@@ -197,29 +212,31 @@
             scores = dot_nt(projected[2, rows, lanes], projected[3, rows, lanes]) * root
             sigma = jax.nn.sigmoid(scores)
             weights = (scores * sigma * scale).astype(BF)
-            weights_o[h, rows, :] = weights
-            dscale[h, rows, :] = sigma * (1.0 + scores * (1.0 - sigma)) * (scale * root)
+            projected[4, rows, lanes] = weights
+            wide[6, rows, lanes] = sigma * (1.0 + scores * (1.0 - sigma)) * (scale * root)
             mixed = dot_nn(weights, projected[1, rows, lanes])
             centered = mixed - jnp.mean(mixed, axis=-1, keepdims=True)
             spread = jnp.mean(centered * centered, axis=-1, keepdims=True)
             inv = lax.rsqrt(spread + EPS_NORM)
             norm = centered * inv
-            norm_o[rows, lanes] = norm
-            inv_o[rows, lanes] = jnp.broadcast_to(inv, norm.shape)
+            wide[4, rows, lanes] = norm
+            wide[5, rows, lanes] = jnp.broadcast_to(inv, norm.shape)
             done = (norm * projected[0, rows, lanes].astype(F32)).astype(BF)
             gated[rows, lanes] = done
-            gated_t[lanes, rows] = done.T
+            turned[width + h * DH : width + (h + 1) * DH, rows] = done.T
     for j in range(mp):
         start = pl.multiple_of(jnp.bitwise_xor(here_mp, j) * quarter, quarter)
         gated_out[j][...] = gated[pl.ds(start, quarter), :]
 
 
-def out_kernel(own, *refs, mp):
-    gathered, weights = refs[:mp], refs[mp : 2 * mp]
-    unit, unit_bf, inv_o = refs[2 * mp :]
+def out_kernel(meta, own, w_out, *refs, mp):
+    gathered = refs[:mp]
+    unit, unit_bf, inv_o = refs[mp:]
+    cols = gathered[0].shape[1]
     total = own[...].astype(F32)
     for j in range(mp):
-        total = total + dot_nn(gathered[j][...], weights[j][...])
+        start = pl.multiple_of(jnp.bitwise_xor(meta[1], j) * cols, cols)
+        total = total + dot_nn(gathered[j][...], w_out[pl.ds(start, cols), :])
     inv = lax.rsqrt(jnp.sum(total * total, axis=-1, keepdims=True) + EPS_UNIT)
     u = total * inv
     unit[...] = u
@@ -227,46 +244,38 @@
     inv_o[...] = jnp.broadcast_to(inv, inv_o.shape)
 
 
-def ask_kernel(owners, rows, wanted, code, *, devices, capacity):
-    events, top = owners.shape
-    eye = (iota((events, events), 0) == iota((events, events), 1)).astype(F32)
-
-    def turned(x):
-        return lax.dot_general(
-            x.astype(F32),
-            eye,
-            (((0,), (0,)), ((), ())),
-            precision=lax.Precision.HIGHEST,
-            preferred_element_type=F32,
-        )
-
-    owners_t = turned(owners[...])
-    rows_t = turned(rows[...])
-    o_id = iota((devices, events), 0).astype(F32)
-    named = jnp.zeros((devices, events), F32)
-    row = jnp.zeros((devices, events), F32)
-    positive = jnp.zeros((devices, events), F32)
-    for j in range(top):
-        same = jnp.where(owners_t[j : j + 1, :] == o_id, 1.0, 0.0)
-        named = named + same
-        row = row + same * rows_t[j : j + 1, :]
-        if j == 0:
-            positive = same
-    before = (iota((events, events), 0) < iota((events, events), 1)).astype(BF)
-    rank = dot_nn(named.astype(BF), before)
-    code[...] = jnp.where(named > 0.0, 2.0 * rank + 1.0 + positive, 0.0)
-    rank = jnp.where(named > 0.0, rank, -1.0)
-    lane = iota((devices, capacity), 1)
-    result = jnp.zeros((devices, capacity), F32)
-    for c in range(capacity):
-        one = jnp.sum(jnp.where(rank == float(c), row, 0.0), axis=1, keepdims=True)
-        result = jnp.where(lane == c, one, result)
-    wanted[...] = result.astype(I32)
-
-
-def look_kernel(incoming, catalogue, looked, *, chunk):
+def look_kernel(meta, *refs, mp, dp, capacity, chunk, share):
+    asked, catalogue, looked, incoming, returning = refs[:mp], *refs[mp:]
     stock, _ = catalogue.shape
-    slots = incoming.shape[1]
+    groups = dp * mp
+    slots = groups * capacity
+    half = dp // 2
+    table = jnp.concatenate([a[...] for a in asked], axis=0).astype(F32)
+    slot = iota((1, slots), 1).astype(F32)
+    group = jnp.floor((slot + 0.5) * (1.0 / capacity))
+    local = slot - group * capacity
+    column = (iota((capacity, slots), 0).astype(F32) == local).astype(F32)
+    spread = lax.dot_general(
+        table,
+        column,
+        (((1,), (0,)), ((), ())),
+        precision=lax.Precision.HIGHEST,
+        preferred_element_type=F32,
+    )
+    line = iota((groups, 1), 0)
+    offset = lax.div(line, dp)
+    index = line - offset * dp
+    side = (index >= half) != (meta[0] >= half)
+    near = jnp.where(index >= half, index - half, index)
+    first = (near * mp + jnp.bitwise_xor(offset, meta[1])) * 2 + side.astype(I32)
+    here = jnp.where(meta[0] >= half, meta[0] - half, meta[0])
+    second = (offset * half + jnp.bitwise_xor(near, here)) * 2 + side.astype(I32)
+    rows = [
+        jnp.sum(jnp.where(group == g.astype(F32), spread, 0.0), axis=0, keepdims=True).astype(I32)
+        for g in (first, second)
+    ]
+    incoming[...] = rows[0]
+    returning[...] = rows[1] if share else rows[0]
     for s in range(0, slots, chunk):
         hot = jnp.where(iota((stock, chunk), 0) == incoming[:, s : s + chunk], 1.0, 0.0).astype(BF)
         looked[s : s + chunk, :] = dot_tn(hot, catalogue[...]).astype(BF)
@@ -326,7 +335,7 @@
 
 
 def slope_kernel(
-    meta, items, expo, inv, total, total_far, slope, slope_far,
+    meta, items, code, code_far, expo, inv, total, total_far, slope, slope_far, ledger,
     *, dp, seqs, seq_dev, steps, chunk,
 ):
     share = shares(meta, expo, total, total_far, dp, seqs, seq_dev, steps)
@@ -335,6 +344,14 @@
     for s in range(0, items.shape[0], chunk):
         rows = slice(s, s + chunk)
         both = both + dot_tn((share(rows) * inv[rows, 0:1]).astype(BF), items[rows, :])
+    near = ledger.shape[0] // 2
+    each = items.shape[0] // near
+    for o in range(near):
+        part = share(slice(o * each, (o + 1) * each))
+        ledger[o : o + 1, :] = jnp.sum(part, axis=0, keepdims=True)
+    half = pl.multiple_of(lax.div(meta[0], dp // 2) * near, near)
+    for side, c in enumerate((code, code_far)):
+        ledger[near:, side * events : (side + 1) * events] = c[pl.ds(half, near), :]
     slope[...] = both[:events]
     slope_far[...] = both[events:].astype(BF)
 
@@ -353,6 +370,32 @@
         sending[rows, :] = (unit_rows * weight).astype(BF)
 
 
+def mail_kernel(meta, *refs, half, mp, capacity):
+    units, ledgers, outs, hots = refs[: 2 * half], refs[2 * half : 3 * half], refs[3 * half : -1], refs[-1]
+    events, width = units[0].shape
+    near = ledgers[0].shape[0] // 2
+    here = jnp.where(meta[0] >= half, meta[0] - half, meta[0])
+    slot = iota((2 * capacity, 2 * events), 0)
+    event = iota((2 * capacity, 2 * events), 1)
+    far = slot >= capacity
+    local = jnp.where(far, slot - capacity, slot).astype(F32)
+    same = far == (event >= events)
+    for j in range(half):
+        weights = []
+        for k in range(mp):
+            o = here * mp + jnp.bitwise_xor(meta[1], k)
+            code = ledgers[j][pl.ds(near + o, 1), :]
+            mine = same & (jnp.floor((code - 1.0) * 0.5) == local)
+            hots[k * 2 * capacity : (k + 1) * 2 * capacity, :] = mine.astype(BF)
+            weight = jnp.where(mine, ledgers[j][pl.ds(o, 1), :], 0.0)
+            weights.append(jnp.sum(weight, axis=1, keepdims=True))
+        rows = dot_nn(hots[:, :events], units[2 * j][...])
+        rows = rows + dot_nn(hots[:, events:], units[2 * j + 1][...])
+        for k in range(mp):
+            part = rows[k * 2 * capacity : (k + 1) * 2 * capacity] * weights[k]
+            outs[k][j * 2 * capacity : (j + 1) * 2 * capacity, :] = part.astype(BF)
+
+
 def out_cot_kernel(unit, inv_out, slope, slope_far, out_cot):
     u = unit[...]
     s = slope[...] + slope_far[...].astype(F32)
@@ -360,54 +403,37 @@
     out_cot[...] = ((s - u * along) * inv_out[:, 0:1]).astype(BF)
 
 
-def spread_kernel(incoming, landed, catalogue, out, *, chunk):
+def spread_kernel(incoming, catalogue, *refs, chunk):
+    landed, out = refs[:-1], refs[-1]
     stock, _ = catalogue.shape
     slots = incoming.shape[1]
     for r in range(0, stock, chunk):
         hot = jnp.where(r + iota((chunk, slots), 0) == incoming[...], 1.0, 0.0).astype(BF)
-        v = dot_nn(hot, landed[...])
+        v, at = 0.0, 0
+        for part in landed:
+            v = v + dot_nn(hot[:, at : at + part.shape[0]], part[...])
+            at += part.shape[0]
         c = catalogue[r : r + chunk, :].astype(F32)
         inv = lax.rsqrt(jnp.sum(c * c, axis=-1, keepdims=True) + EPS_UNIT)
         c = c * inv
         out[r : r + chunk, :] = (v - c * jnp.sum(c * v, axis=-1, keepdims=True)) * inv
 
 
-def put_pieces(outs, index, here, dp, whole, share):
-    if len(outs) == dp:
-        for j in range(dp):
-            start = pl.multiple_of(jnp.bitwise_xor(here, j) * share, share)
-            outs[j][index] = whole[pl.ds(start, share), :]
-    else:
-        for d in range(dp):
-            outs[0][(d,) + index] = whole[d * share : (d + 1) * share, :]
-
-
 def w_out_kernel(meta, *refs, mp, dp):
-    blocks, gated_t, outs, whole = refs[:mp], refs[mp], refs[mp + 1 : -1], refs[-1]
+    blocks, turned, out, whole = refs[:mp], *refs[mp:]
     quarter, width = blocks[0].shape
     for j in range(mp):
         start = pl.multiple_of(jnp.bitwise_xor(meta[1], j) * quarter, quarter)
         whole[pl.ds(start, quarter), :] = blocks[j][...]
-    part = dot_nn(gated_t[...], whole[...]).astype(BF)
+    part = dot_nn(turned[width:, :], whole[...]).astype(BF)
     lanes = width // dp
-    if len(outs) == dp:
-        spare = jnp.stack([part[:, d * lanes : (d + 1) * lanes] for d in range(dp)])
-        for d in range(dp):
-            for j in range(dp):
-
-                @pl.when(jnp.bitwise_xor(meta[0], j) == d)
-                def _(d=d, j=j):
-                    outs[j][...] = spare[d]
-    else:
-        for d in range(dp):
-            outs[0][d] = part[:, d * lanes : (d + 1) * lanes]
+    for d in range(dp):
+        out[d] = part[:, d * lanes : (d + 1) * lanes]
 
 
 def backward_kernel(meta, *refs, mp, dp):
     blocks = refs[:mp]
-    w_out, projected, slope, weights, dscale, norm, inv, normed_t = refs[mp : mp + 8]
-    outs = refs[mp + 8 : -3]
-    whole, cot, parts = refs[-3:]
+    w_out, wide, projected, turned, out, whole, cot = refs[mp:]
     quarter, width = blocks[0].shape
     for j in range(mp):
         start = pl.multiple_of(jnp.bitwise_xor(meta[1], j) * quarter, quarter)
@@ -420,25 +446,26 @@
         for h in range(cols // DH):
             lanes = slice(h * DH, (h + 1) * DH)
             d_gated = gated_cot[rows, lanes]
-            n = norm[rows, lanes]
+            n = wide[4, rows, lanes]
             d_norm = d_gated * projected[0, rows, lanes].astype(F32)
-            d_mixed = inv[rows, lanes] * (
+            d_mixed = wide[5, rows, lanes] * (
                 d_norm
                 - jnp.mean(d_norm, axis=-1, keepdims=True)
                 - n * jnp.mean(d_norm * n, axis=-1, keepdims=True)
             )
             d_mixed = d_mixed.astype(BF)
             d_weights = dot_nt(d_mixed, projected[1, rows, lanes]).astype(BF).astype(F32)
-            d_values = dot_tn(weights[h, rows, :], d_mixed)
-            d_scores = (d_weights * dscale[h, rows, :]).astype(BF)
+            d_values = dot_tn(projected[4, rows, lanes], d_mixed)
+            d_scores = (d_weights * wide[6, rows, lanes]).astype(BF)
             d_queries = dot_nn(d_scores, projected[3, rows, lanes])
             d_keys = dot_tn(d_scores, projected[2, rows, lanes])
             for c, d in enumerate((d_gated * n, d_values, d_queries, d_keys)):
-                cot[c, rows, lanes] = (d.astype(BF).astype(F32) * slope[c, rows, lanes]).astype(BF)
+                cot[c, rows, lanes] = (d.astype(BF).astype(F32) * wide[c, rows, lanes]).astype(BF)
     share = width // dp
     for c in range(4):
-        parts[...] = dot_nn(normed_t[...], cot[c]).astype(BF)
-        put_pieces(outs, (c,), meta[0], dp, parts, share)
+        part = dot_nn(turned[:width, :], cot[c]).astype(BF)
+        for d in range(dp):
+            out[d, c] = part[d * share : (d + 1) * share, :]
 
 
 def swapped(x, axis, bit):
@@ -457,24 +484,13 @@
     return [blocks[j] for j in range(size)]
 
 
-def pieces(n, shape, dtype):
-    S = jax.ShapeDtypeStruct
-    return [S(shape, dtype)] * n if n <= 8 else [S((n,) + shape, dtype)]
-
-
 def exchange(parts, axis):
-    if len(parts) > 1:
-        return [p if j == 0 else swapped(p, axis, j) for j, p in enumerate(parts)]
-    return [lax.all_to_all(parts[0], axis, split_axis=0, concat_axis=0, tiled=True)]
-
-
-def summed(parts):
-    if len(parts) == 1:
-        return jnp.sum(parts[0].astype(F32), axis=0)
-    total = parts[0].astype(F32)
-    for p in parts[1:]:
-        total = total + p.astype(F32)
-    return total
+    return [p if j == 0 else swapped(p, axis, j) for j, p in enumerate(parts)]
+
+
+def summed(x):
+    got = lax.all_to_all(x, "dp", split_axis=0, concat_axis=0, tiled=True)
+    return jnp.sum(got.astype(F32), axis=0)
 
 
 def per_device(history, lengths, source, owners, item_rows, catalogue, w_in, w_out):
@@ -494,7 +510,7 @@
     stock = catalogue.shape[0]
     per_peer = (seq_dev + dp - 1) // dp
     chunk = math.gcd(slots, 512)
-    heads = cols // DH
+    short = dp <= 8
     S = jax.ShapeDtypeStruct
     here_dp = lax.axis_index("dp")
     place = jnp.stack([here_dp, lax.axis_index("mp")]).astype(I32)
@@ -515,46 +531,41 @@
             axis_index_groups=halves,
         ).reshape(slots, width)
 
-    packed = call(
-        functools.partial(pack_kernel, dp=dp, seq_dev=seq_dev, per_peer=per_peer),
-        [S((dp, per_peer, steps, part), BF)],
+    w_out_all = lax.all_gather(w_out, "mp", axis=0, tiled=True)
+    packed, code = call(
+        functools.partial(
+            pack_kernel, dp=dp, seq_dev=seq_dev, per_peer=per_peer, mp=mp, capacity=capacity
+        ),
+        [S((dp, per_peer * steps + 16, part), BF), S((devices, events), F32)],
+        [SM, VM, VM, VM],
+        4,
+    )(meta, history, owners.T, item_rows.T)
+    arrived = lax.all_to_all(packed, "dp", split_axis=0, concat_axis=0, tiled=True)
+    rows, *asked = call(
+        functools.partial(
+            take_kernel, dp=dp, mp=mp, seq_dev=seq_dev, per_peer=per_peer, steps=steps
+        ),
+        [S((rows_all, part), BF)] + [S((dp, capacity), I32)] * mp,
         [SM, VM],
-        3,
-    )(meta, history)
-    w_out_blocks = gather_blocks(w_out, "mp")
-    arrived = exchange(packed, "dp")
-    arrived, w_out_blocks, owners = lax.optimization_barrier((arrived, w_out_blocks, owners))
-    rows = call(
-        functools.partial(take_kernel, dp=dp, seq_dev=seq_dev, per_peer=per_peer, steps=steps),
-        S((rows_all, part), BF),
-        [SM] + [VM] * len(arrived),
         1,
-        scratch=[pltpu.VMEM((dp, per_peer, steps, part), BF)],
-    )(meta, *arrived)
+        scratch=[pltpu.VMEM((dp, 16, part), F32)],
+    )(meta, arrived)
     features = gather_blocks(rows, "mp")
-
-    wanted, code = call(
-        functools.partial(ask_kernel, devices=devices, capacity=capacity),
-        [S((devices, capacity), I32), S((devices, events), F32)],
-        [VM, VM],
-        2,
-    )(owners, item_rows)
-    asked = lax.all_to_all(wanted, ("dp", "mp"), split_axis=0, concat_axis=0, tiled=True)
-    asked = asked.reshape(2, near, capacity)
-    incoming = jnp.where(here_dp < dp // 2, asked, asked[::-1])
-    incoming = incoming.transpose(1, 0, 2).reshape(1, slots)
-    looked = call(
-        functools.partial(look_kernel, chunk=chunk),
-        S((slots, width), BF),
-        [VM, HB],
-        3,
-        out_specs=[HB],
-    )(incoming, catalogue)
+    asked = exchange(asked, "mp")
     code_far = partner(code)
+    looked, incoming, returning = call(
+        functools.partial(
+            look_kernel, mp=mp, dp=dp, capacity=capacity, chunk=chunk, share=short
+        ),
+        [S((slots, width), BF), S((1, slots), I32), S((1, slots), I32)],
+        [SM] + [VM] * mp + [HB],
+        4,
+        out_specs=[HB, VM, VM],
+    )(meta, *asked, catalogue)
     looked, features, code_far = lax.optimization_barrier((looked, features, code_far))
     items = in_half(looked)
 
-    (normed_t, projected, slope, weights, dscale, norm, inv, gated_t, own, *gated) = call(
+    wide, projected, turned, own, *gated = call(
         functools.partial(
             forward_kernel,
             mp=mp,
@@ -566,30 +577,25 @@
             quarter=quarter,
         ),
         [
-            S((width, rows_all), BF),
-            S((4, rows_all, cols), BF),
-            S((4, rows_all, cols), F32),
-            S((heads, rows_all, BLOCK), BF),
-            S((heads, rows_all, BLOCK), F32),
-            S((rows_all, cols), F32),
-            S((rows_all, cols), F32),
-            S((cols, rows_all), BF),
+            S((7, rows_all, cols), F32),
+            S((5, rows_all, cols), BF),
+            S((width + cols, rows_all), BF),
             S((quarter, width), BF),
         ]
         + [S((quarter, cols), BF)] * mp,
         [SM] + [HB] * (mp + 1),
         6,
         scratch=[pltpu.VMEM((rows_all, width), BF), pltpu.VMEM((rows_all, cols), BF)],
-        out_specs=[HB] * 9 + [VM] * mp,
+        out_specs=[HB] * 4 + [VM] * mp,
         limit=24,
     )(meta, *features, w_in)
     gathered = exchange(gated, "mp")
     unit, unit_bf, inv_out = call(
         functools.partial(out_kernel, mp=mp),
         [S((quarter, width), F32), S((quarter, width), BF), S((quarter, BLOCK), F32)],
-        [HB] + [VM] * mp + [HB] * mp,
+        [SM, HB, HB] + [VM] * mp,
         2,
-    )(own, *gathered, *w_out_blocks)
+    )(meta, own, w_out_all, *gathered)
 
     unit_far = partner(unit_bf)
     expo, inv_item, total = call(
@@ -602,56 +608,73 @@
     )(meta, items, code, code_far, unit_bf, unit_far)
     total_far = partner(total)
     sizes = dict(dp=dp, seqs=seqs, seq_dev=seq_dev, steps=steps, chunk=chunk)
-    item_slope, slope_far = call(
+    item_slope, slope_far, ledger = call(
         functools.partial(slope_kernel, **sizes),
-        [S((events, width), F32), S((events, width), BF)],
-        [SM, HB] + [VM] * 4,
-        2,
-    )(meta, items, expo, inv_item, total, total_far)
+        [S((events, width), F32), S((events, width), BF), S((2 * near, 2 * events), F32)],
+        [SM, HB] + [VM] * 6,
+        3,
+    )(meta, items, code, code_far, expo, inv_item, total, total_far)
     slope_back = partner(slope_far)
-    sending = call(
-        functools.partial(send_kernel, **sizes),
-        S((slots, width), BF),
-        [SM] + [VM] * 5,
-        3,
-        out_specs=[HB],
-    )(meta, expo, total, total_far, unit_bf, unit_far)
     out_cot = call(out_cot_kernel, S((events, width), BF), [VM] * 4, 1)(
         unit, inv_out, item_slope, slope_back
     )
-
     cots = gather_blocks(out_cot, "mp")
-    sending, cots = lax.optimization_barrier((sending, cots))
-    landed = in_half(sending)
+    if short:
+        _, mail_unit, mail_far, mail_ledger = lax.optimization_barrier(
+            (out_cot, unit_bf, unit_far, ledger)
+        )
+        ledgers = [ledger] + [swapped(mail_ledger, "dp", j) for j in range(1, dp // 2)]
+        units = [unit_bf, unit_far]
+        for j in range(1, dp // 2):
+            units += [swapped(mail_unit, "dp", j), swapped(mail_far, "dp", j)]
+
     w_out_part = call(
         functools.partial(w_out_kernel, mp=mp, dp=dp),
-        pieces(dp, (cols, width // dp), BF),
+        S((dp, cols, width // dp), BF),
         [SM] + [HB] * (mp + 1),
         2,
         scratch=[pltpu.VMEM((rows_all, width), BF)],
-    )(meta, *cots, gated_t)
+    )(meta, *cots, turned)
     w_in_part = call(
         functools.partial(backward_kernel, mp=mp, dp=dp),
-        pieces(dp, (4, width // dp, cols), BF),
-        [SM] + [HB] * (mp + 8),
+        S((dp, 4, width // dp, cols), BF),
+        [SM] + [HB] * (mp + 4),
         6,
         scratch=[
             pltpu.VMEM((rows_all, width), BF),
             pltpu.VMEM((4, rows_all, cols), BF),
-            pltpu.VMEM((width, cols), BF),
         ],
         limit=24,
-    )(meta, *cots, w_out, projected, slope, weights, dscale, norm, inv, normed_t)
-    w_out_grad = summed(exchange(w_out_part, "dp"))
-    w_in_grad = summed(exchange(w_in_part, "dp"))
+    )(meta, *cots, w_out, wide, projected, turned)
+    w_out_grad = summed(w_out_part)
+    w_in_grad = summed(w_in_part)
+
+    if short:
+        _, units, ledgers = lax.optimization_barrier((w_in_part, units, ledgers))
+        mail = call(
+            functools.partial(mail_kernel, half=dp // 2, mp=mp, capacity=capacity),
+            [S((dp * capacity, width), BF)] * mp,
+            [SM] + [HB] * len(units) + [VM] * len(ledgers),
+            4,
+            scratch=[pltpu.VMEM((mp * 2 * capacity, 2 * events), BF)],
+        )(meta, *units, *ledgers)
+        landed = exchange(mail, "mp")
+    else:
+        sending = call(
+            functools.partial(send_kernel, **sizes),
+            S((slots, width), BF),
+            [SM] + [VM] * 5,
+            3,
+        )(meta, expo, total, total_far, unit_bf, unit_far)
+        landed = [in_half(sending)]
     cat_grad = call(
         functools.partial(spread_kernel, chunk=math.gcd(stock, 128)),
         S((stock, width), F32),
-        [VM, HB, HB],
+        [VM, HB] + [HB] * len(landed),
         4,
         out_specs=[HB],
         limit=24,
-    )(incoming, landed, catalogue)
+    )(returning, catalogue, *landed)
     return (w_in_grad, w_out_grad, cat_grad)
 
 

time: 282 us -> 313 us (1.11)
  waiting for transfers between devices: 129 us -> 155 us
  between operations: 1.12 us -> 14.3 us
  starting transfers between devices: 65.9 us -> 55.2 us
    ppermute x30 -> x28, waiting for transfers between devices: 127 us -> 150 us  [swapped(): return lax.ppermute(x, axis, [(a, a ^ bit) for a in range(size)])]
    ppermute x30 -> x28, starting transfers between devices: 46.7 us -> 36.4 us  [swapped(): return lax.ppermute(x, axis, [(a, a ^ bit) for a in range(size)])]
    all_to_all x2 -> x1, starting transfers between devices: 13.3 us -> 4.96 us  [in_half(): lax.all_to_all(x.reshape(near, 2 * capacity, width), ('dp', 'mp'), split_...]
    all_to_all x1 -> x2, starting transfers between devices: 5.9 us -> 13.6 us  [summed(): got = lax.all_to_all(x, 'dp', split_axis=0, concat_axis=0, tiled=True)]
    all_gather x0 -> x1, waiting for transfers between devices: none -> 3.23 us  [per_device(): w_out_all = lax.all_gather(w_out, 'mp', axis=0, tiled=True)]
    pallas_call x13 -> x12, Pallas kernels: 32.9 us -> 34.9 us  [run(): pl.pallas_call(kernel, out_shape=outs, in_specs=list(in_specs), out_specs...]
    unnamed x97 -> x88, local copies, waits for them, and re-layouts: 34.4 us -> 33.5 us
  transfers between devices with their start and end apart: 33 -> 32, of which waited for: 16 -> 21; matrix products, arithmetic and copies ran while one was open for 2% -> 1% of each run, Pallas kernels for 8% -> 7%
where the time goes in v5:
time: 313 us; the launch traced here: 310 us
  waiting for transfers between devices  155 us (50%)
  starting transfers between devices  55.2 us (18%)
  Pallas kernels  34.9 us (11%)
  local copies, waits for them, and re-layouts  33.5 us (11%)
  between operations  14.3 us (5%)
  blocking collectives  13.7 us (4%)
  other arithmetic  3.61 us (1%)
    ppermute x28, waiting for transfers between devices, swapped(): return lax.ppermute(x, axis, [(a, a ^ bit) for a in range(size)])  150 us
    ppermute x28, starting transfers between devices, swapped(): return lax.ppermute(x, axis, [(a, a ^ bit) for a in range(size)])  36.4 us
    pallas_call x12, Pallas kernels, run(): pl.pallas_call(kernel, out_shape=outs, in_specs=list(in_specs), out_specs...  34.9 us
    unnamed x88, local copies, waits for them, and re-layouts  33.5 us
    all_to_all x1, blocking collectives, per_device(): lax.all_to_all(packed, 'dp', split_axis=0, concat_axis=0, tiled=True)  13.7 us
    all_to_all x2, starting transfers between devices, summed(): got = lax.all_to_all(x, 'dp', split_axis=0, concat_axis=0, tiled=True)  13.6 us
  transfers between devices with their start and end apart: 32, of which 21 were waited for; matrix products, arithmetic and copies ran while one was open for 1% of the time, Pallas kernels for 7%

profile of v5, /device:TPU:13, one launch (start us, length us, event | category | flops | bytes accessed | tf_op | source)
XLA Modules:
  0.0 309.8 jit_solution(5506835323035579433)
XLA Ops:
  10.2 3.4 %shard_map.103 = (bf16[8,80,256]{2,1,0:T(8,128)(2,1)S(1)}, f32[32,128]{1,0:T(8,128)S(1)}) custom-call(s32[258]{0:T(512)S(1)} %pad_add_fusion.refs_0_, bf16[16,32,256]{2,1,0:T(8,128)(2,1)S(1)} %copy-done.27, s32[8,128]{1,0:T(8,128)S(1)} %bitcast.9, s32[8,128]{1,0:T(8,128)S(1)} %bitcast.10), custom_call_target="tpu_custom_call" | custom-call | bytes 13200000 | tf_op jit(solution)/shard_map/pallas_call | solution.py:63
  13.7 13.7 %all_to_all.20.refs_1_ = bf16[8,80,256]{2,1,0:T(8,128)(2,1)S(1)} all-to-all(bf16[8,80,256]{2,1,0:T(8,128)(2,1)S(1)} %get-tuple-element.54), channel_id=1, replica_groups=mesh['dp'=8,'mp'=4] {'dp'}, dimensions={0} | all-to-all | bytes 655360 | tf_op jit(solution)/shard_map/all_to_all | solution.py:543
  28.4 3.0 collective-permute-start.3
  31.4 2.0 collective-permute-done.4.refs_3_
  33.4 3.8 %collective-permute-start.5 = (bf16[512,256]{1,0:T(8,128)(2,1)S(1)}, bf16[512,256]{1,0:T(8,128)(2,1)S(1)}, u32[]{:S(2)}, u32[]{:S(2)}) collective-permute-start(bf16[512,256]{1,0:T(8,128)(2,1)S(1)} %collective-permute-done.4.refs_3_), channel_id=1, source_target_pairs={{0,1},{1,0},{2,3},{3,2},{4,5},{5,4},{6,7},{7,6},{8,9},{9,8},{10,11... | collective-permute-start | bytes 786440 | tf_op jit(solution)/shard_map/ppermute | solution.py:473
  37.3 1.9 collective-permute-start.6
  42.0 1.5 collective-permute-done.2.refs_4_
  44.6 3.6 %shard_map.105 = (bf16[1536,1024]{1,0:T(8,128)(2,1)S(1)}, s32[1,1536]{1,0:T(1,128)}, s32[1,1536]{1,0:T(1,128)S(1)}) custom-call(s32[258]{0:T(512)S(1)} %pad_add_fusion.refs_0_, s32[8,48]{1,0:T(8,128)S(1)} %get-tuple-element.55.refs_1_, s32[8,48]{1,0:T(8,128)S(1)} %collective-permute-done.refs_2_, s32[8,48]{1,0:T(8,128)S(1)} %collective-permute-done.1.refs_3_, ...), custom_call_target="tpu_custom_call" | custom-call | bytes 13200000 | tf_op jit(solution)/shard_map/pallas_call | solution.py:63
  48.3 1.6 copy-done.6
  51.3 5.0 %all-to-all-start.1 = ((bf16[16,96,1024]{2,1,0:T(8,128)(2,1)}), bf16[16,96,1024]{2,1,0:T(8,128)(2,1)S(1)}, u32[]{:S(2)}, u32[]{:S(2)}) async-start(bf16[16,96,1024]{2,1,0:T(8,128)(2,1)} %bitcast.8), calls=%async_computation.1 | async-start | bytes 6291456 | tf_op jit(solution)/shard_map/all_to_all | solution.py:525
  57.0 1.6 copy-done.7
  61.5 5.0 %shard_map.106 = (f32[7,512,256]{2,1,0:T(8,128)S(1)}, bf16[5,512,256]{2,1,0:T(8,128)(2,1)S(1)}, bf16[1280,512]{1,0:T(8,128)(2,1)S(1)}, bf16[128,1024]{1,0:T(8,12...) custom-call(s32[258]{0:T(512)S(1)} %pad_add_fusion.refs_0_, ...), custom_call_target="tpu_custom_call" | custom-call | bytes 19800000 | tf_op jit(solution)/shard_map/pallas_call | solution.py:63
  67.5 1.8 copy-done.4
  72.3 1.5 collective-permute-start.9
  74.5 26.3 %collective-permute-done.8.refs_5_ = bf16[128,256]{1,0:T(8,128)(2,1)S(1)} collective-permute-done((bf16[128,256]{1,0:T(8,128)(2,1)S(1)}, bf16[128,256]{1,0:T(8,128)(2,1)S(1)}, u32[]{:S(2)}, u32[]{:S(2)}) %collective-permute-start.8) | collective-permute-done | bytes 65568 | tf_op jit(solution)/shard_map/ppermute | solution.py:473
  101.4 2.2 collective-permute-done.9.refs_6_
  104.2 3.2 %all-gather.2.cloned.1.call-done.refs_2_ = bf16[1024,1024]{1,0:T(8,128)(2,1)} async-done(((bf16[256,1024]{1,0:T(8,128)(2,1)}), bf16[1024,1024]{1,0:T(8,128)(2,1)}) %all-gather.2.cloned.1.call-update) | async-done | bytes 2097168 | tf_op jit(solution)/shard_map/all_gather | solution.py:534
  107.4 1.6 copy-done.8
  113.3 1.3 shard_map.107
  116.2 11.4 %collective-permute-done.10.refs_5_.refs_2_ = bf16[128,1024]{1,0:T(8,128)(2,1)S(1)} collective-permute-done((bf16[128,1024]{1,0:T(8,128)(2,1)S(1)}, bf16[128,1024]{1,0:T(8,128)(2,1)S(1)}, u32[]{:S(2)}, u32[]{:S(2)}) %collective-permute-start.10) | collective-permute-done | bytes 262176 | tf_op jit(solution)/shard_map/ppermute | solution.py:473
  129.3 3.3 %shard_map.108 = (f32[1536,256]{1,0:T(8,128)S(1)}, f32[1536,128]{1,0:T(8,128)S(1)}, f32[1,256]{1,0:T(1,128)S(1)}) custom-call(s32[258]{0:T(512)S(1)} %pad_add_fusion.refs_0_, bf16[1536,1024]{1,0:T(8,128)(2,1)S(1)} %bitcast.6, f32[32,128]{1,0:T(8,128)S(1)} %get-tuple-element.61.refs_2_, f32[32,128]{1,0:T(8,128)S(1)} %collective-permute-done.6.refs_3_, ...), custom_call_target="tpu_custom_call" | custom-call | bytes 13200000 | tf_op jit(solution)/shard_map/pallas_call | solution.py:63
  132.6 3.2 %collective-permute-start.11 = (f32[1,256]{1,0:T(1,128)S(1)}, f32[1,256]{1,0:T(1,128)S(1)}, u32[]{:S(2)}, u32[]{:S(2)}) collective-permute-start(f32[1,256]{1,0:T(1,128)S(1)} %get-tuple-element.78.refs_6_), channel_id=1, source_target_pairs={{0,16},{4,20},{8,24},{12,28},{16,0},{20,4},{24,8},{28,12},{1,17},{... | collective-permute-start | bytes 3080 | tf_op jit(solution)/shard_map/ppermute | solution.py:473
  136.7 2.2 shard_map.109
  139.0 2.4 collective-permute-start.12
  141.4 10.3 %collective-permute-done.12.refs_3_ = bf16[128,1024]{1,0:T(8,128)(2,1)S(1)} collective-permute-done((bf16[128,1024]{1,0:T(8,128)(2,1)S(1)}, bf16[128,1024]{1,0:T(8,128)(2,1)S(1)}, u32[]{:S(2)}, u32[]{:S(2)}) %collective-permute-start.12) | collective-permute-done | bytes 262176 | tf_op jit(solution)/shard_map/ppermute | solution.py:473
  152.0 1.5 collective-permute-start.14
  154.2 5.2 %collective-permute-done.14.refs_3_ = bf16[128,1024]{1,0:T(8,128)(2,1)S(1)} collective-permute-done((bf16[128,1024]{1,0:T(8,128)(2,1)S(1)}, bf16[128,1024]{1,0:T(8,128)(2,1)S(1)}, u32[]{:S(2)}, u32[]{:S(2)}) %collective-permute-start.14) | collective-permute-done | bytes 262176 | tf_op jit(solution)/shard_map/ppermute | solution.py:473
  159.4 1.3 collective-permute-start.15
  161.9 2.1 shard_map.112
  166.1 7.3 %all-to-all-start.3 = ((bf16[8,256,128]{2,1,0:T(8,128)(2,1)}), bf16[8,256,128]{2,1,0:T(8,128)(2,1)}, u32[]{:S(2)}, u32[]{:S(2)}) async-start(bf16[8,256,128]{2,1,0:T(8,128)(2,1)} %shard_map.112), calls=%async_computation.3 | async-start | bytes 1048576 | tf_op jit(solution)/shard_map/all_to_all | solution.py:492
  173.4 2.0 copy-done.5
  178.3 6.0 %shard_map.111 = bf16[8,4,128,256]{3,2,1,0:T(8,128)(2,1)} custom-call(s32[258]{0:T(512)S(1)} %pad_add_fusion.refs_0_, bf16[128,1024]{1,0:T(8,128)(2,1)S(1)} %shard_map.110.refs_1_, bf16[128,1024]{1,0:T(8,128)(2,1)S(1)} %copy-done.20, bf16[128,1024]{1,0:T(8,128)(2,1)S(1)} %copy-done.18, bf16[128,1024]{1,0:T(8,128)(2,1)S(1)} %copy-done.22, ...), custom_call_target="tpu_custom_call" | custom-call | bytes 19800000 | tf_op jit(solution)/shard_map/pallas_call | solution.py:63
  185.4 6.3 %all-to-all-start.2 = ((bf16[8,4,128,256]{3,2,1,0:T(8,128)(2,1)}), bf16[8,4,128,256]{3,2,1,0:T(8,128)(2,1)S(1)}, u32[]{:S(2)}, u32[]{:S(2)}) async-start(bf16[8,4,128,256]{3,2,1,0:T(8,128)(2,1)} %shard_map.111), calls=%async_computation.2 | async-start | bytes 4194304 | tf_op jit(solution)/shard_map/all_to_all | solution.py:492
  191.7 1.2 collective-permute-start.20
  194.2 1.4 collective-permute-start.22
  196.8 39.4 %collective-permute-done.24.refs_12_ = f32[32,256]{1,0:T(8,128)S(1)} collective-permute-done((f32[32,256]{1,0:T(8,128)S(1)}, f32[32,256]{1,0:T(8,128)S(1)}, u32[]{:S(2)}, u32[]{:S(2)}) %collective-permute-start.24) | collective-permute-done | bytes 32800 | tf_op jit(solution)/shard_map/ppermute | solution.py:473
  236.3 2.6 collective-permute-start.19
  239.5 1.9 collective-permute-done.16.refs_3_
  241.4 6.2 %collective-permute-done.21.refs_8_ = bf16[128,1024]{1,0:T(8,128)(2,1)S(1)} collective-permute-done((bf16[128,1024]{1,0:T(8,128)(2,1)S(1)}, bf16[128,1024]{1,0:T(8,128)(2,1)S(1)}, u32[]{:S(2)}, u32[]{:S(2)}) %collective-permute-start.21) | collective-permute-done | bytes 262176 | tf_op jit(solution)/shard_map/ppermute | solution.py:473
  247.5 1.3 collective-permute-done.19.refs_6_
  248.9 3.5 %collective-permute-done.17.refs_4_ = bf16[128,1024]{1,0:T(8,128)(2,1)S(1)} collective-permute-done((bf16[128,1024]{1,0:T(8,128)(2,1)S(1)}, bf16[128,1024]{1,0:T(8,128)(2,1)S(1)}, u32[]{:S(2)}, u32[]{:S(2)}) %collective-permute-start.17) | collective-permute-done | bytes 262176 | tf_op jit(solution)/shard_map/ppermute | solution.py:473
  252.4 2.6 shard_map.113
  255.0 3.8 %collective-permute-start.25 = (bf16[384,1024]{1,0:T(8,128)(2,1)S(1)}, bf16[384,1024]{1,0:T(8,128)(2,1)S(1)}, u32[]{:S(2)}, u32[]{:S(2)}) collective-permute-start(bf16[384,1024]{1,0:T(8,128)(2,1)S(1)} %get-tuple-element.102), channel_id=1, source_target_pairs={{0,1},{1,0},{2,3},{3,2},{4,5},{5,4},{6,7},{7,6},{8,9},{9,8},{10,11... | collective-permute-start | bytes 2359304 | tf_op jit(solution)/shard_map/ppermute | solution.py:473
  258.8 2.2 collective-permute-start.26
  261.0 17.8 %collective-permute-done.26.refs_4_ = bf16[384,1024]{1,0:T(8,128)(2,1)S(1)} collective-permute-done((bf16[384,1024]{1,0:T(8,128)(2,1)S(1)}, bf16[384,1024]{1,0:T(8,128)(2,1)S(1)}, u32[]{:S(2)}, u32[]{:S(2)}) %collective-permute-start.26) | collective-permute-done | bytes 786464 | tf_op jit(solution)/shard_map/ppermute | solution.py:473
  278.8 16.9 %collective-permute-done.27.refs_5_ = bf16[384,1024]{1,0:T(8,128)(2,1)S(1)} collective-permute-done((bf16[384,1024]{1,0:T(8,128)(2,1)S(1)}, bf16[384,1024]{1,0:T(8,128)(2,1)S(1)}, u32[]{:S(2)}, u32[]{:S(2)}) %collective-permute-start.27) | collective-permute-done | bytes 786464 | tf_op jit(solution)/shard_map/ppermute | solution.py:473
  295.6 4.4 %shard_map.114 = f32[512,1024]{1,0:T(8,128)} custom-call(s32[1,1536]{1,0:T(1,128)S(1)} %get-tuple-element.84.refs_0_, bf16[512,1024]{1,0:T(8,128)(2,1)S(1)} %copy-done.3, bf16[384,1024]{1,0:T(8,128)(2,1)S(1)} %get-tuple-element.101.refs_2_, bf16[384,1024]{1,0:T(8,128)(2,1)S(1)} %collective-permute-done.25.refs_3_, ...), custom_call_target="tpu_custom_call" | custom-call | bytes 13200000 | tf_op jit(solution)/shard_map/pallas_call | solution.py:63
  300.1 1.8 convert_reduce_fusion.1
  (121 shorter events, 40.1 us)
Async XLA Ops:
  28.1 5.3 %collective-permute-start.4 = (bf16[512,256]{1,0:T(8,128)(2,1)S(1)}, bf16[512,256]{1,0:T(8,128)(2,1)S(1)}, u32[]{:S(2)}, u32[]{:S(2)}) collective-permute-start(bf16[512,256]{1,0:T(8,128)(2,1)S(1)} %get-tuple-element.62.refs_1_), channel_id=1, source_target_pairs={{0,2},{1,3},{2,0},{3,1},{4,6},{5,7},{6,4},{7,5},{8,10},{9,11},{10,... | collective-permute-start | bytes 786440 | tf_op jit(solution)/shard_map/ppermute | solution.py:473
  28.4 21.4 %collective-permute-start.3 = (bf16[512,256]{1,0:T(8,128)(2,1)S(1)}, bf16[512,256]{1,0:T(8,128)(2,1)S(1)}, u32[]{:S(2)}, u32[]{:S(2)}) collective-permute-start(bf16[512,256]{1,0:T(8,128)(2,1)S(1)} %get-tuple-element.62.refs_1_), channel_id=1, source_target_pairs={{0,1},{1,0},{2,3},{3,2},{4,5},{5,4},{6,7},{7,6},{8,9},{9,8},{10,11... | collective-permute-start | bytes 786440 | tf_op jit(solution)/shard_map/ppermute | solution.py:473
  33.4 16.4 %copy-start.28 = (bf16[512,256]{1,0:T(8,128)(2,1)}, bf16[512,256]{1,0:T(8,128)(2,1)S(1)}, u32[]{:S(2)}) copy-start(bf16[512,256]{1,0:T(8,128)(2,1)S(1)} %collective-permute-done.4.refs_3_) | copy-start | bytes 786436
  33.4 17.2 %collective-permute-start.5 = (bf16[512,256]{1,0:T(8,128)(2,1)S(1)}, bf16[512,256]{1,0:T(8,128)(2,1)S(1)}, u32[]{:S(2)}, u32[]{:S(2)}) collective-permute-start(bf16[512,256]{1,0:T(8,128)(2,1)S(1)} %collective-permute-done.4.refs_3_), channel_id=1, source_target_pairs={{0,1},{1,0},{2,3},{3,2},{4,5},{5,4},{6,7},{7,6},{8,9},{9,8},{10,11... | collective-permute-start | bytes 786440 | tf_op jit(solution)/shard_map/ppermute | solution.py:473
  37.3 12.6 %collective-permute-start.6 = (f32[32,128]{1,0:T(8,128)S(1)}, f32[32,128]{1,0:T(8,128)S(1)}, u32[]{:S(2)}, u32[]{:S(2)}) collective-permute-start(f32[32,128]{1,0:T(8,128)S(1)} %get-tuple-element.61.refs_2_), channel_id=1, source_target_pairs={{0,16},{4,20},{8,24},{12,28},{16,0},{20,4},{24,8},{28,12},{1,17},{... | collective-permute-start | bytes 49160 | tf_op jit(solution)/shard_map/ppermute | solution.py:473
  39.2 1.2 collective-permute-start
  39.5 2.5 collective-permute-start.1
  40.4 3.0 collective-permute-start.2
  43.4 1.2 copy-start.2
  48.2 1.6 copy-start.6
  51.3 77.1 %all-to-all-start.1 = ((bf16[16,96,1024]{2,1,0:T(8,128)(2,1)}), bf16[16,96,1024]{2,1,0:T(8,128)(2,1)S(1)}, u32[]{:S(2)}, u32[]{:S(2)}) async-start(bf16[16,96,1024]{2,1,0:T(8,128)(2,1)} %bitcast.8), calls=%async_computation.1 | async-start | bytes 6291456 | tf_op jit(solution)/shard_map/all_to_all | solution.py:525
  56.3 51.1 %all-gather.2.cloned.1.call-start = ((), (), s32[]{:S(2)}) async-start(), calls=%async_computation.4 | async-start | bytes 2621440 | tf_op jit(solution)/shard_map/all_gather | solution.py:534
  57.0 1.6 copy-start.7
  66.4 1.1 copy-start
  67.5 1.8 copy-start.4
  71.7 2.2 collective-permute-start.7
  72.1 28.7 %collective-permute-start.8 = (bf16[128,256]{1,0:T(8,128)(2,1)S(1)}, bf16[128,256]{1,0:T(8,128)(2,1)S(1)}, u32[]{:S(2)}, u32[]{:S(2)}) collective-permute-start(bf16[128,256]{1,0:T(8,128)(2,1)S(1)} %get-tuple-element.69), channel_id=1, source_target_pairs={{0,2},{1,3},{2,0},{3,1},{4,6},{5,7},{6,4},{7,5},{8,10},{9,11},{10,... | collective-permute-start | bytes 196616 | tf_op jit(solution)/shard_map/ppermute | solution.py:473
  72.3 31.2 %collective-permute-start.9 = (bf16[128,256]{1,0:T(8,128)(2,1)S(1)}, bf16[128,256]{1,0:T(8,128)(2,1)S(1)}, u32[]{:S(2)}, u32[]{:S(2)}) collective-permute-start(bf16[128,256]{1,0:T(8,128)(2,1)S(1)} %get-tuple-element.70), channel_id=1, source_target_pairs={{0,3},{1,2},{2,1},{3,0},{4,7},{5,6},{6,5},{7,4},{8,11},{9,10},{10,... | collective-permute-start | bytes 196616 | tf_op jit(solution)/shard_map/ppermute | solution.py:473
  107.4 1.6 copy-start.8
  115.4 23.5 %copy-start.12 = (bf16[128,1024]{1,0:T(8,128)(2,1)}, bf16[128,1024]{1,0:T(8,128)(2,1)S(1)}, u32[]{:S(2)}) copy-start(bf16[128,1024]{1,0:T(8,128)(2,1)S(1)} %get-tuple-element.89.refs_4_.refs_1_) | copy-start | bytes 786436
  115.4 12.2 %collective-permute-start.10 = (bf16[128,1024]{1,0:T(8,128)(2,1)S(1)}, bf16[128,1024]{1,0:T(8,128)(2,1)S(1)}, u32[]{:S(2)}, u32[]{:S(2)}) collective-permute-start(bf16[128,1024]{1,0:T(8,128)(2,1)S(1)} %get-tuple-element.89.refs_4_.refs_1_), channel_id=1, source_target_pairs={{0,16},{4,20},{8,24},{12,28},{16,0},{20,4},{24,8},{28,12},{1,17},{... | collective-permute-start | bytes 786440 | tf_op jit(solution)/shard_map/ppermute | solution.py:473
  132.6 4.1 %collective-permute-start.11 = (f32[1,256]{1,0:T(1,128)S(1)}, f32[1,256]{1,0:T(1,128)S(1)}, u32[]{:S(2)}, u32[]{:S(2)}) collective-permute-start(f32[1,256]{1,0:T(1,128)S(1)} %get-tuple-element.78.refs_6_), channel_id=1, source_target_pairs={{0,16},{4,20},{8,24},{12,28},{16,0},{20,4},{24,8},{28,12},{1,17},{... | collective-permute-start | bytes 3080 | tf_op jit(solution)/shard_map/ppermute | solution.py:473
  136.7 15.0 %copy-start.24 = (f32[128,1024]{1,0:T(8,128)S(1)}, f32[128,1024]{1,0:T(8,128)}, u32[]{:S(2)}) copy-start(f32[128,1024]{1,0:T(8,128)} %copy-done.23) | copy-start | bytes 1572868
  138.9 23.0 %copy-start.1 = (bf16[1280,512]{1,0:T(8,128)(2,1)S(1)}, bf16[1280,512]{1,0:T(8,128)(2,1)}, u32[]{:S(2)}) copy-start(bf16[1280,512]{1,0:T(8,128)(2,1)} %copy-done) | copy-start | bytes 3932164
  139.0 12.7 %collective-permute-start.12 = (bf16[128,1024]{1,0:T(8,128)(2,1)S(1)}, bf16[128,1024]{1,0:T(8,128)(2,1)S(1)}, u32[]{:S(2)}, u32[]{:S(2)}) collective-permute-start(bf16[128,1024]{1,0:T(8,128)(2,1)S(1)} %get-tuple-element.80), channel_id=1, source_target_pairs={{0,16},{4,20},{8,24},{12,28},{16,0},{20,4},{24,8},{28,12},{1,17},{... | collective-permute-start | bytes 786440 | tf_op jit(solution)/shard_map/ppermute | solution.py:473
  151.9 21.5 %copy-start.9 = (bf16[256,1024]{1,0:T(8,128)(2,1)S(1)}, bf16[256,1024]{1,0:T(8,128)(2,1)}, u32[]{:S(2)}) copy-start(bf16[256,1024]{1,0:T(8,128)(2,1)} %refs_5_.5) | copy-start | bytes 1572868
  152.0 21.5 %copy-start.11 = (bf16[5,512,256]{2,1,0:T(8,128)(2,1)S(1)}, bf16[5,512,256]{2,1,0:T(8,128)(2,1)}, u32[]{:S(2)}) copy-start(bf16[5,512,256]{2,1,0:T(8,128)(2,1)} %copy-done.10) | copy-start | bytes 3932164
  152.0 7.4 %collective-permute-start.14 = (bf16[128,1024]{1,0:T(8,128)(2,1)S(1)}, bf16[128,1024]{1,0:T(8,128)(2,1)S(1)}, u32[]{:S(2)}, u32[]{:S(2)}) collective-permute-start(bf16[128,1024]{1,0:T(8,128)(2,1)S(1)} %shard_map.110.refs_1_), channel_id=1, source_target_pairs={{0,2},{1,3},{2,0},{3,1},{4,6},{5,7},{6,4},{7,5},{8,10},{9,11},{10,... | collective-permute-start | bytes 786440 | tf_op jit(solution)/shard_map/ppermute | solution.py:473
  153.4 7.3 %collective-permute-start.13 = (bf16[128,1024]{1,0:T(8,128)(2,1)S(1)}, bf16[128,1024]{1,0:T(8,128)(2,1)S(1)}, u32[]{:S(2)}, u32[]{:S(2)}) collective-permute-start(bf16[128,1024]{1,0:T(8,128)(2,1)S(1)} %shard_map.110.refs_1_), channel_id=1, source_target_pairs={{0,1},{1,0},{2,3},{3,2},{4,5},{5,4},{6,7},{7,6},{8,9},{9,8},{10,11... | collective-permute-start | bytes 786440 | tf_op jit(solution)/shard_map/ppermute | solution.py:473
  159.4 2.5 collective-permute-start.15
  166.1 19.2 %all-to-all-start.3 = ((bf16[8,256,128]{2,1,0:T(8,128)(2,1)}), bf16[8,256,128]{2,1,0:T(8,128)(2,1)}, u32[]{:S(2)}, u32[]{:S(2)}) async-start(bf16[8,256,128]{2,1,0:T(8,128)(2,1)} %shard_map.112), calls=%async_computation.3 | async-start | bytes 1048576 | tf_op jit(solution)/shard_map/all_to_all | solution.py:492
  173.4 2.0 copy-start.5
  184.3 7.4 %copy-start.13 = (bf16[128,1024]{1,0:T(8,128)(2,1)S(1)}, bf16[128,1024]{1,0:T(8,128)(2,1)}, u32[]{:S(2)}) copy-start(bf16[128,1024]{1,0:T(8,128)(2,1)} %copy-done.12) | copy-start | bytes 786436
  184.3 51.8 %copy-start.16 = (bf16[128,1024]{1,0:T(8,128)(2,1)S(1)}, bf16[128,1024]{1,0:T(8,128)(2,1)}, u32[]{:S(2)}) copy-start(bf16[128,1024]{1,0:T(8,128)(2,1)} %copy-done.14) | copy-start | bytes 786436
  185.4 116.5 %all-to-all-start.2 = ((bf16[8,4,128,256]{3,2,1,0:T(8,128)(2,1)}), bf16[8,4,128,256]{3,2,1,0:T(8,128)(2,1)S(1)}, u32[]{:S(2)}, u32[]{:S(2)}) async-start(bf16[8,4,128,256]{3,2,1,0:T(8,128)(2,1)} %shard_map.111), calls=%async_computation.2 | async-start | bytes 4194304 | tf_op jit(solution)/shard_map/all_to_all | solution.py:492
  191.7 103.9 %copy-start.3 = (bf16[512,1024]{1,0:T(8,128)(2,1)S(1)}, bf16[512,1024]{1,0:T(8,128)(2,1)}, u32[]{:S(2)}) copy-start(bf16[512,1024]{1,0:T(8,128)(2,1)} %refs_1_.3) | copy-start | bytes 3145732
  191.7 47.1 %collective-permute-start.20 = (bf16[128,1024]{1,0:T(8,128)(2,1)S(1)}, bf16[128,1024]{1,0:T(8,128)(2,1)S(1)}, u32[]{:S(2)}, u32[]{:S(2)}) collective-permute-start(bf16[128,1024]{1,0:T(8,128)(2,1)S(1)} %copy-done.13), channel_id=1, source_target_pairs={{0,12},{4,8},{8,4},{12,0},{16,28},{20,24},{24,20},{28,16},{1,13},{... | collective-permute-start | bytes 786440 | tf_op jit(solution)/shard_map/ppermute | solution.py:473
  193.0 43.2 %collective-permute-start.24 = (f32[32,256]{1,0:T(8,128)S(1)}, f32[32,256]{1,0:T(8,128)S(1)}, u32[]{:S(2)}, u32[]{:S(2)}) collective-permute-start(f32[32,256]{1,0:T(8,128)S(1)} %get-tuple-element.97.refs_9_), channel_id=1, source_target_pairs={{0,12},{4,8},{8,4},{12,0},{16,28},{20,24},{24,20},{28,16},{1,13},{... | collective-permute-start | bytes 98312 | tf_op jit(solution)/shard_map/ppermute | solution.py:473
  194.1 42.0 %collective-permute-start.23 = (f32[32,256]{1,0:T(8,128)S(1)}, f32[32,256]{1,0:T(8,128)S(1)}, u32[]{:S(2)}, u32[]{:S(2)}) collective-permute-start(f32[32,256]{1,0:T(8,128)S(1)} %get-tuple-element.97.refs_9_), channel_id=1, source_target_pairs={{0,8},{4,12},{8,0},{12,4},{16,24},{20,28},{24,16},{28,20},{1,9},{5... | collective-permute-start | bytes 98312 | tf_op jit(solution)/shard_map/ppermute | solution.py:473
  194.2 42.0 %collective-permute-start.22 = (f32[32,256]{1,0:T(8,128)S(1)}, f32[32,256]{1,0:T(8,128)S(1)}, u32[]{:S(2)}, u32[]{:S(2)}) collective-permute-start(f32[32,256]{1,0:T(8,128)S(1)} %get-tuple-element.97.refs_9_), channel_id=1, source_target_pairs={{0,4},{4,0},{8,12},{12,8},{16,20},{20,16},{24,28},{28,24},{1,5},{5... | collective-permute-start | bytes 98312 | tf_op jit(solution)/shard_map/ppermute | solution.py:473
  195.6 43.9 %collective-permute-start.18 = (bf16[128,1024]{1,0:T(8,128)(2,1)S(1)}, bf16[128,1024]{1,0:T(8,128)(2,1)S(1)}, u32[]{:S(2)}, u32[]{:S(2)}) collective-permute-start(bf16[128,1024]{1,0:T(8,128)(2,1)S(1)} %copy-done.13), channel_id=1, source_target_pairs={{0,8},{4,12},{8,0},{12,4},{16,24},{20,28},{24,16},{28,20},{1,9},{5... | collective-permute-start | bytes 786440 | tf_op jit(solution)/shard_map/ppermute | solution.py:473
  236.2 5.2 %collective-permute-start.16 = (bf16[128,1024]{1,0:T(8,128)(2,1)S(1)}, bf16[128,1024]{1,0:T(8,128)(2,1)S(1)}, u32[]{:S(2)}, u32[]{:S(2)}) collective-permute-start(bf16[128,1024]{1,0:T(8,128)(2,1)S(1)} %copy-done.13), channel_id=1, source_target_pairs={{0,4},{4,0},{8,12},{12,8},{16,20},{20,16},{24,28},{28,24},{1,5},{5... | collective-permute-start | bytes 786440 | tf_op jit(solution)/shard_map/ppermute | solution.py:473
  236.2 11.4 %collective-permute-start.21 = (bf16[128,1024]{1,0:T(8,128)(2,1)S(1)}, bf16[128,1024]{1,0:T(8,128)(2,1)S(1)}, u32[]{:S(2)}, u32[]{:S(2)}) collective-permute-start(bf16[128,1024]{1,0:T(8,128)(2,1)S(1)} %copy-done.16), channel_id=1, source_target_pairs={{0,12},{4,8},{8,4},{12,0},{16,28},{20,24},{24,20},{28,16},{1,13},{... | collective-permute-start | bytes 786440 | tf_op jit(solution)/shard_map/ppermute | solution.py:473
  236.3 12.6 %collective-permute-start.19 = (bf16[128,1024]{1,0:T(8,128)(2,1)S(1)}, bf16[128,1024]{1,0:T(8,128)(2,1)S(1)}, u32[]{:S(2)}, u32[]{:S(2)}) collective-permute-start(bf16[128,1024]{1,0:T(8,128)(2,1)S(1)} %copy-done.16), channel_id=1, source_target_pairs={{0,8},{4,12},{8,0},{12,4},{16,24},{20,28},{24,16},{28,20},{1,9},{5... | collective-permute-start | bytes 786440 | tf_op jit(solution)/shard_map/ppermute | solution.py:473
  238.8 13.6 %collective-permute-start.17 = (bf16[128,1024]{1,0:T(8,128)(2,1)S(1)}, bf16[128,1024]{1,0:T(8,128)(2,1)S(1)}, u32[]{:S(2)}, u32[]{:S(2)}) collective-permute-start(bf16[128,1024]{1,0:T(8,128)(2,1)S(1)} %copy-done.16), channel_id=1, source_target_pairs={{0,4},{4,0},{8,12},{12,8},{16,20},{20,16},{24,28},{28,24},{1,5},{5... | collective-permute-start | bytes 786440 | tf_op jit(solution)/shard_map/ppermute | solution.py:473
  255.0 6.0 %collective-permute-start.25 = (bf16[384,1024]{1,0:T(8,128)(2,1)S(1)}, bf16[384,1024]{1,0:T(8,128)(2,1)S(1)}, u32[]{:S(2)}, u32[]{:S(2)}) collective-permute-start(bf16[384,1024]{1,0:T(8,128)(2,1)S(1)} %get-tuple-element.102), channel_id=1, source_target_pairs={{0,1},{1,0},{2,3},{3,2},{4,5},{5,4},{6,7},{7,6},{8,9},{9,8},{10,11... | collective-permute-start | bytes 2359304 | tf_op jit(solution)/shard_map/ppermute | solution.py:473
  258.8 20.0 %collective-permute-start.26 = (bf16[384,1024]{1,0:T(8,128)(2,1)S(1)}, bf16[384,1024]{1,0:T(8,128)(2,1)S(1)}, u32[]{:S(2)}, u32[]{:S(2)}) collective-permute-start(bf16[384,1024]{1,0:T(8,128)(2,1)S(1)} %get-tuple-element.103), channel_id=1, source_target_pairs={{0,2},{1,3},{2,0},{3,1},{4,6},{5,7},{6,4},{7,5},{8,10},{9,11},{10,... | collective-permute-start | bytes 2359304 | tf_op jit(solution)/shard_map/ppermute | solution.py:473
  261.0 34.7 %collective-permute-start.27 = (bf16[384,1024]{1,0:T(8,128)(2,1)S(1)}, bf16[384,1024]{1,0:T(8,128)(2,1)S(1)}, u32[]{:S(2)}, u32[]{:S(2)}) collective-permute-start(bf16[384,1024]{1,0:T(8,128)(2,1)S(1)} %get-tuple-element.104), channel_id=1, source_target_pairs={{0,3},{1,2},{2,1},{3,0},{4,7},{5,6},{6,5},{7,4},{8,11},{9,10},{10,... | collective-permute-start | bytes 2359304 | tf_op jit(solution)/shard_map/ppermute | solution.py:473
  (28 other events, 22.6 us)
Sparse Core Ops, SparseCore 0:
  58.7 48.6 all-gather.1

commit v6 on v5

--- a/solution.py
+++ b/solution.py
@@ -19,7 +19,7 @@
 
 VM = pl.BlockSpec(memory_space=pltpu.VMEM)
 SM = pl.BlockSpec(memory_space=pltpu.SMEM)
-HB = pl.BlockSpec(memory_space=pl.ANY)
+HB = pl.BlockSpec(memory_space=pltpu.HBM)
 
 
 def call(body, out_shape, in_specs, us, scratch=(), limit=16, out_specs=None):
@@ -109,8 +109,10 @@
 
             @pl.when(hit)
             def _():
-                start = pl.multiple_of(count * steps, steps)
-                out[d, pl.ds(start, steps), :] = hist[src - here * seq_dev]
+                value = hist[src - here * seq_dev]
+                for side in range(2):
+                    start = pl.multiple_of((side * per_peer + count) * steps, steps)
+                    out[jnp.bitwise_xor(d, side * (dp // 2)), pl.ds(start, steps), :] = value
 
             return count + hit.astype(I32)
 
@@ -145,43 +147,46 @@
     for d in range(dp):
         mine = slice(d * mp, (d + 1) * mp)
         digits = [high[mine], none, low[mine], none] if mp < 8 else [high[mine], low[mine]]
-        out[d, per_peer * steps :, :] = jnp.concatenate(digits, axis=0).astype(BF)
-
-
-def take_kernel(meta, arrived, out, *refs, dp, mp, seq_dev, per_peer, steps):
-    asked, digits = refs[:mp], refs[mp]
-    here = meta[0]
-    anchors = [lax.div(meta[2 + here * seq_dev + k], seq_dev) for k in range(seq_dev)]
-    for k in range(seq_dev):
-        rank = jnp.int32(0)
-        for earlier in range(k):
-            rank = rank + (anchors[earlier] == anchors[k]).astype(I32)
-        start = pl.multiple_of(rank * steps, steps)
-        out[k * steps : (k + 1) * steps, :] = arrived[anchors[k], pl.ds(start, steps), :]
-    digits[...] = arrived[:, per_peer * steps :, :].astype(F32)
-    capacity = asked[0].shape[1]
-    for j in range(mp):
-        owner = jnp.bitwise_xor(meta[1], j)
-        for d in range(dp):
-            number = 256.0 * digits[d, pl.ds(owner, 1), :] + digits[d, pl.ds(8 + owner, 1), :]
-            asked[j][d : d + 1, :] = number[:, :capacity].astype(I32)
-
-
-def forward_kernel(meta, *refs, mp, seqs, seq_dev, steps, width, cols, quarter):
+        out[d, 2 * per_peer * steps :, :] = jnp.concatenate(digits, axis=0).astype(BF)
+
+
+def take_kernel(meta, arrived, out, *, dp, seq_dev, per_peer, steps):
+    for side in range(2):
+        block = jnp.bitwise_xor(meta[0], side * (dp // 2))
+        anchors = [lax.div(meta[2 + block * seq_dev + k], seq_dev) for k in range(seq_dev)]
+        for k in range(seq_dev):
+            rank = jnp.int32(side * per_peer)
+            for earlier in range(k):
+                rank = rank + (anchors[earlier] == anchors[k]).astype(I32)
+            start = pl.multiple_of(rank * steps, steps)
+            at = (side * seq_dev + k) * steps
+            out[at : at + steps, :] = arrived[anchors[k], pl.ds(start, steps), :]
+    base = 2 * seq_dev * steps
+    for d in range(dp):
+        out[base + d * 16 : base + (d + 1) * 16, :] = arrived[d, 2 * per_peer * steps :, :]
+
+
+def forward_kernel(meta, *refs, mp, dp, seqs, seq_dev, steps, width, cols, quarter):
     blocks = refs[:mp]
     w_in = refs[mp]
     wide, projected, turned, own = refs[mp + 1 : mp + 5]
     gated_out = refs[mp + 5 : 2 * mp + 5]
     feat, gated = refs[2 * mp + 5 :]
-    here_dp = meta[0]
     here_mp = meta[1]
     part = width // mp
-    counts = [length_of(meta, here_dp * seq_dev + k, seqs) for k in range(seq_dev)]
+    counts = [
+        length_of(meta, block * seq_dev + k, seqs)
+        for block in (meta[0], jnp.bitwise_xor(meta[0], dp // 2))
+        for k in range(seq_dev)
+    ]
+    half_rows = seq_dev * steps
+    rows_all = 2 * half_rows
     for j in range(mp):
         start = pl.multiple_of(jnp.bitwise_xor(here_mp, j) * part, part)
-        feat[:, pl.ds(start, part)] = blocks[j][...]
-    rows_all = seq_dev * steps
-    own[...] = feat[pl.ds(pl.multiple_of(here_mp * quarter, quarter), quarter), :]
+        feat[:, pl.ds(start, part)] = blocks[j][:rows_all, :]
+    for side in range(2):
+        start = pl.multiple_of(side * half_rows + here_mp * quarter, quarter)
+        own[side * quarter : (side + 1) * quarter, :] = feat[pl.ds(start, quarter), :]
     for g in range(rows_all // BLOCK):
         rows = slice(g * BLOCK, (g + 1) * BLOCK)
         x = feat[rows, :].astype(F32)
@@ -194,7 +199,7 @@
         pre = dot_nn(feat[...], w_in[c])
         sigma = jax.nn.sigmoid(pre)
         projected[c] = (pre * sigma).astype(BF)
-        wide[c] = sigma * (1.0 + pre * (1.0 - sigma))
+        projected[5 + c] = (sigma * (1.0 + pre * (1.0 - sigma))).astype(BF)
     root = 1.0 / math.sqrt(DH)
     t_id = iota((BLOCK, BLOCK), 0)
     s_id = iota((BLOCK, BLOCK), 1)
@@ -213,30 +218,30 @@
             sigma = jax.nn.sigmoid(scores)
             weights = (scores * sigma * scale).astype(BF)
             projected[4, rows, lanes] = weights
-            wide[6, rows, lanes] = sigma * (1.0 + scores * (1.0 - sigma)) * (scale * root)
+            wide[2, rows, lanes] = sigma * (1.0 + scores * (1.0 - sigma)) * (scale * root)
             mixed = dot_nn(weights, projected[1, rows, lanes])
             centered = mixed - jnp.mean(mixed, axis=-1, keepdims=True)
             spread = jnp.mean(centered * centered, axis=-1, keepdims=True)
             inv = lax.rsqrt(spread + EPS_NORM)
             norm = centered * inv
-            wide[4, rows, lanes] = norm
-            wide[5, rows, lanes] = jnp.broadcast_to(inv, norm.shape)
+            wide[0, rows, lanes] = norm
+            wide[1, rows, lanes] = jnp.broadcast_to(inv, norm.shape)
             done = (norm * projected[0, rows, lanes].astype(F32)).astype(BF)
             gated[rows, lanes] = done
             turned[width + h * DH : width + (h + 1) * DH, rows] = done.T
     for j in range(mp):
-        start = pl.multiple_of(jnp.bitwise_xor(here_mp, j) * quarter, quarter)
-        gated_out[j][...] = gated[pl.ds(start, quarter), :]
-
-
-def out_kernel(meta, own, w_out, *refs, mp):
-    gathered = refs[:mp]
-    unit, unit_bf, inv_o = refs[mp:]
-    cols = gathered[0].shape[1]
+        for side in range(2):
+            start = side * half_rows + jnp.bitwise_xor(here_mp, j) * quarter
+            start = pl.multiple_of(start, quarter)
+            gated_out[j][side * quarter : (side + 1) * quarter, :] = gated[pl.ds(start, quarter), :]
+
+
+def out_kernel(own, *refs, mp):
+    gathered, weights = refs[:mp], refs[mp : 2 * mp]
+    unit, unit_bf, inv_o = refs[2 * mp :]
     total = own[...].astype(F32)
     for j in range(mp):
-        start = pl.multiple_of(jnp.bitwise_xor(meta[1], j) * cols, cols)
-        total = total + dot_nn(gathered[j][...], w_out[pl.ds(start, cols), :])
+        total = total + dot_nn(gathered[j][...], weights[j][...])
     inv = lax.rsqrt(jnp.sum(total * total, axis=-1, keepdims=True) + EPS_UNIT)
     u = total * inv
     unit[...] = u
@@ -245,12 +250,19 @@
 
 
 def look_kernel(meta, *refs, mp, dp, capacity, chunk, share):
-    asked, catalogue, looked, incoming, returning = refs[:mp], *refs[mp:]
+    blocks, catalogue, looked, incoming, returning, digits, asked = refs[:mp], *refs[mp:]
     stock, _ = catalogue.shape
+    base = blocks[0].shape[0] - 16 * dp
+    for j in range(mp):
+        digits[...] = blocks[j][base:, :].astype(F32)
+        for d in range(dp):
+            high = digits[pl.ds(d * 16 + meta[1], 1), :]
+            low = digits[pl.ds(d * 16 + 8 + meta[1], 1), :]
+            asked[j * dp + d : j * dp + d + 1, :] = (256.0 * high + low)[:, :capacity]
     groups = dp * mp
     slots = groups * capacity
     half = dp // 2
-    table = jnp.concatenate([a[...] for a in asked], axis=0).astype(F32)
+    table = asked[...]
     slot = iota((1, slots), 1).astype(F32)
     group = jnp.floor((slot + 0.5) * (1.0 / capacity))
     local = slot - group * capacity
@@ -282,10 +294,10 @@
 
 
 def score_kernel(
-    meta, items, code, code_far, unit, unit_far, expo, inv_o, total_o,
+    meta, items, code, code_far, units, expo, inv_o, total_o,
     *, dp, devices, capacity, chunk,
 ):
-    events = unit.shape[0]
+    events = units.shape[0] // 2
     near = devices // 2
     slots = items.shape[0]
     half = pl.multiple_of(lax.div(meta[0], dp // 2) * near, near)
@@ -296,6 +308,7 @@
         xf = x.astype(F32)
         inv = lax.rsqrt(jnp.sum(xf * xf, axis=-1, keepdims=True) + EPS_UNIT)
         inv_o[rows, :] = jnp.broadcast_to(inv, (chunk, BLOCK))
+        cosines = dot_nt(x, units[...]) * (inv * (1.0 / COSINE_DIVISOR))
         slot = s + iota((chunk, 1), 0).astype(F32)
         owner = jnp.floor((slot + 0.5) * (1.0 / (2 * capacity)))
         local = slot - owner * (2 * capacity)
@@ -304,8 +317,7 @@
         named = owner == iota((chunk, near), 1).astype(F32)
         for side in range(2):
             lanes = slice(side * events, (side + 1) * events)
-            u = (unit, unit_far)[side][...]
-            logits = dot_nt(x, u) * (inv * (1.0 / COSINE_DIVISOR))
+            logits = cosines[:, lanes]
             spread = jnp.where(named & (far == (side == 1)), 1.0, 0.0).astype(BF)
             codes = dot_nn(spread, codes_in[side])
             first = codes == 2.0 * local + 2.0
@@ -335,45 +347,50 @@
 
 
 def slope_kernel(
-    meta, items, code, code_far, expo, inv, total, total_far, slope, slope_far, ledger,
+    meta, items, code, code_far, expo, inv, total, total_far, slopes, slopes_bf, ledger,
     *, dp, seqs, seq_dev, steps, chunk,
 ):
     share = shares(meta, expo, total, total_far, dp, seqs, seq_dev, steps)
-    events, width = slope.shape
+    events, width = slopes.shape[0] // 2, slopes.shape[1]
     both = jnp.zeros((2 * events, width), F32)
     for s in range(0, items.shape[0], chunk):
         rows = slice(s, s + chunk)
         both = both + dot_tn((share(rows) * inv[rows, 0:1]).astype(BF), items[rows, :])
-    near = ledger.shape[0] // 2
+    slopes[...] = both
+    slopes_bf[...] = both.astype(BF)
+    near = ledger.shape[0]
     each = items.shape[0] // near
-    for o in range(near):
-        part = share(slice(o * each, (o + 1) * each))
-        ledger[o : o + 1, :] = jnp.sum(part, axis=0, keepdims=True)
+    weight = jnp.concatenate(
+        [
+            jnp.sum(share(slice(o * each, (o + 1) * each)), axis=0, keepdims=True)
+            for o in range(near)
+        ],
+        axis=0,
+    )
+    high = weight.astype(BF)
+    low = (weight - high.astype(F32)).astype(BF)
     half = pl.multiple_of(lax.div(meta[0], dp // 2) * near, near)
-    for side, c in enumerate((code, code_far)):
-        ledger[near:, side * events : (side + 1) * events] = c[pl.ds(half, near), :]
-    slope[...] = both[:events]
-    slope_far[...] = both[events:].astype(BF)
+    codes = [c[pl.ds(half, near), :].astype(BF) for c in (code, code_far)]
+    for n, part in enumerate([high, low, jnp.concatenate(codes, axis=1)]):
+        ledger[:, n * 2 * events : (n + 1) * 2 * events] = part
 
 
 def send_kernel(
-    meta, expo, total, total_far, unit, unit_far, sending,
+    meta, expo, total, total_far, units, sending,
     *, dp, seqs, seq_dev, steps, chunk,
 ):
     share = shares(meta, expo, total, total_far, dp, seqs, seq_dev, steps)
-    events = unit.shape[0]
     for s in range(0, expo.shape[0], chunk):
         rows = slice(s, s + chunk)
         hot = jnp.where(expo[rows, :] == 0.0, 0.0, 1.0).astype(BF)
-        unit_rows = dot_nn(hot[:, :events], unit[...]) + dot_nn(hot[:, events:], unit_far[...])
+        unit_rows = dot_nn(hot, units[...])
         weight = jnp.sum(share(rows), axis=1, keepdims=True)
         sending[rows, :] = (unit_rows * weight).astype(BF)
 
 
-def mail_kernel(meta, *refs, half, mp, capacity):
-    units, ledgers, outs, hots = refs[: 2 * half], refs[2 * half : 3 * half], refs[3 * half : -1], refs[-1]
-    events, width = units[0].shape
-    near = ledgers[0].shape[0] // 2
+def mail_kernel(meta, *refs, half, mp, events, capacity):
+    units, ledgers, outs = refs[:half], refs[half : 2 * half], refs[2 * half : -2]
+    hots, ledger = refs[-2:]
     here = jnp.where(meta[0] >= half, meta[0] - half, meta[0])
     slot = iota((2 * capacity, 2 * events), 0)
     event = iota((2 * capacity, 2 * events), 1)
@@ -381,26 +398,30 @@
     local = jnp.where(far, slot - capacity, slot).astype(F32)
     same = far == (event >= events)
     for j in range(half):
+        ledger[...] = ledgers[j][...].astype(F32)
         weights = []
         for k in range(mp):
-            o = here * mp + jnp.bitwise_xor(meta[1], k)
-            code = ledgers[j][pl.ds(near + o, 1), :]
+            line = ledger[pl.ds(here * mp + jnp.bitwise_xor(meta[1], k), 1), :]
+            code = line[:, 4 * events : 6 * events]
             mine = same & (jnp.floor((code - 1.0) * 0.5) == local)
             hots[k * 2 * capacity : (k + 1) * 2 * capacity, :] = mine.astype(BF)
-            weight = jnp.where(mine, ledgers[j][pl.ds(o, 1), :], 0.0)
-            weights.append(jnp.sum(weight, axis=1, keepdims=True))
-        rows = dot_nn(hots[:, :events], units[2 * j][...])
-        rows = rows + dot_nn(hots[:, events:], units[2 * j + 1][...])
+            weight = line[:, : 2 * events] + line[:, 2 * events : 4 * events]
+            weights.append(jnp.sum(jnp.where(mine, weight, 0.0), axis=1, keepdims=True))
+        rows = dot_nn(hots[...], units[j][...])
         for k in range(mp):
             part = rows[k * 2 * capacity : (k + 1) * 2 * capacity] * weights[k]
             outs[k][j * 2 * capacity : (j + 1) * 2 * capacity, :] = part.astype(BF)
 
 
-def out_cot_kernel(unit, inv_out, slope, slope_far, out_cot):
-    u = unit[...]
-    s = slope[...] + slope_far[...].astype(F32)
-    along = jnp.sum(u * s, axis=-1, keepdims=True)
-    out_cot[...] = ((s - u * along) * inv_out[:, 0:1]).astype(BF)
+def out_cot_kernel(units, inv_out, slopes, slopes_back, out_cot):
+    events = units.shape[0] // 2
+    for side in range(2):
+        rows = slice(side * events, (side + 1) * events)
+        there = slice((1 - side) * events, (2 - side) * events)
+        u = units[rows, :]
+        s = slopes[rows, :] + slopes_back[there, :].astype(F32)
+        along = jnp.sum(u * s, axis=-1, keepdims=True)
+        out_cot[rows, :] = ((s - u * along) * inv_out[rows, 0:1]).astype(BF)
 
 
 def spread_kernel(incoming, catalogue, *refs, chunk):
@@ -419,36 +440,29 @@
         out[r : r + chunk, :] = (v - c * jnp.sum(c * v, axis=-1, keepdims=True)) * inv
 
 
-def w_out_kernel(meta, *refs, mp, dp):
-    blocks, turned, out, whole = refs[:mp], *refs[mp:]
-    quarter, width = blocks[0].shape
-    for j in range(mp):
-        start = pl.multiple_of(jnp.bitwise_xor(meta[1], j) * quarter, quarter)
-        whole[pl.ds(start, quarter), :] = blocks[j][...]
-    part = dot_nn(turned[width:, :], whole[...]).astype(BF)
-    lanes = width // dp
-    for d in range(dp):
-        out[d] = part[:, d * lanes : (d + 1) * lanes]
-
-
 def backward_kernel(meta, *refs, mp, dp):
     blocks = refs[:mp]
-    w_out, wide, projected, turned, out, whole, cot = refs[mp:]
-    quarter, width = blocks[0].shape
-    for j in range(mp):
-        start = pl.multiple_of(jnp.bitwise_xor(meta[1], j) * quarter, quarter)
-        whole[pl.ds(start, quarter), :] = blocks[j][...]
+    w_out, wide, projected, turned = refs[mp : mp + 4]
+    outs = refs[mp + 4 : -2]
+    whole, cot = refs[-2:]
+    half = dp // 2
+    quarter, width = blocks[0].shape[0] // 2, blocks[0].shape[1]
     rows_all = whole.shape[0]
     cols = w_out.shape[0]
+    for j in range(mp):
+        for side in range(2):
+            start = side * (rows_all // 2) + jnp.bitwise_xor(meta[1], j) * quarter
+            rows = slice(side * quarter, (side + 1) * quarter)
+            whole[pl.ds(pl.multiple_of(start, quarter), quarter), :] = blocks[j][rows, :]
     gated_cot = dot_nt(whole[...], w_out[...]).astype(BF).astype(F32)
     for g in range(rows_all // BLOCK):
         rows = slice(g * BLOCK, (g + 1) * BLOCK)
         for h in range(cols // DH):
             lanes = slice(h * DH, (h + 1) * DH)
             d_gated = gated_cot[rows, lanes]
-            n = wide[4, rows, lanes]
+            n = wide[0, rows, lanes]
             d_norm = d_gated * projected[0, rows, lanes].astype(F32)
-            d_mixed = wide[5, rows, lanes] * (
+            d_mixed = wide[1, rows, lanes] * (
                 d_norm
                 - jnp.mean(d_norm, axis=-1, keepdims=True)
                 - n * jnp.mean(d_norm * n, axis=-1, keepdims=True)
@@ -456,16 +470,32 @@
             d_mixed = d_mixed.astype(BF)
             d_weights = dot_nt(d_mixed, projected[1, rows, lanes]).astype(BF).astype(F32)
             d_values = dot_tn(projected[4, rows, lanes], d_mixed)
-            d_scores = (d_weights * wide[6, rows, lanes]).astype(BF)
+            d_scores = (d_weights * wide[2, rows, lanes]).astype(BF)
             d_queries = dot_nn(d_scores, projected[3, rows, lanes])
             d_keys = dot_tn(d_scores, projected[2, rows, lanes])
             for c, d in enumerate((d_gated * n, d_values, d_queries, d_keys)):
-                cot[c, rows, lanes] = (d.astype(BF).astype(F32) * wide[c, rows, lanes]).astype(BF)
+                step = projected[5 + c, rows, lanes].astype(F32)
+                cot[c, rows, lanes] = (d.astype(BF).astype(F32) * step).astype(BF)
     share = width // dp
-    for c in range(4):
-        part = dot_nn(turned[:width, :], cot[c]).astype(BF)
-        for d in range(dp):
-            out[d, c] = part[d * share : (d + 1) * share, :]
+    mine = pl.multiple_of(lax.div(meta[0], half) * (width // 2), width // 2)
+    here = jnp.where(meta[0] >= half, meta[0] - half, meta[0])
+    normed = turned[pl.ds(mine, width // 2), :]
+    for c in range(5):
+        if c < 4:
+            part = dot_nn(normed, cot[c]).astype(BF)
+        else:
+            lanes = pl.ds(mine, width // 2)
+            part = dot_nn(turned[width:, :], whole[:, lanes]).T.astype(BF)
+        for d in range(half):
+            piece = part[d * share : (d + 1) * share, :]
+            if len(outs) == 1:
+                outs[0][d, c] = piece
+                continue
+            for j in range(half):
+
+                @pl.when(jnp.bitwise_xor(here, j) == d)
+                def _(j=j, piece=piece):
+                    outs[j][c] = piece
 
 
 def swapped(x, axis, bit):
@@ -473,10 +503,10 @@
     return lax.ppermute(x, axis, [(a, a ^ bit) for a in range(size)])
 
 
-def gather_blocks(x, axis):
+def gather_blocks(x, axis, half=None):
     size = lax.axis_size(axis)
-    blocks = {0: x}
-    bit = size // 2
+    blocks = {0: x} if half is None else {0: x, size // 2: half}
+    bit = size // 2 if half is None else size // 4
     while bit:
         for j in list(blocks):
             blocks[j ^ bit] = swapped(blocks[j], axis, bit)
@@ -486,11 +516,6 @@
 
 def exchange(parts, axis):
     return [p if j == 0 else swapped(p, axis, j) for j, p in enumerate(parts)]
-
-
-def summed(x):
-    got = lax.all_to_all(x, "dp", split_axis=0, concat_axis=0, tiled=True)
-    return jnp.sum(got.astype(F32), axis=0)
 
 
 def per_device(history, lengths, source, owners, item_rows, catalogue, w_in, w_out):
@@ -510,7 +535,7 @@
     stock = catalogue.shape[0]
     per_peer = (seq_dev + dp - 1) // dp
     chunk = math.gcd(slots, 512)
-    short = dp <= 8
+    short = dp <= 8 and near <= 16 and 6 * events <= width
     S = jax.ShapeDtypeStruct
     here_dp = lax.axis_index("dp")
     place = jnp.stack([here_dp, lax.axis_index("mp")]).astype(I32)
@@ -531,27 +556,24 @@
             axis_index_groups=halves,
         ).reshape(slots, width)
 
-    w_out_all = lax.all_gather(w_out, "mp", axis=0, tiled=True)
+    w_out_y = swapped(w_out, "mp", mp // 2)
     packed, code = call(
         functools.partial(
             pack_kernel, dp=dp, seq_dev=seq_dev, per_peer=per_peer, mp=mp, capacity=capacity
         ),
-        [S((dp, per_peer * steps + 16, part), BF), S((devices, events), F32)],
+        [S((dp, 2 * per_peer * steps + 16, part), BF), S((devices, events), F32)],
         [SM, VM, VM, VM],
         4,
     )(meta, history, owners.T, item_rows.T)
     arrived = lax.all_to_all(packed, "dp", split_axis=0, concat_axis=0, tiled=True)
-    rows, *asked = call(
-        functools.partial(
-            take_kernel, dp=dp, mp=mp, seq_dev=seq_dev, per_peer=per_peer, steps=steps
-        ),
-        [S((rows_all, part), BF)] + [S((dp, capacity), I32)] * mp,
+    arrived, w_out_y = lax.optimization_barrier((arrived, w_out_y))
+    rows = call(
+        functools.partial(take_kernel, dp=dp, seq_dev=seq_dev, per_peer=per_peer, steps=steps),
+        S((2 * rows_all + 16 * dp, part), BF),
         [SM, VM],
         1,
-        scratch=[pltpu.VMEM((dp, 16, part), F32)],
     )(meta, arrived)
     features = gather_blocks(rows, "mp")
-    asked = exchange(asked, "mp")
     code_far = partner(code)
     looked, incoming, returning = call(
         functools.partial(
@@ -560,8 +582,8 @@
         [S((slots, width), BF), S((1, slots), I32), S((1, slots), I32)],
         [SM] + [VM] * mp + [HB],
         4,
-        out_specs=[HB, VM, VM],
-    )(meta, *asked, catalogue)
+        scratch=[pltpu.VMEM((16 * dp, part), F32), pltpu.VMEM((devices, capacity), F32)],
+    )(meta, *features, catalogue)
     looked, features, code_far = lax.optimization_barrier((looked, features, code_far))
     items = in_half(looked)
 
@@ -569,6 +591,7 @@
         functools.partial(
             forward_kernel,
             mp=mp,
+            dp=dp,
             seqs=seqs,
             seq_dev=seq_dev,
             steps=steps,
@@ -577,95 +600,105 @@
             quarter=quarter,
         ),
         [
-            S((7, rows_all, cols), F32),
-            S((5, rows_all, cols), BF),
-            S((width + cols, rows_all), BF),
-            S((quarter, width), BF),
+            S((3, 2 * rows_all, cols), F32),
+            S((9, 2 * rows_all, cols), BF),
+            S((width + cols, 2 * rows_all), BF),
+            S((2 * quarter, width), BF),
         ]
-        + [S((quarter, cols), BF)] * mp,
-        [SM] + [HB] * (mp + 1),
-        6,
-        scratch=[pltpu.VMEM((rows_all, width), BF), pltpu.VMEM((rows_all, cols), BF)],
+        + [S((2 * quarter, cols), BF)] * mp,
+        [SM] + [VM] * mp + [HB],
+        10,
+        scratch=[pltpu.VMEM((2 * rows_all, width), BF), pltpu.VMEM((2 * rows_all, cols), BF)],
         out_specs=[HB] * 4 + [VM] * mp,
-        limit=24,
+        limit=36,
     )(meta, *features, w_in)
     gathered = exchange(gated, "mp")
-    unit, unit_bf, inv_out = call(
+    w_out_blocks = gather_blocks(w_out, "mp", w_out_y)
+    units, units_bf, inv_out = call(
         functools.partial(out_kernel, mp=mp),
-        [S((quarter, width), F32), S((quarter, width), BF), S((quarter, BLOCK), F32)],
-        [SM, HB, HB] + [VM] * mp,
+        [
+            S((2 * quarter, width), F32),
+            S((2 * quarter, width), BF),
+            S((2 * quarter, BLOCK), F32),
+        ],
+        [HB] + [VM] * (2 * mp),
         2,
-    )(meta, own, w_out_all, *gathered)
-
-    unit_far = partner(unit_bf)
+    )(own, *gathered, *w_out_blocks)
+
     expo, inv_item, total = call(
         functools.partial(
             score_kernel, dp=dp, devices=devices, capacity=capacity, chunk=chunk
         ),
         [S((slots, 2 * events), F32), S((slots, BLOCK), F32), S((1, 2 * events), F32)],
-        [SM, HB] + [VM] * 4,
+        [SM, HB] + [VM] * 3,
         4,
-    )(meta, items, code, code_far, unit_bf, unit_far)
+    )(meta, items, code, code_far, units_bf)
     total_far = partner(total)
     sizes = dict(dp=dp, seqs=seqs, seq_dev=seq_dev, steps=steps, chunk=chunk)
-    item_slope, slope_far, ledger = call(
+    slopes, slopes_bf, ledger = call(
         functools.partial(slope_kernel, **sizes),
-        [S((events, width), F32), S((events, width), BF), S((2 * near, 2 * events), F32)],
+        [
+            S((2 * events, width), F32),
+            S((2 * events, width), BF),
+            S((near, width), BF),
+        ],
         [SM, HB] + [VM] * 6,
         3,
     )(meta, items, code, code_far, expo, inv_item, total, total_far)
-    slope_back = partner(slope_far)
-    out_cot = call(out_cot_kernel, S((events, width), BF), [VM] * 4, 1)(
-        unit, inv_out, item_slope, slope_back
+    slopes_back = partner(slopes_bf)
+    if short:
+        column = range(1, dp // 2)
+        ledgers = [ledger] + [swapped(ledger, "dp", j) for j in column]
+        all_units = [units_bf] + [swapped(units_bf, "dp", j) for j in column]
+        mail = call(
+            functools.partial(
+                mail_kernel, half=dp // 2, mp=mp, events=events, capacity=capacity
+            ),
+            [S((dp * capacity, width), BF)] * mp,
+            [SM] + [VM] * dp,
+            4,
+            scratch=[
+                pltpu.VMEM((mp * 2 * capacity, 2 * events), BF),
+                pltpu.VMEM((near, width), F32),
+            ],
+        )(meta, *all_units, *ledgers)
+        slopes_back, mail = lax.optimization_barrier((slopes_back, mail))
+        landed = exchange(mail, "mp")
+    out_cot = call(out_cot_kernel, S((2 * events, width), BF), [VM] * 4, 1)(
+        units, inv_out, slopes, slopes_back
     )
     cots = gather_blocks(out_cot, "mp")
+    pieces = [S((5, width // dp, cols), BF)] * (dp // 2)
+    parts = call(
+        functools.partial(backward_kernel, mp=mp, dp=dp),
+        pieces if short else [S((dp // 2, 5, width // dp, cols), BF)],
+        [SM] + [VM] * mp + [HB] * 4,
+        10,
+        scratch=[
+            pltpu.VMEM((2 * rows_all, width), BF),
+            pltpu.VMEM((4, 2 * rows_all, cols), BF),
+        ],
+        limit=36,
+    )(meta, *cots, w_out, wide, projected, turned)
     if short:
-        _, mail_unit, mail_far, mail_ledger = lax.optimization_barrier(
-            (out_cot, unit_bf, unit_far, ledger)
+        parts, landed = lax.optimization_barrier((parts, landed))
+        grads = sum(p.astype(F32) for p in exchange(parts, "dp"))
+    else:
+        got = lax.all_to_all(
+            parts[0],
+            "dp",
+            split_axis=0,
+            concat_axis=0,
+            tiled=True,
+            axis_index_groups=[list(range(dp // 2)), list(range(dp // 2, dp))],
         )
-        ledgers = [ledger] + [swapped(mail_ledger, "dp", j) for j in range(1, dp // 2)]
-        units = [unit_bf, unit_far]
-        for j in range(1, dp // 2):
-            units += [swapped(mail_unit, "dp", j), swapped(mail_far, "dp", j)]
-
-    w_out_part = call(
-        functools.partial(w_out_kernel, mp=mp, dp=dp),
-        S((dp, cols, width // dp), BF),
-        [SM] + [HB] * (mp + 1),
-        2,
-        scratch=[pltpu.VMEM((rows_all, width), BF)],
-    )(meta, *cots, turned)
-    w_in_part = call(
-        functools.partial(backward_kernel, mp=mp, dp=dp),
-        S((dp, 4, width // dp, cols), BF),
-        [SM] + [HB] * (mp + 4),
-        6,
-        scratch=[
-            pltpu.VMEM((rows_all, width), BF),
-            pltpu.VMEM((4, rows_all, cols), BF),
-        ],
-        limit=24,
-    )(meta, *cots, w_out, wide, projected, turned)
-    w_out_grad = summed(w_out_part)
-    w_in_grad = summed(w_in_part)
-
-    if short:
-        _, units, ledgers = lax.optimization_barrier((w_in_part, units, ledgers))
-        mail = call(
-            functools.partial(mail_kernel, half=dp // 2, mp=mp, capacity=capacity),
-            [S((dp * capacity, width), BF)] * mp,
-            [SM] + [HB] * len(units) + [VM] * len(ledgers),
-            4,
-            scratch=[pltpu.VMEM((mp * 2 * capacity, 2 * events), BF)],
-        )(meta, *units, *ledgers)
-        landed = exchange(mail, "mp")
-    else:
+        grads = jnp.sum(got.astype(F32), axis=0)
         sending = call(
             functools.partial(send_kernel, **sizes),
             S((slots, width), BF),
-            [SM] + [VM] * 5,
+            [SM] + [VM] * 4,
             3,
-        )(meta, expo, total, total_far, unit_bf, unit_far)
+        )(meta, expo, total, total_far, units_bf)
         landed = [in_half(sending)]
     cat_grad = call(
         functools.partial(spread_kernel, chunk=math.gcd(stock, 128)),
@@ -675,7 +708,7 @@
         out_specs=[HB],
         limit=24,
     )(returning, catalogue, *landed)
-    return (w_in_grad, w_out_grad, cat_grad)
+    return (grads[:4], grads[4].T, cat_grad)
 
 
 def solution(mesh):

time: 313 us -> 211 us (0.67)
  waiting for transfers between devices: 155 us -> 103 us
  local copies, waits for them, and re-layouts: 33.5 us -> 17 us
  blocking collectives: 13.7 us -> 0 us
  between operations: 14.3 us -> 0.92 us
  starting transfers between devices: 55.2 us -> 44.8 us
  Pallas kernels: 34.9 us -> 41.9 us
    ppermute x28 -> x27, waiting for transfers between devices: 150 us -> 103 us  [swapped(): return lax.ppermute(x, axis, [(a, a ^ bit) for a in range(size)])]
    unnamed x88 -> x53, local copies, waits for them, and re-layouts: 33.5 us -> 16.2 us
    all_to_all x1 -> x0, blocking collectives: 13.7 us -> none  [per_device(): lax.all_to_all(packed, 'dp', split_axis=0, concat_axis=0, tiled=True)]
    all_to_all x2 -> x1, starting transfers between devices: 13.6 us -> 5.69 us  [per_device(): lax.all_to_all(packed, 'dp', split_axis=0, concat_axis=0, tiled=True)]
    pallas_call x12 -> x11, Pallas kernels: 34.9 us -> 41.9 us  [run(): pl.pallas_call(kernel, out_shape=outs, in_specs=list(in_specs), out_specs...]
    ppermute x28 -> x27, starting transfers between devices: 36.4 us -> 33.1 us  [swapped(): return lax.ppermute(x, axis, [(a, a ^ bit) for a in range(size)])]
    all_gather x1 -> x0, waiting for transfers between devices: 3.23 us -> none  [per_device(): w_out_all = lax.all_gather(w_out, 'mp', axis=0, tiled=True)]
  transfers between devices with their start and end apart: 32 -> 29, of which waited for: 21 -> 14; matrix products, arithmetic and copies ran while one was open for 1% -> 0% of each run, Pallas kernels for 7% -> 17%
where the time goes in v6:
time: 211 us; the launch traced here: 209 us
  waiting for transfers between devices  103 us (49%)
  starting transfers between devices  44.8 us (21%)
  Pallas kernels  41.9 us (20%)
  local copies, waits for them, and re-layouts  17 us (8%)
    ppermute x27, waiting for transfers between devices, swapped(): return lax.ppermute(x, axis, [(a, a ^ bit) for a in range(size)])  103 us
    pallas_call x11, Pallas kernels, run(): pl.pallas_call(kernel, out_shape=outs, in_specs=list(in_specs), out_specs...  41.9 us
    ppermute x27, starting transfers between devices, swapped(): return lax.ppermute(x, axis, [(a, a ^ bit) for a in range(size)])  33.1 us
    unnamed x53, local copies, waits for them, and re-layouts  16.2 us
    all_to_all x1, starting transfers between devices, in_half(): lax.all_to_all(x.reshape(near, 2 * capacity, width), ('dp', 'mp'), split_...  5.92 us
    all_to_all x1, starting transfers between devices, per_device(): lax.all_to_all(packed, 'dp', split_axis=0, concat_axis=0, tiled=True)  5.69 us
  transfers between devices with their start and end apart: 29, of which 14 were waited for; matrix products, arithmetic and copies ran while one was open for 0% of the time, Pallas kernels for 17%

profile of v6, /device:TPU:13, one launch (start us, length us, event | category | flops | bytes accessed | tf_op | source)
XLA Modules:
  0.0 208.6 jit_solution(17720009500040394523)
XLA Ops:
  1.5 0.9 copy-done.21
  3.8 4.3 %shard_map.103 = (bf16[8,144,256]{2,1,0:T(8,128)(2,1)}, f32[32,128]{1,0:T(8,128)S(1)}) custom-call(s32[258]{0:T(512)S(1)} %pad_add_fusion.refs_0_, bf16[16,32,256]{2,1,0:T(8,128)(2,1)S(1)} %copy-done.21, s32[8,128]{1,0:T(8,128)S(1)} %bitcast.15, s32[8,128]{1,0:T(8,128)S(1)} %bitcast.16), custom_call_target="tpu_custom_call" | custom-call | bytes 13200000 | tf_op jit(solution)/shard_map/pallas_call | solution.py:63
  8.1 5.7 %all-to-all-start = ((bf16[8,144,256]{2,1,0:T(8,128)(2,1)}), bf16[8,144,256]{2,1,0:T(8,128)(2,1)S(1)}, u32[]{:S(2)}, u32[]{:S(2)}) async-start(bf16[8,144,256]{2,1,0:T(8,128)(2,1)} %get-tuple-element.53), calls=%async_computation | async-start | bytes 1179648 | tf_op jit(solution)/shard_map/all_to_all | solution.py:568
  14.0 12.3 %collective-permute-done.refs_7_ = bf16[256,1024]{1,0:T(8,128)(2,1)} collective-permute-done((bf16[256,1024]{1,0:T(8,128)(2,1)}, bf16[256,1024]{1,0:T(8,128)(2,1)}, u32[]{:S(2)}, u32[]{:S(2)}) %collective-permute-start) | collective-permute-done | bytes 524320 | tf_op jit(solution)/shard_map/ppermute | solution.py:503
  26.3 1.0 shard_map.104.refs_1_
  27.5 3.6 %collective-permute-start.1 = (bf16[1152,256]{1,0:T(8,128)(2,1)S(1)}, bf16[1152,256]{1,0:T(8,128)(2,1)S(1)}, u32[]{:S(2)}, u32[]{:S(2)}) collective-permute-start(bf16[1152,256]{1,0:T(8,128)(2,1)S(1)} %shard_map.104.refs_1_), channel_id=1, source_target_pairs={{0,1},{1,0},{2,3},{3,2},{4,5},{5,4},{6,7},{7,6},{8,9},{9,8},{10,11... | collective-permute-start | bytes 1769480 | tf_op jit(solution)/shard_map/ppermute | solution.py:503
  31.1 7.8 %collective-permute-done.2.refs_3_ = bf16[1152,256]{1,0:T(8,128)(2,1)S(1)} collective-permute-done((bf16[1152,256]{1,0:T(8,128)(2,1)S(1)}, bf16[1152,256]{1,0:T(8,128)(2,1)S(1)}, u32[]{:S(2)}, u32[]{:S(2)}) %collective-permute-start.2) | collective-permute-done | bytes 589856 | tf_op jit(solution)/shard_map/ppermute | solution.py:503
  38.9 4.2 %collective-permute-start.3 = (bf16[1152,256]{1,0:T(8,128)(2,1)S(1)}, bf16[1152,256]{1,0:T(8,128)(2,1)S(1)}, u32[]{:S(2)}, u32[]{:S(2)}) collective-permute-start(bf16[1152,256]{1,0:T(8,128)(2,1)S(1)} %collective-permute-done.2.refs_3_), channel_id=1, source_target_pairs={{0,1},{1,0},{2,3},{3,2},{4,5},{5,4},{6,7},{7,6},{8,9},{9,8},{10,11... | collective-permute-start | bytes 1769480 | tf_op jit(solution)/shard_map/ppermute | solution.py:503
  43.1 3.0 %collective-permute-start.4 = (f32[32,128]{1,0:T(8,128)S(1)}, f32[32,128]{1,0:T(8,128)S(1)}, u32[]{:S(2)}, u32[]{:S(2)}) collective-permute-start(f32[32,128]{1,0:T(8,128)S(1)} %get-tuple-element.56.refs_2_), channel_id=1, source_target_pairs={{0,16},{4,20},{8,24},{12,28},{16,0},{20,4},{24,8},{28,12},{1,17},{... | collective-permute-start | bytes 49160 | tf_op jit(solution)/shard_map/ppermute | solution.py:503
  46.1 2.9 %shard_map.105 = (bf16[1536,1024]{1,0:T(8,128)(2,1)S(1)}, s32[1,1536]{1,0:T(1,128)}, s32[1,1536]{1,0:T(1,128)S(1)}) custom-call(s32[258]{0:T(512)S(1)} %pad_add_fusion.refs_0_, bf16[1152,256]{1,0:T(8,128)(2,1)S(1)} %shard_map.104.refs_1_, bf16[1152,256]{1,0:T(8,128)(2,1)S(1)} %collective-permute-done.1.refs_2_, ...), custom_call_target="tpu_custom_call" | custom-call | bytes 13200000 | tf_op jit(solution)/shard_map/pallas_call | solution.py:63
  49.8 1.7 copy-done.5
  51.5 5.9 %all-to-all-start.1 = ((bf16[16,96,1024]{2,1,0:T(8,128)(2,1)}), bf16[16,96,1024]{2,1,0:T(8,128)(2,1)S(1)}, u32[]{:S(2)}, u32[]{:S(2)}) async-start(bf16[16,96,1024]{2,1,0:T(8,128)(2,1)} %bitcast.14), calls=%async_computation.1 | async-start | bytes 6291456 | tf_op jit(solution)/shard_map/all_to_all | solution.py:550
  58.0 1.1 copy-done.1
  59.1 1.1 copy-done.11
  60.1 1.1 copy-done.13
  61.2 1.1 copy-done.15
  62.3 1.6 copy-done.16
  63.8 8.6 %shard_map.106 = (f32[3,1024,256]{2,1,0:T(8,128)S(1)}, bf16[9,1024,256]{2,1,0:T(8,128)(2,1)S(1)}, bf16[1280,1024]{1,0:T(8,128)(2,1)S(1)}, bf16[256,1024]{1,0:T(8...) custom-call(s32[258]{0:T(512)S(1)} %pad_add_fusion.refs_0_, ...), custom_call_target="tpu_custom_call" | custom-call | bytes 33000000 | tf_op jit(solution)/shard_map/pallas_call | solution.py:63
  72.4 2.2 %copy-done.2 = bf16[9,1024,256]{2,1,0:T(8,128)(2,1)} copy-done((bf16[9,1024,256]{2,1,0:T(8,128)(2,1)}, bf16[9,1024,256]{2,1,0:T(8,128)(2,1)S(1)}, u32[]{:S(2)}) %copy-start.2) | copy-done | bytes 4718616
  74.6 1.5 copy-done.8
  76.8 1.5 collective-permute-start.7
  78.3 12.1 %collective-permute-done.6.refs_3_ = bf16[256,256]{1,0:T(8,128)(2,1)S(1)} collective-permute-done((bf16[256,256]{1,0:T(8,128)(2,1)S(1)}, bf16[256,256]{1,0:T(8,128)(2,1)S(1)}, u32[]{:S(2)}, u32[]{:S(2)}) %collective-permute-start.6) | collective-permute-done | bytes 131104 | tf_op jit(solution)/shard_map/ppermute | solution.py:503
  90.4 7.8 %collective-permute-done.7.refs_4_ = bf16[256,256]{1,0:T(8,128)(2,1)S(1)} collective-permute-done((bf16[256,256]{1,0:T(8,128)(2,1)S(1)}, bf16[256,256]{1,0:T(8,128)(2,1)S(1)}, u32[]{:S(2)}, u32[]{:S(2)}) %collective-permute-start.7) | collective-permute-done | bytes 131104 | tf_op jit(solution)/shard_map/ppermute | solution.py:503
  98.2 2.7 %shard_map.107 = (f32[256,1024]{1,0:T(8,128)S(1)}, bf16[256,1024]{1,0:T(8,128)(2,1)}, f32[256,128]{1,0:T(8,128)S(1)}) custom-call(bf16[256,1024]{1,0:T(8,128)(2,1)S(1)} %get-tuple-element.61.refs_0_, bf16[256,256]{1,0:T(8,128)(2,1)S(1)} %get-tuple-element.62.refs_1_, bf16[256,256]{1,0:T(8,128)(2,1)S(1)} %collective-permute-done.5.refs_2_, ...), custom_call_target="tpu_custom_call" | custom-call | bytes 6600000 | tf_op jit(solution)/shard_map/pallas_call | solution.py:63
  100.9 1.0 copy-done.19
  102.1 3.5 %shard_map.108 = (f32[1536,256]{1,0:T(8,128)S(1)}, f32[1536,128]{1,0:T(8,128)S(1)}, f32[1,256]{1,0:T(1,128)S(1)}) custom-call(s32[258]{0:T(512)S(1)} %pad_add_fusion.refs_0_, bf16[1536,1024]{1,0:T(8,128)(2,1)S(1)} %bitcast.10, f32[32,128]{1,0:T(8,128)S(1)} %get-tuple-element.56.refs_2_, f32[32,128]{1,0:T(8,128)S(1)} %collective-permute-done.4.refs_3_, ...), custom_call_target="tpu_custom_call" | custom-call | bytes 13200000 | tf_op jit(solution)/shard_map/pallas_call | solution.py:63
  105.5 1.8 collective-permute-start.10
  107.3 2.5 %collective-permute-start.14 = (bf16[256,1024]{1,0:T(8,128)(2,1)}, bf16[256,1024]{1,0:T(8,128)(2,1)S(1)}, u32[]{:S(2)}, u32[]{:S(2)}) collective-permute-start(bf16[256,1024]{1,0:T(8,128)(2,1)} %get-tuple-element.71.refs_4_.refs_1_), channel_id=1, source_target_pairs={{0,12},{4,8},{8,4},{12,0},{16,28},{20,24},{24,20},{28,16},{1,13},{... | collective-permute-start | bytes 1572872 | tf_op jit(solution)/shard_map/ppermute | solution.py:503
  109.8 5.5 %collective-permute-done.10.refs_7_ = f32[1,256]{1,0:T(1,128)S(1)} collective-permute-done((f32[1,256]{1,0:T(1,128)S(1)}, f32[1,256]{1,0:T(1,128)S(1)}, u32[]{:S(2)}, u32[]{:S(2)}) %collective-permute-start.10) | collective-permute-done | bytes 1056 | tf_op jit(solution)/shard_map/ppermute | solution.py:503
  115.3 2.4 %shard_map.109 = (f32[256,1024]{1,0:T(8,128)S(1)}, bf16[256,1024]{1,0:T(8,128)(2,1)S(1)}, bf16[16,1024]{1,0:T(8,128)(2,1)S(1)}) custom-call(s32[258]{0:T(512)S(1)} %pad_add_fusion.refs_0_, bf16[1536,1024]{1,0:T(8,128)(2,1)S(1)} %bitcast.11, f32[32,128]{1,0:T(8,128)S(1)} %get-tuple-element.56.refs_2_, f32[32,128]{1,0:T(8,128)S(1)} %collective-permute-done.4.refs_3_, ...), custom_call_target="tpu_custom_call" | custom-call | bytes 9900000 | tf_op jit(solution)/shard_map/pallas_call | solution.py:63
  117.9 1.2 collective-permute-start.15
  119.1 2.1 %collective-permute-start.16 = (bf16[16,1024]{1,0:T(8,128)(2,1)S(1)}, bf16[16,1024]{1,0:T(8,128)(2,1)S(1)}, u32[]{:S(2)}, u32[]{:S(2)}) collective-permute-start(bf16[16,1024]{1,0:T(8,128)(2,1)S(1)} %get-tuple-element.77.refs_5_), channel_id=1, source_target_pairs={{0,8},{4,12},{8,0},{12,4},{16,24},{20,28},{24,16},{28,20},{1,9},{5... | collective-permute-start | bytes 98312 | tf_op jit(solution)/shard_map/ppermute | solution.py:503
  121.3 10.9 %collective-permute-done.14.refs_4_ = bf16[256,1024]{1,0:T(8,128)(2,1)S(1)} collective-permute-done((bf16[256,1024]{1,0:T(8,128)(2,1)}, bf16[256,1024]{1,0:T(8,128)(2,1)S(1)}, u32[]{:S(2)}, u32[]{:S(2)}) %collective-permute-start.14) | collective-permute-done | bytes 524320 | tf_op jit(solution)/shard_map/ppermute | solution.py:503
  132.2 6.5 %collective-permute-done.16.refs_7_ = bf16[16,1024]{1,0:T(8,128)(2,1)S(1)} collective-permute-done((bf16[16,1024]{1,0:T(8,128)(2,1)S(1)}, bf16[16,1024]{1,0:T(8,128)(2,1)S(1)}, u32[]{:S(2)}, u32[]{:S(2)}) %collective-permute-start.16) | collective-permute-done | bytes 32800 | tf_op jit(solution)/shard_map/ppermute | solution.py:503
  138.7 1.3 collective-permute-done.17.refs_8_
  140.0 2.4 %shard_map.110 = (bf16[384,1024]{1,0:T(8,128)(2,1)S(1)}, bf16[384,1024]{1,0:T(8,128)(2,1)S(1)}, bf16[384,1024]{1,0:T(8,128)(2,1)S(1)}, bf16[384,1024]{1,0:T(8,128)(2,1)S(1)}) custom-call(s32[258]{0:T(512)S(1)} %pad_add_fusion.refs_0_, bf16[256,1024]{1,0:T(8,128)(2,1)} %get-tuple-element.71.refs_4_.refs_1_, ...), custom_call_target="tpu_custom_call" | custom-call | bytes 13200000 | tf_op jit(solution)/shard_map/pallas_call | solution.py:63
  142.8 1.7 collective-permute-start.21
  144.5 1.7 collective-permute-start.22
  146.6 8.0 %collective-permute-done.19.refs_3_ = bf16[256,1024]{1,0:T(8,128)(2,1)S(1)} collective-permute-done((bf16[256,1024]{1,0:T(8,128)(2,1)S(1)}, bf16[256,1024]{1,0:T(8,128)(2,1)S(1)}, u32[]{:S(2)}, u32[]{:S(2)}) %collective-permute-start.19) | collective-permute-done | bytes 524320 | tf_op jit(solution)/shard_map/ppermute | solution.py:503
  154.6 4.7 %collective-permute-start.20 = (bf16[256,1024]{1,0:T(8,128)(2,1)S(1)}, bf16[256,1024]{1,0:T(8,128)(2,1)S(1)}, u32[]{:S(2)}, u32[]{:S(2)}) collective-permute-start(bf16[256,1024]{1,0:T(8,128)(2,1)S(1)} %collective-permute-done.19.refs_3_), channel_id=1, source_target_pairs={{0,1},{1,0},{2,3},{3,2},{4,5},{5,4},{6,7},{7,6},{8,9},{9,8},{10,11... | collective-permute-start | bytes 1572872 | tf_op jit(solution)/shard_map/ppermute | solution.py:503
  159.3 1.5 collective-permute-done.20.refs_4_
  160.9 9.5 %shard_map.112 = (bf16[5,128,256]{2,1,0:T(8,128)(2,1)S(1)}, bf16[5,128,256]{2,1,0:T(8,128)(2,1)S(1)}, bf16[5,128,256]{2,1,0:T(8,128)(2,1)S(1)}, bf16[5,128,256]{2,1,0:T(8,128)(2,1)S(1)}) custom-call(s32[258]{0:T(512)S(1)} %pad_add_fusion.refs_0_, bf16[256,1024]{1,0:T(8,128)(2,1)S(1)} %shard_map.111.refs_1_, ...), custom_call_target="tpu_custom_call" | custom-call | bytes 33000000 | tf_op jit(solution)/shard_map/pallas_call | solution.py:63
  170.4 1.0 collective-permute-done.22.refs_4_
  171.5 18.7 %collective-permute-done.23.refs_5_ = bf16[384,1024]{1,0:T(8,128)(2,1)S(1)} collective-permute-done((bf16[384,1024]{1,0:T(8,128)(2,1)S(1)}, bf16[384,1024]{1,0:T(8,128)(2,1)S(1)}, u32[]{:S(2)}, u32[]{:S(2)}) %collective-permute-start.23) | collective-permute-done | bytes 786464 | tf_op jit(solution)/shard_map/ppermute | solution.py:503
  190.2 1.8 collective-permute-start.25
  192.8 4.4 %shard_map.113 = f32[512,1024]{1,0:T(8,128)} custom-call(s32[1,1536]{1,0:T(1,128)S(1)} %get-tuple-element.98.refs_0_, bf16[512,1024]{1,0:T(8,128)(2,1)S(1)} %copy-done.4, bf16[384,1024]{1,0:T(8,128)(2,1)S(1)} %get-tuple-element.99.refs_2_, bf16[384,1024]{1,0:T(8,128)(2,1)S(1)} %collective-permute-done.21.refs_3_, ...), custom_call_target="tpu_custom_call" | custom-call | bytes 13200000 | tf_op jit(solution)/shard_map/pallas_call | solution.py:63
  197.2 3.3 %collective-permute-done.26 = bf16[5,128,256]{2,1,0:T(8,128)(2,1)S(1)} collective-permute-done((bf16[5,128,256]{2,1,0:T(8,128)(2,1)S(1)}, bf16[5,128,256]{2,1,0:T(8,128)(2,1)S(1)}, u32[]{:S(2)}, u32[]{:S(2)}) %collective-permute-start.26) | collective-permute-done | bytes 327712 | tf_op jit(solution)/shard_map/ppermute | solution.py:503
  200.6 6.3 %collective-permute-done.25 = bf16[5,128,256]{2,1,0:T(8,128)(2,1)S(1)} collective-permute-done((bf16[5,128,256]{2,1,0:T(8,128)(2,1)S(1)}, bf16[5,128,256]{2,1,0:T(8,128)(2,1)S(1)}, u32[]{:S(2)}, u32[]{:S(2)}) %collective-permute-start.25) | collective-permute-done | bytes 327712 | tf_op jit(solution)/shard_map/ppermute | solution.py:503
  (79 shorter events, 8.7 us)
Async XLA Ops:
  0.6 45.4 %copy-start.3 = (bf16[512,1024]{1,0:T(8,128)(2,1)S(1)}, bf16[512,1024]{1,0:T(8,128)(2,1)}, u32[]{:S(2)}) copy-start(bf16[512,1024]{1,0:T(8,128)(2,1)} %refs_1_.3) | copy-start | bytes 3145732
  8.1 18.2 %all-to-all-start = ((bf16[8,144,256]{2,1,0:T(8,128)(2,1)}), bf16[8,144,256]{2,1,0:T(8,128)(2,1)S(1)}, u32[]{:S(2)}, u32[]{:S(2)}) async-start(bf16[8,144,256]{2,1,0:T(8,128)(2,1)} %get-tuple-element.53), calls=%async_computation | async-start | bytes 1179648 | tf_op jit(solution)/shard_map/all_to_all | solution.py:568
  13.8 12.5 %collective-permute-start = (bf16[256,1024]{1,0:T(8,128)(2,1)}, bf16[256,1024]{1,0:T(8,128)(2,1)}, u32[]{:S(2)}, u32[]{:S(2)}) collective-permute-start(bf16[256,1024]{1,0:T(8,128)(2,1)} %refs_5_.7), channel_id=1, source_target_pairs={{0,2},{1,3},{2,0},{3,1},{4,6},{5,7},{6,4},{7,5},{8,10},{9,11},{10,... | collective-permute-start | bytes 1572872 | tf_op jit(solution)/shard_map/ppermute | solution.py:503
  27.2 11.6 %collective-permute-start.2 = (bf16[1152,256]{1,0:T(8,128)(2,1)S(1)}, bf16[1152,256]{1,0:T(8,128)(2,1)S(1)}, u32[]{:S(2)}, u32[]{:S(2)}) collective-permute-start(bf16[1152,256]{1,0:T(8,128)(2,1)S(1)} %shard_map.104.refs_1_), channel_id=1, source_target_pairs={{0,2},{1,3},{2,0},{3,1},{4,6},{5,7},{6,4},{7,5},{8,10},{9,11},{10,... | collective-permute-start | bytes 1769480 | tf_op jit(solution)/shard_map/ppermute | solution.py:503
  27.5 18.5 %collective-permute-start.1 = (bf16[1152,256]{1,0:T(8,128)(2,1)S(1)}, bf16[1152,256]{1,0:T(8,128)(2,1)S(1)}, u32[]{:S(2)}, u32[]{:S(2)}) collective-permute-start(bf16[1152,256]{1,0:T(8,128)(2,1)S(1)} %shard_map.104.refs_1_), channel_id=1, source_target_pairs={{0,1},{1,0},{2,3},{3,2},{4,5},{5,4},{6,7},{7,6},{8,9},{9,8},{10,11... | collective-permute-start | bytes 1769480 | tf_op jit(solution)/shard_map/ppermute | solution.py:503
  38.9 10.1 %copy-start.10 = (bf16[1152,256]{1,0:T(8,128)(2,1)}, bf16[1152,256]{1,0:T(8,128)(2,1)S(1)}, u32[]{:S(2)}) copy-start(bf16[1152,256]{1,0:T(8,128)(2,1)S(1)} %collective-permute-done.2.refs_3_) | copy-start | bytes 1769476
  38.9 7.2 %collective-permute-start.3 = (bf16[1152,256]{1,0:T(8,128)(2,1)S(1)}, bf16[1152,256]{1,0:T(8,128)(2,1)S(1)}, u32[]{:S(2)}, u32[]{:S(2)}) collective-permute-start(bf16[1152,256]{1,0:T(8,128)(2,1)S(1)} %collective-permute-done.2.refs_3_), channel_id=1, source_target_pairs={{0,1},{1,0},{2,3},{3,2},{4,5},{5,4},{6,7},{7,6},{8,9},{9,8},{10,11... | collective-permute-start | bytes 1769480 | tf_op jit(solution)/shard_map/ppermute | solution.py:503
  43.1 8.4 %collective-permute-start.4 = (f32[32,128]{1,0:T(8,128)S(1)}, f32[32,128]{1,0:T(8,128)S(1)}, u32[]{:S(2)}, u32[]{:S(2)}) collective-permute-start(f32[32,128]{1,0:T(8,128)S(1)} %get-tuple-element.56.refs_2_), channel_id=1, source_target_pairs={{0,16},{4,20},{8,24},{12,28},{16,0},{20,4},{24,8},{28,12},{1,17},{... | collective-permute-start | bytes 49160 | tf_op jit(solution)/shard_map/ppermute | solution.py:503
  46.1 5.4 %copy-start.12 = (bf16[1152,256]{1,0:T(8,128)(2,1)}, bf16[1152,256]{1,0:T(8,128)(2,1)S(1)}, u32[]{:S(2)}) copy-start(bf16[1152,256]{1,0:T(8,128)(2,1)S(1)} %collective-permute-done.1.refs_2_) | copy-start | bytes 1769476
  46.1 5.4 %copy-start.14 = (bf16[1152,256]{1,0:T(8,128)(2,1)}, bf16[1152,256]{1,0:T(8,128)(2,1)S(1)}, u32[]{:S(2)}) copy-start(bf16[1152,256]{1,0:T(8,128)(2,1)S(1)} %collective-permute-done.3.refs_4_) | copy-start | bytes 1769476
  49.8 1.7 copy-start.5
  51.5 50.6 %all-to-all-start.1 = ((bf16[16,96,1024]{2,1,0:T(8,128)(2,1)}), bf16[16,96,1024]{2,1,0:T(8,128)(2,1)S(1)}, u32[]{:S(2)}, u32[]{:S(2)}) async-start(bf16[16,96,1024]{2,1,0:T(8,128)(2,1)} %bitcast.14), calls=%async_computation.1 | async-start | bytes 6291456 | tf_op jit(solution)/shard_map/all_to_all | solution.py:550
  57.4 20.9 %collective-permute-start.8 = (bf16[256,1024]{1,0:T(8,128)(2,1)}, bf16[256,1024]{1,0:T(8,128)(2,1)S(1)}, u32[]{:S(2)}, u32[]{:S(2)}) collective-permute-start(bf16[256,1024]{1,0:T(8,128)(2,1)} %refs_5_.7), channel_id=1, source_target_pairs={{0,1},{1,0},{2,3},{3,2},{4,5},{5,4},{6,7},{7,6},{8,9},{9,8},{10,11... | collective-permute-start | bytes 1572872 | tf_op jit(solution)/shard_map/ppermute | solution.py:503
  57.8 20.5 %collective-permute-start.9 = (bf16[256,1024]{1,0:T(8,128)(2,1)}, bf16[256,1024]{1,0:T(8,128)(2,1)S(1)}, u32[]{:S(2)}, u32[]{:S(2)}) collective-permute-start(bf16[256,1024]{1,0:T(8,128)(2,1)} %collective-permute-done.refs_7_), channel_id=1, source_target_pairs={{0,1},{1,0},{2,3},{3,2},{4,5},{5,4},{6,7},{7,6},{8,9},{9,8},{10,11... | collective-permute-start | bytes 1572872 | tf_op jit(solution)/shard_map/ppermute | solution.py:503
  58.0 1.1 copy-start.1
  59.1 1.1 copy-start.11
  62.2 1.6 copy-start.16
  63.8 34.3 %copy-start.17 = (bf16[256,1024]{1,0:T(8,128)(2,1)S(1)}, bf16[256,1024]{1,0:T(8,128)(2,1)}, u32[]{:S(2)}) copy-start(bf16[256,1024]{1,0:T(8,128)(2,1)} %refs_5_.7) | copy-start | bytes 1572868
  72.4 2.2 %copy-start.2 = (bf16[9,1024,256]{2,1,0:T(8,128)(2,1)}, bf16[9,1024,256]{2,1,0:T(8,128)(2,1)S(1)}, u32[]{:S(2)}) copy-start(bf16[9,1024,256]{2,1,0:T(8,128)(2,1)S(1)} %get-tuple-element.84.refs_7_) | copy-start | bytes 14155780
  74.6 1.5 copy-start.8
  76.1 25.8 %copy-start.6 = (f32[3,1024,256]{2,1,0:T(8,128)}, f32[3,1024,256]{2,1,0:T(8,128)S(1)}, u32[]{:S(2)}) copy-start(f32[3,1024,256]{2,1,0:T(8,128)S(1)} %get-tuple-element.83.refs_6_) | copy-start | bytes 9437188
  76.1 2.2 %collective-permute-start.5 = (bf16[256,256]{1,0:T(8,128)(2,1)S(1)}, bf16[256,256]{1,0:T(8,128)(2,1)S(1)}, u32[]{:S(2)}, u32[]{:S(2)}) collective-permute-start(bf16[256,256]{1,0:T(8,128)(2,1)S(1)} %get-tuple-element.63), channel_id=1, source_target_pairs={{0,1},{1,0},{2,3},{3,2},{4,5},{5,4},{6,7},{7,6},{8,9},{9,8},{10,11... | collective-permute-start | bytes 393224 | tf_op jit(solution)/shard_map/ppermute | solution.py:503
  76.5 13.9 %collective-permute-start.6 = (bf16[256,256]{1,0:T(8,128)(2,1)S(1)}, bf16[256,256]{1,0:T(8,128)(2,1)S(1)}, u32[]{:S(2)}, u32[]{:S(2)}) collective-permute-start(bf16[256,256]{1,0:T(8,128)(2,1)S(1)} %get-tuple-element.64), channel_id=1, source_target_pairs={{0,2},{1,3},{2,0},{3,1},{4,6},{5,7},{6,4},{7,5},{8,10},{9,11},{10,... | collective-permute-start | bytes 393224 | tf_op jit(solution)/shard_map/ppermute | solution.py:503
  76.8 21.4 %collective-permute-start.7 = (bf16[256,256]{1,0:T(8,128)(2,1)S(1)}, bf16[256,256]{1,0:T(8,128)(2,1)S(1)}, u32[]{:S(2)}, u32[]{:S(2)}) collective-permute-start(bf16[256,256]{1,0:T(8,128)(2,1)S(1)} %get-tuple-element.65), channel_id=1, source_target_pairs={{0,3},{1,2},{2,1},{3,0},{4,7},{5,6},{6,5},{7,4},{8,11},{9,10},{10,... | collective-permute-start | bytes 393224 | tf_op jit(solution)/shard_map/ppermute | solution.py:503
  101.9 17.2 %collective-permute-start.12 = (bf16[256,1024]{1,0:T(8,128)(2,1)}, bf16[256,1024]{1,0:T(8,128)(2,1)}, u32[]{:S(2)}, u32[]{:S(2)}) collective-permute-start(bf16[256,1024]{1,0:T(8,128)(2,1)} %get-tuple-element.71.refs_4_.refs_1_), channel_id=1, source_target_pairs={{0,4},{4,0},{8,12},{12,8},{16,20},{20,16},{24,28},{28,24},{1,5},{5... | collective-permute-start | bytes 1572872 | tf_op jit(solution)/shard_map/ppermute | solution.py:503
  101.9 19.3 %collective-permute-start.13 = (bf16[256,1024]{1,0:T(8,128)(2,1)}, bf16[256,1024]{1,0:T(8,128)(2,1)}, u32[]{:S(2)}, u32[]{:S(2)}) collective-permute-start(bf16[256,1024]{1,0:T(8,128)(2,1)} %get-tuple-element.71.refs_4_.refs_1_), channel_id=1, source_target_pairs={{0,8},{4,12},{8,0},{12,4},{16,24},{20,28},{24,16},{28,20},{1,9},{5... | collective-permute-start | bytes 1572872 | tf_op jit(solution)/shard_map/ppermute | solution.py:503
  102.1 40.3 %copy-start.20 = (f32[256,1024]{1,0:T(8,128)S(1)}, f32[256,1024]{1,0:T(8,128)}, u32[]{:S(2)}) copy-start(f32[256,1024]{1,0:T(8,128)} %copy-done.19) | copy-start | bytes 3145732
  105.5 9.8 %collective-permute-start.10 = (f32[1,256]{1,0:T(1,128)S(1)}, f32[1,256]{1,0:T(1,128)S(1)}, u32[]{:S(2)}, u32[]{:S(2)}) collective-permute-start(f32[1,256]{1,0:T(1,128)S(1)} %get-tuple-element.74.refs_6_), channel_id=1, source_target_pairs={{0,16},{4,20},{8,24},{12,28},{16,0},{20,4},{24,8},{28,12},{1,17},{... | collective-permute-start | bytes 3080 | tf_op jit(solution)/shard_map/ppermute | solution.py:503
  107.3 24.9 %collective-permute-start.14 = (bf16[256,1024]{1,0:T(8,128)(2,1)}, bf16[256,1024]{1,0:T(8,128)(2,1)S(1)}, u32[]{:S(2)}, u32[]{:S(2)}) collective-permute-start(bf16[256,1024]{1,0:T(8,128)(2,1)} %get-tuple-element.71.refs_4_.refs_1_), channel_id=1, source_target_pairs={{0,12},{4,8},{8,4},{12,0},{16,28},{20,24},{24,20},{28,16},{1,13},{... | collective-permute-start | bytes 1572872 | tf_op jit(solution)/shard_map/ppermute | solution.py:503
  115.3 45.5 %slice-start = ((s8[4718592]{0:T(1024)(128)(4,1)}), s8[4194304]{0:T(1024)(128)(4,1)S(1)}, s32[]{:S(2)}) async-start(s8[4718592]{0:T(1024)(128)(4,1)} %bitcast.12), calls=%async_computation.2 | async-start | bytes 8388608
  115.3 45.5 %slice-start.1 = ((s8[4718592]{0:T(1024)(128)(4,1)}), s8[524288]{0:T(1024)(128)(4,1)S(1)}, s32[]{:S(2)}) async-start(s8[4718592]{0:T(1024)(128)(4,1)} %bitcast.12), calls=%async_computation.3 | async-start | bytes 1048576
  115.3 45.5 %copy-start.9 = (bf16[1280,1024]{1,0:T(8,128)(2,1)S(1)}, bf16[1280,1024]{1,0:T(8,128)(2,1)}, u32[]{:S(2)}) copy-start(bf16[1280,1024]{1,0:T(8,128)(2,1)} %copy-done.8) | copy-start | bytes 7864324
  117.8 43.1 %copy-start.7 = (f32[3,1024,256]{2,1,0:T(8,128)S(1)}, f32[3,1024,256]{2,1,0:T(8,128)}, u32[]{:S(2)}) copy-start(f32[3,1024,256]{2,1,0:T(8,128)} %copy-done.6) | copy-start | bytes 9437188
  117.8 43.1 %copy-start.18 = (bf16[256,1024]{1,0:T(8,128)(2,1)S(1)}, bf16[256,1024]{1,0:T(8,128)(2,1)}, u32[]{:S(2)}) copy-start(bf16[256,1024]{1,0:T(8,128)(2,1)} %refs_5_.7) | copy-start | bytes 1572868
  117.8 24.6 %collective-permute-start.11 = (bf16[256,1024]{1,0:T(8,128)(2,1)S(1)}, bf16[256,1024]{1,0:T(8,128)(2,1)S(1)}, u32[]{:S(2)}, u32[]{:S(2)}) collective-permute-start(bf16[256,1024]{1,0:T(8,128)(2,1)S(1)} %get-tuple-element.76), channel_id=1, source_target_pairs={{0,16},{4,20},{8,24},{12,28},{16,0},{20,4},{24,8},{28,12},{1,17},{... | collective-permute-start | bytes 1572872 | tf_op jit(solution)/shard_map/ppermute | solution.py:503
  117.9 14.3 %collective-permute-start.15 = (bf16[16,1024]{1,0:T(8,128)(2,1)S(1)}, bf16[16,1024]{1,0:T(8,128)(2,1)S(1)}, u32[]{:S(2)}, u32[]{:S(2)}) collective-permute-start(bf16[16,1024]{1,0:T(8,128)(2,1)S(1)} %get-tuple-element.77.refs_5_), channel_id=1, source_target_pairs={{0,4},{4,0},{8,12},{12,8},{16,20},{20,16},{24,28},{28,24},{1,5},{5... | collective-permute-start | bytes 98312 | tf_op jit(solution)/shard_map/ppermute | solution.py:503
  119.1 19.7 %collective-permute-start.16 = (bf16[16,1024]{1,0:T(8,128)(2,1)S(1)}, bf16[16,1024]{1,0:T(8,128)(2,1)S(1)}, u32[]{:S(2)}, u32[]{:S(2)}) collective-permute-start(bf16[16,1024]{1,0:T(8,128)(2,1)S(1)} %get-tuple-element.77.refs_5_), channel_id=1, source_target_pairs={{0,8},{4,12},{8,0},{12,4},{16,24},{20,28},{24,16},{28,20},{1,9},{5... | collective-permute-start | bytes 98312 | tf_op jit(solution)/shard_map/ppermute | solution.py:503
  121.2 18.8 %collective-permute-start.17 = (bf16[16,1024]{1,0:T(8,128)(2,1)S(1)}, bf16[16,1024]{1,0:T(8,128)(2,1)S(1)}, u32[]{:S(2)}, u32[]{:S(2)}) collective-permute-start(bf16[16,1024]{1,0:T(8,128)(2,1)S(1)} %get-tuple-element.77.refs_5_), channel_id=1, source_target_pairs={{0,12},{4,8},{8,4},{12,0},{16,28},{20,24},{24,20},{28,16},{1,13},{... | collective-permute-start | bytes 98312 | tf_op jit(solution)/shard_map/ppermute | solution.py:503
  142.8 11.8 %collective-permute-start.19 = (bf16[256,1024]{1,0:T(8,128)(2,1)S(1)}, bf16[256,1024]{1,0:T(8,128)(2,1)S(1)}, u32[]{:S(2)}, u32[]{:S(2)}) collective-permute-start(bf16[256,1024]{1,0:T(8,128)(2,1)S(1)} %shard_map.111.refs_1_), channel_id=1, source_target_pairs={{0,2},{1,3},{2,0},{3,1},{4,6},{5,7},{6,4},{7,5},{8,10},{9,11},{10,... | collective-permute-start | bytes 1572872 | tf_op jit(solution)/shard_map/ppermute | solution.py:503
  142.8 27.6 %collective-permute-start.21 = (bf16[384,1024]{1,0:T(8,128)(2,1)S(1)}, bf16[384,1024]{1,0:T(8,128)(2,1)S(1)}, u32[]{:S(2)}, u32[]{:S(2)}) collective-permute-start(bf16[384,1024]{1,0:T(8,128)(2,1)S(1)} %get-tuple-element.91), channel_id=1, source_target_pairs={{0,1},{1,0},{2,3},{3,2},{4,5},{5,4},{6,7},{7,6},{8,9},{9,8},{10,11... | collective-permute-start | bytes 2359304 | tf_op jit(solution)/shard_map/ppermute | solution.py:503
  144.5 26.9 %collective-permute-start.22 = (bf16[384,1024]{1,0:T(8,128)(2,1)S(1)}, bf16[384,1024]{1,0:T(8,128)(2,1)S(1)}, u32[]{:S(2)}, u32[]{:S(2)}) collective-permute-start(bf16[384,1024]{1,0:T(8,128)(2,1)S(1)} %get-tuple-element.92), channel_id=1, source_target_pairs={{0,2},{1,3},{2,0},{3,1},{4,6},{5,7},{6,4},{7,5},{8,10},{9,11},{10,... | collective-permute-start | bytes 2359304 | tf_op jit(solution)/shard_map/ppermute | solution.py:503
  146.2 44.0 %collective-permute-start.23 = (bf16[384,1024]{1,0:T(8,128)(2,1)S(1)}, bf16[384,1024]{1,0:T(8,128)(2,1)S(1)}, u32[]{:S(2)}, u32[]{:S(2)}) collective-permute-start(bf16[384,1024]{1,0:T(8,128)(2,1)S(1)} %get-tuple-element.93), channel_id=1, source_target_pairs={{0,3},{1,2},{2,1},{3,0},{4,7},{5,6},{6,5},{7,4},{8,11},{9,10},{10,... | collective-permute-start | bytes 2359304 | tf_op jit(solution)/shard_map/ppermute | solution.py:503
  146.3 13.1 %collective-permute-start.18 = (bf16[256,1024]{1,0:T(8,128)(2,1)S(1)}, bf16[256,1024]{1,0:T(8,128)(2,1)S(1)}, u32[]{:S(2)}, u32[]{:S(2)}) collective-permute-start(bf16[256,1024]{1,0:T(8,128)(2,1)S(1)} %shard_map.111.refs_1_), channel_id=1, source_target_pairs={{0,1},{1,0},{2,3},{3,2},{4,5},{5,4},{6,7},{7,6},{8,9},{9,8},{10,11... | collective-permute-start | bytes 1572872 | tf_op jit(solution)/shard_map/ppermute | solution.py:503
  154.6 6.2 %collective-permute-start.20 = (bf16[256,1024]{1,0:T(8,128)(2,1)S(1)}, bf16[256,1024]{1,0:T(8,128)(2,1)S(1)}, u32[]{:S(2)}, u32[]{:S(2)}) collective-permute-start(bf16[256,1024]{1,0:T(8,128)(2,1)S(1)} %collective-permute-done.19.refs_3_), channel_id=1, source_target_pairs={{0,1},{1,0},{2,3},{3,2},{4,5},{5,4},{6,7},{7,6},{8,9},{9,8},{10,11... | collective-permute-start | bytes 1572872 | tf_op jit(solution)/shard_map/ppermute | solution.py:503
  160.9 31.9 %copy-start.4 = (bf16[512,1024]{1,0:T(8,128)(2,1)S(1)}, bf16[512,1024]{1,0:T(8,128)(2,1)}, u32[]{:S(2)}) copy-start(bf16[512,1024]{1,0:T(8,128)(2,1)} %refs_1_.3) | copy-start | bytes 3145732
  190.2 10.4 %collective-permute-start.26 = (bf16[5,128,256]{2,1,0:T(8,128)(2,1)S(1)}, bf16[5,128,256]{2,1,0:T(8,128)(2,1)S(1)}, u32[]{:S(2)}, u32[]{:S(2)}) collective-permute-start(bf16[5,128,256]{2,1,0:T(8,128)(2,1)S(1)} %get-tuple-element.97), channel_id=1, source_target_pairs={{0,12},{4,8},{8,4},{12,0},{16,28},{20,24},{24,20},{28,16},{1,13},{... | collective-permute-start | bytes 983048 | tf_op jit(solution)/shard_map/ppermute | solution.py:503
  190.2 16.6 %collective-permute-start.25 = (bf16[5,128,256]{2,1,0:T(8,128)(2,1)S(1)}, bf16[5,128,256]{2,1,0:T(8,128)(2,1)S(1)}, u32[]{:S(2)}, u32[]{:S(2)}) collective-permute-start(bf16[5,128,256]{2,1,0:T(8,128)(2,1)S(1)} %get-tuple-element.96), channel_id=1, source_target_pairs={{0,8},{4,12},{8,0},{12,4},{16,24},{20,28},{24,16},{28,20},{1,9},{5... | collective-permute-start | bytes 983048 | tf_op jit(solution)/shard_map/ppermute | solution.py:503
  192.0 14.8 %collective-permute-start.24 = (bf16[5,128,256]{2,1,0:T(8,128)(2,1)S(1)}, bf16[5,128,256]{2,1,0:T(8,128)(2,1)S(1)}, u32[]{:S(2)}, u32[]{:S(2)}) collective-permute-start(bf16[5,128,256]{2,1,0:T(8,128)(2,1)S(1)} %get-tuple-element.95), channel_id=1, source_target_pairs={{0,4},{4,0},{8,12},{12,8},{16,20},{20,16},{24,28},{28,24},{1,5},{5... | collective-permute-start | bytes 983048 | tf_op jit(solution)/shard_map/ppermute | solution.py:503
  (7 other events, 6.2 us)

commit v7 on v6

--- a/solution.py
+++ b/solution.py
@@ -22,7 +22,7 @@
 HB = pl.BlockSpec(memory_space=pltpu.HBM)
 
 
-def call(body, out_shape, in_specs, us, scratch=(), limit=16, out_specs=None):
+def call(body, out_shape, in_specs, us, scratch=(), limit=16, out_specs=None, lazy=False):
     many = isinstance(out_shape, (list, tuple))
     outs = list(out_shape) if many else [out_shape]
     out_specs = list(out_specs or [VM] * len(outs))
@@ -47,14 +47,21 @@
                 ins[n] = held[m]
             for c in copies:
                 c.start()
-            for c in copies:
-                c.wait()
+            arriving = dict(zip(far_in, copies))
+
+            def ready(*places):
+                for n in places:
+                    arriving.pop(n).wait()
+
+            more = {"ready": ready} if lazy else {}
+            if not lazy:
+                ready(*far_in)
             copies = []
             for m, n in enumerate(far_out):
                 m += len(far_in)
                 copies.append(pltpu.make_async_copy(held[m], res[n], sems.at[m]))
                 res[n] = held[m]
-            body(*ins, *res, *own)
+            body(*ins, *res, *own, **more)
             for c in copies:
                 c.start()
             for c in copies:
@@ -150,7 +157,7 @@
         out[d, 2 * per_peer * steps :, :] = jnp.concatenate(digits, axis=0).astype(BF)
 
 
-def take_kernel(meta, arrived, out, *, dp, seq_dev, per_peer, steps):
+def take_kernel(meta, arrived, out, digits, *, dp, seq_dev, per_peer, steps):
     for side in range(2):
         block = jnp.bitwise_xor(meta[0], side * (dp // 2))
         anchors = [lax.div(meta[2 + block * seq_dev + k], seq_dev) for k in range(seq_dev)]
@@ -161,9 +168,8 @@
             start = pl.multiple_of(rank * steps, steps)
             at = (side * seq_dev + k) * steps
             out[at : at + steps, :] = arrived[anchors[k], pl.ds(start, steps), :]
-    base = 2 * seq_dev * steps
     for d in range(dp):
-        out[base + d * 16 : base + (d + 1) * 16, :] = arrived[d, 2 * per_peer * steps :, :]
+        digits[d * 16 : (d + 1) * 16, :] = arrived[d, 2 * per_peer * steps :, :]
 
 
 def forward_kernel(meta, *refs, mp, dp, seqs, seq_dev, steps, width, cols, quarter):
@@ -183,7 +189,7 @@
     rows_all = 2 * half_rows
     for j in range(mp):
         start = pl.multiple_of(jnp.bitwise_xor(here_mp, j) * part, part)
-        feat[:, pl.ds(start, part)] = blocks[j][:rows_all, :]
+        feat[:, pl.ds(start, part)] = blocks[j][...]
     for side in range(2):
         start = pl.multiple_of(side * half_rows + here_mp * quarter, quarter)
         own[side * quarter : (side + 1) * quarter, :] = feat[pl.ds(start, quarter), :]
@@ -252,9 +258,8 @@
 def look_kernel(meta, *refs, mp, dp, capacity, chunk, share):
     blocks, catalogue, looked, incoming, returning, digits, asked = refs[:mp], *refs[mp:]
     stock, _ = catalogue.shape
-    base = blocks[0].shape[0] - 16 * dp
     for j in range(mp):
-        digits[...] = blocks[j][base:, :].astype(F32)
+        digits[...] = blocks[j][...].astype(F32)
         for d in range(dp):
             high = digits[pl.ds(d * 16 + meta[1], 1), :]
             low = digits[pl.ds(d * 16 + 8 + meta[1], 1), :]
@@ -498,6 +503,16 @@
                     outs[j][c] = piece
 
 
+def sum_kernel(*refs):
+    parts, w_in_grad, w_out_grad = refs[:-2], *refs[-2:]
+    for c in range(5):
+        total = sum(p[c].astype(F32) for p in parts)
+        if c < 4:
+            w_in_grad[c] = total
+        else:
+            w_out_grad[...] = total.T
+
+
 def swapped(x, axis, bit):
     size = lax.axis_size(axis)
     return lax.ppermute(x, axis, [(a, a ^ bit) for a in range(size)])
@@ -562,29 +577,34 @@
             pack_kernel, dp=dp, seq_dev=seq_dev, per_peer=per_peer, mp=mp, capacity=capacity
         ),
         [S((dp, 2 * per_peer * steps + 16, part), BF), S((devices, events), F32)],
-        [SM, VM, VM, VM],
+        [SM, HB, HB, HB],
         4,
+        limit=58,
     )(meta, history, owners.T, item_rows.T)
     arrived = lax.all_to_all(packed, "dp", split_axis=0, concat_axis=0, tiled=True)
     arrived, w_out_y = lax.optimization_barrier((arrived, w_out_y))
-    rows = call(
+    rows, digits = call(
         functools.partial(take_kernel, dp=dp, seq_dev=seq_dev, per_peer=per_peer, steps=steps),
-        S((2 * rows_all + 16 * dp, part), BF),
+        [S((2 * rows_all, part), BF), S((16 * dp, part), BF)],
         [SM, VM],
         1,
     )(meta, arrived)
-    features = gather_blocks(rows, "mp")
+    digits_y = swapped(digits, "mp", mp // 2)
+    rows, digits_y = lax.optimization_barrier((rows, digits_y))
+    rows_y = swapped(rows, "mp", mp // 2)
+    digits = gather_blocks(digits, "mp", digits_y)
     code_far = partner(code)
     looked, incoming, returning = call(
         functools.partial(
             look_kernel, mp=mp, dp=dp, capacity=capacity, chunk=chunk, share=short
         ),
         [S((slots, width), BF), S((1, slots), I32), S((1, slots), I32)],
-        [SM] + [VM] * mp + [HB],
+        [SM] + [VM] * mp + [VM],
         4,
         scratch=[pltpu.VMEM((16 * dp, part), F32), pltpu.VMEM((devices, capacity), F32)],
-    )(meta, *features, catalogue)
-    looked, features, code_far = lax.optimization_barrier((looked, features, code_far))
+    )(meta, *digits, catalogue)
+    looked, rows_y, code_far = lax.optimization_barrier((looked, rows_y, code_far))
+    features = gather_blocks(rows, "mp", rows_y)
     items = in_half(looked)
 
     wide, projected, turned, own, *gated = call(
@@ -606,10 +626,9 @@
             S((2 * quarter, width), BF),
         ]
         + [S((2 * quarter, cols), BF)] * mp,
-        [SM] + [VM] * mp + [HB],
+        [SM] + [VM] * mp + [VM],
         10,
         scratch=[pltpu.VMEM((2 * rows_all, width), BF), pltpu.VMEM((2 * rows_all, cols), BF)],
-        out_specs=[HB] * 4 + [VM] * mp,
         limit=36,
     )(meta, *features, w_in)
     gathered = exchange(gated, "mp")
@@ -621,7 +640,7 @@
             S((2 * quarter, width), BF),
             S((2 * quarter, BLOCK), F32),
         ],
-        [HB] + [VM] * (2 * mp),
+        [VM] + [VM] * (2 * mp),
         2,
     )(own, *gathered, *w_out_blocks)
 
@@ -630,7 +649,7 @@
             score_kernel, dp=dp, devices=devices, capacity=capacity, chunk=chunk
         ),
         [S((slots, 2 * events), F32), S((slots, BLOCK), F32), S((1, 2 * events), F32)],
-        [SM, HB] + [VM] * 3,
+        [SM, VM] + [VM] * 3,
         4,
     )(meta, items, code, code_far, units_bf)
     total_far = partner(total)
@@ -642,7 +661,7 @@
             S((2 * events, width), BF),
             S((near, width), BF),
         ],
-        [SM, HB] + [VM] * 6,
+        [SM, VM] + [VM] * 6,
         3,
     )(meta, items, code, code_far, expo, inv_item, total, total_far)
     slopes_back = partner(slopes_bf)
@@ -672,7 +691,7 @@
     parts = call(
         functools.partial(backward_kernel, mp=mp, dp=dp),
         pieces if short else [S((dp // 2, 5, width // dp, cols), BF)],
-        [SM] + [VM] * mp + [HB] * 4,
+        [SM] + [VM] * (mp + 4),
         10,
         scratch=[
             pltpu.VMEM((2 * rows_all, width), BF),
@@ -681,8 +700,14 @@
         limit=36,
     )(meta, *cots, w_out, wide, projected, turned)
     if short:
+        parts = exchange(parts, "dp")
         parts, landed = lax.optimization_barrier((parts, landed))
-        grads = sum(p.astype(F32) for p in exchange(parts, "dp"))
+        w_in_grad, w_out_grad = call(
+            sum_kernel,
+            [S((4, width // dp, cols), F32), S((cols, width // dp), F32)],
+            [VM] * len(parts),
+            1,
+        )(*parts)
     else:
         got = lax.all_to_all(
             parts[0],
@@ -693,6 +718,7 @@
             axis_index_groups=[list(range(dp // 2)), list(range(dp // 2, dp))],
         )
         grads = jnp.sum(got.astype(F32), axis=0)
+        w_in_grad, w_out_grad = grads[:4], grads[4].T
         sending = call(
             functools.partial(send_kernel, **sizes),
             S((slots, width), BF),
@@ -703,12 +729,12 @@
     cat_grad = call(
         functools.partial(spread_kernel, chunk=math.gcd(stock, 128)),
         S((stock, width), F32),
-        [VM, HB] + [HB] * len(landed),
+        [VM, VM] + [VM] * len(landed),
         4,
         out_specs=[HB],
         limit=24,
     )(returning, catalogue, *landed)
-    return (grads[:4], grads[4].T, cat_grad)
+    return (w_in_grad, w_out_grad, cat_grad)
 
 
 def solution(mesh):

time: 211 us -> 194 us (0.919)
  waiting for transfers between devices: 103 us -> 97 us
  starting transfers between devices: 44.8 us -> 39.3 us
  local copies, waits for them, and re-layouts: 17 us -> 13.4 us
    ppermute x27 -> x30, starting transfers between devices: 33.1 us -> 26 us  [swapped(): return lax.ppermute(x, axis, [(a, a ^ bit) for a in range(size)])]
    ppermute x27 -> x30, waiting for transfers between devices: 103 us -> 96.9 us  [swapped(): return lax.ppermute(x, axis, [(a, a ^ bit) for a in range(size)])]
    unnamed x53 -> x46, local copies, waits for them, and re-layouts: 16.2 us -> 13.4 us
    pallas_call x11 -> x12, Pallas kernels: 41.9 us -> 41.1 us  [run(): pl.pallas_call(kernel, out_shape=outs, in_specs=list(in_specs), out_specs...]
  transfers between devices with their start and end apart: 29 -> 32, of which waited for: 14 -> 15; matrix products, arithmetic and copies ran while one was open for 0% -> 0% of each run, Pallas kernels for 17% -> 15%
where the time goes in v7:
time: 194 us; the launch traced here: 193 us
  waiting for transfers between devices  97 us (50%)
  Pallas kernels  41.1 us (21%)
  starting transfers between devices  39.3 us (20%)
  local copies, waits for them, and re-layouts  13.4 us (7%)
    ppermute x30, waiting for transfers between devices, swapped(): return lax.ppermute(x, axis, [(a, a ^ bit) for a in range(size)])  96.9 us
    pallas_call x12, Pallas kernels, run(): pl.pallas_call(kernel, out_shape=outs, in_specs=list(in_specs), out_specs...  41.1 us
    ppermute x30, starting transfers between devices, swapped(): return lax.ppermute(x, axis, [(a, a ^ bit) for a in range(size)])  26 us
    unnamed x46, local copies, waits for them, and re-layouts  13.4 us
    all_to_all x1, starting transfers between devices, in_half(): lax.all_to_all(x.reshape(near, 2 * capacity, width), ('dp', 'mp'), split_...  7.78 us
    all_to_all x1, starting transfers between devices, per_device(): lax.all_to_all(packed, 'dp', split_axis=0, concat_axis=0, tiled=True)  5.55 us
  transfers between devices with their start and end apart: 32, of which 15 were waited for; matrix products, arithmetic and copies ran while one was open for 0% of the time, Pallas kernels for 15%

profile of v7, /device:TPU:13, one launch (start us, length us, event | category | flops | bytes accessed | tf_op | source)
XLA Modules:
  0.0 193.1 jit_solution(7947809193719071167)
XLA Ops:
  0.6 1.3 pad_add_fusion.refs_0_
  2.0 5.1 %shard_map.103 = (bf16[8,144,256]{2,1,0:T(8,128)(2,1)}, f32[32,128]{1,0:T(8,128)}) custom-call(s32[258]{0:T(512)} %pad_add_fusion.refs_0_, bf16[16,32,256]{2,1,0:T(8,128)(2,1)} %refs_1_.2, s32[8,128]{1,0:T(8,128)} %bitcast.11, s32[8,128]{1,0:T(8,128)} %bitcast.12), custom_call_target="tpu_custom_call" | custom-call | bytes 13200000 | tf_op jit(solution)/shard_map/pallas_call | solution.py:70
  7.0 5.6 %all-to-all-start = ((bf16[8,144,256]{2,1,0:T(8,128)(2,1)}), bf16[8,144,256]{2,1,0:T(8,128)(2,1)S(1)}, u32[]{:S(2)}, u32[]{:S(2)}) async-start(bf16[8,144,256]{2,1,0:T(8,128)(2,1)} %get-tuple-element.56), calls=%async_computation | async-start | bytes 1179648 | tf_op jit(solution)/shard_map/all_to_all | solution.py:584
  12.8 12.3 %collective-permute-done.refs_7_ = bf16[256,1024]{1,0:T(8,128)(2,1)} collective-permute-done((bf16[256,1024]{1,0:T(8,128)(2,1)}, bf16[256,1024]{1,0:T(8,128)(2,1)}, u32[]{:S(2)}, u32[]{:S(2)}) %collective-permute-start) | collective-permute-done | bytes 524320 | tf_op jit(solution)/shard_map/ppermute | solution.py:518
  25.1 0.7 copy-done.17
  25.8 1.0 shard_map.104
  27.0 2.9 %collective-permute-done.1.refs_3_ = bf16[128,256]{1,0:T(8,128)(2,1)S(1)} collective-permute-done((bf16[128,256]{1,0:T(8,128)(2,1)S(1)}, bf16[128,256]{1,0:T(8,128)(2,1)S(1)}, u32[]{:S(2)}, u32[]{:S(2)}) %collective-permute-start.1) | collective-permute-done | bytes 65568 | tf_op jit(solution)/shard_map/ppermute | solution.py:518
  30.1 5.4 %collective-permute-start.3 = (bf16[128,256]{1,0:T(8,128)(2,1)S(1)}, bf16[128,256]{1,0:T(8,128)(2,1)S(1)}, u32[]{:S(2)}, u32[]{:S(2)}) collective-permute-start(bf16[128,256]{1,0:T(8,128)(2,1)S(1)} %get-tuple-element.59.refs_1_), channel_id=1, source_target_pairs={{0,1},{1,0},{2,3},{3,2},{4,5},{5,4},{6,7},{7,6},{8,9},{9,8},{10,11... | collective-permute-start | bytes 196616 | tf_op jit(solution)/shard_map/ppermute | solution.py:518
  36.8 1.2 copy-done.1
  38.0 0.7 copy-done.18
  38.6 2.8 %shard_map.105 = (bf16[1536,1024]{1,0:T(8,128)(2,1)S(1)}, s32[1,1536]{1,0:T(1,128)}, s32[1,1536]{1,0:T(1,128)S(1)}) custom-call(s32[258]{0:T(512)S(1)} %copy-done.18, bf16[128,256]{1,0:T(8,128)(2,1)S(1)} %get-tuple-element.59.refs_1_, bf16[128,256]{1,0:T(8,128)(2,1)S(1)} %collective-permute-done.3.refs_2_, ...), custom_call_target="tpu_custom_call" | custom-call | bytes 13200000 | tf_op jit(solution)/shard_map/pallas_call | solution.py:70
  41.4 1.6 copy-done.3
  43.1 0.8 copy-done.15
  43.9 7.8 %all-to-all-start.1 = ((bf16[16,96,1024]{2,1,0:T(8,128)(2,1)}), bf16[16,96,1024]{2,1,0:T(8,128)(2,1)S(1)}, u32[]{:S(2)}, u32[]{:S(2)}) async-start(bf16[16,96,1024]{2,1,0:T(8,128)(2,1)} %bitcast.10), calls=%async_computation.1 | async-start | bytes 6291456 | tf_op jit(solution)/shard_map/all_to_all | solution.py:565
  52.8 1.2 collective-permute-done.2.refs_2_
  53.9 0.7 collective-permute-done.7.refs_4_
  54.7 1.6 copy-done.10
  56.3 1.0 copy-done.14
  57.3 1.0 copy-done.16
  58.3 7.7 %shard_map.106 = (f32[3,1024,256]{2,1,0:T(8,128)S(1)}, bf16[9,1024,256]{2,1,0:T(8,128)(2,1)S(1)}, bf16[1280,1024]{1,0:T(8,128)(2,1)S(1)}, bf16[256,1024]{1,0:T(8...) custom-call(s32[258]{0:T(512)S(1)} %copy-done.19, ...), custom_call_target="tpu_custom_call" | custom-call | bytes 33000000 | tf_op jit(solution)/shard_map/pallas_call | solution.py:70
  66.0 2.2 %copy-done = bf16[9,1024,256]{2,1,0:T(8,128)(2,1)} copy-done((bf16[9,1024,256]{2,1,0:T(8,128)(2,1)}, bf16[9,1024,256]{2,1,0:T(8,128)(2,1)S(1)}, u32[]{:S(2)}) %copy-start) | copy-done | bytes 4718616
  68.2 1.5 copy-done.6
  70.3 1.6 collective-permute-start.10
  71.9 12.7 %collective-permute-done.9.refs_3_ = bf16[256,256]{1,0:T(8,128)(2,1)S(1)} collective-permute-done((bf16[256,256]{1,0:T(8,128)(2,1)S(1)}, bf16[256,256]{1,0:T(8,128)(2,1)S(1)}, u32[]{:S(2)}, u32[]{:S(2)}) %collective-permute-start.9) | collective-permute-done | bytes 131104 | tf_op jit(solution)/shard_map/ppermute | solution.py:518
  84.6 7.8 %collective-permute-done.10.refs_4_ = bf16[256,256]{1,0:T(8,128)(2,1)S(1)} collective-permute-done((bf16[256,256]{1,0:T(8,128)(2,1)S(1)}, bf16[256,256]{1,0:T(8,128)(2,1)S(1)}, u32[]{:S(2)}, u32[]{:S(2)}) %collective-permute-start.10) | collective-permute-done | bytes 131104 | tf_op jit(solution)/shard_map/ppermute | solution.py:518
  92.4 2.7 %shard_map.107 = (f32[256,1024]{1,0:T(8,128)S(1)}, bf16[256,1024]{1,0:T(8,128)(2,1)}, f32[256,128]{1,0:T(8,128)S(1)}) custom-call(bf16[256,1024]{1,0:T(8,128)(2,1)S(1)} %get-tuple-element.65.refs_0_, bf16[256,256]{1,0:T(8,128)(2,1)S(1)} %get-tuple-element.66.refs_1_, bf16[256,256]{1,0:T(8,128)(2,1)S(1)} %collective-permute-done.8.refs_2_, ...), custom_call_target="tpu_custom_call" | custom-call | bytes 6600000 | tf_op jit(solution)/shard_map/pallas_call | solution.py:70
  95.1 1.0 copy-done.11
  96.2 3.2 %shard_map.108 = (f32[1536,256]{1,0:T(8,128)S(1)}, f32[1536,128]{1,0:T(8,128)S(1)}, f32[1,256]{1,0:T(1,128)S(1)}) custom-call(s32[258]{0:T(512)S(1)} %copy-done.19, bf16[1536,1024]{1,0:T(8,128)(2,1)S(1)} %bitcast.6, f32[32,128]{1,0:T(8,128)S(1)} %copy-done.20, f32[32,128]{1,0:T(8,128)S(1)} %collective-permute-done.6.refs_3_, ...), custom_call_target="tpu_custom_call" | custom-call | bytes 13200000 | tf_op jit(solution)/shard_map/pallas_call | solution.py:70
  99.5 2.2 %collective-permute-start.13 = (f32[1,256]{1,0:T(1,128)S(1)}, f32[1,256]{1,0:T(1,128)S(1)}, u32[]{:S(2)}, u32[]{:S(2)}) collective-permute-start(f32[1,256]{1,0:T(1,128)S(1)} %get-tuple-element.78.refs_6_), channel_id=1, source_target_pairs={{0,16},{4,20},{8,24},{12,28},{16,0},{20,4},{24,8},{28,12},{1,17},{... | collective-permute-start | bytes 3080 | tf_op jit(solution)/shard_map/ppermute | solution.py:518
  101.7 2.5 %collective-permute-start.17 = (bf16[256,1024]{1,0:T(8,128)(2,1)}, bf16[256,1024]{1,0:T(8,128)(2,1)S(1)}, u32[]{:S(2)}, u32[]{:S(2)}) collective-permute-start(bf16[256,1024]{1,0:T(8,128)(2,1)} %get-tuple-element.75.refs_4_.refs_1_), channel_id=1, source_target_pairs={{0,12},{4,8},{8,4},{12,0},{16,28},{20,24},{24,20},{28,16},{1,13},{... | collective-permute-start | bytes 1572872 | tf_op jit(solution)/shard_map/ppermute | solution.py:518
  104.2 5.8 %collective-permute-done.13.refs_7_ = f32[1,256]{1,0:T(1,128)S(1)} collective-permute-done((f32[1,256]{1,0:T(1,128)S(1)}, f32[1,256]{1,0:T(1,128)S(1)}, u32[]{:S(2)}, u32[]{:S(2)}) %collective-permute-start.13) | collective-permute-done | bytes 1056 | tf_op jit(solution)/shard_map/ppermute | solution.py:518
  110.0 2.0 %shard_map.109 = (f32[256,1024]{1,0:T(8,128)S(1)}, bf16[256,1024]{1,0:T(8,128)(2,1)S(1)}, bf16[16,1024]{1,0:T(8,128)(2,1)S(1)}) custom-call(s32[258]{0:T(512)S(1)} %copy-done.19, bf16[1536,1024]{1,0:T(8,128)(2,1)S(1)} %bitcast.7, f32[32,128]{1,0:T(8,128)S(1)} %copy-done.20, f32[32,128]{1,0:T(8,128)S(1)} %collective-permute-done.6.refs_3_, ...), custom_call_target="tpu_custom_call" | custom-call | bytes 9900000 | tf_op jit(solution)/shard_map/pallas_call | solution.py:70
  112.0 1.2 collective-permute-start.18
  113.2 1.7 collective-permute-start.19
  115.0 12.3 %collective-permute-done.17.refs_4_ = bf16[256,1024]{1,0:T(8,128)(2,1)S(1)} collective-permute-done((bf16[256,1024]{1,0:T(8,128)(2,1)}, bf16[256,1024]{1,0:T(8,128)(2,1)S(1)}, u32[]{:S(2)}, u32[]{:S(2)}) %collective-permute-start.17) | collective-permute-done | bytes 524320 | tf_op jit(solution)/shard_map/ppermute | solution.py:518
  127.3 5.6 %collective-permute-done.19.refs_7_ = bf16[16,1024]{1,0:T(8,128)(2,1)S(1)} collective-permute-done((bf16[16,1024]{1,0:T(8,128)(2,1)S(1)}, bf16[16,1024]{1,0:T(8,128)(2,1)S(1)}, u32[]{:S(2)}, u32[]{:S(2)}) %collective-permute-start.19) | collective-permute-done | bytes 32800 | tf_op jit(solution)/shard_map/ppermute | solution.py:518
  132.9 1.4 collective-permute-done.20.refs_8_
  134.3 2.6 %shard_map.110 = (bf16[384,1024]{1,0:T(8,128)(2,1)S(1)}, bf16[384,1024]{1,0:T(8,128)(2,1)S(1)}, bf16[384,1024]{1,0:T(8,128)(2,1)S(1)}, bf16[384,1024]{1,0:T(8,128)(2,1)S(1)}) custom-call(s32[258]{0:T(512)S(1)} %copy-done.19, bf16[256,1024]{1,0:T(8,128)(2,1)} %get-tuple-element.75.refs_4_.refs_1_, bf16[256,1024]{1,0:T(8,128)(2,1)} %collective-permute-done.15.refs_2_, ...), custom_call_target="tpu_custom_call" | custom-call | bytes 13200000 | tf_op jit(solution)/shard_map/pallas_call | solution.py:70
  137.4 1.5 collective-permute-start.27
  139.0 10.3 %collective-permute-done.22.refs_3_ = bf16[256,1024]{1,0:T(8,128)(2,1)S(1)} collective-permute-done((bf16[256,1024]{1,0:T(8,128)(2,1)S(1)}, bf16[256,1024]{1,0:T(8,128)(2,1)S(1)}, u32[]{:S(2)}, u32[]{:S(2)}) %collective-permute-start.22) | collective-permute-done | bytes 524320 | tf_op jit(solution)/shard_map/ppermute | solution.py:518
  149.3 2.4 %collective-permute-start.23 = (bf16[256,1024]{1,0:T(8,128)(2,1)S(1)}, bf16[256,1024]{1,0:T(8,128)(2,1)S(1)}, u32[]{:S(2)}, u32[]{:S(2)}) collective-permute-start(bf16[256,1024]{1,0:T(8,128)(2,1)S(1)} %collective-permute-done.22.refs_3_), channel_id=1, source_target_pairs={{0,1},{1,0},{2,3},{3,2},{4,5},{5,4},{6,7},{7,6},{8,9},{9,8},{10,11... | collective-permute-start | bytes 1572872 | tf_op jit(solution)/shard_map/ppermute | solution.py:518
  151.7 1.6 collective-permute-start.29
  153.4 8.7 %shard_map.112 = (bf16[5,128,256]{2,1,0:T(8,128)(2,1)S(1)}, bf16[5,128,256]{2,1,0:T(8,128)(2,1)S(1)}, bf16[5,128,256]{2,1,0:T(8,128)(2,1)S(1)}, bf16[5,128,256]{2,1,0:T(8,128)(2,1)S(1)}) custom-call(s32[258]{0:T(512)S(1)} %copy-done.19, bf16[256,1024]{1,0:T(8,128)(2,1)S(1)} %shard_map.111.refs_1_, bf16[256,1024]{1,0:T(8,128)(2,1)S(1)} %collective-permute-done.21.refs_2_, ...), custom_call_target="tpu_custom_call" | custom-call | bytes 33000000 | tf_op jit(solution)/shard_map/pallas_call | solution.py:70
  162.7 2.2 %collective-permute-start.26 = (bf16[5,128,256]{2,1,0:T(8,128)(2,1)S(1)}, bf16[5,128,256]{2,1,0:T(8,128)(2,1)S(1)}, u32[]{:S(2)}, u32[]{:S(2)}) collective-permute-start(bf16[5,128,256]{2,1,0:T(8,128)(2,1)S(1)} %get-tuple-element.93), channel_id=1, source_target_pairs={{0,12},{4,8},{8,4},{12,0},{16,28},{20,24},{24,20},{28,16},{1,13},{... | collective-permute-start | bytes 983048 | tf_op jit(solution)/shard_map/ppermute | solution.py:518
  164.9 6.0 %collective-permute-done.28.refs_4_ = bf16[384,1024]{1,0:T(8,128)(2,1)S(1)} collective-permute-done((bf16[384,1024]{1,0:T(8,128)(2,1)S(1)}, bf16[384,1024]{1,0:T(8,128)(2,1)S(1)}, u32[]{:S(2)}, u32[]{:S(2)}) %collective-permute-start.28) | collective-permute-done | bytes 786464 | tf_op jit(solution)/shard_map/ppermute | solution.py:518
  170.9 16.9 %collective-permute-done.29.refs_5_ = bf16[384,1024]{1,0:T(8,128)(2,1)S(1)} collective-permute-done((bf16[384,1024]{1,0:T(8,128)(2,1)S(1)}, bf16[384,1024]{1,0:T(8,128)(2,1)S(1)}, u32[]{:S(2)}, u32[]{:S(2)}) %collective-permute-start.29) | collective-permute-done | bytes 786464 | tf_op jit(solution)/shard_map/ppermute | solution.py:518
  187.9 1.0 shard_map.113
  188.8 4.1 %shard_map.114 = f32[512,1024]{1,0:T(8,128)} custom-call(s32[1,1536]{1,0:T(1,128)S(1)} %get-tuple-element.104.refs_0_, bf16[512,1024]{1,0:T(8,128)(2,1)S(1)} %copy-done.2, bf16[384,1024]{1,0:T(8,128)(2,1)S(1)} %get-tuple-element.105.refs_2_, bf16[384,1024]{1,0:T(8,128)(2,1)S(1)} %collective-permute-done.27.refs_3_, ...), custom_call_target="tpu_custom_call" | custom-call | bytes 13200000 | tf_op jit(solution)/shard_map/pallas_call | solution.py:70
  (76 shorter events, 5.1 us)
Async XLA Ops:
  7.0 18.0 %all-to-all-start = ((bf16[8,144,256]{2,1,0:T(8,128)(2,1)}), bf16[8,144,256]{2,1,0:T(8,128)(2,1)S(1)}, u32[]{:S(2)}, u32[]{:S(2)}) async-start(bf16[8,144,256]{2,1,0:T(8,128)(2,1)} %get-tuple-element.56), calls=%async_computation | async-start | bytes 1179648 | tf_op jit(solution)/shard_map/all_to_all | solution.py:584
  12.6 12.5 %collective-permute-start = (bf16[256,1024]{1,0:T(8,128)(2,1)}, bf16[256,1024]{1,0:T(8,128)(2,1)}, u32[]{:S(2)}, u32[]{:S(2)}) collective-permute-start(bf16[256,1024]{1,0:T(8,128)(2,1)} %refs_5_.7), channel_id=1, source_target_pairs={{0,2},{1,3},{2,0},{3,1},{4,6},{5,7},{6,4},{7,5},{8,10},{9,11},{10,... | collective-permute-start | bytes 1572872 | tf_op jit(solution)/shard_map/ppermute | solution.py:518
  26.7 14.7 %copy-start.13 = (bf16[1024,256]{1,0:T(8,128)(2,1)}, bf16[1024,256]{1,0:T(8,128)(2,1)S(1)}, u32[]{:S(2)}) copy-start(bf16[1024,256]{1,0:T(8,128)(2,1)S(1)} %get-tuple-element.60.refs_1_) | copy-start | bytes 1572868
  26.7 3.2 %collective-permute-start.1 = (bf16[128,256]{1,0:T(8,128)(2,1)S(1)}, bf16[128,256]{1,0:T(8,128)(2,1)S(1)}, u32[]{:S(2)}, u32[]{:S(2)}) collective-permute-start(bf16[128,256]{1,0:T(8,128)(2,1)S(1)} %get-tuple-element.59.refs_1_), channel_id=1, source_target_pairs={{0,2},{1,3},{2,0},{3,1},{4,6},{5,7},{6,4},{7,5},{8,10},{9,11},{10,... | collective-permute-start | bytes 196616 | tf_op jit(solution)/shard_map/ppermute | solution.py:518
  29.9 13.2 %collective-permute-start.5 = (bf16[1024,256]{1,0:T(8,128)(2,1)S(1)}, bf16[1024,256]{1,0:T(8,128)(2,1)S(1)}, u32[]{:S(2)}, u32[]{:S(2)}) collective-permute-start(bf16[1024,256]{1,0:T(8,128)(2,1)S(1)} %get-tuple-element.60.refs_1_), channel_id=1, source_target_pairs={{0,2},{1,3},{2,0},{3,1},{4,6},{5,7},{6,4},{7,5},{8,10},{9,11},{10,... | collective-permute-start | bytes 1572872 | tf_op jit(solution)/shard_map/ppermute | solution.py:518
  30.1 6.3 %collective-permute-start.3 = (bf16[128,256]{1,0:T(8,128)(2,1)S(1)}, bf16[128,256]{1,0:T(8,128)(2,1)S(1)}, u32[]{:S(2)}, u32[]{:S(2)}) collective-permute-start(bf16[128,256]{1,0:T(8,128)(2,1)S(1)} %get-tuple-element.59.refs_1_), channel_id=1, source_target_pairs={{0,1},{1,0},{2,3},{3,2},{4,5},{5,4},{6,7},{7,6},{8,9},{9,8},{10,11... | collective-permute-start | bytes 196616 | tf_op jit(solution)/shard_map/ppermute | solution.py:518
  35.5 1.3 collective-permute-start.4
  35.5 7.6 %collective-permute-start.6 = (f32[32,128]{1,0:T(8,128)}, f32[32,128]{1,0:T(8,128)S(1)}, u32[]{:S(2)}, u32[]{:S(2)}) collective-permute-start(f32[32,128]{1,0:T(8,128)} %get-tuple-element.63.refs_2_), channel_id=1, source_target_pairs={{0,16},{4,20},{8,24},{12,28},{16,0},{20,4},{24,8},{28,12},{1,17},{... | collective-permute-start | bytes 49160 | tf_op jit(solution)/shard_map/ppermute | solution.py:518
  41.4 1.6 copy-start.3
  43.9 10.8 %copy-start.19 = (s32[258]{0:T(512)S(1)}, s32[258]{0:T(512)}, u32[]{:S(2)}) copy-start(s32[258]{0:T(512)} %pad_add_fusion.refs_0_) | copy-start | bytes 3100
  43.9 52.4 %copy-start.20 = (f32[32,128]{1,0:T(8,128)S(1)}, f32[32,128]{1,0:T(8,128)}, u32[]{:S(2)}) copy-start(f32[32,128]{1,0:T(8,128)} %get-tuple-element.63.refs_2_) | copy-start | bytes 49156
  43.9 52.4 %all-to-all-start.1 = ((bf16[16,96,1024]{2,1,0:T(8,128)(2,1)}), bf16[16,96,1024]{2,1,0:T(8,128)(2,1)S(1)}, u32[]{:S(2)}, u32[]{:S(2)}) async-start(bf16[16,96,1024]{2,1,0:T(8,128)(2,1)} %bitcast.10), calls=%async_computation.1 | async-start | bytes 6291456 | tf_op jit(solution)/shard_map/all_to_all | solution.py:565
  51.7 40.8 %copy-start.8 = (bf16[256,1024]{1,0:T(8,128)(2,1)S(1)}, bf16[256,1024]{1,0:T(8,128)(2,1)}, u32[]{:S(2)}) copy-start(bf16[256,1024]{1,0:T(8,128)(2,1)} %refs_5_.7) | copy-start | bytes 1572868
  51.7 2.2 %collective-permute-start.2 = (bf16[1024,256]{1,0:T(8,128)(2,1)}, bf16[1024,256]{1,0:T(8,128)(2,1)S(1)}, u32[]{:S(2)}, u32[]{:S(2)}) collective-permute-start(bf16[1024,256]{1,0:T(8,128)(2,1)} %copy-done.13), channel_id=1, source_target_pairs={{0,1},{1,0},{2,3},{3,2},{4,5},{5,4},{6,7},{7,6},{8,9},{9,8},{10,11... | collective-permute-start | bytes 1572872 | tf_op jit(solution)/shard_map/ppermute | solution.py:518
  52.1 2.6 %collective-permute-start.7 = (bf16[1024,256]{1,0:T(8,128)(2,1)}, bf16[1024,256]{1,0:T(8,128)(2,1)S(1)}, u32[]{:S(2)}, u32[]{:S(2)}) collective-permute-start(bf16[1024,256]{1,0:T(8,128)(2,1)} %copy-done.15), channel_id=1, source_target_pairs={{0,1},{1,0},{2,3},{3,2},{4,5},{5,4},{6,7},{7,6},{8,9},{9,8},{10,11... | collective-permute-start | bytes 1572872 | tf_op jit(solution)/shard_map/ppermute | solution.py:518
  52.2 19.6 %collective-permute-start.11 = (bf16[256,1024]{1,0:T(8,128)(2,1)}, bf16[256,1024]{1,0:T(8,128)(2,1)S(1)}, u32[]{:S(2)}, u32[]{:S(2)}) collective-permute-start(bf16[256,1024]{1,0:T(8,128)(2,1)} %refs_5_.7), channel_id=1, source_target_pairs={{0,1},{1,0},{2,3},{3,2},{4,5},{5,4},{6,7},{7,6},{8,9},{9,8},{10,11... | collective-permute-start | bytes 1572872 | tf_op jit(solution)/shard_map/ppermute | solution.py:518
  52.6 19.3 %collective-permute-start.12 = (bf16[256,1024]{1,0:T(8,128)(2,1)}, bf16[256,1024]{1,0:T(8,128)(2,1)S(1)}, u32[]{:S(2)}, u32[]{:S(2)}) collective-permute-start(bf16[256,1024]{1,0:T(8,128)(2,1)} %collective-permute-done.refs_7_), channel_id=1, source_target_pairs={{0,1},{1,0},{2,3},{3,2},{4,5},{5,4},{6,7},{7,6},{8,9},{9,8},{10,11... | collective-permute-start | bytes 1572872 | tf_op jit(solution)/shard_map/ppermute | solution.py:518
  54.7 1.6 copy-start.10
  66.0 2.2 %copy-start = (bf16[9,1024,256]{2,1,0:T(8,128)(2,1)}, bf16[9,1024,256]{2,1,0:T(8,128)(2,1)S(1)}, u32[]{:S(2)}) copy-start(bf16[9,1024,256]{2,1,0:T(8,128)(2,1)S(1)} %get-tuple-element.88.refs_7_) | copy-start | bytes 14155780
  68.2 1.5 copy-start.6
  69.7 26.3 %copy-start.4 = (f32[3,1024,256]{2,1,0:T(8,128)}, f32[3,1024,256]{2,1,0:T(8,128)S(1)}, u32[]{:S(2)}) copy-start(f32[3,1024,256]{2,1,0:T(8,128)S(1)} %get-tuple-element.87.refs_6_) | copy-start | bytes 9437188
  69.7 2.2 %collective-permute-start.8 = (bf16[256,256]{1,0:T(8,128)(2,1)S(1)}, bf16[256,256]{1,0:T(8,128)(2,1)S(1)}, u32[]{:S(2)}, u32[]{:S(2)}) collective-permute-start(bf16[256,256]{1,0:T(8,128)(2,1)S(1)} %get-tuple-element.67), channel_id=1, source_target_pairs={{0,1},{1,0},{2,3},{3,2},{4,5},{5,4},{6,7},{7,6},{8,9},{9,8},{10,11... | collective-permute-start | bytes 393224 | tf_op jit(solution)/shard_map/ppermute | solution.py:518
  70.0 14.6 %collective-permute-start.9 = (bf16[256,256]{1,0:T(8,128)(2,1)S(1)}, bf16[256,256]{1,0:T(8,128)(2,1)S(1)}, u32[]{:S(2)}, u32[]{:S(2)}) collective-permute-start(bf16[256,256]{1,0:T(8,128)(2,1)S(1)} %get-tuple-element.68), channel_id=1, source_target_pairs={{0,2},{1,3},{2,0},{3,1},{4,6},{5,7},{6,4},{7,5},{8,10},{9,11},{10,... | collective-permute-start | bytes 393224 | tf_op jit(solution)/shard_map/ppermute | solution.py:518
  70.3 22.1 %collective-permute-start.10 = (bf16[256,256]{1,0:T(8,128)(2,1)S(1)}, bf16[256,256]{1,0:T(8,128)(2,1)S(1)}, u32[]{:S(2)}, u32[]{:S(2)}) collective-permute-start(bf16[256,256]{1,0:T(8,128)(2,1)S(1)} %get-tuple-element.69), channel_id=1, source_target_pairs={{0,3},{1,2},{2,1},{3,0},{4,7},{5,6},{6,5},{7,4},{8,11},{9,10},{10,... | collective-permute-start | bytes 393224 | tf_op jit(solution)/shard_map/ppermute | solution.py:518
  96.1 17.2 %collective-permute-start.15 = (bf16[256,1024]{1,0:T(8,128)(2,1)}, bf16[256,1024]{1,0:T(8,128)(2,1)}, u32[]{:S(2)}, u32[]{:S(2)}) collective-permute-start(bf16[256,1024]{1,0:T(8,128)(2,1)} %get-tuple-element.75.refs_4_.refs_1_), channel_id=1, source_target_pairs={{0,4},{4,0},{8,12},{12,8},{16,20},{20,16},{24,28},{28,24},{1,5},{5... | collective-permute-start | bytes 1572872 | tf_op jit(solution)/shard_map/ppermute | solution.py:518
  96.1 18.8 %collective-permute-start.16 = (bf16[256,1024]{1,0:T(8,128)(2,1)}, bf16[256,1024]{1,0:T(8,128)(2,1)}, u32[]{:S(2)}, u32[]{:S(2)}) collective-permute-start(bf16[256,1024]{1,0:T(8,128)(2,1)} %get-tuple-element.75.refs_4_.refs_1_), channel_id=1, source_target_pairs={{0,8},{4,12},{8,0},{12,4},{16,24},{20,28},{24,16},{28,20},{1,9},{5... | collective-permute-start | bytes 1572872 | tf_op jit(solution)/shard_map/ppermute | solution.py:518
  96.2 40.7 %copy-start.12 = (f32[256,1024]{1,0:T(8,128)S(1)}, f32[256,1024]{1,0:T(8,128)}, u32[]{:S(2)}) copy-start(f32[256,1024]{1,0:T(8,128)} %copy-done.11) | copy-start | bytes 3145732
  99.5 10.5 %collective-permute-start.13 = (f32[1,256]{1,0:T(1,128)S(1)}, f32[1,256]{1,0:T(1,128)S(1)}, u32[]{:S(2)}, u32[]{:S(2)}) collective-permute-start(f32[1,256]{1,0:T(1,128)S(1)} %get-tuple-element.78.refs_6_), channel_id=1, source_target_pairs={{0,16},{4,20},{8,24},{12,28},{16,0},{20,4},{24,8},{28,12},{1,17},{... | collective-permute-start | bytes 3080 | tf_op jit(solution)/shard_map/ppermute | solution.py:518
  101.7 25.6 %collective-permute-start.17 = (bf16[256,1024]{1,0:T(8,128)(2,1)}, bf16[256,1024]{1,0:T(8,128)(2,1)S(1)}, u32[]{:S(2)}, u32[]{:S(2)}) collective-permute-start(bf16[256,1024]{1,0:T(8,128)(2,1)} %get-tuple-element.75.refs_4_.refs_1_), channel_id=1, source_target_pairs={{0,12},{4,8},{8,4},{12,0},{16,28},{20,24},{24,20},{28,16},{1,13},{... | collective-permute-start | bytes 1572872 | tf_op jit(solution)/shard_map/ppermute | solution.py:518
  109.9 43.4 %slice-start = ((s8[4718592]{0:T(1024)(128)(4,1)}), s8[4194304]{0:T(1024)(128)(4,1)S(1)}, s32[]{:S(2)}) async-start(s8[4718592]{0:T(1024)(128)(4,1)} %bitcast.8), calls=%async_computation.2 | async-start | bytes 8388608
  110.0 43.4 %slice-start.1 = ((s8[4718592]{0:T(1024)(128)(4,1)}), s8[524288]{0:T(1024)(128)(4,1)S(1)}, s32[]{:S(2)}) async-start(s8[4718592]{0:T(1024)(128)(4,1)} %bitcast.8), calls=%async_computation.3 | async-start | bytes 1048576
  110.0 43.4 %copy-start.7 = (bf16[1280,1024]{1,0:T(8,128)(2,1)S(1)}, bf16[1280,1024]{1,0:T(8,128)(2,1)}, u32[]{:S(2)}) copy-start(bf16[1280,1024]{1,0:T(8,128)(2,1)} %copy-done.6) | copy-start | bytes 7864324
  111.9 41.5 %copy-start.5 = (f32[3,1024,256]{2,1,0:T(8,128)S(1)}, f32[3,1024,256]{2,1,0:T(8,128)}, u32[]{:S(2)}) copy-start(f32[3,1024,256]{2,1,0:T(8,128)} %copy-done.4) | copy-start | bytes 9437188
  111.9 41.5 %copy-start.9 = (bf16[256,1024]{1,0:T(8,128)(2,1)S(1)}, bf16[256,1024]{1,0:T(8,128)(2,1)}, u32[]{:S(2)}) copy-start(bf16[256,1024]{1,0:T(8,128)(2,1)} %refs_5_.7) | copy-start | bytes 1572868
  111.9 25.0 %collective-permute-start.14 = (bf16[256,1024]{1,0:T(8,128)(2,1)S(1)}, bf16[256,1024]{1,0:T(8,128)(2,1)S(1)}, u32[]{:S(2)}, u32[]{:S(2)}) collective-permute-start(bf16[256,1024]{1,0:T(8,128)(2,1)S(1)} %get-tuple-element.80), channel_id=1, source_target_pairs={{0,16},{4,20},{8,24},{12,28},{16,0},{20,4},{24,8},{28,12},{1,17},{... | collective-permute-start | bytes 1572872 | tf_op jit(solution)/shard_map/ppermute | solution.py:518
  112.0 15.3 %collective-permute-start.18 = (bf16[16,1024]{1,0:T(8,128)(2,1)S(1)}, bf16[16,1024]{1,0:T(8,128)(2,1)S(1)}, u32[]{:S(2)}, u32[]{:S(2)}) collective-permute-start(bf16[16,1024]{1,0:T(8,128)(2,1)S(1)} %get-tuple-element.81.refs_5_), channel_id=1, source_target_pairs={{0,4},{4,0},{8,12},{12,8},{16,20},{20,16},{24,28},{28,24},{1,5},{5... | collective-permute-start | bytes 98312 | tf_op jit(solution)/shard_map/ppermute | solution.py:518
  113.2 19.7 %collective-permute-start.19 = (bf16[16,1024]{1,0:T(8,128)(2,1)S(1)}, bf16[16,1024]{1,0:T(8,128)(2,1)S(1)}, u32[]{:S(2)}, u32[]{:S(2)}) collective-permute-start(bf16[16,1024]{1,0:T(8,128)(2,1)S(1)} %get-tuple-element.81.refs_5_), channel_id=1, source_target_pairs={{0,8},{4,12},{8,0},{12,4},{16,24},{20,28},{24,16},{28,20},{1,9},{5... | collective-permute-start | bytes 98312 | tf_op jit(solution)/shard_map/ppermute | solution.py:518
  114.9 19.4 %collective-permute-start.20 = (bf16[16,1024]{1,0:T(8,128)(2,1)S(1)}, bf16[16,1024]{1,0:T(8,128)(2,1)S(1)}, u32[]{:S(2)}, u32[]{:S(2)}) collective-permute-start(bf16[16,1024]{1,0:T(8,128)(2,1)S(1)} %get-tuple-element.81.refs_5_), channel_id=1, source_target_pairs={{0,12},{4,8},{8,4},{12,0},{16,28},{20,24},{24,20},{28,16},{1,13},{... | collective-permute-start | bytes 98312 | tf_op jit(solution)/shard_map/ppermute | solution.py:518
  137.3 12.0 %collective-permute-start.22 = (bf16[256,1024]{1,0:T(8,128)(2,1)S(1)}, bf16[256,1024]{1,0:T(8,128)(2,1)S(1)}, u32[]{:S(2)}, u32[]{:S(2)}) collective-permute-start(bf16[256,1024]{1,0:T(8,128)(2,1)S(1)} %shard_map.111.refs_1_), channel_id=1, source_target_pairs={{0,2},{1,3},{2,0},{3,1},{4,6},{5,7},{6,4},{7,5},{8,10},{9,11},{10,... | collective-permute-start | bytes 1572872 | tf_op jit(solution)/shard_map/ppermute | solution.py:518
  137.4 25.3 %collective-permute-start.27 = (bf16[384,1024]{1,0:T(8,128)(2,1)S(1)}, bf16[384,1024]{1,0:T(8,128)(2,1)S(1)}, u32[]{:S(2)}, u32[]{:S(2)}) collective-permute-start(bf16[384,1024]{1,0:T(8,128)(2,1)S(1)} %get-tuple-element.95), channel_id=1, source_target_pairs={{0,1},{1,0},{2,3},{3,2},{4,5},{5,4},{6,7},{7,6},{8,9},{9,8},{10,11... | collective-permute-start | bytes 2359304 | tf_op jit(solution)/shard_map/ppermute | solution.py:518
  138.9 14.4 %collective-permute-start.21 = (bf16[256,1024]{1,0:T(8,128)(2,1)S(1)}, bf16[256,1024]{1,0:T(8,128)(2,1)S(1)}, u32[]{:S(2)}, u32[]{:S(2)}) collective-permute-start(bf16[256,1024]{1,0:T(8,128)(2,1)S(1)} %shard_map.111.refs_1_), channel_id=1, source_target_pairs={{0,1},{1,0},{2,3},{3,2},{4,5},{5,4},{6,7},{7,6},{8,9},{9,8},{10,11... | collective-permute-start | bytes 1572872 | tf_op jit(solution)/shard_map/ppermute | solution.py:518
  149.3 4.0 %collective-permute-start.23 = (bf16[256,1024]{1,0:T(8,128)(2,1)S(1)}, bf16[256,1024]{1,0:T(8,128)(2,1)S(1)}, u32[]{:S(2)}, u32[]{:S(2)}) collective-permute-start(bf16[256,1024]{1,0:T(8,128)(2,1)S(1)} %collective-permute-done.22.refs_3_), channel_id=1, source_target_pairs={{0,1},{1,0},{2,3},{3,2},{4,5},{5,4},{6,7},{7,6},{8,9},{9,8},{10,11... | collective-permute-start | bytes 1572872 | tf_op jit(solution)/shard_map/ppermute | solution.py:518
  151.7 19.2 %collective-permute-start.28 = (bf16[384,1024]{1,0:T(8,128)(2,1)S(1)}, bf16[384,1024]{1,0:T(8,128)(2,1)S(1)}, u32[]{:S(2)}, u32[]{:S(2)}) collective-permute-start(bf16[384,1024]{1,0:T(8,128)(2,1)S(1)} %get-tuple-element.96), channel_id=1, source_target_pairs={{0,2},{1,3},{2,0},{3,1},{4,6},{5,7},{6,4},{7,5},{8,10},{9,11},{10,... | collective-permute-start | bytes 2359304 | tf_op jit(solution)/shard_map/ppermute | solution.py:518
  151.7 36.1 %collective-permute-start.29 = (bf16[384,1024]{1,0:T(8,128)(2,1)S(1)}, bf16[384,1024]{1,0:T(8,128)(2,1)S(1)}, u32[]{:S(2)}, u32[]{:S(2)}) collective-permute-start(bf16[384,1024]{1,0:T(8,128)(2,1)S(1)} %get-tuple-element.97), channel_id=1, source_target_pairs={{0,3},{1,2},{2,1},{3,0},{4,7},{5,6},{6,5},{7,4},{8,11},{9,10},{10,... | collective-permute-start | bytes 2359304 | tf_op jit(solution)/shard_map/ppermute | solution.py:518
  153.4 35.4 %copy-start.2 = (bf16[512,1024]{1,0:T(8,128)(2,1)S(1)}, bf16[512,1024]{1,0:T(8,128)(2,1)}, u32[]{:S(2)}) copy-start(bf16[512,1024]{1,0:T(8,128)(2,1)} %refs_1_.3) | copy-start | bytes 3145732
  162.2 25.7 %collective-permute-start.24 = (bf16[5,128,256]{2,1,0:T(8,128)(2,1)S(1)}, bf16[5,128,256]{2,1,0:T(8,128)(2,1)S(1)}, u32[]{:S(2)}, u32[]{:S(2)}) collective-permute-start(bf16[5,128,256]{2,1,0:T(8,128)(2,1)S(1)} %get-tuple-element.91), channel_id=1, source_target_pairs={{0,4},{4,0},{8,12},{12,8},{16,20},{20,16},{24,28},{28,24},{1,5},{5... | collective-permute-start | bytes 983048 | tf_op jit(solution)/shard_map/ppermute | solution.py:518
  162.7 25.2 %collective-permute-start.25 = (bf16[5,128,256]{2,1,0:T(8,128)(2,1)S(1)}, bf16[5,128,256]{2,1,0:T(8,128)(2,1)S(1)}, u32[]{:S(2)}, u32[]{:S(2)}) collective-permute-start(bf16[5,128,256]{2,1,0:T(8,128)(2,1)S(1)} %get-tuple-element.92), channel_id=1, source_target_pairs={{0,8},{4,12},{8,0},{12,4},{16,24},{20,28},{24,16},{28,20},{1,9},{5... | collective-permute-start | bytes 983048 | tf_op jit(solution)/shard_map/ppermute | solution.py:518
  162.7 25.2 %collective-permute-start.26 = (bf16[5,128,256]{2,1,0:T(8,128)(2,1)S(1)}, bf16[5,128,256]{2,1,0:T(8,128)(2,1)S(1)}, u32[]{:S(2)}, u32[]{:S(2)}) collective-permute-start(bf16[5,128,256]{2,1,0:T(8,128)(2,1)S(1)} %get-tuple-element.93), channel_id=1, source_target_pairs={{0,12},{4,8},{8,4},{12,0},{16,28},{20,24},{24,20},{28,16},{1,13},{... | collective-permute-start | bytes 983048 | tf_op jit(solution)/shard_map/ppermute | solution.py:518
  (7 other events, 6.4 us)

commit v8 on v7

--- a/solution.py
+++ b/solution.py
@@ -429,20 +429,30 @@
         out_cot[rows, :] = ((s - u * along) * inv_out[rows, 0:1]).astype(BF)
 
 
-def spread_kernel(incoming, catalogue, *refs, chunk):
+def spread_kernel(incoming, *refs, at, chunk):
     landed, out = refs[:-1], refs[-1]
-    stock, _ = catalogue.shape
-    slots = incoming.shape[1]
-    for r in range(0, stock, chunk):
-        hot = jnp.where(r + iota((chunk, slots), 0) == incoming[...], 1.0, 0.0).astype(BF)
-        v, at = 0.0, 0
+    for r in range(0, out.shape[0], chunk):
+        v, first = 0.0, at
         for part in landed:
-            v = v + dot_nn(hot[:, at : at + part.shape[0]], part[...])
-            at += part.shape[0]
-        c = catalogue[r : r + chunk, :].astype(F32)
+            slots = slice(first, first + part.shape[0])
+            line = r + iota((chunk, part.shape[0]), 0)
+            hot = jnp.where(line == incoming[:, slots], 1.0, 0.0).astype(BF)
+            v = v + dot_nn(hot, part[...])
+            first += part.shape[0]
+        out[r : r + chunk, :] = v
+
+
+def finish_kernel(incoming, catalogue, before, landed, out, *, at, chunk):
+    slots = landed.shape[0]
+    for r in range(0, out.shape[0], chunk):
+        rows = slice(r, r + chunk)
+        line = r + iota((chunk, slots), 0)
+        hot = jnp.where(line == incoming[:, at : at + slots], 1.0, 0.0).astype(BF)
+        v = before[rows, :] + dot_nn(hot, landed[...])
+        c = catalogue[rows, :].astype(F32)
         inv = lax.rsqrt(jnp.sum(c * c, axis=-1, keepdims=True) + EPS_UNIT)
         c = c * inv
-        out[r : r + chunk, :] = (v - c * jnp.sum(c * v, axis=-1, keepdims=True)) * inv
+        out[rows, :] = (v - c * jnp.sum(c * v, axis=-1, keepdims=True)) * inv
 
 
 def backward_kernel(meta, *refs, mp, dp):
@@ -681,7 +691,6 @@
                 pltpu.VMEM((near, width), F32),
             ],
         )(meta, *all_units, *ledgers)
-        slopes_back, mail = lax.optimization_barrier((slopes_back, mail))
         landed = exchange(mail, "mp")
     out_cot = call(out_cot_kernel, S((2 * events, width), BF), [VM] * 4, 1)(
         units, inv_out, slopes, slopes_back
@@ -701,7 +710,7 @@
     )(meta, *cots, w_out, wide, projected, turned)
     if short:
         parts = exchange(parts, "dp")
-        parts, landed = lax.optimization_barrier((parts, landed))
+        parts, landed[:-1] = lax.optimization_barrier((parts, landed[:-1]))
         w_in_grad, w_out_grad = call(
             sum_kernel,
             [S((4, width // dp, cols), F32), S((cols, width // dp), F32)],
@@ -726,14 +735,25 @@
             3,
         )(meta, expo, total, total_far, units_bf)
         landed = [in_half(sending)]
+    rows_chunk = math.gcd(stock, 128)
+    last = slots // 4
+    if len(landed) == 1:
+        landed = [landed[0][: slots - last], landed[0][slots - last :]]
+    before = call(
+        functools.partial(spread_kernel, at=0, chunk=rows_chunk),
+        S((stock, width), F32),
+        [VM] * len(landed),
+        3,
+    )(returning, *landed[:-1])
+    if short:
+        before, _ = lax.optimization_barrier((before, w_in_grad))
     cat_grad = call(
-        functools.partial(spread_kernel, chunk=math.gcd(stock, 128)),
+        functools.partial(finish_kernel, at=slots - last, chunk=rows_chunk),
         S((stock, width), F32),
-        [VM, VM] + [VM] * len(landed),
-        4,
+        [VM] * 4,
+        3,
         out_specs=[HB],
-        limit=24,
-    )(returning, catalogue, *landed)
+    )(returning, catalogue, before, landed[-1])
     return (w_in_grad, w_out_grad, cat_grad)
 
 

time: 194 us -> 190 us (0.979)
  waiting for transfers between devices: 97 us -> 89.4 us
  starting transfers between devices: 39.3 us -> 42.5 us
  local copies, waits for them, and re-layouts: 13.4 us -> 11.2 us
    ppermute x30, waiting for transfers between devices: 96.9 us -> 89.4 us  [swapped(): return lax.ppermute(x, axis, [(a, a ^ bit) for a in range(size)])]
    unnamed x46 -> x40, local copies, waits for them, and re-layouts: 13.4 us -> 11.2 us
    pallas_call x12 -> x13, Pallas kernels: 41.1 us -> 41.8 us  [run(): pl.pallas_call(kernel, out_shape=outs, in_specs=list(in_specs), out_specs...]
  transfers between devices with their start and end apart: 32 -> 32, of which waited for: 15 -> 20; matrix products, arithmetic and copies ran while one was open for 0% -> 0% of each run, Pallas kernels for 15% -> 15%
where the time goes in v8:
time: 190 us; the launch traced here: 187 us
  waiting for transfers between devices  89.4 us (47%)
  starting transfers between devices  42.5 us (22%)
  Pallas kernels  41.8 us (22%)
  local copies, waits for them, and re-layouts  11.2 us (6%)
    ppermute x30, waiting for transfers between devices, swapped(): return lax.ppermute(x, axis, [(a, a ^ bit) for a in range(size)])  89.4 us
    pallas_call x13, Pallas kernels, run(): pl.pallas_call(kernel, out_shape=outs, in_specs=list(in_specs), out_specs...  41.8 us
    ppermute x30, starting transfers between devices, swapped(): return lax.ppermute(x, axis, [(a, a ^ bit) for a in range(size)])  27.3 us
    unnamed x40, local copies, waits for them, and re-layouts  11.2 us
    all_to_all x1, starting transfers between devices, in_half(): lax.all_to_all(x.reshape(near, 2 * capacity, width), ('dp', 'mp'), split_...  9.71 us
    all_to_all x1, starting transfers between devices, per_device(): lax.all_to_all(packed, 'dp', split_axis=0, concat_axis=0, tiled=True)  5.55 us
  transfers between devices with their start and end apart: 32, of which 20 were waited for; matrix products, arithmetic and copies ran while one was open for 0% of the time, Pallas kernels for 15%

profile of v8, /device:TPU:13, one launch (start us, length us, event | category | flops | bytes accessed | tf_op | source)
XLA Modules:
  0.0 187.3 jit_solution(10698884262658770186)
XLA Ops:
  0.6 1.4 pad_add_fusion.refs_0_
  2.0 5.1 %shard_map.103 = (bf16[8,144,256]{2,1,0:T(8,128)(2,1)}, f32[32,128]{1,0:T(8,128)}) custom-call(s32[258]{0:T(512)} %pad_add_fusion.refs_0_, bf16[16,32,256]{2,1,0:T(8,128)(2,1)} %refs_1_.2, s32[8,128]{1,0:T(8,128)} %bitcast.11, s32[8,128]{1,0:T(8,128)} %bitcast.12), custom_call_target="tpu_custom_call" | custom-call | bytes 13200000 | tf_op jit(solution)/shard_map/pallas_call | solution.py:70
  7.1 5.6 %all-to-all-start = ((bf16[8,144,256]{2,1,0:T(8,128)(2,1)}), bf16[8,144,256]{2,1,0:T(8,128)(2,1)S(1)}, u32[]{:S(2)}, u32[]{:S(2)}) async-start(bf16[8,144,256]{2,1,0:T(8,128)(2,1)} %get-tuple-element.51), calls=%async_computation | async-start | bytes 1179648 | tf_op jit(solution)/shard_map/all_to_all | solution.py:594
  12.9 12.3 %collective-permute-done.refs_7_ = bf16[256,1024]{1,0:T(8,128)(2,1)} collective-permute-done((bf16[256,1024]{1,0:T(8,128)(2,1)}, bf16[256,1024]{1,0:T(8,128)(2,1)}, u32[]{:S(2)}, u32[]{:S(2)}) %collective-permute-start) | collective-permute-done | bytes 524320 | tf_op jit(solution)/shard_map/ppermute | solution.py:528
  25.8 1.0 shard_map.104
  27.1 2.9 %collective-permute-done.1.refs_3_ = bf16[128,256]{1,0:T(8,128)(2,1)S(1)} collective-permute-done((bf16[128,256]{1,0:T(8,128)(2,1)S(1)}, bf16[128,256]{1,0:T(8,128)(2,1)S(1)}, u32[]{:S(2)}, u32[]{:S(2)}) %collective-permute-start.1) | collective-permute-done | bytes 65568 | tf_op jit(solution)/shard_map/ppermute | solution.py:528
  30.2 5.4 %collective-permute-start.3 = (bf16[128,256]{1,0:T(8,128)(2,1)S(1)}, bf16[128,256]{1,0:T(8,128)(2,1)S(1)}, u32[]{:S(2)}, u32[]{:S(2)}) collective-permute-start(bf16[128,256]{1,0:T(8,128)(2,1)S(1)} %get-tuple-element.54.refs_1_), channel_id=1, source_target_pairs={{0,1},{1,0},{2,3},{3,2},{4,5},{5,4},{6,7},{7,6},{8,9},{9,8},{10,11... | collective-permute-start | bytes 196616 | tf_op jit(solution)/shard_map/ppermute | solution.py:528
  36.8 2.8 %shard_map.105 = (bf16[1536,1024]{1,0:T(8,128)(2,1)S(1)}, s32[1,1536]{1,0:T(1,128)}, s32[1,1536]{1,0:T(1,128)S(1)}) custom-call(s32[258]{0:T(512)S(1)} %copy-done.15, bf16[128,256]{1,0:T(8,128)(2,1)S(1)} %get-tuple-element.54.refs_1_, bf16[128,256]{1,0:T(8,128)(2,1)S(1)} %collective-permute-done.3.refs_2_, ...), custom_call_target="tpu_custom_call" | custom-call | bytes 13200000 | tf_op jit(solution)/shard_map/pallas_call | solution.py:70
  39.8 1.5 copy-done.3
  41.3 9.7 %all-to-all-start.1 = ((bf16[16,96,1024]{2,1,0:T(8,128)(2,1)}), bf16[16,96,1024]{2,1,0:T(8,128)(2,1)S(1)}, u32[]{:S(2)}, u32[]{:S(2)}) async-start(bf16[16,96,1024]{2,1,0:T(8,128)(2,1)} %bitcast.10), calls=%async_computation.1 | async-start | bytes 6291456 | tf_op jit(solution)/shard_map/all_to_all | solution.py:575
  52.1 1.2 collective-permute-done.2.refs_2_
  53.3 0.7 collective-permute-done.7.refs_4_
  54.0 1.6 copy-done.10
  55.6 1.0 copy-done.14
  56.7 8.2 %shard_map.106 = (f32[3,1024,256]{2,1,0:T(8,128)S(1)}, bf16[9,1024,256]{2,1,0:T(8,128)(2,1)S(1)}, bf16[1280,1024]{1,0:T(8,128)(2,1)S(1)}, bf16[256,1024]{1,0:T(8...) custom-call(s32[258]{0:T(512)S(1)} %copy-done.16, ...), custom_call_target="tpu_custom_call" | custom-call | bytes 33000000 | tf_op jit(solution)/shard_map/pallas_call | solution.py:70
  64.9 2.2 %copy-done = bf16[9,1024,256]{2,1,0:T(8,128)(2,1)} copy-done((bf16[9,1024,256]{2,1,0:T(8,128)(2,1)}, bf16[9,1024,256]{2,1,0:T(8,128)(2,1)S(1)}, u32[]{:S(2)}) %copy-start) | copy-done | bytes 4718616
  67.0 1.6 copy-done.4
  68.7 1.5 copy-done.6
  70.8 1.6 collective-permute-start.10
  72.4 11.6 %collective-permute-done.9.refs_3_ = bf16[256,256]{1,0:T(8,128)(2,1)S(1)} collective-permute-done((bf16[256,256]{1,0:T(8,128)(2,1)S(1)}, bf16[256,256]{1,0:T(8,128)(2,1)S(1)}, u32[]{:S(2)}, u32[]{:S(2)}) %collective-permute-start.9) | collective-permute-done | bytes 131104 | tf_op jit(solution)/shard_map/ppermute | solution.py:528
  84.0 7.8 %collective-permute-done.10.refs_4_ = bf16[256,256]{1,0:T(8,128)(2,1)S(1)} collective-permute-done((bf16[256,256]{1,0:T(8,128)(2,1)S(1)}, bf16[256,256]{1,0:T(8,128)(2,1)S(1)}, u32[]{:S(2)}, u32[]{:S(2)}) %collective-permute-start.10) | collective-permute-done | bytes 131104 | tf_op jit(solution)/shard_map/ppermute | solution.py:528
  91.8 2.7 %shard_map.107 = (f32[256,1024]{1,0:T(8,128)S(1)}, bf16[256,1024]{1,0:T(8,128)(2,1)}, f32[256,128]{1,0:T(8,128)S(1)}) custom-call(bf16[256,1024]{1,0:T(8,128)(2,1)S(1)} %get-tuple-element.60.refs_0_, bf16[256,256]{1,0:T(8,128)(2,1)S(1)} %get-tuple-element.61.refs_1_, bf16[256,256]{1,0:T(8,128)(2,1)S(1)} %collective-permute-done.8.refs_2_, ...), custom_call_target="tpu_custom_call" | custom-call | bytes 6600000 | tf_op jit(solution)/shard_map/pallas_call | solution.py:70
  94.5 1.0 copy-done.11
  95.5 3.2 %shard_map.108 = (f32[1536,256]{1,0:T(8,128)S(1)}, f32[1536,128]{1,0:T(8,128)S(1)}, f32[1,256]{1,0:T(1,128)S(1)}) custom-call(s32[258]{0:T(512)S(1)} %copy-done.16, bf16[1536,1024]{1,0:T(8,128)(2,1)S(1)} %bitcast.6, f32[32,128]{1,0:T(8,128)S(1)} %copy-done.17, f32[32,128]{1,0:T(8,128)S(1)} %collective-permute-done.6.refs_3_, ...), custom_call_target="tpu_custom_call" | custom-call | bytes 13200000 | tf_op jit(solution)/shard_map/pallas_call | solution.py:70
  98.7 2.2 %collective-permute-start.13 = (f32[1,256]{1,0:T(1,128)S(1)}, f32[1,256]{1,0:T(1,128)S(1)}, u32[]{:S(2)}, u32[]{:S(2)}) collective-permute-start(f32[1,256]{1,0:T(1,128)S(1)} %get-tuple-element.73.refs_6_), channel_id=1, source_target_pairs={{0,16},{4,20},{8,24},{12,28},{16,0},{20,4},{24,8},{28,12},{1,17},{... | collective-permute-start | bytes 3080 | tf_op jit(solution)/shard_map/ppermute | solution.py:528
  100.9 1.2 collective-permute-done.13.refs_7_
  102.1 2.0 %shard_map.109 = (f32[256,1024]{1,0:T(8,128)S(1)}, bf16[256,1024]{1,0:T(8,128)(2,1)S(1)}, bf16[16,1024]{1,0:T(8,128)(2,1)S(1)}) custom-call(s32[258]{0:T(512)S(1)} %copy-done.16, bf16[1536,1024]{1,0:T(8,128)(2,1)S(1)} %bitcast.7, f32[32,128]{1,0:T(8,128)S(1)} %copy-done.17, f32[32,128]{1,0:T(8,128)S(1)} %collective-permute-done.6.refs_3_, ...), custom_call_target="tpu_custom_call" | custom-call | bytes 9900000 | tf_op jit(solution)/shard_map/pallas_call | solution.py:70
  104.1 2.2 %collective-permute-start.14 = (bf16[256,1024]{1,0:T(8,128)(2,1)S(1)}, bf16[256,1024]{1,0:T(8,128)(2,1)S(1)}, u32[]{:S(2)}, u32[]{:S(2)}) collective-permute-start(bf16[256,1024]{1,0:T(8,128)(2,1)S(1)} %get-tuple-element.75), channel_id=1, source_target_pairs={{0,16},{4,20},{8,24},{12,28},{16,0},{20,4},{24,8},{28,12},{1,17},{... | collective-permute-start | bytes 1572872 | tf_op jit(solution)/shard_map/ppermute | solution.py:528
  106.3 1.7 collective-permute-start.21
  108.0 0.9 collective-permute-start.22
  109.2 19.8 %collective-permute-done.14.refs_3_ = bf16[256,1024]{1,0:T(8,128)(2,1)S(1)} collective-permute-done((bf16[256,1024]{1,0:T(8,128)(2,1)S(1)}, bf16[256,1024]{1,0:T(8,128)(2,1)S(1)}, u32[]{:S(2)}, u32[]{:S(2)}) %collective-permute-start.14) | collective-permute-done | bytes 524320 | tf_op jit(solution)/shard_map/ppermute | solution.py:528
  129.5 1.3 collective-permute-start.24
  130.8 2.2 %collective-permute-start.25 = (bf16[16,1024]{1,0:T(8,128)(2,1)S(1)}, bf16[16,1024]{1,0:T(8,128)(2,1)S(1)}, u32[]{:S(2)}, u32[]{:S(2)}) collective-permute-start(bf16[16,1024]{1,0:T(8,128)(2,1)S(1)} %get-tuple-element.83.refs_5_), channel_id=1, source_target_pairs={{0,8},{4,12},{8,0},{12,4},{16,24},{20,28},{24,16},{28,20},{1,9},{5... | collective-permute-start | bytes 98312 | tf_op jit(solution)/shard_map/ppermute | solution.py:528
  133.0 9.3 %collective-permute-done.23.refs_4_ = bf16[256,1024]{1,0:T(8,128)(2,1)S(1)} collective-permute-done((bf16[256,1024]{1,0:T(8,128)(2,1)}, bf16[256,1024]{1,0:T(8,128)(2,1)S(1)}, u32[]{:S(2)}, u32[]{:S(2)}) %collective-permute-start.23) | collective-permute-done | bytes 524320 | tf_op jit(solution)/shard_map/ppermute | solution.py:528
  142.3 1.4 collective-permute-done.26.refs_8_
  143.7 2.3 %shard_map.112 = (bf16[384,1024]{1,0:T(8,128)(2,1)S(1)}, bf16[384,1024]{1,0:T(8,128)(2,1)S(1)}, bf16[384,1024]{1,0:T(8,128)(2,1)S(1)}, bf16[384,1024]{1,0:T(8,128)(2,1)S(1)}) custom-call(s32[258]{0:T(512)S(1)} %copy-done.16, bf16[256,1024]{1,0:T(8,128)(2,1)} %get-tuple-element.70.refs_4_.refs_1_, bf16[256,1024]{1,0:T(8,128)(2,1)S(1)} %collective-permute-done.21.refs_2_, ...), custom_call_target="tpu_custom_call" | custom-call | bytes 13200000 | tf_op jit(solution)/shard_map/pallas_call | solution.py:70
  146.0 1.8 collective-permute-start.27
  148.3 1.7 collective-permute-start.29
  150.5 0.7 collective-permute-done.17.refs_4_
  151.3 8.8 %shard_map.111 = (bf16[5,128,256]{2,1,0:T(8,128)(2,1)S(1)}, bf16[5,128,256]{2,1,0:T(8,128)(2,1)S(1)}, bf16[5,128,256]{2,1,0:T(8,128)(2,1)S(1)}, bf16[5,128,256]{2,1,0:T(8,128)(2,1)S(1)}) custom-call(s32[258]{0:T(512)S(1)} %copy-done.16, bf16[256,1024]{1,0:T(8,128)(2,1)S(1)} %shard_map.110.refs_1_, bf16[256,1024]{1,0:T(8,128)(2,1)S(1)} %collective-permute-done.15.refs_2_, ...), custom_call_target="tpu_custom_call" | custom-call | bytes 33000000 | tf_op jit(solution)/shard_map/pallas_call | solution.py:70
  160.1 1.9 %collective-permute-start.19 = (bf16[5,128,256]{2,1,0:T(8,128)(2,1)S(1)}, bf16[5,128,256]{2,1,0:T(8,128)(2,1)S(1)}, u32[]{:S(2)}, u32[]{:S(2)}) collective-permute-start(bf16[5,128,256]{2,1,0:T(8,128)(2,1)S(1)} %get-tuple-element.81), channel_id=1, source_target_pairs={{0,8},{4,12},{8,0},{12,4},{16,24},{20,28},{24,16},{28,20},{1,9},{5... | collective-permute-start | bytes 983048 | tf_op jit(solution)/shard_map/ppermute | solution.py:528
  162.8 4.7 %collective-permute-done.28.refs_3_ = bf16[384,1024]{1,0:T(8,128)(2,1)S(1)} collective-permute-done((bf16[384,1024]{1,0:T(8,128)(2,1)S(1)}, bf16[384,1024]{1,0:T(8,128)(2,1)S(1)}, u32[]{:S(2)}, u32[]{:S(2)}) %collective-permute-start.28) | collective-permute-done | bytes 786464 | tf_op jit(solution)/shard_map/ppermute | solution.py:528
  167.5 1.6 collective-permute-done.18.refs_1_
  169.5 7.4 %collective-permute-done.20.refs_3_ = bf16[5,128,256]{2,1,0:T(8,128)(2,1)S(1)} collective-permute-done((bf16[5,128,256]{2,1,0:T(8,128)(2,1)S(1)}, bf16[5,128,256]{2,1,0:T(8,128)(2,1)S(1)}, u32[]{:S(2)}, u32[]{:S(2)}) %collective-permute-start.20) | collective-permute-done | bytes 327712 | tf_op jit(solution)/shard_map/ppermute | solution.py:528
  176.9 1.0 shard_map.113
  177.9 1.8 shard_map.114.refs_2_
  179.7 4.8 %collective-permute-done.29.refs_3_ = bf16[384,1024]{1,0:T(8,128)(2,1)S(1)} collective-permute-done((bf16[384,1024]{1,0:T(8,128)(2,1)S(1)}, bf16[384,1024]{1,0:T(8,128)(2,1)S(1)}, u32[]{:S(2)}, u32[]{:S(2)}) %collective-permute-start.29) | collective-permute-done | bytes 786464 | tf_op jit(solution)/shard_map/ppermute | solution.py:528
  184.5 2.7 %shard_map.115 = f32[512,1024]{1,0:T(8,128)} custom-call(s32[1,1536]{1,0:T(1,128)S(1)} %get-tuple-element.93.refs_0_, bf16[512,1024]{1,0:T(8,128)(2,1)S(1)} %copy-done.2, f32[512,1024]{1,0:T(8,128)S(1)} %shard_map.114.refs_2_, bf16[384,1024]{1,0:T(8,128)(2,1)S(1)} %collective-permute-done.29.refs_3_), custom_call_target="tpu_custom_call" | custom-call | bytes 9900000 | tf_op jit(solution)/shard_map/pallas_call | solution.py:70
  (71 shorter events, 7.6 us)
Async XLA Ops:
  0.6 36.2 %copy-start.1 = (bf16[512,1024]{1,0:T(8,128)(2,1)S(1)}, bf16[512,1024]{1,0:T(8,128)(2,1)}, u32[]{:S(2)}) copy-start(bf16[512,1024]{1,0:T(8,128)(2,1)} %refs_1_.3) | copy-start | bytes 3145732
  7.1 18.0 %all-to-all-start = ((bf16[8,144,256]{2,1,0:T(8,128)(2,1)}), bf16[8,144,256]{2,1,0:T(8,128)(2,1)S(1)}, u32[]{:S(2)}, u32[]{:S(2)}) async-start(bf16[8,144,256]{2,1,0:T(8,128)(2,1)} %get-tuple-element.51), calls=%async_computation | async-start | bytes 1179648 | tf_op jit(solution)/shard_map/all_to_all | solution.py:594
  12.7 12.5 %collective-permute-start = (bf16[256,1024]{1,0:T(8,128)(2,1)}, bf16[256,1024]{1,0:T(8,128)(2,1)}, u32[]{:S(2)}, u32[]{:S(2)}) collective-permute-start(bf16[256,1024]{1,0:T(8,128)(2,1)} %refs_5_.7), channel_id=1, source_target_pairs={{0,2},{1,3},{2,0},{3,1},{4,6},{5,7},{6,4},{7,5},{8,10},{9,11},{10,... | collective-permute-start | bytes 1572872 | tf_op jit(solution)/shard_map/ppermute | solution.py:528
  26.8 12.8 %copy-start.13 = (bf16[1024,256]{1,0:T(8,128)(2,1)}, bf16[1024,256]{1,0:T(8,128)(2,1)S(1)}, u32[]{:S(2)}) copy-start(bf16[1024,256]{1,0:T(8,128)(2,1)S(1)} %get-tuple-element.55.refs_1_) | copy-start | bytes 1572868
  26.8 3.2 %collective-permute-start.1 = (bf16[128,256]{1,0:T(8,128)(2,1)S(1)}, bf16[128,256]{1,0:T(8,128)(2,1)S(1)}, u32[]{:S(2)}, u32[]{:S(2)}) collective-permute-start(bf16[128,256]{1,0:T(8,128)(2,1)S(1)} %get-tuple-element.54.refs_1_), channel_id=1, source_target_pairs={{0,2},{1,3},{2,0},{3,1},{4,6},{5,7},{6,4},{7,5},{8,10},{9,11},{10,... | collective-permute-start | bytes 196616 | tf_op jit(solution)/shard_map/ppermute | solution.py:528
  30.0 9.9 %collective-permute-start.5 = (bf16[1024,256]{1,0:T(8,128)(2,1)S(1)}, bf16[1024,256]{1,0:T(8,128)(2,1)}, u32[]{:S(2)}, u32[]{:S(2)}) collective-permute-start(bf16[1024,256]{1,0:T(8,128)(2,1)S(1)} %get-tuple-element.55.refs_1_), channel_id=1, source_target_pairs={{0,2},{1,3},{2,0},{3,1},{4,6},{5,7},{6,4},{7,5},{8,10},{9,11},{10,... | collective-permute-start | bytes 1572872 | tf_op jit(solution)/shard_map/ppermute | solution.py:528
  30.2 6.3 %collective-permute-start.3 = (bf16[128,256]{1,0:T(8,128)(2,1)S(1)}, bf16[128,256]{1,0:T(8,128)(2,1)S(1)}, u32[]{:S(2)}, u32[]{:S(2)}) collective-permute-start(bf16[128,256]{1,0:T(8,128)(2,1)S(1)} %get-tuple-element.54.refs_1_), channel_id=1, source_target_pairs={{0,1},{1,0},{2,3},{3,2},{4,5},{5,4},{6,7},{7,6},{8,9},{9,8},{10,11... | collective-permute-start | bytes 196616 | tf_op jit(solution)/shard_map/ppermute | solution.py:528
  35.5 1.3 collective-permute-start.4
  35.6 4.1 %collective-permute-start.6 = (f32[32,128]{1,0:T(8,128)}, f32[32,128]{1,0:T(8,128)S(1)}, u32[]{:S(2)}, u32[]{:S(2)}) collective-permute-start(f32[32,128]{1,0:T(8,128)} %get-tuple-element.58.refs_2_), channel_id=1, source_target_pairs={{0,16},{4,20},{8,24},{12,28},{16,0},{20,4},{24,8},{28,12},{1,17},{... | collective-permute-start | bytes 49160 | tf_op jit(solution)/shard_map/ppermute | solution.py:528
  39.6 1.7 copy-start.3
  41.3 12.7 %copy-start.16 = (s32[258]{0:T(512)S(1)}, s32[258]{0:T(512)}, u32[]{:S(2)}) copy-start(s32[258]{0:T(512)} %pad_add_fusion.refs_0_) | copy-start | bytes 3100
  41.3 54.1 %all-to-all-start.1 = ((bf16[16,96,1024]{2,1,0:T(8,128)(2,1)}), bf16[16,96,1024]{2,1,0:T(8,128)(2,1)S(1)}, u32[]{:S(2)}, u32[]{:S(2)}) async-start(bf16[16,96,1024]{2,1,0:T(8,128)(2,1)} %bitcast.10), calls=%async_computation.1 | async-start | bytes 6291456 | tf_op jit(solution)/shard_map/all_to_all | solution.py:575
  51.0 40.8 %copy-start.8 = (bf16[256,1024]{1,0:T(8,128)(2,1)S(1)}, bf16[256,1024]{1,0:T(8,128)(2,1)}, u32[]{:S(2)}) copy-start(bf16[256,1024]{1,0:T(8,128)(2,1)} %refs_5_.7) | copy-start | bytes 1572868
  51.0 2.2 %collective-permute-start.2 = (bf16[1024,256]{1,0:T(8,128)(2,1)}, bf16[1024,256]{1,0:T(8,128)(2,1)S(1)}, u32[]{:S(2)}, u32[]{:S(2)}) collective-permute-start(bf16[1024,256]{1,0:T(8,128)(2,1)} %copy-done.13), channel_id=1, source_target_pairs={{0,1},{1,0},{2,3},{3,2},{4,5},{5,4},{6,7},{7,6},{8,9},{9,8},{10,11... | collective-permute-start | bytes 1572872 | tf_op jit(solution)/shard_map/ppermute | solution.py:528
  51.5 2.6 %collective-permute-start.7 = (bf16[1024,256]{1,0:T(8,128)(2,1)}, bf16[1024,256]{1,0:T(8,128)(2,1)S(1)}, u32[]{:S(2)}, u32[]{:S(2)}) collective-permute-start(bf16[1024,256]{1,0:T(8,128)(2,1)} %collective-permute-done.5.refs_3_), channel_id=1, source_target_pairs={{0,1},{1,0},{2,3},{3,2},{4,5},{5,4},{6,7},{7,6},{8,9},{9,8},{10,11... | collective-permute-start | bytes 1572872 | tf_op jit(solution)/shard_map/ppermute | solution.py:528
  51.6 20.8 %collective-permute-start.11 = (bf16[256,1024]{1,0:T(8,128)(2,1)}, bf16[256,1024]{1,0:T(8,128)(2,1)S(1)}, u32[]{:S(2)}, u32[]{:S(2)}) collective-permute-start(bf16[256,1024]{1,0:T(8,128)(2,1)} %refs_5_.7), channel_id=1, source_target_pairs={{0,1},{1,0},{2,3},{3,2},{4,5},{5,4},{6,7},{7,6},{8,9},{9,8},{10,11... | collective-permute-start | bytes 1572872 | tf_op jit(solution)/shard_map/ppermute | solution.py:528
  52.0 20.4 %collective-permute-start.12 = (bf16[256,1024]{1,0:T(8,128)(2,1)}, bf16[256,1024]{1,0:T(8,128)(2,1)S(1)}, u32[]{:S(2)}, u32[]{:S(2)}) collective-permute-start(bf16[256,1024]{1,0:T(8,128)(2,1)} %collective-permute-done.refs_7_), channel_id=1, source_target_pairs={{0,1},{1,0},{2,3},{3,2},{4,5},{5,4},{6,7},{7,6},{8,9},{9,8},{10,11... | collective-permute-start | bytes 1572872 | tf_op jit(solution)/shard_map/ppermute | solution.py:528
  54.0 1.6 copy-start.10
  64.9 2.2 %copy-start = (bf16[9,1024,256]{2,1,0:T(8,128)(2,1)}, bf16[9,1024,256]{2,1,0:T(8,128)(2,1)S(1)}, u32[]{:S(2)}) copy-start(bf16[9,1024,256]{2,1,0:T(8,128)(2,1)S(1)} %get-tuple-element.77.refs_7_) | copy-start | bytes 14155780
  67.0 1.6 copy-start.4
  70.2 25.2 %copy-start.17 = (f32[32,128]{1,0:T(8,128)S(1)}, f32[32,128]{1,0:T(8,128)}, u32[]{:S(2)}) copy-start(f32[32,128]{1,0:T(8,128)} %get-tuple-element.58.refs_2_) | copy-start | bytes 49156
  70.2 2.2 %collective-permute-start.8 = (bf16[256,256]{1,0:T(8,128)(2,1)S(1)}, bf16[256,256]{1,0:T(8,128)(2,1)S(1)}, u32[]{:S(2)}, u32[]{:S(2)}) collective-permute-start(bf16[256,256]{1,0:T(8,128)(2,1)S(1)} %get-tuple-element.62), channel_id=1, source_target_pairs={{0,1},{1,0},{2,3},{3,2},{4,5},{5,4},{6,7},{7,6},{8,9},{9,8},{10,11... | collective-permute-start | bytes 393224 | tf_op jit(solution)/shard_map/ppermute | solution.py:528
  70.5 13.5 %collective-permute-start.9 = (bf16[256,256]{1,0:T(8,128)(2,1)S(1)}, bf16[256,256]{1,0:T(8,128)(2,1)S(1)}, u32[]{:S(2)}, u32[]{:S(2)}) collective-permute-start(bf16[256,256]{1,0:T(8,128)(2,1)S(1)} %get-tuple-element.63), channel_id=1, source_target_pairs={{0,2},{1,3},{2,0},{3,1},{4,6},{5,7},{6,4},{7,5},{8,10},{9,11},{10,... | collective-permute-start | bytes 393224 | tf_op jit(solution)/shard_map/ppermute | solution.py:528
  70.8 21.0 %collective-permute-start.10 = (bf16[256,256]{1,0:T(8,128)(2,1)S(1)}, bf16[256,256]{1,0:T(8,128)(2,1)S(1)}, u32[]{:S(2)}, u32[]{:S(2)}) collective-permute-start(bf16[256,256]{1,0:T(8,128)(2,1)S(1)} %get-tuple-element.64), channel_id=1, source_target_pairs={{0,3},{1,2},{2,1},{3,0},{4,7},{5,6},{6,5},{7,4},{8,11},{9,10},{10,... | collective-permute-start | bytes 393224 | tf_op jit(solution)/shard_map/ppermute | solution.py:528
  95.5 33.6 %copy-start.12 = (f32[256,1024]{1,0:T(8,128)S(1)}, f32[256,1024]{1,0:T(8,128)}, u32[]{:S(2)}) copy-start(f32[256,1024]{1,0:T(8,128)} %copy-done.11) | copy-start | bytes 3145732
  98.7 3.4 %collective-permute-start.13 = (f32[1,256]{1,0:T(1,128)S(1)}, f32[1,256]{1,0:T(1,128)S(1)}, u32[]{:S(2)}, u32[]{:S(2)}) collective-permute-start(f32[1,256]{1,0:T(1,128)S(1)} %get-tuple-element.73.refs_6_), channel_id=1, source_target_pairs={{0,16},{4,20},{8,24},{12,28},{16,0},{20,4},{24,8},{28,12},{1,17},{... | collective-permute-start | bytes 3080 | tf_op jit(solution)/shard_map/ppermute | solution.py:528
  102.1 49.2 %slice-start = ((s8[4718592]{0:T(1024)(128)(4,1)}), s8[4194304]{0:T(1024)(128)(4,1)S(1)}, s32[]{:S(2)}) async-start(s8[4718592]{0:T(1024)(128)(4,1)} %bitcast.8), calls=%async_computation.2 | async-start | bytes 8388608
  102.1 49.2 %slice-start.1 = ((s8[4718592]{0:T(1024)(128)(4,1)}), s8[524288]{0:T(1024)(128)(4,1)S(1)}, s32[]{:S(2)}) async-start(s8[4718592]{0:T(1024)(128)(4,1)} %bitcast.8), calls=%async_computation.3 | async-start | bytes 1048576
  102.1 49.2 %copy-start.7 = (bf16[1280,1024]{1,0:T(8,128)(2,1)S(1)}, bf16[1280,1024]{1,0:T(8,128)(2,1)}, u32[]{:S(2)}) copy-start(bf16[1280,1024]{1,0:T(8,128)(2,1)} %copy-done.6) | copy-start | bytes 7864324
  104.1 24.9 %collective-permute-start.14 = (bf16[256,1024]{1,0:T(8,128)(2,1)S(1)}, bf16[256,1024]{1,0:T(8,128)(2,1)S(1)}, u32[]{:S(2)}, u32[]{:S(2)}) collective-permute-start(bf16[256,1024]{1,0:T(8,128)(2,1)S(1)} %get-tuple-element.75), channel_id=1, source_target_pairs={{0,16},{4,20},{8,24},{12,28},{16,0},{20,4},{24,8},{28,12},{1,17},{... | collective-permute-start | bytes 1572872 | tf_op jit(solution)/shard_map/ppermute | solution.py:528
  106.3 24.5 %collective-permute-start.21 = (bf16[256,1024]{1,0:T(8,128)(2,1)}, bf16[256,1024]{1,0:T(8,128)(2,1)S(1)}, u32[]{:S(2)}, u32[]{:S(2)}) collective-permute-start(bf16[256,1024]{1,0:T(8,128)(2,1)} %get-tuple-element.70.refs_4_.refs_1_), channel_id=1, source_target_pairs={{0,4},{4,0},{8,12},{12,8},{16,20},{20,16},{24,28},{28,24},{1,5},{5... | collective-permute-start | bytes 1572872 | tf_op jit(solution)/shard_map/ppermute | solution.py:528
  108.0 25.0 %collective-permute-start.22 = (bf16[256,1024]{1,0:T(8,128)(2,1)}, bf16[256,1024]{1,0:T(8,128)(2,1)S(1)}, u32[]{:S(2)}, u32[]{:S(2)}) collective-permute-start(bf16[256,1024]{1,0:T(8,128)(2,1)} %get-tuple-element.70.refs_4_.refs_1_), channel_id=1, source_target_pairs={{0,8},{4,12},{8,0},{12,4},{16,24},{20,28},{24,16},{28,20},{1,9},{5... | collective-permute-start | bytes 1572872 | tf_op jit(solution)/shard_map/ppermute | solution.py:528
  108.9 33.4 %collective-permute-start.23 = (bf16[256,1024]{1,0:T(8,128)(2,1)}, bf16[256,1024]{1,0:T(8,128)(2,1)S(1)}, u32[]{:S(2)}, u32[]{:S(2)}) collective-permute-start(bf16[256,1024]{1,0:T(8,128)(2,1)} %get-tuple-element.70.refs_4_.refs_1_), channel_id=1, source_target_pairs={{0,12},{4,8},{8,4},{12,0},{16,28},{20,24},{24,20},{28,16},{1,13},{... | collective-permute-start | bytes 1572872 | tf_op jit(solution)/shard_map/ppermute | solution.py:528
  129.0 22.2 %copy-start.5 = (f32[3,1024,256]{2,1,0:T(8,128)S(1)}, f32[3,1024,256]{2,1,0:T(8,128)}, u32[]{:S(2)}) copy-start(f32[3,1024,256]{2,1,0:T(8,128)} %copy-done.4) | copy-start | bytes 9437188
  129.0 22.2 %copy-start.9 = (bf16[256,1024]{1,0:T(8,128)(2,1)S(1)}, bf16[256,1024]{1,0:T(8,128)(2,1)}, u32[]{:S(2)}) copy-start(bf16[256,1024]{1,0:T(8,128)(2,1)} %refs_5_.7) | copy-start | bytes 1572868
  129.4 18.5 %collective-permute-start.16 = (bf16[256,1024]{1,0:T(8,128)(2,1)S(1)}, bf16[256,1024]{1,0:T(8,128)(2,1)S(1)}, u32[]{:S(2)}, u32[]{:S(2)}) collective-permute-start(bf16[256,1024]{1,0:T(8,128)(2,1)S(1)} %shard_map.110.refs_1_), channel_id=1, source_target_pairs={{0,2},{1,3},{2,0},{3,1},{4,6},{5,7},{6,4},{7,5},{8,10},{9,11},{10,... | collective-permute-start | bytes 1572872 | tf_op jit(solution)/shard_map/ppermute | solution.py:528
  129.5 12.8 %collective-permute-start.24 = (bf16[16,1024]{1,0:T(8,128)(2,1)S(1)}, bf16[16,1024]{1,0:T(8,128)(2,1)S(1)}, u32[]{:S(2)}, u32[]{:S(2)}) collective-permute-start(bf16[16,1024]{1,0:T(8,128)(2,1)S(1)} %get-tuple-element.83.refs_5_), channel_id=1, source_target_pairs={{0,4},{4,0},{8,12},{12,8},{16,20},{20,16},{24,28},{28,24},{1,5},{5... | collective-permute-start | bytes 98312 | tf_op jit(solution)/shard_map/ppermute | solution.py:528
  130.8 11.5 %collective-permute-start.25 = (bf16[16,1024]{1,0:T(8,128)(2,1)S(1)}, bf16[16,1024]{1,0:T(8,128)(2,1)S(1)}, u32[]{:S(2)}, u32[]{:S(2)}) collective-permute-start(bf16[16,1024]{1,0:T(8,128)(2,1)S(1)} %get-tuple-element.83.refs_5_), channel_id=1, source_target_pairs={{0,8},{4,12},{8,0},{12,4},{16,24},{20,28},{24,16},{28,20},{1,9},{5... | collective-permute-start | bytes 98312 | tf_op jit(solution)/shard_map/ppermute | solution.py:528
  133.0 10.7 %collective-permute-start.26 = (bf16[16,1024]{1,0:T(8,128)(2,1)S(1)}, bf16[16,1024]{1,0:T(8,128)(2,1)S(1)}, u32[]{:S(2)}, u32[]{:S(2)}) collective-permute-start(bf16[16,1024]{1,0:T(8,128)(2,1)S(1)} %get-tuple-element.83.refs_5_), channel_id=1, source_target_pairs={{0,12},{4,8},{8,4},{12,0},{16,28},{20,24},{24,20},{28,16},{1,13},{... | collective-permute-start | bytes 98312 | tf_op jit(solution)/shard_map/ppermute | solution.py:528
  146.0 16.1 %collective-permute-start.27 = (bf16[384,1024]{1,0:T(8,128)(2,1)S(1)}, bf16[384,1024]{1,0:T(8,128)(2,1)S(1)}, u32[]{:S(2)}, u32[]{:S(2)}) collective-permute-start(bf16[384,1024]{1,0:T(8,128)(2,1)S(1)} %get-tuple-element.85), channel_id=1, source_target_pairs={{0,1},{1,0},{2,3},{3,2},{4,5},{5,4},{6,7},{7,6},{8,9},{9,8},{10,11... | collective-permute-start | bytes 2359304 | tf_op jit(solution)/shard_map/ppermute | solution.py:528
  147.8 2.7 %collective-permute-start.15 = (bf16[256,1024]{1,0:T(8,128)(2,1)S(1)}, bf16[256,1024]{1,0:T(8,128)(2,1)S(1)}, u32[]{:S(2)}, u32[]{:S(2)}) collective-permute-start(bf16[256,1024]{1,0:T(8,128)(2,1)S(1)} %shard_map.110.refs_1_), channel_id=1, source_target_pairs={{0,1},{1,0},{2,3},{3,2},{4,5},{5,4},{6,7},{7,6},{8,9},{9,8},{10,11... | collective-permute-start | bytes 1572872 | tf_op jit(solution)/shard_map/ppermute | solution.py:528
  147.9 3.3 %collective-permute-start.17 = (bf16[256,1024]{1,0:T(8,128)(2,1)S(1)}, bf16[256,1024]{1,0:T(8,128)(2,1)S(1)}, u32[]{:S(2)}, u32[]{:S(2)}) collective-permute-start(bf16[256,1024]{1,0:T(8,128)(2,1)S(1)} %collective-permute-done.16.refs_3_), channel_id=1, source_target_pairs={{0,1},{1,0},{2,3},{3,2},{4,5},{5,4},{6,7},{7,6},{8,9},{9,8},{10,11... | collective-permute-start | bytes 1572872 | tf_op jit(solution)/shard_map/ppermute | solution.py:528
  148.3 19.1 %collective-permute-start.28 = (bf16[384,1024]{1,0:T(8,128)(2,1)S(1)}, bf16[384,1024]{1,0:T(8,128)(2,1)S(1)}, u32[]{:S(2)}, u32[]{:S(2)}) collective-permute-start(bf16[384,1024]{1,0:T(8,128)(2,1)S(1)} %get-tuple-element.86), channel_id=1, source_target_pairs={{0,2},{1,3},{2,0},{3,1},{4,6},{5,7},{6,4},{7,5},{8,10},{9,11},{10,... | collective-permute-start | bytes 2359304 | tf_op jit(solution)/shard_map/ppermute | solution.py:528
  148.3 36.1 %collective-permute-start.29 = (bf16[384,1024]{1,0:T(8,128)(2,1)S(1)}, bf16[384,1024]{1,0:T(8,128)(2,1)S(1)}, u32[]{:S(2)}, u32[]{:S(2)}) collective-permute-start(bf16[384,1024]{1,0:T(8,128)(2,1)S(1)} %get-tuple-element.98), channel_id=1, source_target_pairs={{0,3},{1,2},{2,1},{3,0},{4,7},{5,6},{6,5},{7,4},{8,11},{9,10},{10,... | collective-permute-start | bytes 2359304 | tf_op jit(solution)/shard_map/ppermute | solution.py:528
  160.0 9.0 %collective-permute-start.18 = (bf16[5,128,256]{2,1,0:T(8,128)(2,1)S(1)}, bf16[5,128,256]{2,1,0:T(8,128)(2,1)S(1)}, u32[]{:S(2)}, u32[]{:S(2)}) collective-permute-start(bf16[5,128,256]{2,1,0:T(8,128)(2,1)S(1)} %get-tuple-element.80), channel_id=1, source_target_pairs={{0,4},{4,0},{8,12},{12,8},{16,20},{20,16},{24,28},{28,24},{1,5},{5... | collective-permute-start | bytes 983048 | tf_op jit(solution)/shard_map/ppermute | solution.py:528
  160.1 9.4 %collective-permute-start.19 = (bf16[5,128,256]{2,1,0:T(8,128)(2,1)S(1)}, bf16[5,128,256]{2,1,0:T(8,128)(2,1)S(1)}, u32[]{:S(2)}, u32[]{:S(2)}) collective-permute-start(bf16[5,128,256]{2,1,0:T(8,128)(2,1)S(1)} %get-tuple-element.81), channel_id=1, source_target_pairs={{0,8},{4,12},{8,0},{12,4},{16,24},{20,28},{24,16},{28,20},{1,9},{5... | collective-permute-start | bytes 983048 | tf_op jit(solution)/shard_map/ppermute | solution.py:528
  162.0 14.9 %collective-permute-start.20 = (bf16[5,128,256]{2,1,0:T(8,128)(2,1)S(1)}, bf16[5,128,256]{2,1,0:T(8,128)(2,1)S(1)}, u32[]{:S(2)}, u32[]{:S(2)}) collective-permute-start(bf16[5,128,256]{2,1,0:T(8,128)(2,1)S(1)} %get-tuple-element.82), channel_id=1, source_target_pairs={{0,12},{4,8},{8,4},{12,0},{16,28},{20,24},{24,20},{28,16},{1,13},{... | collective-permute-start | bytes 983048 | tf_op jit(solution)/shard_map/ppermute | solution.py:528
  176.9 7.6 %copy-start.2 = (bf16[512,1024]{1,0:T(8,128)(2,1)S(1)}, bf16[512,1024]{1,0:T(8,128)(2,1)}, u32[]{:S(2)}) copy-start(bf16[512,1024]{1,0:T(8,128)(2,1)} %refs_1_.3) | copy-start | bytes 3145732
  (4 other events, 4.2 us)

commit v9 on v8

--- a/solution.py
+++ b/solution.py
@@ -129,6 +129,7 @@
     lax.fori_loop(0, dp, per_dest, jnp.int32(0))
     top, events = owners_t.shape
     devices = dp * mp
+    lanes = -(-capacity // 128) * 128
     o_id = iota((devices, events), 0)
     named = jnp.zeros((devices, events), F32)
     row = jnp.zeros((devices, events), F32)
@@ -143,18 +144,18 @@
     rank = dot_nn(named.astype(BF), before)
     code[...] = jnp.where(named > 0.0, 2.0 * rank + 1.0 + positive, 0.0)
     rank = jnp.where(named > 0.0, rank, -1.0)
-    lane = iota((devices, part), 1)
-    wanted = jnp.zeros((devices, part), F32)
+    lane = iota((devices, lanes), 1)
+    wanted = jnp.zeros((devices, lanes), F32)
     for c in range(capacity):
         one = jnp.sum(jnp.where(rank == float(c), row, 0.0), axis=1, keepdims=True)
         wanted = jnp.where(lane == c, one, wanted)
     high = jnp.floor(wanted * (1.0 / 256.0))
     low = wanted - 256.0 * high
-    none = jnp.zeros((8 - mp, part), F32)
+    none = jnp.zeros((8 - mp, lanes), F32)
     for d in range(dp):
         mine = slice(d * mp, (d + 1) * mp)
         digits = [high[mine], none, low[mine], none] if mp < 8 else [high[mine], low[mine]]
-        out[d, 2 * per_peer * steps :, :] = jnp.concatenate(digits, axis=0).astype(BF)
+        out[d, 2 * per_peer * steps :, :lanes] = jnp.concatenate(digits, axis=0).astype(BF)
 
 
 def take_kernel(meta, arrived, out, digits, *, dp, seq_dev, per_peer, steps):
@@ -244,15 +245,18 @@
 
 def out_kernel(own, *refs, mp):
     gathered, weights = refs[:mp], refs[mp : 2 * mp]
-    unit, unit_bf, inv_o = refs[2 * mp :]
-    total = own[...].astype(F32)
-    for j in range(mp):
-        total = total + dot_nn(gathered[j][...], weights[j][...])
-    inv = lax.rsqrt(jnp.sum(total * total, axis=-1, keepdims=True) + EPS_UNIT)
-    u = total * inv
-    unit[...] = u
-    unit_bf[...] = u.astype(BF)
-    inv_o[...] = jnp.broadcast_to(inv, inv_o.shape)
+    unit, unit_bf, inv_o, *sides = refs[2 * mp :]
+    half = own.shape[0] // 2
+    for side, rows in enumerate((slice(0, half), slice(half, 2 * half))):
+        total = own[rows, :].astype(F32)
+        for j in range(mp):
+            total = total + dot_nn(gathered[j][rows, :], weights[j][...])
+        inv = lax.rsqrt(jnp.sum(total * total, axis=-1, keepdims=True) + EPS_UNIT)
+        u = total * inv
+        unit[rows, :] = u
+        unit_bf[rows, :] = u.astype(BF)
+        sides[side][...] = u.astype(BF)
+        inv_o[rows, :] = jnp.broadcast_to(inv, (half, BLOCK))
 
 
 def look_kernel(meta, *refs, mp, dp, capacity, chunk, share):
@@ -394,7 +398,7 @@
 
 
 def mail_kernel(meta, *refs, half, mp, events, capacity):
-    units, ledgers, outs = refs[:half], refs[half : 2 * half], refs[2 * half : -2]
+    units, ledgers, outs = refs[: 2 * half], refs[2 * half : 3 * half], refs[3 * half : -2]
     hots, ledger = refs[-2:]
     here = jnp.where(meta[0] >= half, meta[0] - half, meta[0])
     slot = iota((2 * capacity, 2 * events), 0)
@@ -412,7 +416,8 @@
             hots[k * 2 * capacity : (k + 1) * 2 * capacity, :] = mine.astype(BF)
             weight = line[:, : 2 * events] + line[:, 2 * events : 4 * events]
             weights.append(jnp.sum(jnp.where(mine, weight, 0.0), axis=1, keepdims=True))
-        rows = dot_nn(hots[...], units[j][...])
+        rows = dot_nn(hots[:, :events], units[j][...])
+        rows = rows + dot_nn(hots[:, events:], units[half + j][...])
         for k in range(mp):
             part = rows[k * 2 * capacity : (k + 1) * 2 * capacity] * weights[k]
             outs[k][j * 2 * capacity : (j + 1) * 2 * capacity, :] = part.astype(BF)
@@ -528,8 +533,8 @@
     return lax.ppermute(x, axis, [(a, a ^ bit) for a in range(size)])
 
 
-def gather_blocks(x, axis, half=None):
-    size = lax.axis_size(axis)
+def gather_blocks(x, axis, half=None, size=None):
+    size = size or lax.axis_size(axis)
     blocks = {0: x} if half is None else {0: x, size // 2: half}
     bit = size // 2 if half is None else size // 4
     while bit:
@@ -643,12 +648,14 @@
     )(meta, *features, w_in)
     gathered = exchange(gated, "mp")
     w_out_blocks = gather_blocks(w_out, "mp", w_out_y)
-    units, units_bf, inv_out = call(
+    units, units_bf, inv_out, *unit_sides = call(
         functools.partial(out_kernel, mp=mp),
         [
             S((2 * quarter, width), F32),
             S((2 * quarter, width), BF),
             S((2 * quarter, BLOCK), F32),
+            S((quarter, width), BF),
+            S((quarter, width), BF),
         ],
         [VM] + [VM] * (2 * mp),
         2,
@@ -678,13 +685,13 @@
     if short:
         column = range(1, dp // 2)
         ledgers = [ledger] + [swapped(ledger, "dp", j) for j in column]
-        all_units = [units_bf] + [swapped(units_bf, "dp", j) for j in column]
+        all_units = [b for u in unit_sides for b in gather_blocks(u, "dp", size=dp // 2)]
         mail = call(
             functools.partial(
                 mail_kernel, half=dp // 2, mp=mp, events=events, capacity=capacity
             ),
             [S((dp * capacity, width), BF)] * mp,
-            [SM] + [VM] * dp,
+            [SM] + [VM] * (dp + dp // 2),
             4,
             scratch=[
                 pltpu.VMEM((mp * 2 * capacity, 2 * events), BF),

time: 190 us -> 189 us (level)
  waiting for transfers between devices: 89.4 us -> 81.5 us
  local copies, waits for them, and re-layouts: 11.2 us -> 18.5 us
  Pallas kernels: 41.8 us -> 39.7 us
    ppermute x30 -> x33, waiting for transfers between devices: 89.4 us -> 81.5 us  [swapped(): return lax.ppermute(x, axis, [(a, a ^ bit) for a in range(size)])]
    unnamed x40 -> x62, local copies, waits for them, and re-layouts: 11.2 us -> 18.5 us
    ppermute x30 -> x33, starting transfers between devices: 27.3 us -> 29.8 us  [swapped(): return lax.ppermute(x, axis, [(a, a ^ bit) for a in range(size)])]
    pallas_call x13, Pallas kernels: 41.8 us -> 39.7 us  [run(): pl.pallas_call(kernel, out_shape=outs, in_specs=list(in_specs), out_specs...]
  transfers between devices with their start and end apart: 32 -> 35, of which waited for: 20 -> 20; matrix products, arithmetic and copies ran while one was open for 0% -> 0% of each run, Pallas kernels for 15% -> 14%
where the time goes in v9:
time: 189 us; the launch traced here: 186 us
  waiting for transfers between devices  81.5 us (43%)
  starting transfers between devices  44.1 us (23%)
  Pallas kernels  39.7 us (21%)
  local copies, waits for them, and re-layouts  18.5 us (10%)
    ppermute x33, waiting for transfers between devices, swapped(): return lax.ppermute(x, axis, [(a, a ^ bit) for a in range(size)])  81.5 us
    pallas_call x13, Pallas kernels, run(): pl.pallas_call(kernel, out_shape=outs, in_specs=list(in_specs), out_specs...  39.7 us
    ppermute x33, starting transfers between devices, swapped(): return lax.ppermute(x, axis, [(a, a ^ bit) for a in range(size)])  29.8 us
    unnamed x62, local copies, waits for them, and re-layouts  18.5 us
    all_to_all x1, starting transfers between devices, in_half(): lax.all_to_all(x.reshape(near, 2 * capacity, width), ('dp', 'mp'), split_...  8.4 us
    all_to_all x1, starting transfers between devices, per_device(): lax.all_to_all(packed, 'dp', split_axis=0, concat_axis=0, tiled=True)  5.82 us
  transfers between devices with their start and end apart: 35, of which 20 were waited for; matrix products, arithmetic and copies ran while one was open for 0% of the time, Pallas kernels for 14%

profile of v9, /device:TPU:13, one launch (start us, length us, event | category | flops | bytes accessed | tf_op | source)
XLA Modules:
  0.0 186.2 jit_solution(12834532822713730155)
XLA Ops:
  0.6 1.4 pad_add_fusion.refs_0_
  2.1 4.9 %shard_map.103 = (bf16[8,144,256]{2,1,0:T(8,128)(2,1)}, f32[32,128]{1,0:T(8,128)}) custom-call(s32[258]{0:T(512)} %pad_add_fusion.refs_0_, bf16[16,32,256]{2,1,0:T(8,128)(2,1)} %refs_1_.2, s32[8,128]{1,0:T(8,128)} %bitcast.11, s32[8,128]{1,0:T(8,128)} %bitcast.12), custom_call_target="tpu_custom_call" | custom-call | bytes 13200000 | tf_op jit(solution)/shard_map/pallas_call | solution.py:70
  7.0 5.8 %all-to-all-start = ((bf16[8,144,256]{2,1,0:T(8,128)(2,1)}), bf16[8,144,256]{2,1,0:T(8,128)(2,1)S(1)}, u32[]{:S(2)}, u32[]{:S(2)}) async-start(bf16[8,144,256]{2,1,0:T(8,128)(2,1)} %get-tuple-element.53), calls=%async_computation | async-start | bytes 1179648 | tf_op jit(solution)/shard_map/all_to_all | solution.py:599
  13.1 12.3 %collective-permute-done.refs_7_ = bf16[256,1024]{1,0:T(8,128)(2,1)} collective-permute-done((bf16[256,1024]{1,0:T(8,128)(2,1)}, bf16[256,1024]{1,0:T(8,128)(2,1)}, u32[]{:S(2)}, u32[]{:S(2)}) %collective-permute-start) | collective-permute-done | bytes 524320 | tf_op jit(solution)/shard_map/ppermute | solution.py:533
  27.3 2.9 %collective-permute-done.1.refs_3_ = bf16[128,256]{1,0:T(8,128)(2,1)S(1)} collective-permute-done((bf16[128,256]{1,0:T(8,128)(2,1)S(1)}, bf16[128,256]{1,0:T(8,128)(2,1)S(1)}, u32[]{:S(2)}, u32[]{:S(2)}) %collective-permute-start.1) | collective-permute-done | bytes 65568 | tf_op jit(solution)/shard_map/ppermute | solution.py:533
  30.4 5.4 %collective-permute-start.3 = (bf16[128,256]{1,0:T(8,128)(2,1)S(1)}, bf16[128,256]{1,0:T(8,128)(2,1)S(1)}, u32[]{:S(2)}, u32[]{:S(2)}) collective-permute-start(bf16[128,256]{1,0:T(8,128)(2,1)S(1)} %get-tuple-element.56.refs_1_), channel_id=1, source_target_pairs={{0,1},{1,0},{2,3},{3,2},{4,5},{5,4},{6,7},{7,6},{8,9},{9,8},{10,11... | collective-permute-start | bytes 196616 | tf_op jit(solution)/shard_map/ppermute | solution.py:533
  37.7 2.8 %shard_map.105 = (bf16[1536,1024]{1,0:T(8,128)(2,1)S(1)}, s32[1,1536]{1,0:T(1,128)}, s32[1,1536]{1,0:T(1,128)S(1)}) custom-call(s32[258]{0:T(512)S(1)} %copy-done.22, bf16[128,256]{1,0:T(8,128)(2,1)S(1)} %get-tuple-element.56.refs_1_, bf16[128,256]{1,0:T(8,128)(2,1)S(1)} %collective-permute-done.3.refs_2_, ...), custom_call_target="tpu_custom_call" | custom-call | bytes 13200000 | tf_op jit(solution)/shard_map/pallas_call | solution.py:70
  40.5 1.6 copy-done.3
  43.5 8.4 %all-to-all-start.1 = ((bf16[16,96,1024]{2,1,0:T(8,128)(2,1)}), bf16[16,96,1024]{2,1,0:T(8,128)(2,1)S(1)}, u32[]{:S(2)}, u32[]{:S(2)}) async-start(bf16[16,96,1024]{2,1,0:T(8,128)(2,1)} %bitcast.10), calls=%async_computation.1 | async-start | bytes 6291456 | tf_op jit(solution)/shard_map/all_to_all | solution.py:580
  53.0 1.2 collective-permute-done.2.refs_2_
  54.9 1.6 copy-done.10
  56.5 1.0 copy-done.16
  57.6 1.0 copy-done.18
  58.6 7.7 %shard_map.106 = (f32[3,1024,256]{2,1,0:T(8,128)S(1)}, bf16[9,1024,256]{2,1,0:T(8,128)(2,1)S(1)}, bf16[1280,1024]{1,0:T(8,128)(2,1)S(1)}, bf16[256,1024]{1,0:T(8...) custom-call(s32[258]{0:T(512)S(1)} %copy-done.23, ...), custom_call_target="tpu_custom_call" | custom-call | bytes 33000000 | tf_op jit(solution)/shard_map/pallas_call | solution.py:70
  66.3 2.2 %copy-done = bf16[9,1024,256]{2,1,0:T(8,128)(2,1)} copy-done((bf16[9,1024,256]{2,1,0:T(8,128)(2,1)}, bf16[9,1024,256]{2,1,0:T(8,128)(2,1)S(1)}, u32[]{:S(2)}) %copy-start) | copy-done | bytes 4718616
  68.5 1.7 copy-done.4
  70.2 1.5 copy-done.6
  72.4 1.2 collective-permute-start.9
  73.6 11.3 %collective-permute-done.10.refs_4_ = bf16[256,256]{1,0:T(8,128)(2,1)S(1)} collective-permute-done((bf16[256,256]{1,0:T(8,128)(2,1)S(1)}, bf16[256,256]{1,0:T(8,128)(2,1)S(1)}, u32[]{:S(2)}, u32[]{:S(2)}) %collective-permute-start.10) | collective-permute-done | bytes 131104 | tf_op jit(solution)/shard_map/ppermute | solution.py:533
  84.9 7.8 %collective-permute-done.9.refs_3_ = bf16[256,256]{1,0:T(8,128)(2,1)S(1)} collective-permute-done((bf16[256,256]{1,0:T(8,128)(2,1)S(1)}, bf16[256,256]{1,0:T(8,128)(2,1)S(1)}, u32[]{:S(2)}, u32[]{:S(2)}) %collective-permute-start.9) | collective-permute-done | bytes 131104 | tf_op jit(solution)/shard_map/ppermute | solution.py:533
  92.7 2.0 %shard_map.107 = (f32[256,1024]{1,0:T(8,128)S(1)}, bf16[256,1024]{1,0:T(8,128)(2,1)S(1)}, f32[256,128]{1,0:T(8,128)S(1)}, bf16[128,1024]{1,0:T(8,128)(2,1)S(1)}, bf16[128,1024]{1,0:T(8,128)(2,1)S(1)}) custom-call(bf16[256,1024]{1,0:T(8,128)(2,1)S(1)} %get-tuple-element.62.refs_0_, bf16[256,256]{1,0:T(8,128)(2,1)S(1)} %get-tuple-element.63.refs_1_, ...), custom_call_target="tpu_custom_call" | custom-call | bytes 6600000 | tf_op jit(solution)/shard_map/pallas_call | solution.py:70
  94.7 1.0 copy-done.11
  97.2 1.0 copy-done.14
  99.7 2.6 %shard_map.108 = (f32[1536,256]{1,0:T(8,128)S(1)}, f32[1536,128]{1,0:T(8,128)S(1)}, f32[1,256]{1,0:T(1,128)S(1)}) custom-call(s32[258]{0:T(512)S(1)} %copy-done.23, bf16[1536,1024]{1,0:T(8,128)(2,1)S(1)} %bitcast.6, f32[32,128]{1,0:T(8,128)S(1)} %copy-done.24, f32[32,128]{1,0:T(8,128)S(1)} %copy-done.27, bf16[256,1024]{1,0:T(8,128)(2,1)S(1)} %copy-done.14), custom_call_target="tpu_custom_call" | custom-call | bytes 13200000 | tf_op jit(solution)/shard_map/pallas_call | solution.py:70
  102.3 2.2 %collective-permute-start.13 = (f32[1,256]{1,0:T(1,128)S(1)}, f32[1,256]{1,0:T(1,128)S(1)}, u32[]{:S(2)}, u32[]{:S(2)}) collective-permute-start(f32[1,256]{1,0:T(1,128)S(1)} %get-tuple-element.75.refs_6_), channel_id=1, source_target_pairs={{0,16},{4,20},{8,24},{12,28},{16,0},{20,4},{24,8},{28,12},{1,17},{... | collective-permute-start | bytes 3080 | tf_op jit(solution)/shard_map/ppermute | solution.py:533
  104.5 1.2 collective-permute-done.13.refs_7_
  105.7 2.0 %shard_map.109 = (f32[256,1024]{1,0:T(8,128)S(1)}, bf16[256,1024]{1,0:T(8,128)(2,1)S(1)}, bf16[16,1024]{1,0:T(8,128)(2,1)S(1)}) custom-call(s32[258]{0:T(512)S(1)} %copy-done.23, bf16[1536,1024]{1,0:T(8,128)(2,1)S(1)} %bitcast.7, f32[32,128]{1,0:T(8,128)S(1)} %copy-done.25, f32[32,128]{1,0:T(8,128)S(1)} %copy-done.28, ...), custom_call_target="tpu_custom_call" | custom-call | bytes 9900000 | tf_op jit(solution)/shard_map/pallas_call | solution.py:70
  107.7 2.2 %collective-permute-start.14 = (bf16[256,1024]{1,0:T(8,128)(2,1)S(1)}, bf16[256,1024]{1,0:T(8,128)(2,1)S(1)}, u32[]{:S(2)}, u32[]{:S(2)}) collective-permute-start(bf16[256,1024]{1,0:T(8,128)(2,1)S(1)} %get-tuple-element.77), channel_id=1, source_target_pairs={{0,16},{4,20},{8,24},{12,28},{16,0},{20,4},{24,8},{28,12},{1,17},{... | collective-permute-start | bytes 1572872 | tf_op jit(solution)/shard_map/ppermute | solution.py:533
  110.0 1.4 collective-permute-start.25
  112.8 13.0 %collective-permute-done.22.refs_3_ = bf16[128,1024]{1,0:T(8,128)(2,1)S(1)} collective-permute-done((bf16[128,1024]{1,0:T(8,128)(2,1)S(1)}, bf16[128,1024]{1,0:T(8,128)(2,1)S(1)}, u32[]{:S(2)}, u32[]{:S(2)}) %collective-permute-start.22) | collective-permute-done | bytes 262176 | tf_op jit(solution)/shard_map/ppermute | solution.py:533
  125.8 2.5 %collective-permute-start.23 = (bf16[128,1024]{1,0:T(8,128)(2,1)S(1)}, bf16[128,1024]{1,0:T(8,128)(2,1)S(1)}, u32[]{:S(2)}, u32[]{:S(2)}) collective-permute-start(bf16[128,1024]{1,0:T(8,128)(2,1)S(1)} %collective-permute-done.22.refs_3_), channel_id=1, source_target_pairs={{0,4},{4,0},{8,12},{12,8},{16,20},{20,16},{24,28},{28,24},{1,5},{5... | collective-permute-start | bytes 786440 | tf_op jit(solution)/shard_map/ppermute | solution.py:533
  128.3 4.3 %collective-permute-done.14.refs_3_ = bf16[256,1024]{1,0:T(8,128)(2,1)S(1)} collective-permute-done((bf16[256,1024]{1,0:T(8,128)(2,1)S(1)}, bf16[256,1024]{1,0:T(8,128)(2,1)S(1)}, u32[]{:S(2)}, u32[]{:S(2)}) %collective-permute-start.14) | collective-permute-done | bytes 524320 | tf_op jit(solution)/shard_map/ppermute | solution.py:533
  134.6 1.2 collective-permute-start.28
  135.8 1.4 collective-permute-start.29
  137.2 4.7 %collective-permute-done.26.refs_8_ = bf16[128,1024]{1,0:T(8,128)(2,1)S(1)} collective-permute-done((bf16[128,1024]{1,0:T(8,128)(2,1)S(1)}, bf16[128,1024]{1,0:T(8,128)(2,1)S(1)}, u32[]{:S(2)}, u32[]{:S(2)}) %collective-permute-start.26) | collective-permute-done | bytes 262176 | tf_op jit(solution)/shard_map/ppermute | solution.py:533
  141.9 1.1 collective-permute-done.27.refs_10_
  142.9 2.4 %shard_map.112 = (bf16[384,1024]{1,0:T(8,128)(2,1)S(1)}, bf16[384,1024]{1,0:T(8,128)(2,1)S(1)}, bf16[384,1024]{1,0:T(8,128)(2,1)S(1)}, bf16[384,1024]{1,0:T(8,128)(2,1)S(1)}) custom-call(s32[258]{0:T(512)S(1)} %copy-done.23, bf16[128,1024]{1,0:T(8,128)(2,1)S(1)} %get-tuple-element.85.refs_1_, bf16[128,1024]{1,0:T(8,128)(2,1)S(1)} %collective-permute-done.21.refs_2_, ...), custom_call_target="tpu_custom_call" | custom-call | bytes 13200000 | tf_op jit(solution)/shard_map/pallas_call | solution.py:70
  145.3 1.4 collective-permute-start.30
  147.6 1.4 collective-permute-start.32
  150.2 8.7 %shard_map.111 = (bf16[5,128,256]{2,1,0:T(8,128)(2,1)S(1)}, bf16[5,128,256]{2,1,0:T(8,128)(2,1)S(1)}, bf16[5,128,256]{2,1,0:T(8,128)(2,1)S(1)}, bf16[5,128,256]{2,1,0:T(8,128)(2,1)S(1)}) custom-call(s32[258]{0:T(512)S(1)} %copy-done.23, bf16[256,1024]{1,0:T(8,128)(2,1)S(1)} %shard_map.110.refs_1_, bf16[256,1024]{1,0:T(8,128)(2,1)S(1)} %collective-permute-done.15.refs_2_, ...), custom_call_target="tpu_custom_call" | custom-call | bytes 33000000 | tf_op jit(solution)/shard_map/pallas_call | solution.py:70
  160.6 1.0 collective-permute-start.20
  161.6 4.9 %collective-permute-done.31.refs_3_ = bf16[384,1024]{1,0:T(8,128)(2,1)S(1)} collective-permute-done((bf16[384,1024]{1,0:T(8,128)(2,1)S(1)}, bf16[384,1024]{1,0:T(8,128)(2,1)S(1)}, u32[]{:S(2)}, u32[]{:S(2)}) %collective-permute-start.31) | collective-permute-done | bytes 786464 | tf_op jit(solution)/shard_map/ppermute | solution.py:533
  166.6 1.3 collective-permute-done.18.refs_1_
  168.4 7.4 %collective-permute-done.20.refs_3_ = bf16[5,128,256]{2,1,0:T(8,128)(2,1)S(1)} collective-permute-done((bf16[5,128,256]{2,1,0:T(8,128)(2,1)S(1)}, bf16[5,128,256]{2,1,0:T(8,128)(2,1)S(1)}, u32[]{:S(2)}, u32[]{:S(2)}) %collective-permute-start.20) | collective-permute-done | bytes 327712 | tf_op jit(solution)/shard_map/ppermute | solution.py:533
  175.8 1.8 shard_map.114.refs_2_
  177.6 1.0 shard_map.113
  178.5 5.0 %collective-permute-done.32.refs_3_ = bf16[384,1024]{1,0:T(8,128)(2,1)S(1)} collective-permute-done((bf16[384,1024]{1,0:T(8,128)(2,1)S(1)}, bf16[384,1024]{1,0:T(8,128)(2,1)S(1)}, u32[]{:S(2)}, u32[]{:S(2)}) %collective-permute-start.32) | collective-permute-done | bytes 786464 | tf_op jit(solution)/shard_map/ppermute | solution.py:533
  183.5 2.6 %shard_map.115 = f32[512,1024]{1,0:T(8,128)} custom-call(s32[1,1536]{1,0:T(1,128)S(1)} %get-tuple-element.97.refs_0_, bf16[512,1024]{1,0:T(8,128)(2,1)S(1)} %copy-done.2, f32[512,1024]{1,0:T(8,128)S(1)} %shard_map.114.refs_2_, bf16[384,1024]{1,0:T(8,128)(2,1)S(1)} %collective-permute-done.32.refs_3_), custom_call_target="tpu_custom_call" | custom-call | bytes 9900000 | tf_op jit(solution)/shard_map/pallas_call | solution.py:70
  (99 shorter events, 19.0 us)
Async XLA Ops:
  0.6 36.4 %copy-start.1 = (bf16[512,1024]{1,0:T(8,128)(2,1)S(1)}, bf16[512,1024]{1,0:T(8,128)(2,1)}, u32[]{:S(2)}) copy-start(bf16[512,1024]{1,0:T(8,128)(2,1)} %refs_1_.3) | copy-start | bytes 3145732
  7.0 18.3 %all-to-all-start = ((bf16[8,144,256]{2,1,0:T(8,128)(2,1)}), bf16[8,144,256]{2,1,0:T(8,128)(2,1)S(1)}, u32[]{:S(2)}, u32[]{:S(2)}) async-start(bf16[8,144,256]{2,1,0:T(8,128)(2,1)} %get-tuple-element.53), calls=%async_computation | async-start | bytes 1179648 | tf_op jit(solution)/shard_map/all_to_all | solution.py:599
  12.8 12.5 %collective-permute-start = (bf16[256,1024]{1,0:T(8,128)(2,1)}, bf16[256,1024]{1,0:T(8,128)(2,1)}, u32[]{:S(2)}, u32[]{:S(2)}) collective-permute-start(bf16[256,1024]{1,0:T(8,128)(2,1)} %refs_5_.7), channel_id=1, source_target_pairs={{0,2},{1,3},{2,0},{3,1},{4,6},{5,7},{6,4},{7,5},{8,10},{9,11},{10,... | collective-permute-start | bytes 1572872 | tf_op jit(solution)/shard_map/ppermute | solution.py:533
  27.0 13.5 %copy-start.15 = (bf16[1024,256]{1,0:T(8,128)(2,1)}, bf16[1024,256]{1,0:T(8,128)(2,1)S(1)}, u32[]{:S(2)}) copy-start(bf16[1024,256]{1,0:T(8,128)(2,1)S(1)} %get-tuple-element.57.refs_1_) | copy-start | bytes 1572868
  27.0 3.2 %collective-permute-start.1 = (bf16[128,256]{1,0:T(8,128)(2,1)S(1)}, bf16[128,256]{1,0:T(8,128)(2,1)S(1)}, u32[]{:S(2)}, u32[]{:S(2)}) collective-permute-start(bf16[128,256]{1,0:T(8,128)(2,1)S(1)} %get-tuple-element.56.refs_1_), channel_id=1, source_target_pairs={{0,2},{1,3},{2,0},{3,1},{4,6},{5,7},{6,4},{7,5},{8,10},{9,11},{10,... | collective-permute-start | bytes 196616 | tf_op jit(solution)/shard_map/ppermute | solution.py:533
  30.2 12.5 %collective-permute-start.5 = (bf16[1024,256]{1,0:T(8,128)(2,1)S(1)}, bf16[1024,256]{1,0:T(8,128)(2,1)S(1)}, u32[]{:S(2)}, u32[]{:S(2)}) collective-permute-start(bf16[1024,256]{1,0:T(8,128)(2,1)S(1)} %get-tuple-element.57.refs_1_), channel_id=1, source_target_pairs={{0,2},{1,3},{2,0},{3,1},{4,6},{5,7},{6,4},{7,5},{8,10},{9,11},{10,... | collective-permute-start | bytes 1572872 | tf_op jit(solution)/shard_map/ppermute | solution.py:533
  30.4 6.3 %collective-permute-start.3 = (bf16[128,256]{1,0:T(8,128)(2,1)S(1)}, bf16[128,256]{1,0:T(8,128)(2,1)S(1)}, u32[]{:S(2)}, u32[]{:S(2)}) collective-permute-start(bf16[128,256]{1,0:T(8,128)(2,1)S(1)} %get-tuple-element.56.refs_1_), channel_id=1, source_target_pairs={{0,1},{1,0},{2,3},{3,2},{4,5},{5,4},{6,7},{7,6},{8,9},{9,8},{10,11... | collective-permute-start | bytes 196616 | tf_op jit(solution)/shard_map/ppermute | solution.py:533
  35.8 1.3 collective-permute-start.4
  35.8 6.4 %collective-permute-start.6 = (f32[32,128]{1,0:T(8,128)}, f32[32,128]{1,0:T(8,128)S(1)}, u32[]{:S(2)}, u32[]{:S(2)}) collective-permute-start(f32[32,128]{1,0:T(8,128)} %get-tuple-element.60.refs_2_), channel_id=1, source_target_pairs={{0,16},{4,20},{8,24},{12,28},{16,0},{20,4},{24,8},{28,12},{1,17},{... | collective-permute-start | bytes 49160 | tf_op jit(solution)/shard_map/ppermute | solution.py:533
  43.5 11.4 %copy-start.23 = (s32[258]{0:T(512)S(1)}, s32[258]{0:T(512)}, u32[]{:S(2)}) copy-start(s32[258]{0:T(512)} %pad_add_fusion.refs_0_) | copy-start | bytes 3100
  43.5 53.7 %all-to-all-start.1 = ((bf16[16,96,1024]{2,1,0:T(8,128)(2,1)}), bf16[16,96,1024]{2,1,0:T(8,128)(2,1)S(1)}, u32[]{:S(2)}, u32[]{:S(2)}) async-start(bf16[16,96,1024]{2,1,0:T(8,128)(2,1)} %bitcast.10), calls=%async_computation.1 | async-start | bytes 6291456 | tf_op jit(solution)/shard_map/all_to_all | solution.py:580
  51.9 40.8 %copy-start.8 = (bf16[256,1024]{1,0:T(8,128)(2,1)S(1)}, bf16[256,1024]{1,0:T(8,128)(2,1)}, u32[]{:S(2)}) copy-start(bf16[256,1024]{1,0:T(8,128)(2,1)} %refs_5_.7) | copy-start | bytes 1572868
  51.9 2.2 %collective-permute-start.2 = (bf16[1024,256]{1,0:T(8,128)(2,1)}, bf16[1024,256]{1,0:T(8,128)(2,1)S(1)}, u32[]{:S(2)}, u32[]{:S(2)}) collective-permute-start(bf16[1024,256]{1,0:T(8,128)(2,1)} %copy-done.15), channel_id=1, source_target_pairs={{0,1},{1,0},{2,3},{3,2},{4,5},{5,4},{6,7},{7,6},{8,9},{9,8},{10,11... | collective-permute-start | bytes 1572872 | tf_op jit(solution)/shard_map/ppermute | solution.py:533
  52.4 2.6 %collective-permute-start.7 = (bf16[1024,256]{1,0:T(8,128)(2,1)}, bf16[1024,256]{1,0:T(8,128)(2,1)S(1)}, u32[]{:S(2)}, u32[]{:S(2)}) collective-permute-start(bf16[1024,256]{1,0:T(8,128)(2,1)} %copy-done.17), channel_id=1, source_target_pairs={{0,1},{1,0},{2,3},{3,2},{4,5},{5,4},{6,7},{7,6},{8,9},{9,8},{10,11... | collective-permute-start | bytes 1572872 | tf_op jit(solution)/shard_map/ppermute | solution.py:533
  52.5 21.0 %collective-permute-start.11 = (bf16[256,1024]{1,0:T(8,128)(2,1)}, bf16[256,1024]{1,0:T(8,128)(2,1)S(1)}, u32[]{:S(2)}, u32[]{:S(2)}) collective-permute-start(bf16[256,1024]{1,0:T(8,128)(2,1)} %refs_5_.7), channel_id=1, source_target_pairs={{0,1},{1,0},{2,3},{3,2},{4,5},{5,4},{6,7},{7,6},{8,9},{9,8},{10,11... | collective-permute-start | bytes 1572872 | tf_op jit(solution)/shard_map/ppermute | solution.py:533
  52.9 20.7 %collective-permute-start.12 = (bf16[256,1024]{1,0:T(8,128)(2,1)}, bf16[256,1024]{1,0:T(8,128)(2,1)S(1)}, u32[]{:S(2)}, u32[]{:S(2)}) collective-permute-start(bf16[256,1024]{1,0:T(8,128)(2,1)} %collective-permute-done.refs_7_), channel_id=1, source_target_pairs={{0,1},{1,0},{2,3},{3,2},{4,5},{5,4},{6,7},{7,6},{8,9},{9,8},{10,11... | collective-permute-start | bytes 1572872 | tf_op jit(solution)/shard_map/ppermute | solution.py:533
  71.7 13.2 %collective-permute-start.10 = (bf16[256,256]{1,0:T(8,128)(2,1)S(1)}, bf16[256,256]{1,0:T(8,128)(2,1)S(1)}, u32[]{:S(2)}, u32[]{:S(2)}) collective-permute-start(bf16[256,256]{1,0:T(8,128)(2,1)S(1)} %get-tuple-element.66), channel_id=1, source_target_pairs={{0,3},{1,2},{2,1},{3,0},{4,7},{5,6},{6,5},{7,4},{8,11},{9,10},{10,... | collective-permute-start | bytes 393224 | tf_op jit(solution)/shard_map/ppermute | solution.py:533
  72.2 12.7 %collective-permute-start.8 = (bf16[256,256]{1,0:T(8,128)(2,1)S(1)}, bf16[256,256]{1,0:T(8,128)(2,1)S(1)}, u32[]{:S(2)}, u32[]{:S(2)}) collective-permute-start(bf16[256,256]{1,0:T(8,128)(2,1)S(1)} %get-tuple-element.64), channel_id=1, source_target_pairs={{0,1},{1,0},{2,3},{3,2},{4,5},{5,4},{6,7},{7,6},{8,9},{9,8},{10,11... | collective-permute-start | bytes 393224 | tf_op jit(solution)/shard_map/ppermute | solution.py:533
  72.4 20.4 %collective-permute-start.9 = (bf16[256,256]{1,0:T(8,128)(2,1)S(1)}, bf16[256,256]{1,0:T(8,128)(2,1)S(1)}, u32[]{:S(2)}, u32[]{:S(2)}) collective-permute-start(bf16[256,256]{1,0:T(8,128)(2,1)S(1)} %get-tuple-element.65), channel_id=1, source_target_pairs={{0,2},{1,3},{2,0},{3,1},{4,6},{5,7},{6,4},{7,5},{8,10},{9,11},{10,... | collective-permute-start | bytes 393224 | tf_op jit(solution)/shard_map/ppermute | solution.py:533
  99.7 6.0 %copy-start.28 = (f32[32,128]{1,0:T(8,128)S(1)}, f32[32,128]{1,0:T(8,128)}, u32[]{:S(2)}) copy-start(f32[32,128]{1,0:T(8,128)} %copy-done.26) | copy-start | bytes 49156
  99.7 10.4 %copy-start.20 = (bf16[128,1024]{1,0:T(8,128)(2,1)S(1)}, bf16[128,1024]{1,0:T(8,128)(2,1)}, u32[]{:S(2)}) copy-start(bf16[128,1024]{1,0:T(8,128)(2,1)} %copy-done.19) | copy-start | bytes 786436
  99.7 33.0 %copy-start.12 = (f32[256,1024]{1,0:T(8,128)S(1)}, f32[256,1024]{1,0:T(8,128)}, u32[]{:S(2)}) copy-start(f32[256,1024]{1,0:T(8,128)} %copy-done.11) | copy-start | bytes 3145732
  102.3 3.4 %collective-permute-start.13 = (f32[1,256]{1,0:T(1,128)S(1)}, f32[1,256]{1,0:T(1,128)S(1)}, u32[]{:S(2)}, u32[]{:S(2)}) collective-permute-start(f32[1,256]{1,0:T(1,128)S(1)} %get-tuple-element.75.refs_6_), channel_id=1, source_target_pairs={{0,16},{4,20},{8,24},{12,28},{16,0},{20,4},{24,8},{28,12},{1,17},{... | collective-permute-start | bytes 3080 | tf_op jit(solution)/shard_map/ppermute | solution.py:533
  105.7 44.4 %slice-start = ((s8[4718592]{0:T(1024)(128)(4,1)}), s8[4194304]{0:T(1024)(128)(4,1)S(1)}, s32[]{:S(2)}) async-start(s8[4718592]{0:T(1024)(128)(4,1)} %bitcast.8), calls=%async_computation.2 | async-start | bytes 8388608
  105.7 44.4 %slice-start.1 = ((s8[4718592]{0:T(1024)(128)(4,1)}), s8[524288]{0:T(1024)(128)(4,1)S(1)}, s32[]{:S(2)}) async-start(s8[4718592]{0:T(1024)(128)(4,1)} %bitcast.8), calls=%async_computation.3 | async-start | bytes 1048576
  105.7 44.4 %copy-start.7 = (bf16[1280,1024]{1,0:T(8,128)(2,1)S(1)}, bf16[1280,1024]{1,0:T(8,128)(2,1)}, u32[]{:S(2)}) copy-start(bf16[1280,1024]{1,0:T(8,128)(2,1)} %copy-done.6) | copy-start | bytes 7864324
  107.7 24.9 %collective-permute-start.14 = (bf16[256,1024]{1,0:T(8,128)(2,1)S(1)}, bf16[256,1024]{1,0:T(8,128)(2,1)S(1)}, u32[]{:S(2)}, u32[]{:S(2)}) collective-permute-start(bf16[256,1024]{1,0:T(8,128)(2,1)S(1)} %get-tuple-element.77), channel_id=1, source_target_pairs={{0,16},{4,20},{8,24},{12,28},{16,0},{20,4},{24,8},{28,12},{1,17},{... | collective-permute-start | bytes 1572872 | tf_op jit(solution)/shard_map/ppermute | solution.py:533
  109.9 15.9 %collective-permute-start.22 = (bf16[128,1024]{1,0:T(8,128)(2,1)S(1)}, bf16[128,1024]{1,0:T(8,128)(2,1)S(1)}, u32[]{:S(2)}, u32[]{:S(2)}) collective-permute-start(bf16[128,1024]{1,0:T(8,128)(2,1)S(1)} %get-tuple-element.85.refs_1_), channel_id=1, source_target_pairs={{0,8},{4,12},{8,0},{12,4},{16,24},{20,28},{24,16},{28,20},{1,9},{5... | collective-permute-start | bytes 786440 | tf_op jit(solution)/shard_map/ppermute | solution.py:533
  110.0 23.0 %collective-permute-start.25 = (bf16[128,1024]{1,0:T(8,128)(2,1)S(1)}, bf16[128,1024]{1,0:T(8,128)(2,1)S(1)}, u32[]{:S(2)}, u32[]{:S(2)}) collective-permute-start(bf16[128,1024]{1,0:T(8,128)(2,1)S(1)} %copy-done.20), channel_id=1, source_target_pairs={{0,8},{4,12},{8,0},{12,4},{16,24},{20,28},{24,16},{28,20},{1,9},{5... | collective-permute-start | bytes 786440 | tf_op jit(solution)/shard_map/ppermute | solution.py:533
  111.4 22.6 %collective-permute-start.21 = (bf16[128,1024]{1,0:T(8,128)(2,1)S(1)}, bf16[128,1024]{1,0:T(8,128)(2,1)S(1)}, u32[]{:S(2)}, u32[]{:S(2)}) collective-permute-start(bf16[128,1024]{1,0:T(8,128)(2,1)S(1)} %get-tuple-element.85.refs_1_), channel_id=1, source_target_pairs={{0,4},{4,0},{8,12},{12,8},{16,20},{20,16},{24,28},{28,24},{1,5},{5... | collective-permute-start | bytes 786440 | tf_op jit(solution)/shard_map/ppermute | solution.py:533
  112.2 22.4 %collective-permute-start.24 = (bf16[128,1024]{1,0:T(8,128)(2,1)S(1)}, bf16[128,1024]{1,0:T(8,128)(2,1)S(1)}, u32[]{:S(2)}, u32[]{:S(2)}) collective-permute-start(bf16[128,1024]{1,0:T(8,128)(2,1)S(1)} %copy-done.20), channel_id=1, source_target_pairs={{0,4},{4,0},{8,12},{12,8},{16,20},{20,16},{24,28},{28,24},{1,5},{5... | collective-permute-start | bytes 786440 | tf_op jit(solution)/shard_map/ppermute | solution.py:533
  125.8 10.0 %collective-permute-start.23 = (bf16[128,1024]{1,0:T(8,128)(2,1)S(1)}, bf16[128,1024]{1,0:T(8,128)(2,1)S(1)}, u32[]{:S(2)}, u32[]{:S(2)}) collective-permute-start(bf16[128,1024]{1,0:T(8,128)(2,1)S(1)} %collective-permute-done.22.refs_3_), channel_id=1, source_target_pairs={{0,4},{4,0},{8,12},{12,8},{16,20},{20,16},{24,28},{28,24},{1,5},{5... | collective-permute-start | bytes 786440 | tf_op jit(solution)/shard_map/ppermute | solution.py:533
  132.6 17.5 %copy-start.5 = (f32[3,1024,256]{2,1,0:T(8,128)S(1)}, f32[3,1024,256]{2,1,0:T(8,128)}, u32[]{:S(2)}) copy-start(f32[3,1024,256]{2,1,0:T(8,128)} %copy-done.4) | copy-start | bytes 9437188
  132.6 17.5 %copy-start.9 = (bf16[256,1024]{1,0:T(8,128)(2,1)S(1)}, bf16[256,1024]{1,0:T(8,128)(2,1)}, u32[]{:S(2)}) copy-start(bf16[256,1024]{1,0:T(8,128)(2,1)} %refs_5_.7) | copy-start | bytes 1572868
  133.0 13.8 %collective-permute-start.16 = (bf16[256,1024]{1,0:T(8,128)(2,1)S(1)}, bf16[256,1024]{1,0:T(8,128)(2,1)S(1)}, u32[]{:S(2)}, u32[]{:S(2)}) collective-permute-start(bf16[256,1024]{1,0:T(8,128)(2,1)S(1)} %shard_map.110.refs_1_), channel_id=1, source_target_pairs={{0,2},{1,3},{2,0},{3,1},{4,6},{5,7},{6,4},{7,5},{8,10},{9,11},{10,... | collective-permute-start | bytes 1572872 | tf_op jit(solution)/shard_map/ppermute | solution.py:533
  133.1 8.8 %collective-permute-start.26 = (bf16[128,1024]{1,0:T(8,128)(2,1)S(1)}, bf16[128,1024]{1,0:T(8,128)(2,1)S(1)}, u32[]{:S(2)}, u32[]{:S(2)}) collective-permute-start(bf16[128,1024]{1,0:T(8,128)(2,1)S(1)} %collective-permute-done.25.refs_7_), channel_id=1, source_target_pairs={{0,4},{4,0},{8,12},{12,8},{16,20},{20,16},{24,28},{28,24},{1,5},{5... | collective-permute-start | bytes 786440 | tf_op jit(solution)/shard_map/ppermute | solution.py:533
  134.0 9.0 %collective-permute-start.27 = (bf16[16,1024]{1,0:T(8,128)(2,1)S(1)}, bf16[16,1024]{1,0:T(8,128)(2,1)S(1)}, u32[]{:S(2)}, u32[]{:S(2)}) collective-permute-start(bf16[16,1024]{1,0:T(8,128)(2,1)S(1)} %get-tuple-element.87.refs_9_), channel_id=1, source_target_pairs={{0,4},{4,0},{8,12},{12,8},{16,20},{20,16},{24,28},{28,24},{1,5},{5... | collective-permute-start | bytes 98312 | tf_op jit(solution)/shard_map/ppermute | solution.py:533
  134.6 8.3 %collective-permute-start.28 = (bf16[16,1024]{1,0:T(8,128)(2,1)S(1)}, bf16[16,1024]{1,0:T(8,128)(2,1)S(1)}, u32[]{:S(2)}, u32[]{:S(2)}) collective-permute-start(bf16[16,1024]{1,0:T(8,128)(2,1)S(1)} %get-tuple-element.87.refs_9_), channel_id=1, source_target_pairs={{0,8},{4,12},{8,0},{12,4},{16,24},{20,28},{24,16},{28,20},{1,9},{5... | collective-permute-start | bytes 98312 | tf_op jit(solution)/shard_map/ppermute | solution.py:533
  135.8 7.1 %collective-permute-start.29 = (bf16[16,1024]{1,0:T(8,128)(2,1)S(1)}, bf16[16,1024]{1,0:T(8,128)(2,1)S(1)}, u32[]{:S(2)}, u32[]{:S(2)}) collective-permute-start(bf16[16,1024]{1,0:T(8,128)(2,1)S(1)} %get-tuple-element.87.refs_9_), channel_id=1, source_target_pairs={{0,12},{4,8},{8,4},{12,0},{16,28},{20,24},{24,20},{28,16},{1,13},{... | collective-permute-start | bytes 98312 | tf_op jit(solution)/shard_map/ppermute | solution.py:533
  145.3 15.3 %collective-permute-start.30 = (bf16[384,1024]{1,0:T(8,128)(2,1)S(1)}, bf16[384,1024]{1,0:T(8,128)(2,1)S(1)}, u32[]{:S(2)}, u32[]{:S(2)}) collective-permute-start(bf16[384,1024]{1,0:T(8,128)(2,1)S(1)} %get-tuple-element.89), channel_id=1, source_target_pairs={{0,1},{1,0},{2,3},{3,2},{4,5},{5,4},{6,7},{7,6},{8,9},{9,8},{10,11... | collective-permute-start | bytes 2359304 | tf_op jit(solution)/shard_map/ppermute | solution.py:533
  146.7 2.7 %collective-permute-start.15 = (bf16[256,1024]{1,0:T(8,128)(2,1)S(1)}, bf16[256,1024]{1,0:T(8,128)(2,1)S(1)}, u32[]{:S(2)}, u32[]{:S(2)}) collective-permute-start(bf16[256,1024]{1,0:T(8,128)(2,1)S(1)} %shard_map.110.refs_1_), channel_id=1, source_target_pairs={{0,1},{1,0},{2,3},{3,2},{4,5},{5,4},{6,7},{7,6},{8,9},{9,8},{10,11... | collective-permute-start | bytes 1572872 | tf_op jit(solution)/shard_map/ppermute | solution.py:533
  146.8 3.3 %collective-permute-start.17 = (bf16[256,1024]{1,0:T(8,128)(2,1)S(1)}, bf16[256,1024]{1,0:T(8,128)(2,1)S(1)}, u32[]{:S(2)}, u32[]{:S(2)}) collective-permute-start(bf16[256,1024]{1,0:T(8,128)(2,1)S(1)} %collective-permute-done.16.refs_3_), channel_id=1, source_target_pairs={{0,1},{1,0},{2,3},{3,2},{4,5},{5,4},{6,7},{7,6},{8,9},{9,8},{10,11... | collective-permute-start | bytes 1572872 | tf_op jit(solution)/shard_map/ppermute | solution.py:533
  147.4 19.2 %collective-permute-start.31 = (bf16[384,1024]{1,0:T(8,128)(2,1)S(1)}, bf16[384,1024]{1,0:T(8,128)(2,1)S(1)}, u32[]{:S(2)}, u32[]{:S(2)}) collective-permute-start(bf16[384,1024]{1,0:T(8,128)(2,1)S(1)} %get-tuple-element.90), channel_id=1, source_target_pairs={{0,2},{1,3},{2,0},{3,1},{4,6},{5,7},{6,4},{7,5},{8,10},{9,11},{10,... | collective-permute-start | bytes 2359304 | tf_op jit(solution)/shard_map/ppermute | solution.py:533
  147.6 35.9 %collective-permute-start.32 = (bf16[384,1024]{1,0:T(8,128)(2,1)S(1)}, bf16[384,1024]{1,0:T(8,128)(2,1)S(1)}, u32[]{:S(2)}, u32[]{:S(2)}) collective-permute-start(bf16[384,1024]{1,0:T(8,128)(2,1)S(1)} %get-tuple-element.102), channel_id=1, source_target_pairs={{0,3},{1,2},{2,1},{3,0},{4,7},{5,6},{6,5},{7,4},{8,11},{9,10},{10,... | collective-permute-start | bytes 2359304 | tf_op jit(solution)/shard_map/ppermute | solution.py:533
  158.9 9.0 %collective-permute-start.18 = (bf16[5,128,256]{2,1,0:T(8,128)(2,1)S(1)}, bf16[5,128,256]{2,1,0:T(8,128)(2,1)S(1)}, u32[]{:S(2)}, u32[]{:S(2)}) collective-permute-start(bf16[5,128,256]{2,1,0:T(8,128)(2,1)S(1)} %get-tuple-element.82), channel_id=1, source_target_pairs={{0,4},{4,0},{8,12},{12,8},{16,20},{20,16},{24,28},{28,24},{1,5},{5... | collective-permute-start | bytes 983048 | tf_op jit(solution)/shard_map/ppermute | solution.py:533
  159.8 8.6 %collective-permute-start.19 = (bf16[5,128,256]{2,1,0:T(8,128)(2,1)S(1)}, bf16[5,128,256]{2,1,0:T(8,128)(2,1)S(1)}, u32[]{:S(2)}, u32[]{:S(2)}) collective-permute-start(bf16[5,128,256]{2,1,0:T(8,128)(2,1)S(1)} %get-tuple-element.83), channel_id=1, source_target_pairs={{0,8},{4,12},{8,0},{12,4},{16,24},{20,28},{24,16},{28,20},{1,9},{5... | collective-permute-start | bytes 983048 | tf_op jit(solution)/shard_map/ppermute | solution.py:533
  160.6 15.2 %collective-permute-start.20 = (bf16[5,128,256]{2,1,0:T(8,128)(2,1)S(1)}, bf16[5,128,256]{2,1,0:T(8,128)(2,1)S(1)}, u32[]{:S(2)}, u32[]{:S(2)}) collective-permute-start(bf16[5,128,256]{2,1,0:T(8,128)(2,1)S(1)} %get-tuple-element.84), channel_id=1, source_target_pairs={{0,12},{4,8},{8,4},{12,0},{16,28},{20,24},{24,20},{28,16},{1,13},{... | collective-permute-start | bytes 983048 | tf_op jit(solution)/shard_map/ppermute | solution.py:533
  175.8 7.8 %copy-start.2 = (bf16[512,1024]{1,0:T(8,128)(2,1)S(1)}, bf16[512,1024]{1,0:T(8,128)(2,1)}, u32[]{:S(2)}) copy-start(bf16[512,1024]{1,0:T(8,128)(2,1)} %refs_1_.3) | copy-start | bytes 3145732
  (18 other events, 24.5 us)

commit v10 on v9

--- a/solution.py
+++ b/solution.py
@@ -245,17 +245,14 @@
 
 def out_kernel(own, *refs, mp):
     gathered, weights = refs[:mp], refs[mp : 2 * mp]
-    unit, unit_bf, inv_o, *sides = refs[2 * mp :]
+    inv_o, *sides = refs[2 * mp :]
     half = own.shape[0] // 2
     for side, rows in enumerate((slice(0, half), slice(half, 2 * half))):
         total = own[rows, :].astype(F32)
         for j in range(mp):
             total = total + dot_nn(gathered[j][rows, :], weights[j][...])
         inv = lax.rsqrt(jnp.sum(total * total, axis=-1, keepdims=True) + EPS_UNIT)
-        u = total * inv
-        unit[rows, :] = u
-        unit_bf[rows, :] = u.astype(BF)
-        sides[side][...] = u.astype(BF)
+        sides[side][...] = (total * inv).astype(BF)
         inv_o[rows, :] = jnp.broadcast_to(inv, (half, BLOCK))
 
 
@@ -303,10 +300,10 @@
 
 
 def score_kernel(
-    meta, items, code, code_far, units, expo, inv_o, total_o,
+    meta, items, code, code_far, unit_near, unit_far, expo, inv_o, total_o,
     *, dp, devices, capacity, chunk,
 ):
-    events = units.shape[0] // 2
+    events = unit_near.shape[0]
     near = devices // 2
     slots = items.shape[0]
     half = pl.multiple_of(lax.div(meta[0], dp // 2) * near, near)
@@ -317,7 +314,7 @@
         xf = x.astype(F32)
         inv = lax.rsqrt(jnp.sum(xf * xf, axis=-1, keepdims=True) + EPS_UNIT)
         inv_o[rows, :] = jnp.broadcast_to(inv, (chunk, BLOCK))
-        cosines = dot_nt(x, units[...]) * (inv * (1.0 / COSINE_DIVISOR))
+        scale = inv * (1.0 / COSINE_DIVISOR)
         slot = s + iota((chunk, 1), 0).astype(F32)
         owner = jnp.floor((slot + 0.5) * (1.0 / (2 * capacity)))
         local = slot - owner * (2 * capacity)
@@ -326,7 +323,7 @@
         named = owner == iota((chunk, near), 1).astype(F32)
         for side in range(2):
             lanes = slice(side * events, (side + 1) * events)
-            logits = cosines[:, lanes]
+            logits = dot_nt(x, (unit_near, unit_far)[side][...]) * scale
             spread = jnp.where(named & (far == (side == 1)), 1.0, 0.0).astype(BF)
             codes = dot_nn(spread, codes_in[side])
             first = codes == 2.0 * local + 2.0
@@ -423,12 +420,12 @@
             outs[k][j * 2 * capacity : (j + 1) * 2 * capacity, :] = part.astype(BF)
 
 
-def out_cot_kernel(units, inv_out, slopes, slopes_back, out_cot):
-    events = units.shape[0] // 2
-    for side in range(2):
+def out_cot_kernel(unit_near, unit_far, inv_out, slopes, slopes_back, out_cot):
+    events = unit_near.shape[0]
+    for side, unit in enumerate((unit_near, unit_far)):
         rows = slice(side * events, (side + 1) * events)
         there = slice((1 - side) * events, (2 - side) * events)
-        u = units[rows, :]
+        u = unit[...].astype(F32)
         s = slopes[rows, :] + slopes_back[there, :].astype(F32)
         along = jnp.sum(u * s, axis=-1, keepdims=True)
         out_cot[rows, :] = ((s - u * along) * inv_out[rows, 0:1]).astype(BF)
@@ -648,11 +645,9 @@
     )(meta, *features, w_in)
     gathered = exchange(gated, "mp")
     w_out_blocks = gather_blocks(w_out, "mp", w_out_y)
-    units, units_bf, inv_out, *unit_sides = call(
+    inv_out, *unit_sides = call(
         functools.partial(out_kernel, mp=mp),
         [
-            S((2 * quarter, width), F32),
-            S((2 * quarter, width), BF),
             S((2 * quarter, BLOCK), F32),
             S((quarter, width), BF),
             S((quarter, width), BF),
@@ -666,9 +661,9 @@
             score_kernel, dp=dp, devices=devices, capacity=capacity, chunk=chunk
         ),
         [S((slots, 2 * events), F32), S((slots, BLOCK), F32), S((1, 2 * events), F32)],
-        [SM, VM] + [VM] * 3,
+        [SM, VM] + [HB] * 4,
         4,
-    )(meta, items, code, code_far, units_bf)
+    )(meta, items, code, code_far, *unit_sides)
     total_far = partner(total)
     sizes = dict(dp=dp, seqs=seqs, seq_dev=seq_dev, steps=steps, chunk=chunk)
     slopes, slopes_bf, ledger = call(
@@ -699,8 +694,8 @@
             ],
         )(meta, *all_units, *ledgers)
         landed = exchange(mail, "mp")
-    out_cot = call(out_cot_kernel, S((2 * events, width), BF), [VM] * 4, 1)(
-        units, inv_out, slopes, slopes_back
+    out_cot = call(out_cot_kernel, S((2 * events, width), BF), [VM] * 5, 1)(
+        *unit_sides, inv_out, slopes, slopes_back
     )
     cots = gather_blocks(out_cot, "mp")
     pieces = [S((5, width // dp, cols), BF)] * (dp // 2)
@@ -740,7 +735,7 @@
             S((slots, width), BF),
             [SM] + [VM] * 4,
             3,
-        )(meta, expo, total, total_far, units_bf)
+        )(meta, expo, total, total_far, jnp.concatenate(unit_sides))
         landed = [in_half(sending)]
     rows_chunk = math.gcd(stock, 128)
     last = slots // 4

time: 189 us -> 189 us (level)
  starting transfers between devices: 44.1 us -> 49.2 us
  waiting for transfers between devices: 81.5 us -> 76.7 us
  local copies, waits for them, and re-layouts: 18.5 us -> 16.6 us
    ppermute x33, starting transfers between devices: 29.8 us -> 35.3 us  [swapped(): return lax.ppermute(x, axis, [(a, a ^ bit) for a in range(size)])]
    ppermute x33, waiting for transfers between devices: 81.5 us -> 76.7 us  [swapped(): return lax.ppermute(x, axis, [(a, a ^ bit) for a in range(size)])]
    unnamed x62 -> x52, local copies, waits for them, and re-layouts: 18.5 us -> 16.6 us
where the time goes in v10:
time: 189 us; the launch traced here: 186 us
  waiting for transfers between devices  76.7 us (41%)
  starting transfers between devices  49.2 us (26%)
  Pallas kernels  40.7 us (22%)
  local copies, waits for them, and re-layouts  16.6 us (9%)
    ppermute x33, waiting for transfers between devices, swapped(): return lax.ppermute(x, axis, [(a, a ^ bit) for a in range(size)])  76.7 us
    pallas_call x13, Pallas kernels, run(): pl.pallas_call(kernel, out_shape=outs, in_specs=list(in_specs), out_specs...  40.7 us
    ppermute x33, starting transfers between devices, swapped(): return lax.ppermute(x, axis, [(a, a ^ bit) for a in range(size)])  35.3 us
    unnamed x52, local copies, waits for them, and re-layouts  16.6 us
    all_to_all x1, starting transfers between devices, in_half(): lax.all_to_all(x.reshape(near, 2 * capacity, width), ('dp', 'mp'), split_...  8.3 us
    all_to_all x1, starting transfers between devices, per_device(): lax.all_to_all(packed, 'dp', split_axis=0, concat_axis=0, tiled=True)  5.55 us
  transfers between devices with their start and end apart: 35, of which 20 were waited for; matrix products, arithmetic and copies ran while one was open for 0% of the time, Pallas kernels for 14%

profile of v10, /device:TPU:13, one launch (start us, length us, event | category | flops | bytes accessed | tf_op | source)
XLA Modules:
  0.0 185.6 jit_solution(14510697102929770605)
XLA Ops:
  0.6 1.4 pad_add_fusion.refs_0_
  2.1 5.1 %shard_map.103 = (bf16[8,144,256]{2,1,0:T(8,128)(2,1)}, f32[32,128]{1,0:T(8,128)}) custom-call(s32[258]{0:T(512)} %pad_add_fusion.refs_0_, bf16[16,32,256]{2,1,0:T(8,128)(2,1)} %refs_1_.2, s32[8,128]{1,0:T(8,128)} %bitcast.11, s32[8,128]{1,0:T(8,128)} %bitcast.12), custom_call_target="tpu_custom_call" | custom-call | bytes 13200000 | tf_op jit(solution)/shard_map/pallas_call | solution.py:70
  7.1 5.6 %all-to-all-start = ((bf16[8,144,256]{2,1,0:T(8,128)(2,1)}), bf16[8,144,256]{2,1,0:T(8,128)(2,1)S(1)}, u32[]{:S(2)}, u32[]{:S(2)}) async-start(bf16[8,144,256]{2,1,0:T(8,128)(2,1)} %get-tuple-element.51), calls=%async_computation | async-start | bytes 1179648 | tf_op jit(solution)/shard_map/all_to_all | solution.py:596
  12.9 12.3 %collective-permute-done.refs_7_ = bf16[256,1024]{1,0:T(8,128)(2,1)} collective-permute-done((bf16[256,1024]{1,0:T(8,128)(2,1)}, bf16[256,1024]{1,0:T(8,128)(2,1)}, u32[]{:S(2)}, u32[]{:S(2)}) %collective-permute-start) | collective-permute-done | bytes 524320 | tf_op jit(solution)/shard_map/ppermute | solution.py:530
  25.9 1.0 shard_map.104
  27.1 2.9 %collective-permute-done.1.refs_3_ = bf16[128,256]{1,0:T(8,128)(2,1)S(1)} collective-permute-done((bf16[128,256]{1,0:T(8,128)(2,1)S(1)}, bf16[128,256]{1,0:T(8,128)(2,1)S(1)}, u32[]{:S(2)}, u32[]{:S(2)}) %collective-permute-start.1) | collective-permute-done | bytes 65568 | tf_op jit(solution)/shard_map/ppermute | solution.py:530
  30.2 5.4 %collective-permute-start.3 = (bf16[128,256]{1,0:T(8,128)(2,1)S(1)}, bf16[128,256]{1,0:T(8,128)(2,1)S(1)}, u32[]{:S(2)}, u32[]{:S(2)}) collective-permute-start(bf16[128,256]{1,0:T(8,128)(2,1)S(1)} %get-tuple-element.54.refs_1_), channel_id=1, source_target_pairs={{0,1},{1,0},{2,3},{3,2},{4,5},{5,4},{6,7},{7,6},{8,9},{9,8},{10,11... | collective-permute-start | bytes 196616 | tf_op jit(solution)/shard_map/ppermute | solution.py:530
  37.5 2.8 %shard_map.105 = (bf16[1536,1024]{1,0:T(8,128)(2,1)S(1)}, s32[1,1536]{1,0:T(1,128)}, s32[1,1536]{1,0:T(1,128)S(1)}) custom-call(s32[258]{0:T(512)S(1)} %copy-done.19, bf16[128,256]{1,0:T(8,128)(2,1)S(1)} %get-tuple-element.54.refs_1_, bf16[128,256]{1,0:T(8,128)(2,1)S(1)} %collective-permute-done.3.refs_2_, ...), custom_call_target="tpu_custom_call" | custom-call | bytes 13200000 | tf_op jit(solution)/shard_map/pallas_call | solution.py:70
  40.3 1.7 copy-done.3
  43.5 8.3 %all-to-all-start.1 = ((bf16[16,96,1024]{2,1,0:T(8,128)(2,1)}), bf16[16,96,1024]{2,1,0:T(8,128)(2,1)S(1)}, u32[]{:S(2)}, u32[]{:S(2)}) async-start(bf16[16,96,1024]{2,1,0:T(8,128)(2,1)} %bitcast.10), calls=%async_computation.1 | async-start | bytes 6291456 | tf_op jit(solution)/shard_map/all_to_all | solution.py:577
  52.9 1.2 collective-permute-done.2.refs_2_
  54.8 1.6 copy-done.13
  56.4 1.0 copy-done.15
  57.4 1.0 copy-done.17
  58.4 7.7 %shard_map.106 = (f32[3,1024,256]{2,1,0:T(8,128)S(1)}, bf16[9,1024,256]{2,1,0:T(8,128)(2,1)S(1)}, bf16[1280,1024]{1,0:T(8,128)(2,1)S(1)}, bf16[256,1024]{1,0:T(8...) custom-call(s32[258]{0:T(512)S(1)} %copy-done.20, ...), custom_call_target="tpu_custom_call" | custom-call | bytes 33000000 | tf_op jit(solution)/shard_map/pallas_call | solution.py:70
  66.1 2.2 %copy-done = bf16[9,1024,256]{2,1,0:T(8,128)(2,1)} copy-done((bf16[9,1024,256]{2,1,0:T(8,128)(2,1)}, bf16[9,1024,256]{2,1,0:T(8,128)(2,1)S(1)}, u32[]{:S(2)}) %copy-start) | copy-done | bytes 4718616
  68.3 1.6 copy-done.4
  69.9 1.5 copy-done.6
  72.0 1.5 collective-permute-start.10
  73.6 11.1 %collective-permute-done.9.refs_3_ = bf16[256,256]{1,0:T(8,128)(2,1)S(1)} collective-permute-done((bf16[256,256]{1,0:T(8,128)(2,1)S(1)}, bf16[256,256]{1,0:T(8,128)(2,1)S(1)}, u32[]{:S(2)}, u32[]{:S(2)}) %collective-permute-start.9) | collective-permute-done | bytes 131104 | tf_op jit(solution)/shard_map/ppermute | solution.py:530
  84.7 7.8 %collective-permute-done.10.refs_4_ = bf16[256,256]{1,0:T(8,128)(2,1)S(1)} collective-permute-done((bf16[256,256]{1,0:T(8,128)(2,1)S(1)}, bf16[256,256]{1,0:T(8,128)(2,1)S(1)}, u32[]{:S(2)}, u32[]{:S(2)}) %collective-permute-start.10) | collective-permute-done | bytes 131104 | tf_op jit(solution)/shard_map/ppermute | solution.py:530
  92.5 1.9 %shard_map.107 = (f32[256,128]{1,0:T(8,128)S(1)}, bf16[128,1024]{1,0:T(8,128)(2,1)S(1)}, bf16[128,1024]{1,0:T(8,128)(2,1)S(1)}) custom-call(bf16[256,1024]{1,0:T(8,128)(2,1)S(1)} %get-tuple-element.60.refs_0_, bf16[256,256]{1,0:T(8,128)(2,1)S(1)} %get-tuple-element.61.refs_1_, bf16[256,256]{1,0:T(8,128)(2,1)S(1)} %collective-permute-done.8.refs_2_, ...), custom_call_target="tpu_custom_call" | custom-call | bytes 6600000 | tf_op jit(solution)/shard_map/pallas_call | solution.py:70
  97.5 3.3 %shard_map.108 = (f32[1536,256]{1,0:T(8,128)S(1)}, f32[1536,128]{1,0:T(8,128)S(1)}, f32[1,256]{1,0:T(1,128)S(1)}) custom-call(s32[258]{0:T(512)S(1)} %copy-done.20, bf16[1536,1024]{1,0:T(8,128)(2,1)S(1)} %bitcast.6, f32[32,128]{1,0:T(8,128)S(1)} %copy-done.21, f32[32,128]{1,0:T(8,128)S(1)} %copy-done.23, ...), custom_call_target="tpu_custom_call" | custom-call | bytes 13200000 | tf_op jit(solution)/shard_map/pallas_call | solution.py:70
  100.9 2.2 %collective-permute-start.13 = (f32[1,256]{1,0:T(1,128)S(1)}, f32[1,256]{1,0:T(1,128)S(1)}, u32[]{:S(2)}, u32[]{:S(2)}) collective-permute-start(f32[1,256]{1,0:T(1,128)S(1)} %get-tuple-element.73.refs_6_), channel_id=1, source_target_pairs={{0,16},{4,20},{8,24},{12,28},{16,0},{20,4},{24,8},{28,12},{1,17},{... | collective-permute-start | bytes 3080 | tf_op jit(solution)/shard_map/ppermute | solution.py:530
  103.1 1.2 collective-permute-done.13.refs_7_
  104.3 2.0 %shard_map.109 = (f32[256,1024]{1,0:T(8,128)S(1)}, bf16[256,1024]{1,0:T(8,128)(2,1)S(1)}, bf16[16,1024]{1,0:T(8,128)(2,1)S(1)}) custom-call(s32[258]{0:T(512)S(1)} %copy-done.20, bf16[1536,1024]{1,0:T(8,128)(2,1)S(1)} %bitcast.7, f32[32,128]{1,0:T(8,128)S(1)} %copy-done.21, f32[32,128]{1,0:T(8,128)S(1)} %copy-done.23, ...), custom_call_target="tpu_custom_call" | custom-call | bytes 9900000 | tf_op jit(solution)/shard_map/pallas_call | solution.py:70
  106.2 2.2 %collective-permute-start.14 = (bf16[256,1024]{1,0:T(8,128)(2,1)S(1)}, bf16[256,1024]{1,0:T(8,128)(2,1)S(1)}, u32[]{:S(2)}, u32[]{:S(2)}) collective-permute-start(bf16[256,1024]{1,0:T(8,128)(2,1)S(1)} %get-tuple-element.75), channel_id=1, source_target_pairs={{0,16},{4,20},{8,24},{12,28},{16,0},{20,4},{24,8},{28,12},{1,17},{... | collective-permute-start | bytes 1572872 | tf_op jit(solution)/shard_map/ppermute | solution.py:530
  108.6 1.3 collective-permute-start.25
  109.9 2.7 %collective-permute-start.21 = (bf16[128,1024]{1,0:T(8,128)(2,1)S(1)}, bf16[128,1024]{1,0:T(8,128)(2,1)S(1)}, u32[]{:S(2)}, u32[]{:S(2)}) collective-permute-start(bf16[128,1024]{1,0:T(8,128)(2,1)S(1)} %get-tuple-element.66.refs_4_.refs_0_.refs_1_), channel_id=1, source_target_pairs={{0,4},{4,0},{8,12},{12,8},{16,20},{20,16},{24,28},{28,24},{1,5},{5... | collective-permute-start | bytes 786440 | tf_op jit(solution)/shard_map/ppermute | solution.py:530
  112.7 12.3 %collective-permute-done.22.refs_3_ = bf16[128,1024]{1,0:T(8,128)(2,1)S(1)} collective-permute-done((bf16[128,1024]{1,0:T(8,128)(2,1)S(1)}, bf16[128,1024]{1,0:T(8,128)(2,1)S(1)}, u32[]{:S(2)}, u32[]{:S(2)}) %collective-permute-start.22) | collective-permute-done | bytes 262176 | tf_op jit(solution)/shard_map/ppermute | solution.py:530
  125.0 3.7 %collective-permute-start.23 = (bf16[128,1024]{1,0:T(8,128)(2,1)S(1)}, bf16[128,1024]{1,0:T(8,128)(2,1)S(1)}, u32[]{:S(2)}, u32[]{:S(2)}) collective-permute-start(bf16[128,1024]{1,0:T(8,128)(2,1)S(1)} %collective-permute-done.22.refs_3_), channel_id=1, source_target_pairs={{0,4},{4,0},{8,12},{12,8},{16,20},{20,16},{24,28},{28,24},{1,5},{5... | collective-permute-start | bytes 786440 | tf_op jit(solution)/shard_map/ppermute | solution.py:530
  128.8 2.5 %collective-permute-done.14.refs_4_ = bf16[256,1024]{1,0:T(8,128)(2,1)S(1)} collective-permute-done((bf16[256,1024]{1,0:T(8,128)(2,1)S(1)}, bf16[256,1024]{1,0:T(8,128)(2,1)S(1)}, u32[]{:S(2)}, u32[]{:S(2)}) %collective-permute-start.14) | collective-permute-done | bytes 524320 | tf_op jit(solution)/shard_map/ppermute | solution.py:530
  131.7 2.7 %collective-permute-start.26 = (bf16[128,1024]{1,0:T(8,128)(2,1)S(1)}, bf16[128,1024]{1,0:T(8,128)(2,1)S(1)}, u32[]{:S(2)}, u32[]{:S(2)}) collective-permute-start(bf16[128,1024]{1,0:T(8,128)(2,1)S(1)} %collective-permute-done.25.refs_7_), channel_id=1, source_target_pairs={{0,4},{4,0},{8,12},{12,8},{16,20},{20,16},{24,28},{28,24},{1,5},{5... | collective-permute-start | bytes 786440 | tf_op jit(solution)/shard_map/ppermute | solution.py:530
  134.4 1.9 collective-permute-start.28
  136.3 1.2 collective-permute-start.29
  137.4 3.5 %collective-permute-done.26.refs_8_ = bf16[128,1024]{1,0:T(8,128)(2,1)S(1)} collective-permute-done((bf16[128,1024]{1,0:T(8,128)(2,1)S(1)}, bf16[128,1024]{1,0:T(8,128)(2,1)S(1)}, u32[]{:S(2)}, u32[]{:S(2)}) %collective-permute-start.26) | collective-permute-done | bytes 262176 | tf_op jit(solution)/shard_map/ppermute | solution.py:530
  141.6 2.4 %shard_map.112 = (bf16[384,1024]{1,0:T(8,128)(2,1)S(1)}, bf16[384,1024]{1,0:T(8,128)(2,1)S(1)}, bf16[384,1024]{1,0:T(8,128)(2,1)S(1)}, bf16[384,1024]{1,0:T(8,128)(2,1)S(1)}) custom-call(s32[258]{0:T(512)S(1)} %copy-done.20, bf16[128,1024]{1,0:T(8,128)(2,1)S(1)} %get-tuple-element.66.refs_4_.refs_0_.refs_1_, ...), custom_call_target="tpu_custom_call" | custom-call | bytes 13200000 | tf_op jit(solution)/shard_map/pallas_call | solution.py:70
  144.0 2.2 %collective-permute-start.30 = (bf16[384,1024]{1,0:T(8,128)(2,1)S(1)}, bf16[384,1024]{1,0:T(8,128)(2,1)S(1)}, u32[]{:S(2)}, u32[]{:S(2)}) collective-permute-start(bf16[384,1024]{1,0:T(8,128)(2,1)S(1)} %get-tuple-element.85), channel_id=1, source_target_pairs={{0,1},{1,0},{2,3},{3,2},{4,5},{5,4},{6,7},{7,6},{8,9},{9,8},{10,11... | collective-permute-start | bytes 2359304 | tf_op jit(solution)/shard_map/ppermute | solution.py:530
  147.2 1.3 collective-permute-start.32
  149.6 9.0 %shard_map.111 = (bf16[5,128,256]{2,1,0:T(8,128)(2,1)S(1)}, bf16[5,128,256]{2,1,0:T(8,128)(2,1)S(1)}, bf16[5,128,256]{2,1,0:T(8,128)(2,1)S(1)}, bf16[5,128,256]{2,1,0:T(8,128)(2,1)S(1)}) custom-call(s32[258]{0:T(512)S(1)} %copy-done.20, bf16[256,1024]{1,0:T(8,128)(2,1)S(1)} %shard_map.110.refs_1_, bf16[256,1024]{1,0:T(8,128)(2,1)S(1)} %collective-permute-done.15.refs_2_, ...), custom_call_target="tpu_custom_call" | custom-call | bytes 33000000 | tf_op jit(solution)/shard_map/pallas_call | solution.py:70
  158.6 1.8 collective-permute-start.18
  161.7 4.1 %collective-permute-done.31.refs_3_ = bf16[384,1024]{1,0:T(8,128)(2,1)S(1)} collective-permute-done((bf16[384,1024]{1,0:T(8,128)(2,1)S(1)}, bf16[384,1024]{1,0:T(8,128)(2,1)S(1)}, u32[]{:S(2)}, u32[]{:S(2)}) %collective-permute-start.31) | collective-permute-done | bytes 786464 | tf_op jit(solution)/shard_map/ppermute | solution.py:530
  165.8 2.4 %collective-permute-done.18.refs_1_ = bf16[5,128,256]{2,1,0:T(8,128)(2,1)S(1)} collective-permute-done((bf16[5,128,256]{2,1,0:T(8,128)(2,1)S(1)}, bf16[5,128,256]{2,1,0:T(8,128)(2,1)S(1)}, u32[]{:S(2)}, u32[]{:S(2)}) %collective-permute-start.18) | collective-permute-done | bytes 327712 | tf_op jit(solution)/shard_map/ppermute | solution.py:530
  169.0 7.1 %collective-permute-done.20.refs_3_ = bf16[5,128,256]{2,1,0:T(8,128)(2,1)S(1)} collective-permute-done((bf16[5,128,256]{2,1,0:T(8,128)(2,1)S(1)}, bf16[5,128,256]{2,1,0:T(8,128)(2,1)S(1)}, u32[]{:S(2)}, u32[]{:S(2)}) %collective-permute-start.20) | collective-permute-done | bytes 327712 | tf_op jit(solution)/shard_map/ppermute | solution.py:530
  176.2 1.0 shard_map.113
  177.1 1.8 shard_map.114.refs_2_
  178.9 3.9 %collective-permute-done.32.refs_3_ = bf16[384,1024]{1,0:T(8,128)(2,1)S(1)} collective-permute-done((bf16[384,1024]{1,0:T(8,128)(2,1)S(1)}, bf16[384,1024]{1,0:T(8,128)(2,1)S(1)}, u32[]{:S(2)}, u32[]{:S(2)}) %collective-permute-start.32) | collective-permute-done | bytes 786464 | tf_op jit(solution)/shard_map/ppermute | solution.py:530
  182.9 2.6 %shard_map.115 = f32[512,1024]{1,0:T(8,128)} custom-call(s32[1,1536]{1,0:T(1,128)S(1)} %get-tuple-element.93.refs_0_, bf16[512,1024]{1,0:T(8,128)(2,1)S(1)} %copy-done.2, f32[512,1024]{1,0:T(8,128)S(1)} %shard_map.114.refs_2_, bf16[384,1024]{1,0:T(8,128)(2,1)S(1)} %collective-permute-done.32.refs_3_), custom_call_target="tpu_custom_call" | custom-call | bytes 9900000 | tf_op jit(solution)/shard_map/pallas_call | solution.py:70
  (89 shorter events, 16.0 us)
Async XLA Ops:
  0.6 36.2 %copy-start.1 = (bf16[512,1024]{1,0:T(8,128)(2,1)S(1)}, bf16[512,1024]{1,0:T(8,128)(2,1)}, u32[]{:S(2)}) copy-start(bf16[512,1024]{1,0:T(8,128)(2,1)} %refs_1_.3) | copy-start | bytes 3145732
  7.1 18.0 %all-to-all-start = ((bf16[8,144,256]{2,1,0:T(8,128)(2,1)}), bf16[8,144,256]{2,1,0:T(8,128)(2,1)S(1)}, u32[]{:S(2)}, u32[]{:S(2)}) async-start(bf16[8,144,256]{2,1,0:T(8,128)(2,1)} %get-tuple-element.51), calls=%async_computation | async-start | bytes 1179648 | tf_op jit(solution)/shard_map/all_to_all | solution.py:596
  12.7 12.5 %collective-permute-start = (bf16[256,1024]{1,0:T(8,128)(2,1)}, bf16[256,1024]{1,0:T(8,128)(2,1)}, u32[]{:S(2)}, u32[]{:S(2)}) collective-permute-start(bf16[256,1024]{1,0:T(8,128)(2,1)} %refs_5_.7), channel_id=1, source_target_pairs={{0,2},{1,3},{2,0},{3,1},{4,6},{5,7},{6,4},{7,5},{8,10},{9,11},{10,... | collective-permute-start | bytes 1572872 | tf_op jit(solution)/shard_map/ppermute | solution.py:530
  26.8 13.5 %copy-start.14 = (bf16[1024,256]{1,0:T(8,128)(2,1)}, bf16[1024,256]{1,0:T(8,128)(2,1)S(1)}, u32[]{:S(2)}) copy-start(bf16[1024,256]{1,0:T(8,128)(2,1)S(1)} %get-tuple-element.55.refs_1_) | copy-start | bytes 1572868
  26.8 3.2 %collective-permute-start.1 = (bf16[128,256]{1,0:T(8,128)(2,1)S(1)}, bf16[128,256]{1,0:T(8,128)(2,1)S(1)}, u32[]{:S(2)}, u32[]{:S(2)}) collective-permute-start(bf16[128,256]{1,0:T(8,128)(2,1)S(1)} %get-tuple-element.54.refs_1_), channel_id=1, source_target_pairs={{0,2},{1,3},{2,0},{3,1},{4,6},{5,7},{6,4},{7,5},{8,10},{9,11},{10,... | collective-permute-start | bytes 196616 | tf_op jit(solution)/shard_map/ppermute | solution.py:530
  30.0 12.6 %collective-permute-start.5 = (bf16[1024,256]{1,0:T(8,128)(2,1)S(1)}, bf16[1024,256]{1,0:T(8,128)(2,1)S(1)}, u32[]{:S(2)}, u32[]{:S(2)}) collective-permute-start(bf16[1024,256]{1,0:T(8,128)(2,1)S(1)} %get-tuple-element.55.refs_1_), channel_id=1, source_target_pairs={{0,2},{1,3},{2,0},{3,1},{4,6},{5,7},{6,4},{7,5},{8,10},{9,11},{10,... | collective-permute-start | bytes 1572872 | tf_op jit(solution)/shard_map/ppermute | solution.py:530
  30.2 6.3 %collective-permute-start.3 = (bf16[128,256]{1,0:T(8,128)(2,1)S(1)}, bf16[128,256]{1,0:T(8,128)(2,1)S(1)}, u32[]{:S(2)}, u32[]{:S(2)}) collective-permute-start(bf16[128,256]{1,0:T(8,128)(2,1)S(1)} %get-tuple-element.54.refs_1_), channel_id=1, source_target_pairs={{0,1},{1,0},{2,3},{3,2},{4,5},{5,4},{6,7},{7,6},{8,9},{9,8},{10,11... | collective-permute-start | bytes 196616 | tf_op jit(solution)/shard_map/ppermute | solution.py:530
  35.6 1.3 collective-permute-start.4
  35.6 6.4 %collective-permute-start.6 = (f32[32,128]{1,0:T(8,128)}, f32[32,128]{1,0:T(8,128)S(1)}, u32[]{:S(2)}, u32[]{:S(2)}) collective-permute-start(f32[32,128]{1,0:T(8,128)} %get-tuple-element.58.refs_2_), channel_id=1, source_target_pairs={{0,16},{4,20},{8,24},{12,28},{16,0},{20,4},{24,8},{28,12},{1,17},{... | collective-permute-start | bytes 49160 | tf_op jit(solution)/shard_map/ppermute | solution.py:530
  40.3 1.7 copy-start.3
  43.5 11.3 %copy-start.20 = (s32[258]{0:T(512)S(1)}, s32[258]{0:T(512)}, u32[]{:S(2)}) copy-start(s32[258]{0:T(512)} %pad_add_fusion.refs_0_) | copy-start | bytes 3100
  43.5 51.7 %all-to-all-start.1 = ((bf16[16,96,1024]{2,1,0:T(8,128)(2,1)}), bf16[16,96,1024]{2,1,0:T(8,128)(2,1)S(1)}, u32[]{:S(2)}, u32[]{:S(2)}) async-start(bf16[16,96,1024]{2,1,0:T(8,128)(2,1)} %bitcast.10), calls=%async_computation.1 | async-start | bytes 6291456 | tf_op jit(solution)/shard_map/all_to_all | solution.py:577
  51.8 40.8 %copy-start.11 = (bf16[256,1024]{1,0:T(8,128)(2,1)S(1)}, bf16[256,1024]{1,0:T(8,128)(2,1)}, u32[]{:S(2)}) copy-start(bf16[256,1024]{1,0:T(8,128)(2,1)} %refs_5_.7) | copy-start | bytes 1572868
  51.8 2.2 %collective-permute-start.2 = (bf16[1024,256]{1,0:T(8,128)(2,1)}, bf16[1024,256]{1,0:T(8,128)(2,1)S(1)}, u32[]{:S(2)}, u32[]{:S(2)}) collective-permute-start(bf16[1024,256]{1,0:T(8,128)(2,1)} %copy-done.14), channel_id=1, source_target_pairs={{0,1},{1,0},{2,3},{3,2},{4,5},{5,4},{6,7},{7,6},{8,9},{9,8},{10,11... | collective-permute-start | bytes 1572872 | tf_op jit(solution)/shard_map/ppermute | solution.py:530
  52.2 2.6 %collective-permute-start.7 = (bf16[1024,256]{1,0:T(8,128)(2,1)}, bf16[1024,256]{1,0:T(8,128)(2,1)S(1)}, u32[]{:S(2)}, u32[]{:S(2)}) collective-permute-start(bf16[1024,256]{1,0:T(8,128)(2,1)} %copy-done.16), channel_id=1, source_target_pairs={{0,1},{1,0},{2,3},{3,2},{4,5},{5,4},{6,7},{7,6},{8,9},{9,8},{10,11... | collective-permute-start | bytes 1572872 | tf_op jit(solution)/shard_map/ppermute | solution.py:530
  52.3 21.2 %collective-permute-start.11 = (bf16[256,1024]{1,0:T(8,128)(2,1)}, bf16[256,1024]{1,0:T(8,128)(2,1)S(1)}, u32[]{:S(2)}, u32[]{:S(2)}) collective-permute-start(bf16[256,1024]{1,0:T(8,128)(2,1)} %refs_5_.7), channel_id=1, source_target_pairs={{0,1},{1,0},{2,3},{3,2},{4,5},{5,4},{6,7},{7,6},{8,9},{9,8},{10,11... | collective-permute-start | bytes 1572872 | tf_op jit(solution)/shard_map/ppermute | solution.py:530
  52.7 20.9 %collective-permute-start.12 = (bf16[256,1024]{1,0:T(8,128)(2,1)}, bf16[256,1024]{1,0:T(8,128)(2,1)S(1)}, u32[]{:S(2)}, u32[]{:S(2)}) collective-permute-start(bf16[256,1024]{1,0:T(8,128)(2,1)} %collective-permute-done.refs_7_), channel_id=1, source_target_pairs={{0,1},{1,0},{2,3},{3,2},{4,5},{5,4},{6,7},{7,6},{8,9},{9,8},{10,11... | collective-permute-start | bytes 1572872 | tf_op jit(solution)/shard_map/ppermute | solution.py:530
  66.1 2.2 %copy-start = (bf16[9,1024,256]{2,1,0:T(8,128)(2,1)}, bf16[9,1024,256]{2,1,0:T(8,128)(2,1)S(1)}, u32[]{:S(2)}) copy-start(bf16[9,1024,256]{2,1,0:T(8,128)(2,1)S(1)} %get-tuple-element.77.refs_7_) | copy-start | bytes 14155780
  71.4 2.2 %collective-permute-start.8 = (bf16[256,256]{1,0:T(8,128)(2,1)S(1)}, bf16[256,256]{1,0:T(8,128)(2,1)S(1)}, u32[]{:S(2)}, u32[]{:S(2)}) collective-permute-start(bf16[256,256]{1,0:T(8,128)(2,1)S(1)} %get-tuple-element.62), channel_id=1, source_target_pairs={{0,1},{1,0},{2,3},{3,2},{4,5},{5,4},{6,7},{7,6},{8,9},{9,8},{10,11... | collective-permute-start | bytes 393224 | tf_op jit(solution)/shard_map/ppermute | solution.py:530
  71.7 13.0 %collective-permute-start.9 = (bf16[256,256]{1,0:T(8,128)(2,1)S(1)}, bf16[256,256]{1,0:T(8,128)(2,1)S(1)}, u32[]{:S(2)}, u32[]{:S(2)}) collective-permute-start(bf16[256,256]{1,0:T(8,128)(2,1)S(1)} %get-tuple-element.63), channel_id=1, source_target_pairs={{0,2},{1,3},{2,0},{3,1},{4,6},{5,7},{6,4},{7,5},{8,10},{9,11},{10,... | collective-permute-start | bytes 393224 | tf_op jit(solution)/shard_map/ppermute | solution.py:530
  72.0 20.5 %collective-permute-start.10 = (bf16[256,256]{1,0:T(8,128)(2,1)S(1)}, bf16[256,256]{1,0:T(8,128)(2,1)S(1)}, u32[]{:S(2)}, u32[]{:S(2)}) collective-permute-start(bf16[256,256]{1,0:T(8,128)(2,1)S(1)} %get-tuple-element.64), channel_id=1, source_target_pairs={{0,3},{1,2},{2,1},{3,0},{4,7},{5,6},{6,5},{7,4},{8,11},{9,10},{10,... | collective-permute-start | bytes 393224 | tf_op jit(solution)/shard_map/ppermute | solution.py:530
  97.5 11.1 %copy-start.10 = (bf16[128,1024]{1,0:T(8,128)(2,1)S(1)}, bf16[128,1024]{1,0:T(8,128)(2,1)}, u32[]{:S(2)}) copy-start(bf16[128,1024]{1,0:T(8,128)(2,1)} %copy-done.8) | copy-start | bytes 786436
  97.5 52.1 %copy-start.12 = (bf16[256,1024]{1,0:T(8,128)(2,1)S(1)}, bf16[256,1024]{1,0:T(8,128)(2,1)}, u32[]{:S(2)}) copy-start(bf16[256,1024]{1,0:T(8,128)(2,1)} %refs_5_.7) | copy-start | bytes 1572868
  100.9 3.4 %collective-permute-start.13 = (f32[1,256]{1,0:T(1,128)S(1)}, f32[1,256]{1,0:T(1,128)S(1)}, u32[]{:S(2)}, u32[]{:S(2)}) collective-permute-start(f32[1,256]{1,0:T(1,128)S(1)} %get-tuple-element.73.refs_6_), channel_id=1, source_target_pairs={{0,16},{4,20},{8,24},{12,28},{16,0},{20,4},{24,8},{28,12},{1,17},{... | collective-permute-start | bytes 3080 | tf_op jit(solution)/shard_map/ppermute | solution.py:530
  104.3 45.4 %slice-start = ((s8[4718592]{0:T(1024)(128)(4,1)}), s8[4194304]{0:T(1024)(128)(4,1)S(1)}, s32[]{:S(2)}) async-start(s8[4718592]{0:T(1024)(128)(4,1)} %bitcast.8), calls=%async_computation.2 | async-start | bytes 8388608
  104.3 45.4 %slice-start.1 = ((s8[4718592]{0:T(1024)(128)(4,1)}), s8[524288]{0:T(1024)(128)(4,1)S(1)}, s32[]{:S(2)}) async-start(s8[4718592]{0:T(1024)(128)(4,1)} %bitcast.8), calls=%async_computation.3 | async-start | bytes 1048576
  104.3 45.4 %copy-start.7 = (bf16[1280,1024]{1,0:T(8,128)(2,1)S(1)}, bf16[1280,1024]{1,0:T(8,128)(2,1)}, u32[]{:S(2)}) copy-start(bf16[1280,1024]{1,0:T(8,128)(2,1)} %copy-done.6) | copy-start | bytes 7864324
  106.2 43.4 %copy-start.5 = (f32[3,1024,256]{2,1,0:T(8,128)S(1)}, f32[3,1024,256]{2,1,0:T(8,128)}, u32[]{:S(2)}) copy-start(f32[3,1024,256]{2,1,0:T(8,128)} %copy-done.4) | copy-start | bytes 9437188
  106.2 25.0 %collective-permute-start.14 = (bf16[256,1024]{1,0:T(8,128)(2,1)S(1)}, bf16[256,1024]{1,0:T(8,128)(2,1)S(1)}, u32[]{:S(2)}, u32[]{:S(2)}) collective-permute-start(bf16[256,1024]{1,0:T(8,128)(2,1)S(1)} %get-tuple-element.75), channel_id=1, source_target_pairs={{0,16},{4,20},{8,24},{12,28},{16,0},{20,4},{24,8},{28,12},{1,17},{... | collective-permute-start | bytes 1572872 | tf_op jit(solution)/shard_map/ppermute | solution.py:530
  108.5 16.6 %collective-permute-start.22 = (bf16[128,1024]{1,0:T(8,128)(2,1)S(1)}, bf16[128,1024]{1,0:T(8,128)(2,1)S(1)}, u32[]{:S(2)}, u32[]{:S(2)}) collective-permute-start(bf16[128,1024]{1,0:T(8,128)(2,1)S(1)} %get-tuple-element.66.refs_4_.refs_0_.refs_1_), channel_id=1, source_target_pairs={{0,8},{4,12},{8,0},{12,4},{16,24},{20,28},{24,16},{28,20},{1,9},{5... | collective-permute-start | bytes 786440 | tf_op jit(solution)/shard_map/ppermute | solution.py:530
  108.6 23.1 %collective-permute-start.25 = (bf16[128,1024]{1,0:T(8,128)(2,1)S(1)}, bf16[128,1024]{1,0:T(8,128)(2,1)S(1)}, u32[]{:S(2)}, u32[]{:S(2)}) collective-permute-start(bf16[128,1024]{1,0:T(8,128)(2,1)S(1)} %copy-done.10), channel_id=1, source_target_pairs={{0,8},{4,12},{8,0},{12,4},{16,24},{20,28},{24,16},{28,20},{1,9},{5... | collective-permute-start | bytes 786440 | tf_op jit(solution)/shard_map/ppermute | solution.py:530
  109.9 24.4 %collective-permute-start.21 = (bf16[128,1024]{1,0:T(8,128)(2,1)S(1)}, bf16[128,1024]{1,0:T(8,128)(2,1)S(1)}, u32[]{:S(2)}, u32[]{:S(2)}) collective-permute-start(bf16[128,1024]{1,0:T(8,128)(2,1)S(1)} %get-tuple-element.66.refs_4_.refs_0_.refs_1_), channel_id=1, source_target_pairs={{0,4},{4,0},{8,12},{12,8},{16,20},{20,16},{24,28},{28,24},{1,5},{5... | collective-permute-start | bytes 786440 | tf_op jit(solution)/shard_map/ppermute | solution.py:530
  112.7 21.8 %collective-permute-start.24 = (bf16[128,1024]{1,0:T(8,128)(2,1)S(1)}, bf16[128,1024]{1,0:T(8,128)(2,1)S(1)}, u32[]{:S(2)}, u32[]{:S(2)}) collective-permute-start(bf16[128,1024]{1,0:T(8,128)(2,1)S(1)} %copy-done.10), channel_id=1, source_target_pairs={{0,4},{4,0},{8,12},{12,8},{16,20},{20,16},{24,28},{28,24},{1,5},{5... | collective-permute-start | bytes 786440 | tf_op jit(solution)/shard_map/ppermute | solution.py:530
  125.0 11.2 %collective-permute-start.23 = (bf16[128,1024]{1,0:T(8,128)(2,1)S(1)}, bf16[128,1024]{1,0:T(8,128)(2,1)S(1)}, u32[]{:S(2)}, u32[]{:S(2)}) collective-permute-start(bf16[128,1024]{1,0:T(8,128)(2,1)S(1)} %collective-permute-done.22.refs_3_), channel_id=1, source_target_pairs={{0,4},{4,0},{8,12},{12,8},{16,20},{20,16},{24,28},{28,24},{1,5},{5... | collective-permute-start | bytes 786440 | tf_op jit(solution)/shard_map/ppermute | solution.py:530
  131.6 14.7 %collective-permute-start.16 = (bf16[256,1024]{1,0:T(8,128)(2,1)S(1)}, bf16[256,1024]{1,0:T(8,128)(2,1)S(1)}, u32[]{:S(2)}, u32[]{:S(2)}) collective-permute-start(bf16[256,1024]{1,0:T(8,128)(2,1)S(1)} %shard_map.110.refs_1_), channel_id=1, source_target_pairs={{0,2},{1,3},{2,0},{3,1},{4,6},{5,7},{6,4},{7,5},{8,10},{9,11},{10,... | collective-permute-start | bytes 1572872 | tf_op jit(solution)/shard_map/ppermute | solution.py:530
  131.7 9.2 %collective-permute-start.26 = (bf16[128,1024]{1,0:T(8,128)(2,1)S(1)}, bf16[128,1024]{1,0:T(8,128)(2,1)S(1)}, u32[]{:S(2)}, u32[]{:S(2)}) collective-permute-start(bf16[128,1024]{1,0:T(8,128)(2,1)S(1)} %collective-permute-done.25.refs_7_), channel_id=1, source_target_pairs={{0,4},{4,0},{8,12},{12,8},{16,20},{20,16},{24,28},{28,24},{1,5},{5... | collective-permute-start | bytes 786440 | tf_op jit(solution)/shard_map/ppermute | solution.py:530
  134.4 7.2 %collective-permute-start.27 = (bf16[16,1024]{1,0:T(8,128)(2,1)S(1)}, bf16[16,1024]{1,0:T(8,128)(2,1)S(1)}, u32[]{:S(2)}, u32[]{:S(2)}) collective-permute-start(bf16[16,1024]{1,0:T(8,128)(2,1)S(1)} %get-tuple-element.83.refs_9_), channel_id=1, source_target_pairs={{0,4},{4,0},{8,12},{12,8},{16,20},{20,16},{24,28},{28,24},{1,5},{5... | collective-permute-start | bytes 98312 | tf_op jit(solution)/shard_map/ppermute | solution.py:530
  134.4 7.2 %collective-permute-start.28 = (bf16[16,1024]{1,0:T(8,128)(2,1)S(1)}, bf16[16,1024]{1,0:T(8,128)(2,1)S(1)}, u32[]{:S(2)}, u32[]{:S(2)}) collective-permute-start(bf16[16,1024]{1,0:T(8,128)(2,1)S(1)} %get-tuple-element.83.refs_9_), channel_id=1, source_target_pairs={{0,8},{4,12},{8,0},{12,4},{16,24},{20,28},{24,16},{28,20},{1,9},{5... | collective-permute-start | bytes 98312 | tf_op jit(solution)/shard_map/ppermute | solution.py:530
  136.3 5.3 %collective-permute-start.29 = (bf16[16,1024]{1,0:T(8,128)(2,1)S(1)}, bf16[16,1024]{1,0:T(8,128)(2,1)S(1)}, u32[]{:S(2)}, u32[]{:S(2)}) collective-permute-start(bf16[16,1024]{1,0:T(8,128)(2,1)S(1)} %get-tuple-element.83.refs_9_), channel_id=1, source_target_pairs={{0,12},{4,8},{8,4},{12,0},{16,28},{20,24},{24,20},{28,16},{1,13},{... | collective-permute-start | bytes 98312 | tf_op jit(solution)/shard_map/ppermute | solution.py:530
  144.0 17.2 %collective-permute-start.30 = (bf16[384,1024]{1,0:T(8,128)(2,1)S(1)}, bf16[384,1024]{1,0:T(8,128)(2,1)S(1)}, u32[]{:S(2)}, u32[]{:S(2)}) collective-permute-start(bf16[384,1024]{1,0:T(8,128)(2,1)S(1)} %get-tuple-element.85), channel_id=1, source_target_pairs={{0,1},{1,0},{2,3},{3,2},{4,5},{5,4},{6,7},{7,6},{8,9},{9,8},{10,11... | collective-permute-start | bytes 2359304 | tf_op jit(solution)/shard_map/ppermute | solution.py:530
  146.2 2.7 %collective-permute-start.15 = (bf16[256,1024]{1,0:T(8,128)(2,1)S(1)}, bf16[256,1024]{1,0:T(8,128)(2,1)S(1)}, u32[]{:S(2)}, u32[]{:S(2)}) collective-permute-start(bf16[256,1024]{1,0:T(8,128)(2,1)S(1)} %shard_map.110.refs_1_), channel_id=1, source_target_pairs={{0,1},{1,0},{2,3},{3,2},{4,5},{5,4},{6,7},{7,6},{8,9},{9,8},{10,11... | collective-permute-start | bytes 1572872 | tf_op jit(solution)/shard_map/ppermute | solution.py:530
  146.3 3.3 %collective-permute-start.17 = (bf16[256,1024]{1,0:T(8,128)(2,1)S(1)}, bf16[256,1024]{1,0:T(8,128)(2,1)S(1)}, u32[]{:S(2)}, u32[]{:S(2)}) collective-permute-start(bf16[256,1024]{1,0:T(8,128)(2,1)S(1)} %collective-permute-done.16.refs_3_), channel_id=1, source_target_pairs={{0,1},{1,0},{2,3},{3,2},{4,5},{5,4},{6,7},{7,6},{8,9},{9,8},{10,11... | collective-permute-start | bytes 1572872 | tf_op jit(solution)/shard_map/ppermute | solution.py:530
  146.7 19.1 %collective-permute-start.31 = (bf16[384,1024]{1,0:T(8,128)(2,1)S(1)}, bf16[384,1024]{1,0:T(8,128)(2,1)S(1)}, u32[]{:S(2)}, u32[]{:S(2)}) collective-permute-start(bf16[384,1024]{1,0:T(8,128)(2,1)S(1)} %get-tuple-element.86), channel_id=1, source_target_pairs={{0,2},{1,3},{2,0},{3,1},{4,6},{5,7},{6,4},{7,5},{8,10},{9,11},{10,... | collective-permute-start | bytes 2359304 | tf_op jit(solution)/shard_map/ppermute | solution.py:530
  147.2 35.7 %collective-permute-start.32 = (bf16[384,1024]{1,0:T(8,128)(2,1)S(1)}, bf16[384,1024]{1,0:T(8,128)(2,1)S(1)}, u32[]{:S(2)}, u32[]{:S(2)}) collective-permute-start(bf16[384,1024]{1,0:T(8,128)(2,1)S(1)} %get-tuple-element.98), channel_id=1, source_target_pairs={{0,3},{1,2},{2,1},{3,0},{4,7},{5,6},{6,5},{7,4},{8,11},{9,10},{10,... | collective-permute-start | bytes 2359304 | tf_op jit(solution)/shard_map/ppermute | solution.py:530
  158.6 9.6 %collective-permute-start.18 = (bf16[5,128,256]{2,1,0:T(8,128)(2,1)S(1)}, bf16[5,128,256]{2,1,0:T(8,128)(2,1)S(1)}, u32[]{:S(2)}, u32[]{:S(2)}) collective-permute-start(bf16[5,128,256]{2,1,0:T(8,128)(2,1)S(1)} %get-tuple-element.80), channel_id=1, source_target_pairs={{0,4},{4,0},{8,12},{12,8},{16,20},{20,16},{24,28},{28,24},{1,5},{5... | collective-permute-start | bytes 983048 | tf_op jit(solution)/shard_map/ppermute | solution.py:530
  160.4 8.6 %collective-permute-start.19 = (bf16[5,128,256]{2,1,0:T(8,128)(2,1)S(1)}, bf16[5,128,256]{2,1,0:T(8,128)(2,1)S(1)}, u32[]{:S(2)}, u32[]{:S(2)}) collective-permute-start(bf16[5,128,256]{2,1,0:T(8,128)(2,1)S(1)} %get-tuple-element.81), channel_id=1, source_target_pairs={{0,8},{4,12},{8,0},{12,4},{16,24},{20,28},{24,16},{28,20},{1,9},{5... | collective-permute-start | bytes 983048 | tf_op jit(solution)/shard_map/ppermute | solution.py:530
  161.2 14.9 %collective-permute-start.20 = (bf16[5,128,256]{2,1,0:T(8,128)(2,1)S(1)}, bf16[5,128,256]{2,1,0:T(8,128)(2,1)S(1)}, u32[]{:S(2)}, u32[]{:S(2)}) collective-permute-start(bf16[5,128,256]{2,1,0:T(8,128)(2,1)S(1)} %get-tuple-element.82), channel_id=1, source_target_pairs={{0,12},{4,8},{8,4},{12,0},{16,28},{20,24},{24,20},{28,16},{1,13},{... | collective-permute-start | bytes 983048 | tf_op jit(solution)/shard_map/ppermute | solution.py:530
  176.2 6.7 %copy-start.2 = (bf16[512,1024]{1,0:T(8,128)(2,1)S(1)}, bf16[512,1024]{1,0:T(8,128)(2,1)}, u32[]{:S(2)}) copy-start(bf16[512,1024]{1,0:T(8,128)(2,1)} %refs_1_.3) | copy-start | bytes 3145732
  (13 other events, 12.7 us)
